TPU v7x, 32 devices: a whole 2x2x4 slice. The times are simulated.
32 devices in a mesh: row: 8 (over z, x), col: 4 (over y, core).
Axes of the slice: x: 2, y: 2, z: 4, core: 2. Of those that a mesh axis runs over, the one named last changes fastest.
Arguments:
- leaf_mass: bfloat16 [32, 2048, 2048], P(('row', 'col')), as said below
- tile_mask: int32 [32, 16, 16], P(('row', 'col')), may hold values from 0 to 1, as said below
- constraint_modes: bfloat16 [32, 2048, 1024], P(('row', 'col')), may hold values from -0.125 to 0.125
- leaf_fixed_modes: bfloat16 [32, 2048, 128], P(('row', 'col')), may hold values from -6 to 6
- block_map: int32 [32, 2, 4], P(('row', 'col')), may hold values from 0 to 3, each once within a row
- group_mass: float32 [4, 512, 512], P('col', 'row'), as said below
- top_mass: float32 [512, 512], P(('row', 'col')), as said below
- group_basis: float32 [4, 512, 128], P('col', 'row'), may hold values from -6 to 6
- top_basis: float32 [512, 128], P('row'), may hold values from -6 to 6
Outputs:
- coupling: float32 [32, 128, 2, 128], P(('row', 'col'))
- group_modes: float32 [4, 512, 128], P('col', 'row')
- top_modes: float32 [512, 128], P('row')
- group_assembled: float32 [4, 512, 512], P('col', 'row')
- apex_gathered_mass: float32 [512, 512], P(('row', 'col'))
Inputs may be any that keep to these rules, and one draw needn't show every extreme that they name: `tile_mask`: symmetric in its two tile indices, with ones on the diagonal tiles. block_map[l, k] is a permutation of the 4 separator blocks. `leaf_mass`: each leaf's matrix is symmetric and strictly diagonally dominant with a positive diagonal. `group_mass`: each group's matrix is symmetric and strictly diagonally dominant with a positive diagonal. `top_mass`: symmetric and strictly diagonally dominant with a positive diagonal.
All inputs are finite; a program needn't handle non-finite values.
Results may differ from a plain program's by a relative error of at most 0.0029.
Values sent between devices are 32-bit elements; how exact they have to be, the bound alone decides.
No kernel may reach another device: no remote copies, remote signals or barrier semaphores. Data moves between devices by JAX's collectives and lax.ppermute only.
A program may use at most 128 MiB of HBM per device.

v0:
```python
import jax
import jax.numpy as jnp
from jax import lax
from jax.sharding import PartitionSpec as P

TILE = 128
SEP = 512
SEP_BLOCK = 128


def contract_product(left_side, right_side):
    return lax.dot_general(
        left_side, right_side, (((0,), (0,)), ((), ())), preferred_element_type=jnp.float32
    )


def to_separator(partial_value, ordering):
    block_count = SEP // SEP_BLOCK
    inverse = jnp.argsort(ordering)
    blocks = partial_value.reshape(block_count, SEP_BLOCK, block_count, SEP_BLOCK)
    blocks = blocks[inverse][:, :, inverse]
    return blocks.reshape(SEP, SEP)


def to_leaf(mode_rows, ordering):
    block_count = SEP // SEP_BLOCK
    blocks = mode_rows.reshape(block_count, SEP_BLOCK, mode_rows.shape[1])
    return blocks[ordering].reshape(SEP, mode_rows.shape[1])


def gram_terms(matrix_rows, basis_rows, basis_whole):
    applied = jnp.dot(matrix_rows, basis_whole, precision=lax.Precision.HIGHEST)
    return jnp.dot(basis_rows.T, applied, precision=lax.Precision.HIGHEST)


def from_gram(gram_matrix, basis_whole):
    gram_matrix = 0.5 * (gram_matrix + gram_matrix.T)
    lower_factor = jnp.linalg.cholesky(gram_matrix)
    return lax.linalg.triangular_solve(
        lower_factor, basis_whole, left_side=False, lower=True, transpose_a=True
    )


def placed(piece, start):
    empty = jnp.zeros((SEP, SEP), jnp.float32)
    return lax.dynamic_update_slice(empty, piece, (start, jnp.int32(0)))


def body(
    leaf_mass,
    tile_mask,
    constraint_modes,
    leaf_fixed_modes,
    block_map,
    group_mass,
    top_mass,
    group_basis,
    top_basis,
):
    leaf_matrix = leaf_mass[0]
    leaf_rows = leaf_matrix.shape[0]
    tile_count = tile_mask.shape[1]
    chosen = tile_mask[0].astype(jnp.bfloat16)
    masked = (
        leaf_matrix.reshape(tile_count, TILE, tile_count, TILE) * chosen[:, None, :, None]
    ).reshape(leaf_rows, leaf_rows)
    modes_c = constraint_modes[0]
    loaded = jnp.dot(masked, modes_c, preferred_element_type=jnp.float32).astype(jnp.bfloat16)
    partial_group = to_separator(
        contract_product(modes_c[:, :SEP], loaded[:, :SEP]), block_map[0, 0]
    )
    partial_top = to_separator(contract_product(modes_c[:, SEP:], loaded[:, SEP:]), block_map[0, 1])
    projected = contract_product(leaf_fixed_modes[0], loaded)
    line_fraction = group_mass.shape[1]
    top_share = top_mass.shape[0]
    whole_group, whole_top = (
        lax.all_gather(group_basis[0], "row", axis=0, tiled=True),
        lax.all_gather(top_basis, "row", axis=0, tiled=True),
    )
    row_index = lax.axis_index("row")
    col_index = lax.axis_index("col")
    col_count = lax.axis_size("col")
    group_rows = placed(group_mass[0], row_index * line_fraction)
    top_rows = placed(top_mass, (row_index * col_count + col_index) * top_share)
    matrix_group, rows_top = lax.psum((partial_group + group_rows, partial_top + top_rows), "row")
    matrix_top = lax.psum(rows_top, "col")
    gram_group = gram_terms(matrix_group, whole_group, whole_group)
    gram_top = gram_terms(matrix_top, whole_top, whole_top)
    group_kept = lax.dynamic_slice_in_dim(matrix_group, row_index * line_fraction, line_fraction, 0)
    top_kept = lax.dynamic_slice_in_dim(
        matrix_top, (row_index * col_count + col_index) * top_share, top_share, 0
    )
    modes_group = from_gram(gram_group, whole_group)
    modes_top = from_gram(gram_top, whole_top)
    first = jnp.dot(
        projected[:, :SEP], to_leaf(modes_group, block_map[0, 0]), precision=lax.Precision.HIGHEST
    )
    second = jnp.dot(
        projected[:, SEP:], to_leaf(modes_top, block_map[0, 1]), precision=lax.Precision.HIGHEST
    )
    coupling = jnp.stack([first, second], axis=1)[None]
    group_out = lax.dynamic_slice_in_dim(modes_group, row_index * line_fraction, line_fraction, 0)[
        None
    ]
    top_out = lax.dynamic_slice_in_dim(
        modes_top, row_index * top_basis.shape[0], top_basis.shape[0], 0
    )
    group_assembled = (SEP * group_kept)[None]
    apex_gathered_mass = SEP * top_kept
    return (coupling, group_out, top_out, group_assembled, apex_gathered_mass)


def solution(mesh):
    in_specs = (
        P(("row", "col"), None, None),
        P(("row", "col"), None, None),
        P(("row", "col"), None, None),
        P(("row", "col"), None, None),
        P(("row", "col"), None, None),
        P("col", "row", None),
        P(("row", "col"), None),
        P("col", "row", None),
        P("row", None),
    )
    out_specs = (
        P(("row", "col"), None, None, None),
        P("col", "row", None),
        P("row", None),
        P("col", "row", None),
        P(("row", "col"), None),
    )
    return jax.shard_map(body, mesh=mesh, in_specs=in_specs, out_specs=out_specs, check_vma=False)
```

profile of v0, /device:TPU:0, one launch (start us, length us, event | category | flops | bytes accessed | tf_op | source)
XLA Modules:
  0.0 267.0 jit_solution(6607677572128687832)
XLA Ops:
  7.2 0.0 copy-start
  7.2 0.0 all-reduce.6.cloned.1.call-start
  7.2 0.7 convert_bitcast_fusion
  8.0 4.4 %mul.46 = bf16[16,128,16,128]{3,2,1,0:T(8,128)(2,1)} broadcast(bf16[16,16]{1,0:T(8,128)(2,1)S(1)} %convert_bitcast_fusion), dimensions={0,2} | broadcast | bytes 8389120 | tf_op jit(solution)/shard_map/mul | solution.py:65
  12.4 13.3 %mul.47 = bf16[1,2048,2048]{2,1,0:T(8,128)(2,1)} reshape(bf16[16,128,16,128]{3,2,1,0:T(8,128)(2,1)} %mul.46) | data formatting | bytes 16777216 | tf_op jit(solution)/shard_map/mul | solution.py:65
  25.7 15.9 %fusion.3 = bf16[2048,1024]{1,0:T(8,128)(2,1)S(1)} fusion(bf16[1,2048,2048]{2,1,0:T(8,128)(2,1)} %param.12, bf16[1,2048,2048]{2,1,0:T(8,128)(2,1)} %mul.47, bf16[1,2048,1024]{2,1,0:T(8,128)(2,1)} %param.14), kind=kOutput, calls=%fused_computation.9 | convolution fusion | flops 8596226048 | bytes 25165824 | tf_op jit(solution)/shard_map/dot_general | solution.py:68
  41.6 1.3 fusion.17
  42.9 0.0 copy-start.8
  42.9 2.3 fusion.12
  45.2 0.7 sort.32
  45.9 0.7 sort.31
  46.7 0.4 reshape.121
  47.0 0.4 copy.38
  47.4 0.6 gather_fusion.3
  48.0 0.6 gather_fusion.4
  48.7 0.7 copy.39
  49.3 0.1 copy.52
  49.4 1.6 reshape.116
  51.0 1.3 copy.33
  52.3 1.9 gather_fusion
  54.3 1.6 gather_fusion.1
  55.8 1.9 copy.34
  57.7 0.1 copy.53
  57.9 0.9 copy-done.3
  58.9 0.3 copy-done.2
  59.2 0.0 all-reduce.6.cloned.1.call-update
  59.2 0.0 all-reduce.4.cloned.1.call-start
  59.3 34.5 %all-gather = f32[1,512,128]{2,1,0:T(8,128)S(1)} all-gather(f32[1,64,128]{2,1,0:T(8,128)S(1)} %copy-done.6), channel_id=2, replica_groups=mesh['row'=8,'col'=4] {'row'}, dimensions={1}, use_global_device_ids=true | all-gather | bytes 294912 | tf_op jit(solution)/shard_map/all_gather | solution.py:77
  93.8 31.3 %all_gather.7 = f32[512,128]{1,0:T(8,128)S(1)} all-gather(f32[64,128]{1,0:T(8,128)S(1)} %copy-done.7), channel_id=1, replica_groups=mesh['row'=8,'col'=4] {'row'}, dimensions={0}, use_global_device_ids=true | all-gather | bytes 294912 | tf_op jit(solution)/shard_map/all_gather | solution.py:78
  125.1 3.5 %convolution_bitcast_fusion = f32[128,1024]{0,1:T(8,128)S(1)} fusion(bf16[2048,1024]{1,0:T(8,128)(2,1)} %copy-done.1, bf16[1,2048,128]{2,1,0:T(8,128)(2,1)S(1)} %copy-done), kind=kOutput, calls=%fused_computation.18 | convolution fusion | flops 536870912 | bytes 5242880 | tf_op jit(solution)/shard_map/dot_general | solution.py:12
  128.6 38.8 %all-reduce.6.cloned.1.call-done = (f32[512,512]{1,0:T(8,128)}, f32[512,512]{1,0:T(8,128)}) async-done(((f32[512,512]{1,0:T(8,128)}, f32[512,512]{1,0:T(8,128)}), (f32[512,512]{1,0:T(8,128)}, f32[512,512]{1,0:T(8,128)})) %all-reduce.6.cloned.1.call-update) | async-done | bytes 2097168 | tf_op jit(solution)/shard_map/psum | solution.py:85
  167.4 2.2 fusion.28
  169.6 0.6 fusion.26
  170.2 0.1 copy.35
  170.3 0.1 copy.36
  170.5 11.7 %cholesky.44 = f32[128,128]{1,0:T(8,128)S(1)} custom-call(f32[128,128]{1,0:T(8,128)S(1)} %fusion.37), custom_call_target="Cholesky" | custom-call | tf_op jit(solution)/shard_map/jit(cholesky)/cholesky | solution.py:38
  182.2 0.6 compare_reduce_fusion.1
  182.8 0.7 fusion.31
  183.5 9.8 %custom-call.6 = f32[1,128,128]{1,2,0:T(8,128)S(1)} custom-call(f32[1,128,128]{2,1,0:T(8,128)S(1)} %fusion.31), custom_call_target="InvertDiagBlocksLowerTriangular" | custom-call | tf_op jit(solution)/shard_map/triangular_solve/custom-call.0 | solution.py:39
  193.3 0.0 all-reduce.4.cloned.1.call-update
  193.3 0.4 convolution_bitcast_fusion.2
  193.8 0.1 copy.46
  193.9 0.1 constant_dynamic-slice_fusion.1
  194.0 0.7 copy.43
  194.7 0.6 gather_fusion.2
  195.3 1.6 multiply_bitcast_fusion
  196.8 0.6 convolution_bitcast_fusion.4
  197.4 31.9 %all-reduce.4.cloned.1.call-done = f32[512,512]{1,0:T(8,128)} async-done(((f32[512,512]{1,0:T(8,128)}), f32[512,512]{1,0:T(8,128)}) %all-reduce.4.cloned.1.call-update) | async-done | bytes 1048592 | tf_op jit(solution)/shard_map/psum | solution.py:86
  229.4 2.2 fusion.42
  231.6 0.6 fusion.43
  232.2 0.1 copy.40
  232.3 0.1 copy.41
  232.4 11.9 %cholesky.55 = f32[128,128]{1,0:T(8,128)S(1)} custom-call(f32[128,128]{1,0:T(8,128)S(1)} %fusion.34), custom_call_target="Cholesky" | custom-call | tf_op jit(solution)/shard_map/jit(cholesky)/cholesky | solution.py:38
  244.3 0.6 compare_reduce_fusion
  245.0 0.7 fusion.32
  245.6 9.8 %custom-call.7 = f32[1,128,128]{1,2,0:T(8,128)S(1)} custom-call(f32[1,128,128]{2,1,0:T(8,128)S(1)} %fusion.32), custom_call_target="InvertDiagBlocksLowerTriangular" | custom-call | tf_op jit(solution)/shard_map/triangular_solve/custom-call.0 | solution.py:39
  255.5 0.4 convolution_bitcast_fusion.1
  255.9 0.1 copy.47
  256.0 0.1 constant_dynamic-slice_fusion
  256.1 0.6 gather_fusion.5
  256.7 0.6 convolution_bitcast_fusion.3
  257.3 0.8 copy.44
  258.1 0.7 copy.45
  258.8 1.4 dynamic-slice_multiply_fusion
  (33 shorter events, 0.3 us)
Async XLA Ops:
  7.2 117.9 %copy-start = (bf16[1,2048,128]{2,1,0:T(8,128)(2,1)S(1)}, bf16[1,2048,128]{2,1,0:T(8,128)(2,1)}, u32[]{:S(2)}) copy-start(bf16[1,2048,128]{2,1,0:T(8,128)(2,1)} %param.15) | copy-start | bytes 1572868
  7.2 160.2 %all-reduce.6.cloned.1.call-start = ((), (), s32[]{:S(2)}) async-start(), calls=%async_computation.1 | async-start | bytes 4194304 | tf_op jit(solution)/shard_map/psum | solution.py:85
  25.7 15.9 %copy-start.9 = (bf16[1,2048,1024]{2,1,0:T(8,128)(2,1)S(1)}, bf16[1,2048,1024]{2,1,0:T(8,128)(2,1)}, u32[]{:S(2)}) copy-start(bf16[1,2048,1024]{2,1,0:T(8,128)(2,1)} %param.14) | copy-start | bytes 12582916
  41.6 3.6 %copy-start.1 = (bf16[2048,1024]{1,0:T(8,128)(2,1)}, bf16[2048,1024]{1,0:T(8,128)(2,1)S(1)}, u32[]{:S(2)}) copy-start(bf16[2048,1024]{1,0:T(8,128)(2,1)S(1)} %fusion.3) | copy-start | bytes 12582916
  42.9 2.3 copy-start.8
  52.3 5.5 %copy-start.5 = (f32[16,512]{1,0:T(8,128)S(1)}, f32[16,512]{1,0:T(8,128)}, u32[]{:S(2)}) copy-start(f32[16,512]{1,0:T(8,128)} %param.18) | copy-start | bytes 98308
  52.3 5.5 %copy-start.4 = (f32[1,64,512]{2,1,0:T(8,128)S(1)}, f32[1,64,512]{2,1,0:T(8,128)}, u32[]{:S(2)}) copy-start(f32[1,64,512]{2,1,0:T(8,128)} %param.17) | copy-start | bytes 393220
  54.2 5.1 %copy-start.6 = (f32[1,64,128]{2,1,0:T(8,128)S(1)}, f32[1,64,128]{2,1,0:T(8,128)}, u32[]{:S(2)}) copy-start(f32[1,64,128]{2,1,0:T(8,128)} %param.19) | copy-start | bytes 98308
  54.2 39.6 %copy-start.7 = (f32[64,128]{1,0:T(8,128)S(1)}, f32[64,128]{1,0:T(8,128)}, u32[]{:S(2)}) copy-start(f32[64,128]{1,0:T(8,128)} %param.20) | copy-start | bytes 98308
  57.9 1.0 copy-start.3
  57.9 1.3 copy-start.2
  59.2 170.1 %all-reduce.4.cloned.1.call-start = ((), (), s32[]{:S(2)}) async-start(), calls=%async_computation | async-start | bytes 2097152 | tf_op jit(solution)/shard_map/psum | solution.py:86
Sparse Core Ops, SparseCore 0:
  59.3 108.0 all-reduce.5
  193.5 35.8 all-reduce.3
where the time goes:
time: 268 us; the launch traced here: 267 us
  waiting for transfers between devices  70.8 us (26%)
  blocking collectives  65.8 us (25%)
  other arithmetic  51.2 us (19%)
  local copies, waits for them, and re-layouts  34.1 us (13%)
  matrix products  30.5 us (11%)
  between operations  14.5 us (5%)
    psum x1, waiting for transfers between devices, body(): lax.psum((partial_group + group_rows, partial_top + top_rows), 'row')  38.8 us
    all_gather x1, blocking collectives, body(): lax.all_gather(group_basis[0], 'row', axis=0, tiled=True)  34.5 us
    psum x1, waiting for transfers between devices, body(): matrix_top = lax.psum(rows_top, 'col')  31.9 us
    all_gather x1, blocking collectives, body(): lax.all_gather(top_basis, 'row', axis=0, tiled=True)  31.3 us
    another operation x6, other arithmetic, from_gram(): lower_factor = jnp.linalg.cholesky(gram_matrix)  25 us
    another operation x4, other arithmetic, from_gram(): lax.linalg.triangular_solve(lower_factor, basis_whole, left_side=False, l...  20.9 us
    mul x2, local copies, waits for them, and re-layouts, body(): leaf_matrix.reshape(tile_count, TILE, tile_count, TILE)  17.7 us
    dot_general x1, matrix products, body(): jnp.dot(masked, modes_c, preferred_element_type=jnp.float32)  15.9 us
  transfers between devices with their start and end apart: 2, of which 2 were waited for; matrix products, arithmetic and copies ran while one was open for 3% of the time, Pallas kernels for 0%

commit v1 on v0

v1 whole, which is shorter than its diff:
```python
import functools

import jax
import jax.numpy as jnp
from jax import lax
from jax.experimental import pallas as pl
from jax.experimental.pallas import tpu as pltpu
from jax.sharding import PartitionSpec as P

TILE = 128
LANES = 128
SUBLANES = 8
F32 = jnp.float32
BF16 = jnp.bfloat16
EXACT = lax.Precision.HIGHEST
VMEM = pl.BlockSpec(memory_space=pltpu.VMEM)
SMEM = pl.BlockSpec(memory_space=pltpu.SMEM)


def params(megabytes):
    return pltpu.CompilerParams(vmem_limit_bytes=megabytes * 2**20)


def turned(count, step):
    return [(i, (i + step) % count) for i in range(count)]


def crossed(count, bit):
    return [(i, i ^ bit) for i in range(count)]


def rows_first(left, right, precision=None):
    return lax.dot_general(
        left, right, (((0,), (0,)), ((), ())), precision=precision, preferred_element_type=F32
    )


def add_own(ref, own, place):
    share = own.shape[0]
    if share % SUBLANES == 0:
        window = pl.ds(pl.multiple_of(place * share, SUBLANES), share)
        ref[window, :] += own
        return
    fold = SUBLANES // share
    wide = jnp.concatenate([own] * fold, axis=0)
    line = lax.broadcasted_iota(jnp.int32, wide.shape, 0) // share
    window = pl.ds(pl.multiple_of(place // fold * SUBLANES, SUBLANES), SUBLANES)
    ref[window, :] += jnp.where(line == place % fold, wide, 0.0)


def copy_rows(target_ref, start, source_ref, place, share):
    if share % SUBLANES == 0:
        window = pl.ds(pl.multiple_of(place * share, SUBLANES), share)
        target_ref[start : start + share, :] = source_ref[window, :]
        return
    for i in range(share):
        target_ref[start + i : start + i + 1, :] = source_ref[pl.ds(place * share + i, 1), :]


def leaf_kernel(
    half, row_count, col_count, place_ref, mask_ref, map_ref, mass_ref, modes_ref, fixed_ref,
    own_ref, *refs,
):
    whole_ref, moved_ref, chunks = refs[0], refs[1], refs[2:-2]
    partial_ref, projected_ref = refs[-2:]
    step = pl.program_id(0)
    height, width = mass_ref.shape[1], mass_ref.shape[2]
    lines = []
    for a in range(height // TILE):
        pieces = []
        for b in range(width // TILE):
            kept = mask_ref[0, step * (height // TILE) + a, b]
            piece = mass_ref[0, a * TILE : (a + 1) * TILE, b * TILE : (b + 1) * TILE]
            pieces.append(jnp.where(kept != 0, piece, jnp.zeros_like(piece)))
        lines.append(jnp.concatenate(pieces, axis=1))
    masked = jnp.concatenate(lines, axis=0)
    loaded = jnp.dot(masked, modes_ref[0], preferred_element_type=F32).astype(BF16)
    window = pl.ds(pl.multiple_of(step * height, height), height)
    partial = rows_first(modes_ref[0, window, :], loaded)
    projected = rows_first(fixed_ref[0], loaded)

    @pl.when(step == 0)
    def _():
        partial_ref[...] = partial
        projected_ref[...] = projected

    @pl.when(step > 0)
    def _():
        partial_ref[...] += partial
        projected_ref[...] += projected

    @pl.when(step == pl.num_programs(0) - 1)
    def _():
        size = whole_ref.shape[0]
        blocks = map_ref.shape[2]
        block = size // blocks
        to = [pl.multiple_of(map_ref[0, half, a] * block, block) for a in range(blocks)]
        for b in range(blocks):
            source = slice(b * block, (b + 1) * block)
            moved_ref[:, pl.ds(to[b], block)] = projected_ref[:, source]
            for a in range(blocks):
                whole_ref[pl.ds(to[a], block), pl.ds(to[b], block)] = partial_ref[
                    a * block : (a + 1) * block, source
                ]
        row, col = place_ref[0], place_ref[1]
        if half == 0:
            own = own_ref[0]
            place = row
        else:
            own = own_ref[...]
            place = row * col_count + col
        add_own(whole_ref, own, place)
        share = own.shape[0]
        for k, chunk in enumerate(chunks):
            for r in range(chunk.shape[0] // share):
                if half == 0:
                    at = 2 * r + lax.rem(row + k, 2)
                else:
                    at = r * col_count + lax.rem(col + k, col_count)
                copy_rows(chunk, r * share, whole_ref, at, share)


def leaf_half(half, place, tile_mask, block_map, leaf_mass, constraint_modes, fixed, own, counts):
    row_count, col_count = counts
    rows, size = constraint_modes.shape[1], constraint_modes.shape[2] // 2
    modes = fixed.shape[2]
    height = 2 * TILE
    chunk_count = 2 if half == 0 else col_count
    chunk = jax.ShapeDtypeStruct((size // chunk_count, size), F32)
    own_block = (1,) + own.shape[1:] if own.ndim == 3 else own.shape
    outs = [jax.ShapeDtypeStruct((size, size), F32), jax.ShapeDtypeStruct((modes, size), F32)]
    outs += [chunk] * chunk_count
    return pl.pallas_call(
        functools.partial(leaf_kernel, half, row_count, col_count),
        grid=(rows // height,),
        in_specs=[
            SMEM,
            SMEM,
            SMEM,
            pl.BlockSpec((1, height, rows), lambda i: (0, i, 0)),
            pl.BlockSpec((1, rows, size), lambda i: (0, 0, half)),
            pl.BlockSpec((1, height, modes), lambda i: (0, i, 0)),
            pl.BlockSpec(own_block, lambda i: (0,) * len(own_block)),
        ],
        out_specs=[pl.BlockSpec(o.shape, lambda i: (0, 0)) for o in outs],
        out_shape=outs,
        scratch_shapes=[pltpu.VMEM((size, size), F32), pltpu.VMEM((modes, size), F32)],
        compiler_params=params(48),
        cost_estimate=pl.CostEstimate(
            flops=2 * rows * size * (rows + size + modes),
            bytes_accessed=2 * rows * (rows + size + modes) + 8 * size * size,
            transcendentals=0,
        ),
        name="leaf_group" if half == 0 else "leaf_top",
    )(place, tile_mask, block_map, leaf_mass, constraint_modes, fixed, own)


def prepare_kernel(count, place_ref, group_ref, top_ref, first_ref, second_ref, *refs):
    pieces, (packed_ref, terms_ref, basis_ref) = refs[:count], refs[count:]
    row = place_ref[0]
    line = pieces[0].shape[0]
    modes = terms_ref.shape[2]
    for k, piece in enumerate(pieces):
        at = pl.multiple_of(lax.rem(row + count - k, count) * line, line)
        basis_ref[pl.ds(at, line), :] = piece[...]
    grams = []
    for half, (matrix_ref, moved_ref) in enumerate(((group_ref, first_ref), (top_ref, second_ref))):
        basis = basis_ref[:, half * modes : (half + 1) * modes]
        applied = jnp.dot(matrix_ref[...], basis, precision=EXACT, preferred_element_type=F32)
        gram = rows_first(basis, applied, EXACT)
        grams.append(0.5 * (gram + gram.T))
        terms_ref[half] = jnp.dot(
            moved_ref[...], basis, precision=EXACT, preferred_element_type=F32
        )
    down = lax.broadcasted_iota(jnp.int32, (modes, modes), 0)
    across = lax.broadcasted_iota(jnp.int32, (modes, modes), 1)
    packed_ref[:modes, :] = jnp.where(down >= across, grams[0], grams[1])
    diagonal = jnp.sum(jnp.where(down == across, grams[1], 0.0), axis=0, keepdims=True)
    packed_ref[modes:, :] = jnp.broadcast_to(diagonal, (SUBLANES, modes))


def prepare(place, group, top, first, second, pieces):
    modes = first.shape[0]
    size = group.shape[0]
    return pl.pallas_call(
        functools.partial(prepare_kernel, len(pieces)),
        in_specs=[SMEM] + [VMEM] * (4 + len(pieces)),
        out_specs=[VMEM, VMEM],
        out_shape=[
            jax.ShapeDtypeStruct((modes + SUBLANES, modes), F32),
            jax.ShapeDtypeStruct((2, modes, modes), F32),
        ],
        scratch_shapes=[pltpu.VMEM((size, 2 * modes), F32)],
        compiler_params=params(32),
        cost_estimate=pl.CostEstimate(
            flops=24 * size * size * modes, bytes_accessed=12 * size * size, transcendentals=0
        ),
        name="prepare",
    )(place, group, top, first, second, *pieces)


def factor(matrices):
    size = matrices[0].shape[0]
    width = SUBLANES
    down = lax.broadcasted_iota(jnp.int32, (size, size), 0)
    across = lax.broadcasted_iota(jnp.int32, (size, size), 1)
    line = lax.broadcasted_iota(jnp.int32, (width, size), 0)
    lane = lax.broadcasted_iota(jnp.int32, (width, size), 1)
    states = list(matrices)
    diagonals = [[] for _ in matrices]
    for start in range(0, size, width):
        stop = start + width
        for m, state in enumerate(states):
            spread = [
                jnp.broadcast_to(state[:, start + q : start + q + 1], (size, size))
                for q in range(width)
            ]
            strip = state[start:stop, :]
            small = [s[start:stop, :] for s in spread]
            scaled = []
            rest = strip
            for q in range(width):
                scale = lax.rsqrt(small[q][q : q + 1, :])
                tail = [small[t][q : q + 1, :] * scale for t in range(q + 1, width)]
                level = rest[q : q + 1, :] * scale
                rest = rest - small[q] * (scale * level)
                small[q] = jnp.where(line == q, 1.0, small[q]) * scale
                for t in range(q + 1, width):
                    small[t] = jnp.where(line == q, 0.0, small[t]) - small[q] * tail[t - q - 1]
                scaled.append(level)
            small = [jnp.where(line <= q, s, 0.0) for q, s in enumerate(small)]
            solved = small[0] * scaled[0]
            for q in range(1, width):
                solved = solved + small[q] * scaled[q]
            solved = jnp.where(lane >= stop, solved, 0.0)
            update = spread[0] * solved[0:1, :]
            for q in range(1, width):
                update = update + spread[q] * solved[q : q + 1, :]
            block = jnp.where(lane == line + start, 1.0, 0.0)
            kept = jnp.where(lane < start, strip, block) - solved
            parts = []
            if start > 0:
                parts.append(state[:start] - update[:start])
            parts.append(kept)
            if stop < size:
                parts.append(state[stop:] - update[stop:])
            states[m] = jnp.concatenate(parts, axis=0)
            diagonal = jnp.zeros((width, size), F32)
            for q in range(width):
                diagonal = jnp.where(lane == start + q, small[q], diagonal)
            diagonals[m].append(diagonal)
    uppers = [jnp.where(across >= down, state, 0.0) for state in states]
    return uppers, [jnp.concatenate(d, axis=0) for d in diagonals]


def finish_kernel(near_ref, far_ref, terms_ref, basis_ref, coupling_ref, group_ref, top_ref):
    modes = near_ref.shape[1]
    down = lax.broadcasted_iota(jnp.int32, (modes, modes), 0)
    across = lax.broadcasted_iota(jnp.int32, (modes, modes), 1)
    near, far = near_ref[:modes, :], far_ref[:modes, :]
    group = jnp.where(down >= across, near, near.T)
    top = jnp.where(down > across, far.T, far)
    top = jnp.where(down == across, jnp.broadcast_to(far_ref[modes : modes + 1, :], top.shape), top)
    uppers, diagonals = factor([group, top])
    for half in range(2):
        inverse = jnp.dot(
            uppers[half], diagonals[half], precision=EXACT, preferred_element_type=F32
        )
        lane = slice(half * modes, (half + 1) * modes)
        coupling_ref[0, :, half, :] = jnp.dot(
            terms_ref[half], inverse, precision=EXACT, preferred_element_type=F32
        )
        rows = jnp.dot(basis_ref[:, lane], inverse, precision=EXACT, preferred_element_type=F32)
        if half == 0:
            group_ref[0] = rows
        else:
            top_ref[...] = rows


def finish(near, far, terms, basis):
    modes = near.shape[1]
    line = basis.shape[0]
    return pl.pallas_call(
        finish_kernel,
        in_specs=[VMEM] * 4,
        out_specs=[VMEM] * 3,
        out_shape=[
            jax.ShapeDtypeStruct((1, modes, 2, modes), F32),
            jax.ShapeDtypeStruct((1, line, modes), F32),
            jax.ShapeDtypeStruct((line, modes), F32),
        ],
        compiler_params=params(32),
        cost_estimate=pl.CostEstimate(
            flops=20 * modes**3, bytes_accessed=24 * modes * modes, transcendentals=2 * modes
        ),
        name="finish",
    )(near, far, terms, basis)


def merge_kernel(count, part, place_ref, *refs):
    pieces, chunks = refs[:count], refs[count:-1]
    total_ref = refs[-1]
    total = pieces[0][...]
    for piece in pieces[1:]:
        total = total + piece[...]
    total_ref[...] = total
    share = chunks[0].shape[0]
    for k, chunk in enumerate(chunks):
        at = lax.rem(place_ref[0] // part + k, len(chunks))
        copy_rows(chunk, 0, total_ref, at, share)


def merge(place, pieces, chunk_count, part):
    rows, size = pieces[0].shape
    chunk = jax.ShapeDtypeStruct((rows // chunk_count, size), F32)
    return pl.pallas_call(
        functools.partial(merge_kernel, len(pieces), part),
        in_specs=[SMEM] + [VMEM] * len(pieces),
        out_specs=[VMEM] * chunk_count,
        out_shape=[chunk] * chunk_count,
        scratch_shapes=[pltpu.VMEM((rows, size), F32)],
        compiler_params=params(32),
        cost_estimate=pl.CostEstimate(
            flops=len(pieces) * rows * size,
            bytes_accessed=4 * (len(pieces) + 1) * rows * size,
            transcendentals=0,
        ),
        name="merge",
    )(place, *pieces)


def body(
    leaf_mass, tile_mask, constraint_modes, leaf_fixed_modes, block_map, group_mass, top_mass,
    group_basis, top_basis,
):
    row_count, col_count = lax.axis_size("row"), lax.axis_size("col")
    place = jnp.stack([lax.axis_index("row"), lax.axis_index("col")]).astype(jnp.int32)
    counts = (row_count, col_count)
    size = group_mass.shape[2]
    basis = jnp.concatenate([group_basis[0], top_basis], axis=1)
    pieces = [basis] + [
        lax.ppermute(basis, "row", turned(row_count, k)) for k in range(1, row_count)
    ]

    def half_of(half, own):
        return leaf_half(
            half, place, tile_mask, block_map, leaf_mass, constraint_modes, leaf_fixed_modes, own,
            counts,
        )

    group_whole, first, group_keep, group_send = half_of(0, group_mass)
    group_other = lax.ppermute(group_send, "row", crossed(row_count, 1))
    top_whole, second, *top_chunks = half_of(1, top_mass)
    packed, terms = prepare(place, group_whole, top_whole, first, second, pieces)

    near = packed
    bit = 1
    while bit < row_count:
        near = near + lax.ppermute(near, "row", crossed(row_count, bit))
        bit *= 2
    far = near
    bit = 1
    while bit < col_count:
        far = far + lax.ppermute(far, "col", crossed(col_count, bit))
        bit *= 2
    coupling, group_modes, top_modes = finish(near, far, terms, basis)

    lines = row_count // 2
    group_chunks = merge(place, [group_keep, group_other], lines, 2)
    group_total = group_chunks[0]
    for k in range(1, lines):
        group_total = group_total + lax.ppermute(
            group_chunks[k], "row", turned(row_count, 2 * k)
        )
    top_other = [
        lax.ppermute(top_chunks[k], "col", turned(col_count, k)) for k in range(1, col_count)
    ]
    top_chunks = merge(place, [top_chunks[0]] + top_other, row_count, 1)
    top_total = top_chunks[0]
    for k in range(1, row_count):
        top_total = top_total + lax.ppermute(top_chunks[k], "row", turned(row_count, k))
    return coupling, group_modes, top_modes, (size * group_total)[None], size * top_total


def solution(mesh):
    leaf = P(("row", "col"), None, None)
    group = P("col", "row", None)
    in_specs = (
        leaf, leaf, leaf, leaf, leaf, group, P(("row", "col"), None), group, P("row", None),
    )
    out_specs = (
        P(("row", "col"), None, None, None), group, P("row", None), group, P(("row", "col"), None),
    )
    return jax.shard_map(body, mesh=mesh, in_specs=in_specs, out_specs=out_specs, check_vma=False)
```

time: 268 us -> 94.4 us (0.35)
  blocking collectives: 65.8 us -> 0 us
  waiting for transfers between devices: 70.8 us -> 12.2 us
  other arithmetic: 51.2 us -> 2.24 us
  Pallas kernels: 0 us -> 37.7 us
  starting transfers between devices: 0.08 us -> 37.5 us
  local copies, waits for them, and re-layouts: 34.1 us -> 3.32 us
  matrix products: 30.5 us -> 0 us
  between operations: 14.5 us -> 0.79 us
    psum x2 -> x0, waiting for transfers between devices: 70.7 us -> none  [the longest x1 38.8 us: body(): lax.psum((partial_group + group_rows, partial_top + top_rows), 'row')]
    all_gather x2 -> x0, blocking collectives: 65.8 us -> none  [the longest x1 34.5 us: body(): lax.all_gather(group_basis[0], 'row', axis=0, tiled=True)]
    another operation x10 -> x1, other arithmetic: 45.9 us -> 0.07 us  [body(): jnp.stack([lax.axis_index('row'), lax.axis_index('col')]).astype(jnp.int32)]
    pallas_call x0 -> x6, Pallas kernels: none -> 37.7 us  [the longest x2 23.3 us: leaf_half(): pl.pallas_call(functools.partial(leaf_kernel, half, row_count, col_count)...]
    ppermute x0 -> x26, starting transfers between devices: none -> 37.5 us  [the longest x7 12.4 us: body(): lax.ppermute(basis, 'row', turned(row_count, k))]
    dot_general x10 -> x0, matrix products: 29.7 us -> none  [the longest x1 15.9 us: body(): jnp.dot(masked, modes_c, preferred_element_type=jnp.float32)]
    mul x4 -> x0, local copies, waits for them, and re-layouts: 17.8 us -> none  [the longest x2 17.7 us: body(): leaf_matrix.reshape(tile_count, TILE, tile_count, TILE)]
    ppermute x0 -> x26, waiting for transfers between devices: none -> 12.2 us  [the longest x3 10.3 us: body(): near = near + lax.ppermute(near, 'row', crossed(row_count, bit))]
  transfers between devices with their start and end apart: 2 -> 26, of which waited for: 2 -> 4; matrix products, arithmetic and copies ran while one was open for 3% -> 1% of each run, Pallas kernels for 0% -> 40%
where the time goes in v1:
time: 94.4 us; the launch traced here: 93.8 us
  Pallas kernels  37.7 us (40%)
  starting transfers between devices  37.5 us (40%)
  waiting for transfers between devices  12.2 us (13%)
  local copies, waits for them, and re-layouts  3.32 us (4%)
  other arithmetic  2.24 us (2%)
    pallas_call x2, Pallas kernels, leaf_half(): pl.pallas_call(functools.partial(leaf_kernel, half, row_count, col_count)...  23.3 us
    ppermute x7, starting transfers between devices, body(): lax.ppermute(basis, 'row', turned(row_count, k))  12.4 us
    ppermute x3, waiting for transfers between devices, body(): near = near + lax.ppermute(near, 'row', crossed(row_count, bit))  10.3 us
    ppermute x7, starting transfers between devices, body(): lax.ppermute(top_chunks[k], 'row', turned(row_count, k))  10.1 us
    pallas_call x1, Pallas kernels, finish(): pl.pallas_call(finish_kernel, in_specs=[VMEM] * 4, out_specs=[VMEM] * 3,...  7.45 us
    pallas_call x1, Pallas kernels, prepare(): pl.pallas_call(functools.partial(prepare_kernel, len(pieces)), in_specs=[...  5.7 us
    ppermute x3, starting transfers between devices, body(): lax.ppermute(group_chunks[k], 'row', turned(row_count, 2 * k))  5.15 us
    ppermute x3, starting transfers between devices, body(): near = near + lax.ppermute(near, 'row', crossed(row_count, bit))  4.24 us
  transfers between devices with their start and end apart: 26, of which 4 were waited for; matrix products, arithmetic and copies ran while one was open for 1% of the time, Pallas kernels for 40%

profile of v1, /device:TPU:0, one launch (start us, length us, event | category | flops | bytes accessed | tf_op | source)
XLA Modules:
  0.0 93.8 jit_solution(7008615170834666757)
XLA Ops:
  0.6 0.8 pad_maximum_fusion.refs_0_.basis_ref
  1.4 6.0 %collective-permute-start.6 = (f32[64,256]{1,0:T(8,128)S(1)}, f32[64,256]{1,0:T(8,128)S(1)}, u32[]{:S(2)}, u32[]{:S(2)}) collective-permute-start(f32[64,256]{1,0:T(8,128)S(1)} %pad_maximum_fusion.refs_0_.basis_ref), channel_id=1, source_target_pairs={{0,28},{4,0},{8,4},{12,8},{16,12},{20,16},{24,20},{28,24},{1,29},{... | collective-permute-start | bytes 196616 | tf_op jit(solution)/shard_map/ppermute | solution.py:342
  7.4 0.4 collective-permute-start.5
  7.8 0.0 collective-permute-start.4
  7.8 3.0 %collective-permute-start.3 = (f32[64,256]{1,0:T(8,128)S(1)}, f32[64,256]{1,0:T(8,128)S(1)}, u32[]{:S(2)}, u32[]{:S(2)}) collective-permute-start(f32[64,256]{1,0:T(8,128)S(1)} %pad_maximum_fusion.refs_0_.basis_ref), channel_id=1, source_target_pairs={{0,16},{4,20},{8,24},{12,28},{16,0},{20,4},{24,8},{28,12},{1,17},{... | collective-permute-start | bytes 196616 | tf_op jit(solution)/shard_map/ppermute | solution.py:342
  10.9 0.0 collective-permute-start.2
  10.9 0.1 pad_add_fusion.place_ref
  10.9 1.0 %copy-done = bf16[1,2048,128]{2,1,0:T(8,128)(2,1)S(1)} copy-done((bf16[1,2048,128]{2,1,0:T(8,128)(2,1)S(1)}, bf16[1,2048,128]{2,1,0:T(8,128)(2,1)}, u32[]{:S(2)}) %copy-start) | copy-done | bytes 524312
  12.0 0.9 copy-done.1
  12.9 0.7 copy-done.3
  13.6 0.7 copy-done.4
  14.3 11.7 %leaf_group.1 = (f32[512,512]{1,0:T(8,128)S(1)}, f32[128,512]{1,0:T(8,128)S(1)}, f32[256,512]{1,0:T(8,128)S(1)}, f32[256,512]{1,0:T(8,128)S(1)}) custom-call(s32[2]{0:T(128)S(1)} %pad_add_fusion.place_ref, s32[1,16,16]{2,1,0:T(8,128)S(1)} %copy-done.3, s32[1,2,4]{2,1,0:T(2,128)S(1)} %copy-done.4, bf16[1,2048,2048]{2,1,0:T(8,128)(2,1)} %mass_ref.3, ...), custom_call_target="tpu_custom_call" | custom-call | flops 5637144576 | bytes 13107200 | tf_op jit(solution)/shard_map/leaf_group/pallas_call | solution.py:133
  25.9 0.0 collective-permute-done.6.refs_7_
  25.9 1.9 %collective-permute-start.1 = (f32[64,256]{1,0:T(8,128)S(1)}, f32[64,256]{1,0:T(8,128)S(1)}, u32[]{:S(2)}, u32[]{:S(2)}) collective-permute-start(f32[64,256]{1,0:T(8,128)S(1)} %pad_maximum_fusion.refs_0_.basis_ref), channel_id=1, source_target_pairs={{0,8},{4,12},{8,16},{12,20},{16,24},{20,28},{24,0},{28,4},{1,9},{5... | collective-permute-start | bytes 196616 | tf_op jit(solution)/shard_map/ppermute | solution.py:342
  27.8 0.0 collective-permute-done.5.refs_6_
  27.8 1.1 %collective-permute-start = (f32[64,256]{1,0:T(8,128)S(1)}, f32[64,256]{1,0:T(8,128)S(1)}, u32[]{:S(2)}, u32[]{:S(2)}) collective-permute-start(f32[64,256]{1,0:T(8,128)S(1)} %pad_maximum_fusion.refs_0_.basis_ref), channel_id=1, source_target_pairs={{0,4},{4,8},{8,12},{12,16},{16,20},{20,24},{24,28},{28,0},{1,5},{5... | collective-permute-start | bytes 196616 | tf_op jit(solution)/shard_map/ppermute | solution.py:342
  28.9 0.0 collective-permute-done.4.refs_5_
  28.9 1.9 %collective-permute-start.12 = (f32[256,512]{1,0:T(8,128)S(1)}, f32[256,512]{1,0:T(8,128)S(1)}, u32[]{:S(2)}, u32[]{:S(2)}) collective-permute-start(f32[256,512]{1,0:T(8,128)S(1)} %get-tuple-element.42), channel_id=1, source_target_pairs={{0,4},{4,0},{8,12},{12,8},{16,20},{20,16},{24,28},{28,24},{1,5},{5... | collective-permute-start | bytes 1572872 | tf_op jit(solution)/shard_map/ppermute | solution.py:352
  30.9 11.6 %leaf_top.1 = (f32[512,512]{1,0:T(8,128)S(1)}, f32[128,512]{1,0:T(8,128)S(1)}, f32[128,512]{1,0:T(8,128)S(1)}, f32[128,512]{1,0:T(8,128)S(1)}, f32[128,512]{1,0:T(8,128)S(1)}, /*index=5*/f32[128,512]{1,0:T(8,128)S(1)}) custom-call(s32[2]{0:T(128)S(1)} %pad_add_fusion.place_ref, s32[1,16,16]{2,1,0:T(8,128)S(1)} %copy-done.3, s32[1,2,4]{2,1,0:T(2,128)S(1)} %copy-done.4, ...), custom_call_target="tpu_custom_call" | custom-call | flops 5637144576 | bytes 13107200 | tf_op jit(solution)/shard_map/leaf_top/pallas_call | solution.py:133
  42.5 0.0 collective-permute-done.3.refs_4_
  42.5 0.1 collective-permute-start.16
  42.6 0.0 collective-permute-done.2.refs_3_
  42.6 1.6 %collective-permute-start.17 = (f32[128,512]{1,0:T(8,128)S(1)}, f32[128,512]{1,0:T(8,128)S(1)}, u32[]{:S(2)}, u32[]{:S(2)}) collective-permute-start(f32[128,512]{1,0:T(8,128)S(1)} %get-tuple-element.49), channel_id=1, source_target_pairs={{0,2},{1,3},{2,0},{3,1},{4,6},{5,7},{6,4},{7,5},{8,10},{9,11},{10,... | collective-permute-start | bytes 786440 | tf_op jit(solution)/shard_map/ppermute | solution.py:376
  44.2 0.0 collective-permute-done.1.refs_2_
  44.2 1.4 %collective-permute-start.18 = (f32[128,512]{1,0:T(8,128)S(1)}, f32[128,512]{1,0:T(8,128)S(1)}, u32[]{:S(2)}, u32[]{:S(2)}) collective-permute-start(f32[128,512]{1,0:T(8,128)S(1)} %get-tuple-element.50), channel_id=1, source_target_pairs={{0,3},{1,0},{2,1},{3,2},{4,7},{5,4},{6,5},{7,6},{8,11},{9,8},{10,9... | collective-permute-start | bytes 786440 | tf_op jit(solution)/shard_map/ppermute | solution.py:376
  45.6 0.0 collective-permute-done.refs_1_
  45.6 5.7 %prepare.1 = (f32[136,128]{1,0:T(8,128)S(1)}, f32[2,128,128]{2,1,0:T(8,128)S(1)}) custom-call(s32[2]{0:T(128)S(1)} %pad_add_fusion.place_ref, f32[512,512]{1,0:T(8,128)S(1)} %get-tuple-element.32.group_ref, f32[512,512]{1,0:T(8,128)S(1)} %get-tuple-element.33.top_ref, f32[128,512]{1,0:T(8,128)S(1)} %get-tuple-element.34.first_ref, ...), custom_call_target="tpu_custom_call" | custom-call | flops 805306368 | bytes 3145728 | tf_op jit(solution)/shard_map/prepare/pallas_call | solution.py:185
  51.3 0.2 collective-permute-start.7
  51.5 4.2 %collective-permute-done.7 = f32[136,128]{1,0:T(8,128)S(1)} collective-permute-done((f32[136,128]{1,0:T(8,128)S(1)}, f32[136,128]{1,0:T(8,128)S(1)}, u32[]{:S(2)}, u32[]{:S(2)}) %collective-permute-start.7) | collective-permute-done | bytes 69664 | tf_op jit(solution)/shard_map/ppermute | solution.py:359
  55.7 2.5 %collective-permute-start.8 = (f32[136,128]{1,0:T(8,128)S(1)}, f32[136,128]{1,0:T(8,128)S(1)}, u32[]{:S(2)}, u32[]{:S(2)}) collective-permute-start(f32[136,128]{1,0:T(8,128)S(1)} %add.45), channel_id=1, source_target_pairs={{0,8},{4,12},{8,0},{12,4},{16,24},{20,28},{24,16},{28,20},{1,9},{5... | collective-permute-start | bytes 208904 | tf_op jit(solution)/shard_map/ppermute | solution.py:359
  58.2 2.3 %collective-permute-done.8 = f32[136,128]{1,0:T(8,128)S(1)} collective-permute-done((f32[136,128]{1,0:T(8,128)S(1)}, f32[136,128]{1,0:T(8,128)S(1)}, u32[]{:S(2)}, u32[]{:S(2)}) %collective-permute-start.8) | collective-permute-done | bytes 69664 | tf_op jit(solution)/shard_map/ppermute | solution.py:359
  60.5 1.6 %collective-permute-start.9 = (f32[136,128]{1,0:T(8,128)S(1)}, f32[136,128]{1,0:T(8,128)S(1)}, u32[]{:S(2)}, u32[]{:S(2)}) collective-permute-start(f32[136,128]{1,0:T(8,128)S(1)} %add.46), channel_id=1, source_target_pairs={{0,16},{4,20},{8,24},{12,28},{16,0},{20,4},{24,8},{28,12},{1,17},{... | collective-permute-start | bytes 208904 | tf_op jit(solution)/shard_map/ppermute | solution.py:359
  62.1 3.7 %collective-permute-done.9 = f32[136,128]{1,0:T(8,128)S(1)} collective-permute-done((f32[136,128]{1,0:T(8,128)S(1)}, f32[136,128]{1,0:T(8,128)S(1)}, u32[]{:S(2)}, u32[]{:S(2)}) %collective-permute-start.9) | collective-permute-done | bytes 69664 | tf_op jit(solution)/shard_map/ppermute | solution.py:359
  65.8 0.1 collective-permute-start.10
  65.9 0.0 collective-permute-done.16.refs_1_
  65.9 0.0 collective-permute-done.17.refs_2_
  65.9 0.0 collective-permute-done.18.refs_3_
  65.9 0.6 merge.3
  66.6 0.1 collective-permute-start.19
  66.7 2.5 %collective-permute-start.20 = (f32[16,512]{1,0:T(8,128)S(1)}, f32[16,512]{1,0:T(8,128)S(1)}, u32[]{:S(2)}, u32[]{:S(2)}) collective-permute-start(f32[16,512]{1,0:T(8,128)S(1)} %get-tuple-element.53), channel_id=1, source_target_pairs={{0,8},{4,12},{8,16},{12,20},{16,24},{20,28},{24,0},{28,4},{1,9},{5... | collective-permute-start | bytes 98312 | tf_op jit(solution)/shard_map/ppermute | solution.py:381
  69.2 2.2 %collective-permute-start.21 = (f32[16,512]{1,0:T(8,128)S(1)}, f32[16,512]{1,0:T(8,128)S(1)}, u32[]{:S(2)}, u32[]{:S(2)}) collective-permute-start(f32[16,512]{1,0:T(8,128)S(1)} %get-tuple-element.54), channel_id=1, source_target_pairs={{0,12},{4,16},{8,20},{12,24},{16,28},{20,0},{24,4},{28,8},{1,13},{... | collective-permute-start | bytes 98312 | tf_op jit(solution)/shard_map/ppermute | solution.py:381
  71.3 1.9 %collective-permute-done.19 = f32[16,512]{1,0:T(8,128)S(1)} collective-permute-done((f32[16,512]{1,0:T(8,128)S(1)}, f32[16,512]{1,0:T(8,128)S(1)}, u32[]{:S(2)}, u32[]{:S(2)}) %collective-permute-start.19) | collective-permute-done | bytes 32800 | tf_op jit(solution)/shard_map/ppermute | solution.py:381
  73.3 1.2 %collective-permute-start.22 = (f32[16,512]{1,0:T(8,128)S(1)}, f32[16,512]{1,0:T(8,128)S(1)}, u32[]{:S(2)}, u32[]{:S(2)}) collective-permute-start(f32[16,512]{1,0:T(8,128)S(1)} %get-tuple-element.55), channel_id=1, source_target_pairs={{0,16},{4,20},{8,24},{12,28},{16,0},{20,4},{24,8},{28,12},{1,17},{... | collective-permute-start | bytes 98312 | tf_op jit(solution)/shard_map/ppermute | solution.py:381
  74.4 0.0 collective-permute-done.20
  74.4 0.5 collective-permute-start.23
  74.9 0.0 collective-permute-done.10
  74.9 2.3 %collective-permute-start.24 = (f32[16,512]{1,0:T(8,128)S(1)}, f32[16,512]{1,0:T(8,128)S(1)}, u32[]{:S(2)}, u32[]{:S(2)}) collective-permute-start(f32[16,512]{1,0:T(8,128)S(1)} %get-tuple-element.57), channel_id=1, source_target_pairs={{0,24},{4,28},{8,0},{12,4},{16,8},{20,12},{24,16},{28,20},{1,25},{... | collective-permute-start | bytes 98312 | tf_op jit(solution)/shard_map/ppermute | solution.py:381
  77.2 0.0 collective-permute-done.12.refs_1_
  77.2 1.4 %collective-permute-start.25 = (f32[16,512]{1,0:T(8,128)S(1)}, f32[16,512]{1,0:T(8,128)S(1)}, u32[]{:S(2)}, u32[]{:S(2)}) collective-permute-start(f32[16,512]{1,0:T(8,128)S(1)} %get-tuple-element.58), channel_id=1, source_target_pairs={{0,28},{4,0},{8,4},{12,8},{16,12},{20,16},{24,20},{28,24},{1,29},{... | collective-permute-start | bytes 98312 | tf_op jit(solution)/shard_map/ppermute | solution.py:381
  78.6 0.6 merge.2
  79.3 0.0 collective-permute-done.21
  79.3 0.6 collective-permute-start.11
  79.8 0.0 collective-permute-done.22
  79.8 2.0 %collective-permute-start.13 = (f32[64,512]{1,0:T(8,128)S(1)}, f32[64,512]{1,0:T(8,128)S(1)}, u32[]{:S(2)}, u32[]{:S(2)}) collective-permute-start(f32[64,512]{1,0:T(8,128)S(1)} %get-tuple-element.44), channel_id=1, source_target_pairs={{0,8},{4,12},{8,16},{12,20},{16,24},{20,28},{24,0},{28,4},{1,9},{5... | collective-permute-start | bytes 393224 | tf_op jit(solution)/shard_map/ppermute | solution.py:372
  81.8 0.0 collective-permute-done.23
  81.8 0.3 collective-permute-start.14
  82.1 0.0 collective-permute-done.24
  82.1 2.9 %collective-permute-start.15 = (f32[64,512]{1,0:T(8,128)S(1)}, f32[64,512]{1,0:T(8,128)S(1)}, u32[]{:S(2)}, u32[]{:S(2)}) collective-permute-start(f32[64,512]{1,0:T(8,128)S(1)} %get-tuple-element.46), channel_id=1, source_target_pairs={{0,24},{4,28},{8,0},{12,4},{16,8},{20,12},{24,16},{28,20},{1,25},{... | collective-permute-start | bytes 393224 | tf_op jit(solution)/shard_map/ppermute | solution.py:372
  85.0 0.6 add_multiply_fusion
  85.7 7.5 %finish.1 = (f32[1,128,2,128]{3,2,1,0:T(2,128)}, f32[1,64,128]{2,1,0:T(8,128)}, f32[64,128]{1,0:T(8,128)}) custom-call(f32[136,128]{1,0:T(8,128)S(1)} %add.47.near_ref, f32[136,128]{1,0:T(8,128)S(1)} %add.49.far_ref, f32[2,128,128]{2,1,0:T(8,128)S(1)} %get-tuple-element.37.terms_ref, f32[64,256]{1,0:T(8,128)S(1)} %pad_maximum_fusion.refs_0_.basis_ref), custom_call_target="tpu_custom_call" | custom-call | flops 41943040 | bytes 393216 | tf_op jit(solution)/shard_map/finish/pallas_call | solution.py:283
  93.1 0.0 collective-permute-done.13
  93.1 0.0 collective-permute-done.14
  93.1 0.0 collective-permute-done.15
  93.1 0.7 multiply_bitcast_fusion
  (13 shorter events, 0.1 us)
Async XLA Ops:
  1.4 24.5 %collective-permute-start.6 = (f32[64,256]{1,0:T(8,128)S(1)}, f32[64,256]{1,0:T(8,128)S(1)}, u32[]{:S(2)}, u32[]{:S(2)}) collective-permute-start(f32[64,256]{1,0:T(8,128)S(1)} %pad_maximum_fusion.refs_0_.basis_ref), channel_id=1, source_target_pairs={{0,28},{4,0},{8,4},{12,8},{16,12},{20,16},{24,20},{28,24},{1,29},{... | collective-permute-start | bytes 196616 | tf_op jit(solution)/shard_map/ppermute | solution.py:342
  7.4 20.4 %collective-permute-start.5 = (f32[64,256]{1,0:T(8,128)S(1)}, f32[64,256]{1,0:T(8,128)S(1)}, u32[]{:S(2)}, u32[]{:S(2)}) collective-permute-start(f32[64,256]{1,0:T(8,128)S(1)} %pad_maximum_fusion.refs_0_.basis_ref), channel_id=1, source_target_pairs={{0,24},{4,28},{8,0},{12,4},{16,8},{20,12},{24,16},{28,20},{1,25},{... | collective-permute-start | bytes 196616 | tf_op jit(solution)/shard_map/ppermute | solution.py:342
  7.8 21.1 %collective-permute-start.4 = (f32[64,256]{1,0:T(8,128)S(1)}, f32[64,256]{1,0:T(8,128)S(1)}, u32[]{:S(2)}, u32[]{:S(2)}) collective-permute-start(f32[64,256]{1,0:T(8,128)S(1)} %pad_maximum_fusion.refs_0_.basis_ref), channel_id=1, source_target_pairs={{0,20},{4,24},{8,28},{12,0},{16,4},{20,8},{24,12},{28,16},{1,21},{... | collective-permute-start | bytes 196616 | tf_op jit(solution)/shard_map/ppermute | solution.py:342
  7.8 34.7 %collective-permute-start.3 = (f32[64,256]{1,0:T(8,128)S(1)}, f32[64,256]{1,0:T(8,128)S(1)}, u32[]{:S(2)}, u32[]{:S(2)}) collective-permute-start(f32[64,256]{1,0:T(8,128)S(1)} %pad_maximum_fusion.refs_0_.basis_ref), channel_id=1, source_target_pairs={{0,16},{4,20},{8,24},{12,28},{16,0},{20,4},{24,8},{28,12},{1,17},{... | collective-permute-start | bytes 196616 | tf_op jit(solution)/shard_map/ppermute | solution.py:342
  10.9 31.7 %collective-permute-start.2 = (f32[64,256]{1,0:T(8,128)S(1)}, f32[64,256]{1,0:T(8,128)S(1)}, u32[]{:S(2)}, u32[]{:S(2)}) collective-permute-start(f32[64,256]{1,0:T(8,128)S(1)} %pad_maximum_fusion.refs_0_.basis_ref), channel_id=1, source_target_pairs={{0,12},{4,16},{8,20},{12,24},{16,28},{20,0},{24,4},{28,8},{1,13},{... | collective-permute-start | bytes 196616 | tf_op jit(solution)/shard_map/ppermute | solution.py:342
  10.9 1.0 %copy-start = (bf16[1,2048,128]{2,1,0:T(8,128)(2,1)S(1)}, bf16[1,2048,128]{2,1,0:T(8,128)(2,1)}, u32[]{:S(2)}) copy-start(bf16[1,2048,128]{2,1,0:T(8,128)(2,1)} %fixed_ref.3) | copy-start | bytes 1572868
  12.0 0.9 copy-start.1
  12.9 0.7 copy-start.3
  13.6 0.7 copy-start.4
  14.3 16.6 %copy-start.2 = (f32[16,512]{1,0:T(8,128)S(1)}, f32[16,512]{1,0:T(8,128)}, u32[]{:S(2)}) copy-start(f32[16,512]{1,0:T(8,128)} %own_ref.3) | copy-start | bytes 98308
  25.9 18.3 %collective-permute-start.1 = (f32[64,256]{1,0:T(8,128)S(1)}, f32[64,256]{1,0:T(8,128)S(1)}, u32[]{:S(2)}, u32[]{:S(2)}) collective-permute-start(f32[64,256]{1,0:T(8,128)S(1)} %pad_maximum_fusion.refs_0_.basis_ref), channel_id=1, source_target_pairs={{0,8},{4,12},{8,16},{12,20},{16,24},{20,28},{24,0},{28,4},{1,9},{5... | collective-permute-start | bytes 196616 | tf_op jit(solution)/shard_map/ppermute | solution.py:342
  27.8 17.8 %collective-permute-start = (f32[64,256]{1,0:T(8,128)S(1)}, f32[64,256]{1,0:T(8,128)S(1)}, u32[]{:S(2)}, u32[]{:S(2)}) collective-permute-start(f32[64,256]{1,0:T(8,128)S(1)} %pad_maximum_fusion.refs_0_.basis_ref), channel_id=1, source_target_pairs={{0,4},{4,8},{8,12},{12,16},{16,20},{20,24},{24,28},{28,0},{1,5},{5... | collective-permute-start | bytes 196616 | tf_op jit(solution)/shard_map/ppermute | solution.py:342
  28.9 48.3 %collective-permute-start.12 = (f32[256,512]{1,0:T(8,128)S(1)}, f32[256,512]{1,0:T(8,128)S(1)}, u32[]{:S(2)}, u32[]{:S(2)}) collective-permute-start(f32[256,512]{1,0:T(8,128)S(1)} %get-tuple-element.42), channel_id=1, source_target_pairs={{0,4},{4,0},{8,12},{12,8},{16,20},{20,16},{24,28},{28,24},{1,5},{5... | collective-permute-start | bytes 1572872 | tf_op jit(solution)/shard_map/ppermute | solution.py:352
  42.5 23.4 %collective-permute-start.16 = (f32[128,512]{1,0:T(8,128)S(1)}, f32[128,512]{1,0:T(8,128)S(1)}, u32[]{:S(2)}, u32[]{:S(2)}) collective-permute-start(f32[128,512]{1,0:T(8,128)S(1)} %get-tuple-element.48), channel_id=1, source_target_pairs={{0,1},{1,2},{2,3},{3,0},{4,5},{5,6},{6,7},{7,4},{8,9},{9,10},{10,1... | collective-permute-start | bytes 786440 | tf_op jit(solution)/shard_map/ppermute | solution.py:376
  42.6 23.3 %collective-permute-start.17 = (f32[128,512]{1,0:T(8,128)S(1)}, f32[128,512]{1,0:T(8,128)S(1)}, u32[]{:S(2)}, u32[]{:S(2)}) collective-permute-start(f32[128,512]{1,0:T(8,128)S(1)} %get-tuple-element.49), channel_id=1, source_target_pairs={{0,2},{1,3},{2,0},{3,1},{4,6},{5,7},{6,4},{7,5},{8,10},{9,11},{10,... | collective-permute-start | bytes 786440 | tf_op jit(solution)/shard_map/ppermute | solution.py:376
  44.2 21.7 %collective-permute-start.18 = (f32[128,512]{1,0:T(8,128)S(1)}, f32[128,512]{1,0:T(8,128)S(1)}, u32[]{:S(2)}, u32[]{:S(2)}) collective-permute-start(f32[128,512]{1,0:T(8,128)S(1)} %get-tuple-element.50), channel_id=1, source_target_pairs={{0,3},{1,0},{2,1},{3,2},{4,7},{5,4},{6,5},{7,6},{8,11},{9,8},{10,9... | collective-permute-start | bytes 786440 | tf_op jit(solution)/shard_map/ppermute | solution.py:376
  51.3 4.4 %collective-permute-start.7 = (f32[136,128]{1,0:T(8,128)S(1)}, f32[136,128]{1,0:T(8,128)S(1)}, u32[]{:S(2)}, u32[]{:S(2)}) collective-permute-start(f32[136,128]{1,0:T(8,128)S(1)} %get-tuple-element.36), channel_id=1, source_target_pairs={{0,4},{4,0},{8,12},{12,8},{16,20},{20,16},{24,28},{28,24},{1,5},{5... | collective-permute-start | bytes 208904 | tf_op jit(solution)/shard_map/ppermute | solution.py:359
  55.7 4.9 %collective-permute-start.8 = (f32[136,128]{1,0:T(8,128)S(1)}, f32[136,128]{1,0:T(8,128)S(1)}, u32[]{:S(2)}, u32[]{:S(2)}) collective-permute-start(f32[136,128]{1,0:T(8,128)S(1)} %add.45), channel_id=1, source_target_pairs={{0,8},{4,12},{8,0},{12,4},{16,24},{20,28},{24,16},{28,20},{1,9},{5... | collective-permute-start | bytes 208904 | tf_op jit(solution)/shard_map/ppermute | solution.py:359
  60.5 5.3 %collective-permute-start.9 = (f32[136,128]{1,0:T(8,128)S(1)}, f32[136,128]{1,0:T(8,128)S(1)}, u32[]{:S(2)}, u32[]{:S(2)}) collective-permute-start(f32[136,128]{1,0:T(8,128)S(1)} %add.46), channel_id=1, source_target_pairs={{0,16},{4,20},{8,24},{12,28},{16,0},{20,4},{24,8},{28,12},{1,17},{... | collective-permute-start | bytes 208904 | tf_op jit(solution)/shard_map/ppermute | solution.py:359
  65.8 9.1 %collective-permute-start.10 = (f32[136,128]{1,0:T(8,128)S(1)}, f32[136,128]{1,0:T(8,128)S(1)}, u32[]{:S(2)}, u32[]{:S(2)}) collective-permute-start(f32[136,128]{1,0:T(8,128)S(1)} %add.47.near_ref), channel_id=1, source_target_pairs={{0,1},{1,0},{2,3},{3,2},{4,5},{5,4},{6,7},{7,6},{8,9},{9,8},{10,11... | collective-permute-start | bytes 208904 | tf_op jit(solution)/shard_map/ppermute | solution.py:364
  66.6 6.7 %collective-permute-start.19 = (f32[16,512]{1,0:T(8,128)S(1)}, f32[16,512]{1,0:T(8,128)S(1)}, u32[]{:S(2)}, u32[]{:S(2)}) collective-permute-start(f32[16,512]{1,0:T(8,128)S(1)} %get-tuple-element.52), channel_id=1, source_target_pairs={{0,4},{4,8},{8,12},{12,16},{16,20},{20,24},{24,28},{28,0},{1,5},{5... | collective-permute-start | bytes 98312 | tf_op jit(solution)/shard_map/ppermute | solution.py:381
  66.7 7.8 %collective-permute-start.20 = (f32[16,512]{1,0:T(8,128)S(1)}, f32[16,512]{1,0:T(8,128)S(1)}, u32[]{:S(2)}, u32[]{:S(2)}) collective-permute-start(f32[16,512]{1,0:T(8,128)S(1)} %get-tuple-element.53), channel_id=1, source_target_pairs={{0,8},{4,12},{8,16},{12,20},{16,24},{20,28},{24,0},{28,4},{1,9},{5... | collective-permute-start | bytes 98312 | tf_op jit(solution)/shard_map/ppermute | solution.py:381
  69.2 10.1 %collective-permute-start.21 = (f32[16,512]{1,0:T(8,128)S(1)}, f32[16,512]{1,0:T(8,128)S(1)}, u32[]{:S(2)}, u32[]{:S(2)}) collective-permute-start(f32[16,512]{1,0:T(8,128)S(1)} %get-tuple-element.54), channel_id=1, source_target_pairs={{0,12},{4,16},{8,20},{12,24},{16,28},{20,0},{24,4},{28,8},{1,13},{... | collective-permute-start | bytes 98312 | tf_op jit(solution)/shard_map/ppermute | solution.py:381
  73.3 6.6 %collective-permute-start.22 = (f32[16,512]{1,0:T(8,128)S(1)}, f32[16,512]{1,0:T(8,128)S(1)}, u32[]{:S(2)}, u32[]{:S(2)}) collective-permute-start(f32[16,512]{1,0:T(8,128)S(1)} %get-tuple-element.55), channel_id=1, source_target_pairs={{0,16},{4,20},{8,24},{12,28},{16,0},{20,4},{24,8},{28,12},{1,17},{... | collective-permute-start | bytes 98312 | tf_op jit(solution)/shard_map/ppermute | solution.py:381
  74.4 7.4 %collective-permute-start.23 = (f32[16,512]{1,0:T(8,128)S(1)}, f32[16,512]{1,0:T(8,128)S(1)}, u32[]{:S(2)}, u32[]{:S(2)}) collective-permute-start(f32[16,512]{1,0:T(8,128)S(1)} %get-tuple-element.56), channel_id=1, source_target_pairs={{0,20},{4,24},{8,28},{12,0},{16,4},{20,8},{24,12},{28,16},{1,21},{... | collective-permute-start | bytes 98312 | tf_op jit(solution)/shard_map/ppermute | solution.py:381
  74.9 7.2 %collective-permute-start.24 = (f32[16,512]{1,0:T(8,128)S(1)}, f32[16,512]{1,0:T(8,128)S(1)}, u32[]{:S(2)}, u32[]{:S(2)}) collective-permute-start(f32[16,512]{1,0:T(8,128)S(1)} %get-tuple-element.57), channel_id=1, source_target_pairs={{0,24},{4,28},{8,0},{12,4},{16,8},{20,12},{24,16},{28,20},{1,25},{... | collective-permute-start | bytes 98312 | tf_op jit(solution)/shard_map/ppermute | solution.py:381
  77.2 7.8 %collective-permute-start.25 = (f32[16,512]{1,0:T(8,128)S(1)}, f32[16,512]{1,0:T(8,128)S(1)}, u32[]{:S(2)}, u32[]{:S(2)}) collective-permute-start(f32[16,512]{1,0:T(8,128)S(1)} %get-tuple-element.58), channel_id=1, source_target_pairs={{0,28},{4,0},{8,4},{12,8},{16,12},{20,16},{24,20},{28,24},{1,29},{... | collective-permute-start | bytes 98312 | tf_op jit(solution)/shard_map/ppermute | solution.py:381
  79.3 6.4 %collective-permute-start.11 = (f32[136,128]{1,0:T(8,128)S(1)}, f32[136,128]{1,0:T(8,128)S(1)}, u32[]{:S(2)}, u32[]{:S(2)}) collective-permute-start(f32[136,128]{1,0:T(8,128)S(1)} %add.48), channel_id=1, source_target_pairs={{0,2},{1,3},{2,0},{3,1},{4,6},{5,7},{6,4},{7,5},{8,10},{9,11},{10,... | collective-permute-start | bytes 208904 | tf_op jit(solution)/shard_map/ppermute | solution.py:364
  79.8 13.3 %collective-permute-start.13 = (f32[64,512]{1,0:T(8,128)S(1)}, f32[64,512]{1,0:T(8,128)S(1)}, u32[]{:S(2)}, u32[]{:S(2)}) collective-permute-start(f32[64,512]{1,0:T(8,128)S(1)} %get-tuple-element.44), channel_id=1, source_target_pairs={{0,8},{4,12},{8,16},{12,20},{16,24},{20,28},{24,0},{28,4},{1,9},{5... | collective-permute-start | bytes 393224 | tf_op jit(solution)/shard_map/ppermute | solution.py:372
  81.8 11.3 %collective-permute-start.14 = (f32[64,512]{1,0:T(8,128)S(1)}, f32[64,512]{1,0:T(8,128)S(1)}, u32[]{:S(2)}, u32[]{:S(2)}) collective-permute-start(f32[64,512]{1,0:T(8,128)S(1)} %get-tuple-element.45), channel_id=1, source_target_pairs={{0,16},{4,20},{8,24},{12,28},{16,0},{20,4},{24,8},{28,12},{1,17},{... | collective-permute-start | bytes 393224 | tf_op jit(solution)/shard_map/ppermute | solution.py:372
  82.1 11.0 %collective-permute-start.15 = (f32[64,512]{1,0:T(8,128)S(1)}, f32[64,512]{1,0:T(8,128)S(1)}, u32[]{:S(2)}, u32[]{:S(2)}) collective-permute-start(f32[64,512]{1,0:T(8,128)S(1)} %get-tuple-element.46), channel_id=1, source_target_pairs={{0,24},{4,28},{8,0},{12,4},{16,8},{20,12},{24,16},{28,20},{1,25},{... | collective-permute-start | bytes 393224 | tf_op jit(solution)/shard_map/ppermute | solution.py:372

commit v2 on v1

v2 whole, which is shorter than its diff:
```python
import functools

import jax
import jax.numpy as jnp
from jax import lax
from jax.experimental import pallas as pl
from jax.experimental.pallas import tpu as pltpu
from jax.sharding import PartitionSpec as P

TILE = 128
SUBLANES = 8
F32 = jnp.float32
BF16 = jnp.bfloat16
VMEM = pl.BlockSpec(memory_space=pltpu.VMEM)
SMEM = pl.BlockSpec(memory_space=pltpu.SMEM)
HBM = pl.BlockSpec(memory_space=pltpu.HBM)
MASS_PARTS = 4


def params(megabytes):
    return pltpu.CompilerParams(vmem_limit_bytes=megabytes * 2**20)


def crossed(count, bit):
    return [(i, i ^ bit) for i in range(count)]


def rows_first(left, right):
    return lax.dot_general(left, right, (((0,), (0,)), ((), ())), preferred_element_type=F32)


def add_own(ref, own, place):
    share = own.shape[0]
    if share % SUBLANES == 0:
        window = pl.ds(pl.multiple_of(place * share, SUBLANES), share)
        ref[window, :] += own
        return
    fold = SUBLANES // share
    wide = jnp.concatenate([own] * fold, axis=0)
    line = lax.broadcasted_iota(jnp.int32, wide.shape, 0) // share
    window = pl.ds(pl.multiple_of(place // fold * SUBLANES, SUBLANES), SUBLANES)
    ref[window, :] += jnp.where(line == place % fold, wide, 0.0)


def copy_rows(target_ref, start, source_ref, place, share):
    if share % SUBLANES == 0:
        window = pl.ds(pl.multiple_of(place * share, SUBLANES), share)
        target_ref[start : start + share, :] = source_ref[window, :]
        return
    for i in range(share):
        target_ref[start + i : start + i + 1, :] = source_ref[pl.ds(place * share + i, 1), :]


def leaf_kernel(
    half, tiles, table_ref, mass_hbm, modes_hbm, fixed_hbm, own_hbm, moved_ref, *refs
):
    chunks = refs[:-8]
    mass_ref, modes_ref, fixed_ref, own_ref, whole_ref, partial_ref, projected_ref, sems = refs[-8:]
    row, col = lax.axis_index("row"), lax.axis_index("col")
    row_count, col_count = lax.axis_size("row"), lax.axis_size("col")
    rows, size = modes_ref.shape
    height = rows // MASS_PARTS

    def mass_copy(i):
        window = pl.ds(pl.multiple_of(i * height, height), height)
        return pltpu.make_async_copy(
            mass_hbm.at[0, window], mass_ref.at[window], sems.at[3 + i]
        )

    half_modes = modes_hbm.at[0, :, pl.ds(half * size, size)]
    modes_copy = pltpu.make_async_copy(half_modes, modes_ref, sems.at[0])
    fixed_copy = pltpu.make_async_copy(fixed_hbm.at[0], fixed_ref, sems.at[1])
    own_source = own_hbm.at[0] if half == 0 else own_hbm
    own_copy = pltpu.make_async_copy(own_source, own_ref, sems.at[2])
    modes_copy.start()
    mass_copy(0).start()
    fixed_copy.start()
    for i in range(1, MASS_PARTS):
        mass_copy(i).start()
    own_copy.start()
    modes_copy.wait()

    def part(i, first):
        mass_copy(i).wait()
        lines = []
        for a in range(height // TILE):
            pieces = []
            for b in range(tiles):
                kept = table_ref[(i * (height // TILE) + a) * tiles + b]
                window = pl.ds(pl.multiple_of(i * height + a * TILE, TILE), TILE)
                piece = mass_ref[window, b * TILE : (b + 1) * TILE]
                pieces.append(jnp.where(kept != 0, piece, jnp.zeros_like(piece)))
            lines.append(jnp.concatenate(pieces, axis=1))
        masked = jnp.concatenate(lines, axis=0)
        loaded = jnp.dot(masked, modes_ref[...], preferred_element_type=F32).astype(BF16)
        if first:
            fixed_copy.wait()
        window = pl.ds(pl.multiple_of(i * height, height), height)
        partial = rows_first(modes_ref[window, :], loaded)
        projected = rows_first(fixed_ref[window, :], loaded)
        if first:
            partial_ref[...] = partial
            projected_ref[...] = projected
        else:
            partial_ref[...] += partial
            projected_ref[...] += projected

    part(0, True)
    lax.fori_loop(1, MASS_PARTS, lambda i, _: part(i, False), None)

    blocks = size // TILE
    base = tiles * tiles + half * blocks
    to = [pl.multiple_of(table_ref[base + a] * TILE, TILE) for a in range(blocks)]
    for b in range(blocks):
        source = slice(b * TILE, (b + 1) * TILE)
        moved_ref[:, pl.ds(to[b], TILE)] = projected_ref[:, source]
        for a in range(blocks):
            whole_ref[pl.ds(to[a], TILE), pl.ds(to[b], TILE)] = partial_ref[
                a * TILE : (a + 1) * TILE, source
            ]
    own_copy.wait()
    share = own_ref.shape[0]
    if half == 0:
        add_own(whole_ref, own_ref[...], row)
        for k, chunk in enumerate(chunks):
            for r in range(row_count // 2):
                copy_rows(chunk, r * share, whole_ref, 2 * r + lax.rem(row + k, 2), share)
    else:
        add_own(whole_ref, own_ref[...], row * col_count + col)
        for r in range(row_count):
            for c in range(col_count):
                start, place = (c * row_count + r) * share, (r * col_count + c) * share
                chunks[0][start : start + share, :] = whole_ref[place : place + share, :]


def leaf_half(half, tiles, table, leaf_mass, constraint_modes, fixed, own):
    rows, size = constraint_modes.shape[1], constraint_modes.shape[2] // 2
    modes = fixed.shape[2]
    chunk_count = 2 if half == 0 else 1
    outs = [jax.ShapeDtypeStruct((modes, size), F32)]
    outs += [jax.ShapeDtypeStruct((size // chunk_count, size), F32)] * chunk_count
    return pl.pallas_call(
        functools.partial(leaf_kernel, half, tiles),
        in_specs=[SMEM] + [HBM] * 4,
        out_specs=[VMEM] * len(outs),
        out_shape=outs,
        scratch_shapes=[
            pltpu.VMEM((rows, rows), BF16),
            pltpu.VMEM((rows, size), BF16),
            pltpu.VMEM((rows, modes), BF16),
            pltpu.VMEM(own.shape[-2:], F32),
            pltpu.VMEM((size, size), F32),
            pltpu.VMEM((size, size), F32),
            pltpu.VMEM((modes, size), F32),
            pltpu.SemaphoreType.DMA((3 + MASS_PARTS,)),
        ],
        compiler_params=params(48),
        cost_estimate=pl.CostEstimate(
            flops=2 * rows * size * (rows + size + modes),
            bytes_accessed=2 * rows * (rows + size + modes) + 8 * size * size,
            transcendentals=0,
        ),
        name="leaf_group" if half == 0 else "leaf_top",
    )(table, leaf_mass, constraint_modes, fixed, own)


def split(value):
    high = value.astype(BF16)
    return high, (value - high.astype(F32)).astype(BF16)


def three_pass(left, right, turn=False):
    (left_high, left_low), (right_high, right_low) = left, right
    multiply = rows_first if turn else functools.partial(jnp.dot, preferred_element_type=F32)
    width = right_high.shape[1]
    both = multiply(left_high, jnp.concatenate([right_high, right_low], axis=1))
    return both[:, :width] + both[:, width:] + multiply(left_low, right_high)


def prepare_kernel(keep_ref, send_ref, top_ref, first_ref, second_ref, bases_ref, out_ref, terms_ref):
    modes = terms_ref.shape[2]
    size = bases_ref.shape[0]
    row, col = lax.axis_index("row"), lax.axis_index("col")
    row_count, col_count = lax.axis_size("row"), lax.axis_size("col")
    grams = []
    for half in range(2):
        lanes = slice(half * modes, (half + 1) * modes)
        basis = split(bases_ref[:, lanes])
        if half == 0:
            line = size // row_count
            matrix, order = [], []
            for k, ref in enumerate((keep_ref, send_ref)):
                matrix.append(ref[...])
                for r in range(row_count // 2):
                    at = (2 * r + lax.rem(row + k, 2)) * line
                    order.append(bases_ref[pl.ds(pl.multiple_of(at, line), line), lanes])
            matrix = jnp.concatenate(matrix, axis=0)
            ordered = split(jnp.concatenate(order, axis=0))
        else:
            line = size // (row_count * col_count)
            order = [
                bases_ref[(r * col_count + c) * line : (r * col_count + c + 1) * line, lanes]
                for c in range(col_count)
                for r in range(row_count)
            ]
            matrix = top_ref[...]
            ordered = split(jnp.concatenate(order, axis=0))
        applied = three_pass(split(matrix), basis)
        gram = three_pass(ordered, split(applied), turn=True)
        grams.append(0.5 * (gram + gram.T))
        moved = (first_ref, second_ref)[half]
        terms_ref[half] = three_pass(split(moved[...]), basis)
    down = lax.broadcasted_iota(jnp.int32, (modes, modes), 0)
    across = lax.broadcasted_iota(jnp.int32, (modes, modes), 1)
    packed = jnp.where(down >= across, grams[0], grams[1])
    diagonal = jnp.sum(jnp.where(down == across, grams[1], 0.0), axis=0, keepdims=True)
    devices = row_count * col_count
    share, line = modes // devices, out_ref.shape[0] // devices
    diagonal = jnp.broadcast_to(diagonal, (line - share, modes))
    for d in range(devices):
        out_ref[d * line : d * line + share, :] = packed[d * share : (d + 1) * share]
        out_ref[d * line + share : (d + 1) * line, :] = diagonal


def packed_lines(modes, devices):
    share = modes // devices
    return (share + SUBLANES) // SUBLANES * SUBLANES


def prepare(keep, send, top, first, second, bases, devices):
    modes, size = first.shape
    return pl.pallas_call(
        prepare_kernel,
        in_specs=[VMEM] * 6,
        out_specs=[VMEM, VMEM],
        out_shape=[
            jax.ShapeDtypeStruct((devices * packed_lines(modes, devices), modes), F32),
            jax.ShapeDtypeStruct((2, modes, modes), F32),
        ],
        compiler_params=params(32),
        cost_estimate=pl.CostEstimate(
            flops=12 * size * size * modes, bytes_accessed=12 * size * size, transcendentals=0
        ),
        name="prepare",
    )(keep, send, top, first, second, bases)


def total_kernel(in_ref, out_ref):
    row, col = lax.axis_index("row"), lax.axis_index("col")
    row_count, col_count = lax.axis_size("row"), lax.axis_size("col")
    devices = row_count * col_count
    modes = in_ref.shape[1]
    line = in_ref.shape[0] // devices
    share = modes // devices
    groups = []
    for c in range(col_count):
        value = in_ref[c * line : (c + 1) * line, :]
        for r in range(1, row_count):
            at = (r * col_count + c) * line
            value = value + in_ref[at : at + line, :]
        groups.append(value)
    top = functools.reduce(jnp.add, groups)
    down = lax.broadcasted_iota(jnp.int32, (line, modes), 0)
    across = lax.broadcasted_iota(jnp.int32, (line, modes), 1)
    lower = (down < share) & (across <= down + (row * col_count + col) * share)
    for c in range(col_count):
        value = jnp.where(lower, groups[c], top)
        for r in range(row_count):
            at = (r * col_count + c) * line
            out_ref[at : at + line, :] = value


def total(pieces):
    return pl.pallas_call(
        total_kernel,
        in_specs=[VMEM],
        out_specs=VMEM,
        out_shape=jax.ShapeDtypeStruct(pieces.shape, F32),
        cost_estimate=pl.CostEstimate(
            flops=2 * pieces.size, bytes_accessed=8 * pieces.size, transcendentals=0
        ),
        name="total",
    )(pieces)


def factor(matrices):
    size = matrices[0].shape[0]
    width = SUBLANES
    down = lax.broadcasted_iota(jnp.int32, (size, size), 0)
    across = lax.broadcasted_iota(jnp.int32, (size, size), 1)
    line = lax.broadcasted_iota(jnp.int32, (width, size), 0)
    lane = lax.broadcasted_iota(jnp.int32, (width, size), 1)
    states = list(matrices)
    diagonals = [[] for _ in matrices]
    for start in range(0, size, width):
        stop = start + width
        for m, state in enumerate(states):
            spread = [
                jnp.broadcast_to(state[:, start + q : start + q + 1], (size, size))
                for q in range(width)
            ]
            strip = state[start:stop, :]
            small = [s[start:stop, :] for s in spread]
            scaled = []
            rest = strip
            for q in range(width):
                scale = lax.rsqrt(small[q][q : q + 1, :])
                tail = [small[t][q : q + 1, :] * scale for t in range(q + 1, width)]
                level = rest[q : q + 1, :] * scale
                rest = rest - small[q] * (scale * level)
                small[q] = jnp.where(line == q, 1.0, small[q]) * scale
                for t in range(q + 1, width):
                    small[t] = jnp.where(line == q, 0.0, small[t]) - small[q] * tail[t - q - 1]
                scaled.append(level)
            small = [jnp.where(line <= q, s, 0.0) for q, s in enumerate(small)]
            solved = small[0] * scaled[0]
            for q in range(1, width):
                solved = solved + small[q] * scaled[q]
            solved = jnp.where(lane >= stop, solved, 0.0)
            update = spread[0] * solved[0:1, :]
            for q in range(1, width):
                update = update + spread[q] * solved[q : q + 1, :]
            block = jnp.where(lane == line + start, 1.0, 0.0)
            kept = jnp.where(lane < start, strip, block) - solved
            parts = []
            if start > 0:
                parts.append(state[:start] - update[:start])
            parts.append(kept)
            if stop < size:
                parts.append(state[stop:] - update[stop:])
            states[m] = jnp.concatenate(parts, axis=0)
            diagonal = jnp.zeros((width, size), F32)
            for q in range(width):
                diagonal = jnp.where(lane == start + q, small[q], diagonal)
            diagonals[m].append(diagonal)
    uppers = [jnp.where(across >= down, state, 0.0) for state in states]
    return uppers, [jnp.concatenate(d, axis=0) for d in diagonals]


def finish_kernel(packed_ref, terms_ref, group_basis_ref, top_basis_ref, coupling_ref, group_ref, top_ref):
    modes = packed_ref.shape[1]
    devices = lax.axis_size("row") * lax.axis_size("col")
    line, share = packed_ref.shape[0] // devices, modes // devices
    packed = jnp.concatenate(
        [packed_ref[d * line : d * line + share, :] for d in range(devices)], axis=0
    )
    down = lax.broadcasted_iota(jnp.int32, (modes, modes), 0)
    across = lax.broadcasted_iota(jnp.int32, (modes, modes), 1)
    turned = packed.T
    group = jnp.where(down >= across, packed, turned)
    top = jnp.where(down > across, turned, packed)
    diagonal = jnp.broadcast_to(packed_ref[share : share + 1, :], top.shape)
    top = jnp.where(down == across, diagonal, top)
    uppers, diagonals = factor([group, top])
    for half in range(2):
        inverse = split(three_pass(split(uppers[half]), split(diagonals[half])))
        basis = (group_basis_ref[0], top_basis_ref[...])[half]
        left = jnp.concatenate([terms_ref[half], basis], axis=0)
        result = three_pass(split(left), inverse)
        coupling_ref[0, :, half, :] = result[:modes]
        if half == 0:
            group_ref[0] = result[modes:]
        else:
            top_ref[...] = result[modes:]


def finish(packed, terms, group_basis, top_basis):
    modes = packed.shape[1]
    return pl.pallas_call(
        finish_kernel,
        in_specs=[VMEM] * 4,
        out_specs=[VMEM] * 3,
        out_shape=[
            jax.ShapeDtypeStruct((1, modes, 2, modes), F32),
            jax.ShapeDtypeStruct(group_basis.shape, F32),
            jax.ShapeDtypeStruct(top_basis.shape, F32),
        ],
        compiler_params=params(32),
        cost_estimate=pl.CostEstimate(
            flops=20 * modes**3, bytes_accessed=24 * modes * modes, transcendentals=2 * modes
        ),
        name="finish",
    )(packed, terms, group_basis, top_basis)


def body(
    leaf_mass, tile_mask, constraint_modes, leaf_fixed_modes, block_map, group_mass, top_mass,
    group_basis, top_basis,
):
    row_count, col_count = lax.axis_size("row"), lax.axis_size("col")
    both = ("row", "col")
    size = group_mass.shape[2]
    tiles = tile_mask.shape[1]
    table = jnp.concatenate([tile_mask.reshape(-1), block_map.reshape(-1)])
    bases = lax.all_gather(
        jnp.concatenate([group_basis[0], top_basis], axis=1), "row", axis=0, tiled=True
    )

    def half_of(half, own):
        return leaf_half(half, tiles, table, leaf_mass, constraint_modes, leaf_fixed_modes, own)

    first, keep, send = half_of(0, group_mass)
    other = lax.ppermute(send, "row", crossed(row_count, 1))
    second, top = half_of(1, top_mass)
    packed, terms = prepare(keep, send, top, first, second, bases, row_count * col_count)
    packed = lax.all_to_all(packed, both, 0, 0, tiled=True)
    packed = lax.all_to_all(total(packed), both, 0, 0, tiled=True)
    coupling, group_modes, top_modes = finish(packed, terms, group_basis, top_basis)

    parities = [list(range(p, row_count, 2)) for p in range(2)]
    group_rows = lax.all_to_all(
        keep + other, "row", 0, 0, axis_index_groups=parities, tiled=True
    )
    group_rows = group_rows.reshape(row_count // 2, -1, size).sum(axis=0)
    top_rows = lax.all_to_all(top, "col", 0, 0, tiled=True)
    top_rows = top_rows.reshape(col_count, -1, size).sum(axis=0)
    top_rows = lax.all_to_all(top_rows, "row", 0, 0, tiled=True)
    top_rows = top_rows.reshape(row_count, -1, size).sum(axis=0)
    return coupling, group_modes, top_modes, (size * group_rows)[None], size * top_rows


def solution(mesh):
    leaf = P(("row", "col"), None, None)
    group = P("col", "row", None)
    in_specs = (
        leaf, leaf, leaf, leaf, leaf, group, P(("row", "col"), None), group, P("row", None),
    )
    out_specs = (
        P(("row", "col"), None, None, None), group, P("row", None), group, P(("row", "col"), None),
    )
    return jax.shard_map(body, mesh=mesh, in_specs=in_specs, out_specs=out_specs, check_vma=False)
```

time: 94.4 us -> 136 us (1.44)
  blocking collectives: 0 us -> 46.9 us
  starting transfers between devices: 37.5 us -> 14.9 us
  waiting for transfers between devices: 12.2 us -> 33 us
  Pallas kernels: 37.7 us -> 31.3 us
  local copies, waits for them, and re-layouts: 3.32 us -> 5.72 us
    ppermute x26 -> x1, starting transfers between devices: 37.5 us -> 1.7 us  [body(): other = lax.ppermute(send, 'row', crossed(row_count, 1))]
    all_gather x0 -> x1, blocking collectives: none -> 33 us  [body(): lax.all_gather(jnp.concatenate([group_basis[0], top_basis], axis=1), 'row...]
    all_to_all x0 -> x4, waiting for transfers between devices: none -> 28.9 us  [the longest x1 12.8 us: body(): top_rows = lax.all_to_all(top, 'col', 0, 0, tiled=True)]
    all_to_all x0 -> x1, blocking collectives: none -> 13.9 us  [body(): packed = lax.all_to_all(packed, both, 0, 0, tiled=True)]
    all_to_all x0 -> x4, starting transfers between devices: none -> 13.2 us  [the longest x1 3.65 us: body(): lax.all_to_all(keep + other, 'row', 0, 0, axis_index_groups=parities, til...]
    ppermute x26 -> x1, waiting for transfers between devices: 12.2 us -> 4.07 us  [body(): other = lax.ppermute(send, 'row', crossed(row_count, 1))]
    pallas_call x5 -> x4, Pallas kernels: 30.3 us -> 24.1 us  [the longest x2 20 us: leaf_half(): pl.pallas_call(functools.partial(leaf_kernel, half, tiles), in_specs=[SME...]
    reshape x0 -> x2, local copies, waits for them, and re-layouts: none -> 1.54 us  [body(): table = jnp.concatenate([tile_mask.reshape(-1), block_map.reshape(-1)])]
  transfers between devices with their start and end apart: 26 -> 5, of which waited for: 4 -> 5; matrix products, arithmetic and copies ran while one was open for 1% -> 2% of each run, Pallas kernels for 40% -> 6%
where the time goes in v2:
time: 136 us; the launch traced here: 135 us
  blocking collectives  46.9 us (34%)
  waiting for transfers between devices  33 us (24%)
  Pallas kernels  31.3 us (23%)
  starting transfers between devices  14.9 us (11%)
  local copies, waits for them, and re-layouts  5.72 us (4%)
  other arithmetic  3 us (2%)
    all_gather x1, blocking collectives, body(): lax.all_gather(jnp.concatenate([group_basis[0], top_basis], axis=1), 'row...  33 us
    pallas_call x2, Pallas kernels, leaf_half(): pl.pallas_call(functools.partial(leaf_kernel, half, tiles), in_specs=[SME...  20 us
    all_to_all x1, blocking collectives, body(): packed = lax.all_to_all(packed, both, 0, 0, tiled=True)  13.9 us
    all_to_all x1, waiting for transfers between devices, body(): top_rows = lax.all_to_all(top, 'col', 0, 0, tiled=True)  12.8 us
    pallas_call x1, Pallas kernels, finish(): pl.pallas_call(finish_kernel, in_specs=[VMEM] * 4, out_specs=[VMEM] * 3,...  7.19 us
    all_to_all x1, waiting for transfers between devices, body(): packed = lax.all_to_all(total(packed), both, 0, 0, tiled=True)  5.75 us
    all_to_all x1, waiting for transfers between devices, body(): lax.all_to_all(keep + other, 'row', 0, 0, axis_index_groups=parities, til...  5.73 us
    all_to_all x1, waiting for transfers between devices, body(): top_rows = lax.all_to_all(top_rows, 'row', 0, 0, tiled=True)  4.57 us
  transfers between devices with their start and end apart: 5, of which 5 were waited for; matrix products, arithmetic and copies ran while one was open for 2% of the time, Pallas kernels for 6%

profile of v2, /device:TPU:0, one launch (start us, length us, event | category | flops | bytes accessed | tf_op | source)
XLA Modules:
  0.0 135.5 jit_solution(17708134092150631202)
XLA Ops:
  0.6 0.8 reshape.41
  1.4 0.8 reshape.42
  2.2 0.0 copy-start.2
  2.2 2.2 %copy-done.2 = bf16[1,2048,1024]{2,1,0:T(8,128)(2,1)S(1)} copy-done((bf16[1,2048,1024]{2,1,0:T(8,128)(2,1)S(1)}, bf16[1,2048,1024]{2,1,0:T(8,128)(2,1)}, u32[]{:S(2)}) %copy-start.2) | copy-done | bytes 4194328
  4.4 0.0 copy-start.3
  4.4 1.0 copy-done.3
  5.4 0.0 copy-start.4
  5.4 0.9 copy-done.4
  6.3 0.0 copy-start.5
  6.4 9.5 %leaf_group.1 = (f32[128,512]{1,0:T(8,128)S(1)}, f32[256,512]{1,0:T(8,128)S(1)}, f32[256,512]{1,0:T(8,128)S(1)}) custom-call(s32[264]{0:T(512)S(1)} %constant_dynamic-update-slice_fusion.table_ref, bf16[1,2048,2048]{2,1,0:T(8,128)(2,1)} %mass_hbm.3, bf16[1,2048,1024]{2,1,0:T(8,128)(2,1)S(1)} %copy-done.2, bf16[1,2048,128]{2,1,0:T(8,128)(2,1)S(1)} %copy-done.3, ...), custom_call_target="tpu_custom_call" | custom-call | flops 5637144576 | bytes 13107200 | tf_op jit(solution)/shard_map/leaf_group/pallas_call | solution.py:142
  15.9 0.0 copy-done.5
  15.9 0.0 copy-start
  15.9 0.0 copy-start.1
  15.9 10.5 %leaf_top.1 = (f32[128,512]{1,0:T(8,128)S(1)}, f32[512,512]{1,0:T(8,128)}) custom-call(s32[264]{0:T(512)S(1)} %constant_dynamic-update-slice_fusion.table_ref, bf16[1,2048,2048]{2,1,0:T(8,128)(2,1)} %mass_hbm.3, bf16[1,2048,1024]{2,1,0:T(8,128)(2,1)S(1)} %copy-done.2, bf16[1,2048,128]{2,1,0:T(8,128)(2,1)S(1)} %copy-done.3, f32[16,512]{1,0:T(8,128)S(1)} %copy-done.5), custom_call_target="tpu_custom_call" | custom-call | flops 5637144576 | bytes 13107200 | tf_op jit(solution)/shard_map/leaf_top/pallas_call | solution.py:142
  26.4 0.0 copy-done
  26.4 0.0 copy-done.1
  26.5 33.0 %all_gather.3.bases_ref = f32[512,256]{1,0:T(8,128)S(1)} all-gather(f32[64,256]{1,0:T(8,128)S(1)} %pad_maximum_fusion), channel_id=1, replica_groups=mesh['row'=8,'col'=4] {'row'}, dimensions={0}, use_global_device_ids=true | all-gather | bytes 589824 | tf_op jit(solution)/shard_map/all_gather | solution.py:395
  59.5 2.5 %prepare.1 = (f32[256,128]{1,0:T(8,128)S(1)}, f32[2,128,128]{2,1,0:T(8,128)S(1)}) custom-call(f32[256,512]{1,0:T(8,128)S(1)} %get-tuple-element.15.keep_ref, f32[256,512]{1,0:T(8,128)S(1)} %get-tuple-element.16.send_ref, f32[512,512]{1,0:T(8,128)} %get-tuple-element.17.top_ref, f32[128,512]{1,0:T(8,128)S(1)} %get-tuple-element.18.first_ref, ...), custom_call_target="tpu_custom_call" | custom-call | flops 402653184 | bytes 3145728 | tf_op jit(solution)/shard_map/prepare/pallas_call | solution.py:232
  62.0 13.9 %all_to_all.49 = f32[32,8,128]{2,1,0:T(8,128)} all-to-all(f32[32,8,128]{2,1,0:T(8,128)S(1)} %bitcast.11), channel_id=1, replica_groups=mesh['row'=8,'col'=4] {'row','col'}, dimensions={0} | all-to-all | bytes 262144 | tf_op jit(solution)/shard_map/all_to_all | solution.py:406
  75.8 3.5 %all-to-all-start.3 = ((f32[4,128,512]{2,1,0:T(8,128)}), f32[4,128,512]{2,1,0:T(8,128)S(1)}, u32[]{:S(2)}, u32[]{:S(2)}) async-start(f32[4,128,512]{2,1,0:T(8,128)} %bitcast.7), calls=%async_computation.3 | async-start | bytes 2097152 | tf_op jit(solution)/shard_map/all_to_all | solution.py:415
  79.4 1.6 %total.1 = f32[256,128]{1,0:T(8,128)} custom-call(f32[256,128]{1,0:T(8,128)} %bitcast.14), custom_call_target="tpu_custom_call" | custom-call | flops 65536 | bytes 262144 | tf_op jit(solution)/shard_map/total/pallas_call | solution.py:274
  80.9 12.8 %all-to-all-done.3 = f32[4,128,512]{2,1,0:T(8,128)S(1)} async-done(((f32[4,128,512]{2,1,0:T(8,128)}), f32[4,128,512]{2,1,0:T(8,128)S(1)}, u32[]{:S(2)}, u32[]{:S(2)}) %all-to-all-start.3) | async-done | bytes 1048608 | tf_op jit(solution)/shard_map/all_to_all | solution.py:415
  93.8 2.6 %all-to-all-start.1 = ((f32[32,8,128]{2,1,0:T(8,128)}), f32[32,8,128]{2,1,0:T(8,128)S(1)}, u32[]{:S(2)}, u32[]{:S(2)}) async-start(f32[32,8,128]{2,1,0:T(8,128)} %bitcast.13), calls=%async_computation.1 | async-start | bytes 262144 | tf_op jit(solution)/shard_map/all_to_all | solution.py:407
  96.4 1.7 %collective-permute-start = (f32[256,512]{1,0:T(8,128)S(1)}, f32[256,512]{1,0:T(8,128)S(1)}, u32[]{:S(2)}, u32[]{:S(2)}) collective-permute-start(f32[256,512]{1,0:T(8,128)S(1)} %get-tuple-element.16.send_ref), channel_id=1, source_target_pairs={{0,4},{4,0},{8,12},{12,8},{16,20},{20,16},{24,28},{28,24},{1,5},{5... | collective-permute-start | bytes 1572872 | tf_op jit(solution)/shard_map/ppermute | solution.py:403
  98.1 0.8 reduce_sum.28
  98.9 5.8 %all-to-all-done.1 = f32[32,8,128]{2,1,0:T(8,128)S(1)} async-done(((f32[32,8,128]{2,1,0:T(8,128)}), f32[32,8,128]{2,1,0:T(8,128)S(1)}, u32[]{:S(2)}, u32[]{:S(2)}) %all-to-all-start.1) | async-done | bytes 131104 | tf_op jit(solution)/shard_map/all_to_all | solution.py:407
  104.6 3.4 %all-to-all-start.4 = ((f32[8,16,512]{2,1,0:T(8,128)}), f32[8,16,512]{2,1,0:T(8,128)S(1)}, u32[]{:S(2)}, u32[]{:S(2)}) async-start(f32[8,16,512]{2,1,0:T(8,128)} %bitcast.8), calls=%async_computation.4 | async-start | bytes 524288 | tf_op jit(solution)/shard_map/all_to_all | solution.py:417
  108.0 4.1 %collective-permute-done = f32[256,512]{1,0:T(8,128)S(1)} collective-permute-done((f32[256,512]{1,0:T(8,128)S(1)}, f32[256,512]{1,0:T(8,128)S(1)}, u32[]{:S(2)}, u32[]{:S(2)}) %collective-permute-start) | collective-permute-done | bytes 524320 | tf_op jit(solution)/shard_map/ppermute | solution.py:403
  112.1 0.9 add.3
  113.0 4.6 %all-to-all-done.4 = f32[8,16,512]{2,1,0:T(8,128)S(1)} async-done(((f32[8,16,512]{2,1,0:T(8,128)}), f32[8,16,512]{2,1,0:T(8,128)S(1)}, u32[]{:S(2)}, u32[]{:S(2)}) %all-to-all-start.4) | async-done | bytes 262176 | tf_op jit(solution)/shard_map/all_to_all | solution.py:417
  117.5 3.6 %all-to-all-start.2 = ((f32[4,64,512]{2,1,0:T(8,128)}), f32[4,64,512]{2,1,0:T(8,128)S(1)}, u32[]{:S(2)}, u32[]{:S(2)}) async-start(f32[4,64,512]{2,1,0:T(8,128)} %bitcast.5), calls=%async_computation.2 | async-start | bytes 1048576 | tf_op jit(solution)/shard_map/all_to_all | solution.py:411
  121.2 7.2 %finish.1 = (f32[1,128,2,128]{3,2,1,0:T(2,128)}, f32[1,64,128]{2,1,0:T(8,128)}, f32[64,128]{1,0:T(8,128)}) custom-call(f32[256,128]{1,0:T(8,128)S(1)} %bitcast.10, f32[2,128,128]{2,1,0:T(8,128)S(1)} %get-tuple-element.21.terms_ref, f32[1,64,128]{2,1,0:T(8,128)S(1)} %copy-done.1, f32[64,128]{1,0:T(8,128)S(1)} %copy-done), custom_call_target="tpu_custom_call" | custom-call | flops 41943040 | bytes 393216 | tf_op jit(solution)/shard_map/finish/pallas_call | solution.py:369
  128.4 0.6 broadcast_multiply_fusion
  129.0 5.7 %all-to-all-done.2 = f32[4,64,512]{2,1,0:T(8,128)S(1)} async-done(((f32[4,64,512]{2,1,0:T(8,128)}), f32[4,64,512]{2,1,0:T(8,128)S(1)}, u32[]{:S(2)}, u32[]{:S(2)}) %all-to-all-start.2) | async-done | bytes 524320 | tf_op jit(solution)/shard_map/all_to_all | solution.py:411
  134.8 0.7 multiply_bitcast_fusion
  (6 shorter events, 0.1 us)
Async XLA Ops:
  2.2 2.2 %copy-start.2 = (bf16[1,2048,1024]{2,1,0:T(8,128)(2,1)S(1)}, bf16[1,2048,1024]{2,1,0:T(8,128)(2,1)}, u32[]{:S(2)}) copy-start(bf16[1,2048,1024]{2,1,0:T(8,128)(2,1)} %modes_hbm.3) | copy-start | bytes 12582916
  4.4 1.0 copy-start.3
  5.4 0.9 copy-start.4
  6.3 9.5 %copy-start.5 = (f32[16,512]{1,0:T(8,128)S(1)}, f32[16,512]{1,0:T(8,128)}, u32[]{:S(2)}) copy-start(f32[16,512]{1,0:T(8,128)} %own_hbm.3) | copy-start | bytes 98308
  15.9 10.5 %copy-start = (f32[64,128]{1,0:T(8,128)S(1)}, f32[64,128]{1,0:T(8,128)}, u32[]{:S(2)}) copy-start(f32[64,128]{1,0:T(8,128)} %top_basis_ref.1) | copy-start | bytes 98308
  15.9 10.5 %copy-start.1 = (f32[1,64,128]{2,1,0:T(8,128)S(1)}, f32[1,64,128]{2,1,0:T(8,128)}, u32[]{:S(2)}) copy-start(f32[1,64,128]{2,1,0:T(8,128)} %group_basis_ref.1) | copy-start | bytes 98308
  75.8 18.0 %all-to-all-start.3 = ((f32[4,128,512]{2,1,0:T(8,128)}), f32[4,128,512]{2,1,0:T(8,128)S(1)}, u32[]{:S(2)}, u32[]{:S(2)}) async-start(f32[4,128,512]{2,1,0:T(8,128)} %bitcast.7), calls=%async_computation.3 | async-start | bytes 2097152 | tf_op jit(solution)/shard_map/all_to_all | solution.py:415
  93.8 10.8 %all-to-all-start.1 = ((f32[32,8,128]{2,1,0:T(8,128)}), f32[32,8,128]{2,1,0:T(8,128)S(1)}, u32[]{:S(2)}, u32[]{:S(2)}) async-start(f32[32,8,128]{2,1,0:T(8,128)} %bitcast.13), calls=%async_computation.1 | async-start | bytes 262144 | tf_op jit(solution)/shard_map/all_to_all | solution.py:407
  96.4 15.7 %collective-permute-start = (f32[256,512]{1,0:T(8,128)S(1)}, f32[256,512]{1,0:T(8,128)S(1)}, u32[]{:S(2)}, u32[]{:S(2)}) collective-permute-start(f32[256,512]{1,0:T(8,128)S(1)} %get-tuple-element.16.send_ref), channel_id=1, source_target_pairs={{0,4},{4,0},{8,12},{12,8},{16,20},{20,16},{24,28},{28,24},{1,5},{5... | collective-permute-start | bytes 1572872 | tf_op jit(solution)/shard_map/ppermute | solution.py:403
  104.6 12.9 %all-to-all-start.4 = ((f32[8,16,512]{2,1,0:T(8,128)}), f32[8,16,512]{2,1,0:T(8,128)S(1)}, u32[]{:S(2)}, u32[]{:S(2)}) async-start(f32[8,16,512]{2,1,0:T(8,128)} %bitcast.8), calls=%async_computation.4 | async-start | bytes 524288 | tf_op jit(solution)/shard_map/all_to_all | solution.py:417
  117.5 17.2 %all-to-all-start.2 = ((f32[4,64,512]{2,1,0:T(8,128)}), f32[4,64,512]{2,1,0:T(8,128)S(1)}, u32[]{:S(2)}, u32[]{:S(2)}) async-start(f32[4,64,512]{2,1,0:T(8,128)} %bitcast.5), calls=%async_computation.2 | async-start | bytes 1048576 | tf_op jit(solution)/shard_map/all_to_all | solution.py:411

commit v3 on v2

v3 whole, which is shorter than its diff:
```python
import functools

import jax
import jax.numpy as jnp
from jax import lax
from jax.experimental import pallas as pl
from jax.experimental.pallas import tpu as pltpu
from jax.sharding import PartitionSpec as P

TILE = 128
SUBLANES = 8
F32 = jnp.float32
BF16 = jnp.bfloat16
VMEM = pl.BlockSpec(memory_space=pltpu.VMEM)
SMEM = pl.BlockSpec(memory_space=pltpu.SMEM)
HBM = pl.BlockSpec(memory_space=pltpu.HBM)
MASS_PARTS = 4
LEAF_MEGABYTES = 48


def params(megabytes):
    return pltpu.CompilerParams(vmem_limit_bytes=int(megabytes * 2**20))


def crossed(count, bit):
    return [(i, i ^ bit) for i in range(count)]


def rows_first(left, right):
    return lax.dot_general(left, right, (((0,), (0,)), ((), ())), preferred_element_type=F32)


def add_own(ref, own, place):
    share = own.shape[0]
    if share % SUBLANES == 0:
        window = pl.ds(pl.multiple_of(place * share, SUBLANES), share)
        ref[window, :] += own
        return
    fold = SUBLANES // share
    wide = jnp.concatenate([own] * fold, axis=0)
    line = lax.broadcasted_iota(jnp.int32, wide.shape, 0) // share
    window = pl.ds(pl.multiple_of(place // fold * SUBLANES, SUBLANES), SUBLANES)
    ref[window, :] += jnp.where(line == place % fold, wide, 0.0)


def copy_rows(target_ref, start, source_ref, place, share):
    if share % SUBLANES == 0:
        window = pl.ds(pl.multiple_of(place * share, SUBLANES), share)
        target_ref[start : start + share, :] = source_ref[window, :]
        return
    for i in range(share):
        target_ref[start + i : start + i + 1, :] = source_ref[pl.ds(place * share + i, 1), :]


def bits_of(count):
    return count.bit_length() - 1


def exchanges(half, row_count, col_count):
    row = [("row", 1)] + [("row", 1 << b) for b in range(bits_of(row_count) - 1, 0, -1)]
    col = [("col", 1 << b) for b in range(bits_of(col_count))]
    return row if half == 0 else col + row


def cut_order(half, row_count, col_count):
    steps = exchanges(half, row_count, col_count)
    order = [0]
    for axis, bit in reversed(steps):
        stride = 1 if half == 0 or axis == "col" else col_count
        order = order + [place + bit * stride for place in order]
    return order


def leaf_kernel(
    half, mask_ref, map_ref, mass_hbm, modes_hbm, fixed_hbm, own_hbm, after_ref, moved_ref, *refs
):
    chunks = refs[:-8]
    mass_ref, modes_ref, fixed_ref, own_ref, whole_ref, partial_ref, projected_ref, sems = refs[-8:]
    row, col = lax.axis_index("row"), lax.axis_index("col")
    row_count, col_count = lax.axis_size("row"), lax.axis_size("col")
    rows, size = modes_ref.shape
    tiles = rows // TILE
    height = rows // MASS_PARTS

    def mass_copy(i):
        window = pl.ds(pl.multiple_of(i * height, height), height)
        return pltpu.make_async_copy(
            mass_hbm.at[0, window], mass_ref.at[window], sems.at[3 + i]
        )

    half_modes = modes_hbm.at[0, :, pl.ds(half * size, size)]
    modes_copy = pltpu.make_async_copy(half_modes, modes_ref, sems.at[0])
    fixed_copy = pltpu.make_async_copy(fixed_hbm.at[0], fixed_ref, sems.at[1])
    own_source = own_hbm.at[0] if half == 0 else own_hbm
    own_copy = pltpu.make_async_copy(own_source, own_ref, sems.at[2])
    modes_copy.start()
    mass_copy(0).start()
    fixed_copy.start()
    for i in range(1, MASS_PARTS):
        mass_copy(i).start()
    own_copy.start()
    modes_copy.wait()

    def part(i, first):
        mass_copy(i).wait()
        lines = []
        for a in range(height // TILE):
            pieces = []
            for b in range(tiles):
                kept = mask_ref[0, i * (height // TILE) + a, b]
                window = pl.ds(pl.multiple_of(i * height + a * TILE, TILE), TILE)
                piece = mass_ref[window, b * TILE : (b + 1) * TILE]
                pieces.append(jnp.where(kept != 0, piece, jnp.zeros_like(piece)))
            lines.append(jnp.concatenate(pieces, axis=1))
        masked = jnp.concatenate(lines, axis=0)
        loaded = jnp.dot(masked, modes_ref[...], preferred_element_type=F32).astype(BF16)
        if first:
            fixed_copy.wait()
        window = pl.ds(pl.multiple_of(i * height, height), height)
        partial = rows_first(modes_ref[window, :], loaded)
        projected = rows_first(fixed_ref[window, :], loaded)
        if first:
            partial_ref[...] = partial
            projected_ref[...] = projected
        else:
            partial_ref[...] += partial
            projected_ref[...] += projected

    part(0, True)
    lax.fori_loop(1, MASS_PARTS, lambda i, _: part(i, False), None)

    blocks = size // TILE
    to = [pl.multiple_of(map_ref[0, half, a] * TILE, TILE) for a in range(blocks)]
    for b in range(blocks):
        source = slice(b * TILE, (b + 1) * TILE)
        moved_ref[:, pl.ds(to[b], TILE)] = projected_ref[:, source]
        for a in range(blocks):
            whole_ref[pl.ds(to[a], TILE), pl.ds(to[b], TILE)] = partial_ref[
                a * TILE : (a + 1) * TILE, source
            ]
    own_copy.wait()
    share = own_ref.shape[0]
    order = cut_order(half, row_count, col_count)
    add_own(whole_ref, own_ref[...], row if half == 0 else row * col_count + col)
    bit = lax.rem(row if half == 0 else col, 2)
    for k, chunk in enumerate(chunks):
        for i, place in enumerate(order):
            if i < len(order) // 2:
                step = order[i + len(order) // 2] - place
                copy_rows(chunk, i * share, whole_ref, place + step * lax.rem(bit + k, 2), share)


def leaf_half(half, tile_mask, block_map, leaf_mass, constraint_modes, fixed, own, after):
    rows, size = constraint_modes.shape[1], constraint_modes.shape[2] // 2
    modes = fixed.shape[2]
    outs = [jax.ShapeDtypeStruct((modes, size), F32)]
    outs += [jax.ShapeDtypeStruct((size // 2, size), F32)] * 2
    return pl.pallas_call(
        functools.partial(leaf_kernel, half),
        in_specs=[SMEM] * 2 + [HBM] * 4 + [pl.BlockSpec(memory_space=pl.ANY)],
        out_specs=[VMEM] * len(outs),
        out_shape=outs,
        scratch_shapes=[
            pltpu.VMEM((rows, rows), BF16),
            pltpu.VMEM((rows, size), BF16),
            pltpu.VMEM((rows, modes), BF16),
            pltpu.VMEM(own.shape[-2:], F32),
            pltpu.VMEM((size, size), F32),
            pltpu.VMEM((size, size), F32),
            pltpu.VMEM((modes, size), F32),
            pltpu.SemaphoreType.DMA((3 + MASS_PARTS,)),
        ],
        compiler_params=params(LEAF_MEGABYTES),
        cost_estimate=pl.CostEstimate(
            flops=2 * rows * size * (rows + size + modes),
            bytes_accessed=2 * rows * (rows + size + modes) + 8 * size * size,
            transcendentals=0,
        ),
        name="leaf_group" if half == 0 else "leaf_top",
    )(tile_mask, block_map, leaf_mass, constraint_modes, fixed, own, after)


def split(value):
    high = value.astype(BF16)
    return high, (value - high.astype(F32)).astype(BF16)


def three_pass(left, right, turn=False):
    (left_high, left_low), (right_high, right_low) = left, right
    multiply = rows_first if turn else functools.partial(jnp.dot, preferred_element_type=F32)
    width = right_high.shape[1]
    both = multiply(left_high, jnp.concatenate([right_high, right_low], axis=1))
    return both[:, :width] + both[:, width:] + multiply(left_low, right_high)


def halve(step, keep_ref, other_ref, next_ref, send_ref):
    axis, bit = step
    height = next_ref.shape[0]
    mine = lax.rem(lax.axis_index(axis) // bit, 2) == 1
    low = keep_ref[:height, :] + other_ref[:height, :]
    high = keep_ref[height:, :] + other_ref[height:, :]
    next_ref[...] = jnp.where(mine, high, low)
    send_ref[...] = jnp.where(mine, low, high)


def prepare_kernel(
    count, step, keep_ref, send_ref, other_ref, top_keep_ref, top_send_ref, first_ref, second_ref, *refs
):
    pieces = refs[:count]
    packed_ref, terms_ref, next_ref, next_send_ref, bases_ref = refs[count:]
    halve(step, keep_ref, other_ref, next_ref, next_send_ref)
    modes = terms_ref.shape[2]
    size = bases_ref.shape[0]
    row, col = lax.axis_index("row"), lax.axis_index("col")
    row_count, col_count = lax.axis_size("row"), lax.axis_size("col")
    line = size // row_count
    for k, piece in enumerate(pieces):
        pair = lax.bitwise_xor(row // 2, k)
        for i in range(2):
            at = (2 * pair + lax.rem(row + i, 2)) * line
            bases_ref[pl.ds(pl.multiple_of(at, line), line), :] = piece[i * line : (i + 1) * line, :]
    grams = []
    for half in range(2):
        lanes = slice(half * modes, (half + 1) * modes)
        basis = split(bases_ref[:, lanes])
        order = cut_order(half, row_count, col_count)
        share = size // len(order)
        lower = jnp.concatenate(
            [bases_ref[at * share : (at + 1) * share, lanes] for at in order[: len(order) // 2]], axis=0
        )
        upper = jnp.concatenate(
            [bases_ref[at * share : (at + 1) * share, lanes] for at in order[len(order) // 2 :]], axis=0
        )
        swap = lax.rem((row, col)[half], 2) == 1
        ordered = jnp.concatenate(
            [jnp.where(swap, upper, lower), jnp.where(swap, lower, upper)], axis=0
        )
        parts = ((keep_ref, send_ref), (top_keep_ref, top_send_ref))[half]
        matrix = jnp.concatenate([part[...] for part in parts], axis=0)
        applied = three_pass(split(matrix), basis)
        gram = three_pass(split(ordered), split(applied), turn=True)
        grams.append(0.5 * (gram + gram.T))
        moved = (first_ref, second_ref)[half]
        terms_ref[half] = three_pass(split(moved[...]), basis)
    down = lax.broadcasted_iota(jnp.int32, (modes, modes), 0)
    across = lax.broadcasted_iota(jnp.int32, (modes, modes), 1)
    packed_ref[:modes, :] = jnp.where(down >= across, grams[0], grams[1])
    diagonal = jnp.sum(jnp.where(down == across, grams[1], 0.0), axis=0, keepdims=True)
    packed_ref[modes:, :] = jnp.broadcast_to(diagonal, (SUBLANES, modes))


def prepare(step, keep, send, other, top_keep, top_send, first, second, pieces):
    modes, size = first.shape
    part = jax.ShapeDtypeStruct((keep.shape[0] // 2, size), F32)
    return pl.pallas_call(
        functools.partial(prepare_kernel, len(pieces), step),
        in_specs=[VMEM] * (7 + len(pieces)),
        out_specs=[VMEM] * 4,
        out_shape=[
            jax.ShapeDtypeStruct((modes + SUBLANES, modes), F32),
            jax.ShapeDtypeStruct((2, modes, modes), F32),
            part,
            part,
        ],
        scratch_shapes=[pltpu.VMEM((size, 2 * modes), F32)],
        compiler_params=params(32),
        cost_estimate=pl.CostEstimate(
            flops=12 * size * size * modes, bytes_accessed=12 * size * size, transcendentals=0
        ),
        name="prepare",
    )(keep, send, other, top_keep, top_send, first, second, *pieces)


def fold_kernel(step, keep_ref, other_ref, after_ref, next_ref, send_ref):
    halve(step, keep_ref, other_ref, next_ref, send_ref)


def fold(step, keep, other, after):
    part = jax.ShapeDtypeStruct((keep.shape[0] // 2, keep.shape[1]), F32)
    return pl.pallas_call(
        functools.partial(fold_kernel, step),
        in_specs=[VMEM] * 2 + [pl.BlockSpec(memory_space=pl.ANY)],
        out_specs=[VMEM] * 2,
        out_shape=[part, part],
        compiler_params=params(16),
        cost_estimate=pl.CostEstimate(flops=1, bytes_accessed=1, transcendentals=0),
        name="fold",
    )(keep, other, after)


def factor(matrices):
    size = matrices[0].shape[0]
    width = SUBLANES
    down = lax.broadcasted_iota(jnp.int32, (size, size), 0)
    across = lax.broadcasted_iota(jnp.int32, (size, size), 1)
    line = lax.broadcasted_iota(jnp.int32, (width, size), 0)
    lane = lax.broadcasted_iota(jnp.int32, (width, size), 1)
    states = list(matrices)
    diagonals = [[] for _ in matrices]
    for start in range(0, size, width):
        stop = start + width
        for m, state in enumerate(states):
            spread = [
                jnp.broadcast_to(state[:, start + q : start + q + 1], (size, size))
                for q in range(width)
            ]
            strip = state[start:stop, :]
            small = [s[start:stop, :] for s in spread]
            scaled = []
            rest = strip
            for q in range(width):
                scale = lax.rsqrt(small[q][q : q + 1, :])
                tail = [small[t][q : q + 1, :] * scale for t in range(q + 1, width)]
                level = rest[q : q + 1, :] * scale
                rest = rest - small[q] * (scale * level)
                small[q] = jnp.where(line == q, 1.0, small[q]) * scale
                for t in range(q + 1, width):
                    small[t] = jnp.where(line == q, 0.0, small[t]) - small[q] * tail[t - q - 1]
                scaled.append(level)
            small = [jnp.where(line <= q, s, 0.0) for q, s in enumerate(small)]
            solved = small[0] * scaled[0]
            for q in range(1, width):
                solved = solved + small[q] * scaled[q]
            solved = jnp.where(lane >= stop, solved, 0.0)
            update = spread[0] * solved[0:1, :]
            for q in range(1, width):
                update = update + spread[q] * solved[q : q + 1, :]
            block = jnp.where(lane == line + start, 1.0, 0.0)
            kept = jnp.where(lane < start, strip, block) - solved
            parts = []
            if start > 0:
                parts.append(state[:start] - update[:start])
            parts.append(kept)
            if stop < size:
                parts.append(state[stop:] - update[stop:])
            states[m] = jnp.concatenate(parts, axis=0)
            diagonal = jnp.zeros((width, size), F32)
            for q in range(width):
                diagonal = jnp.where(lane == start + q, small[q], diagonal)
            diagonals[m].append(diagonal)
    uppers = [jnp.where(across >= down, state, 0.0) for state in states]
    return uppers, [jnp.concatenate(d, axis=0) for d in diagonals]


def finish_kernel(near_ref, far_ref, terms_ref, group_basis_ref, top_basis_ref, coupling_ref, group_ref, top_ref):
    modes = near_ref.shape[1]
    down = lax.broadcasted_iota(jnp.int32, (modes, modes), 0)
    across = lax.broadcasted_iota(jnp.int32, (modes, modes), 1)
    near, far = near_ref[:modes, :], far_ref[:modes, :]
    group = jnp.where(down >= across, near, near.T)
    top = jnp.where(down > across, far.T, far)
    diagonal = jnp.broadcast_to(far_ref[modes : modes + 1, :], top.shape)
    top = jnp.where(down == across, diagonal, top)
    uppers, diagonals = factor([group, top])
    for half in range(2):
        inverse = split(three_pass(split(uppers[half]), split(diagonals[half])))
        basis = (group_basis_ref[0], top_basis_ref[...])[half]
        left = jnp.concatenate([terms_ref[half], basis], axis=0)
        result = three_pass(split(left), inverse)
        coupling_ref[0, :, half, :] = result[:modes]
        if half == 0:
            group_ref[0] = result[modes:]
        else:
            top_ref[...] = result[modes:]


def finish(near, far, terms, group_basis, top_basis):
    modes = near.shape[1]
    return pl.pallas_call(
        finish_kernel,
        in_specs=[VMEM] * 5,
        out_specs=[VMEM] * 3,
        out_shape=[
            jax.ShapeDtypeStruct((1, modes, 2, modes), F32),
            jax.ShapeDtypeStruct(group_basis.shape, F32),
            jax.ShapeDtypeStruct(top_basis.shape, F32),
        ],
        compiler_params=params(32),
        cost_estimate=pl.CostEstimate(
            flops=20 * modes**3, bytes_accessed=24 * modes * modes, transcendentals=2 * modes
        ),
        name="finish",
    )(near, far, terms, group_basis, top_basis)


def body(
    leaf_mass, tile_mask, constraint_modes, leaf_fixed_modes, block_map, group_mass, top_mass,
    group_basis, top_basis,
):
    row_count, col_count = lax.axis_size("row"), lax.axis_size("col")
    sizes = {"row": row_count, "col": col_count}
    size = group_mass.shape[2]

    def swap(value, axis, bit):
        return lax.ppermute(value, axis, crossed(sizes[axis], bit))

    def half_of(half, own, after):
        return leaf_half(
            half, tile_mask, block_map, leaf_mass, constraint_modes, leaf_fixed_modes, own, after
        )

    basis = jnp.concatenate([group_basis[0], top_basis], axis=1)
    beside = swap(basis, "row", 1)
    first, keep, send = half_of(0, group_mass, basis)
    pair = jnp.concatenate([basis, beside], axis=0)
    pieces = [pair] + [swap(pair, "row", 2 * k) for k in range(1, row_count // 2)]
    second, top_keep, top_send = half_of(1, top_mass, pair)
    group_steps = exchanges(0, row_count, col_count)
    packed, terms, keep, send = prepare(
        group_steps[1], keep, send, swap(send, *group_steps[0]), top_keep, top_send, first, second,
        pieces,
    )

    def summed(value, axis):
        for b in range(bits_of(sizes[axis])):
            value = value + swap(value, axis, 1 << b)
        return value

    near = summed(packed, "row")
    far = summed(near, "col")
    coupling, group_modes, top_modes = finish(near, far, terms, group_basis, top_basis)

    def scattered(keep, send, steps):
        for i, step in enumerate(steps):
            other = swap(send, *step)
            if i == len(steps) - 1:
                return size * (keep + other)
            keep, send = fold(steps[i + 1], keep, other, packed)

    group_assembled = scattered(keep, send, group_steps[1:])[None]
    assembled = scattered(top_keep, top_send, exchanges(1, row_count, col_count))
    return coupling, group_modes, top_modes, group_assembled, assembled


def solution(mesh):
    leaf = P(("row", "col"), None, None)
    group = P("col", "row", None)
    in_specs = (
        leaf, leaf, leaf, leaf, leaf, group, P(("row", "col"), None), group, P("row", None),
    )
    out_specs = (
        P(("row", "col"), None, None, None), group, P("row", None), group, P(("row", "col"), None),
    )
    return jax.shard_map(body, mesh=mesh, in_specs=in_specs, out_specs=out_specs, check_vma=False)
```

time: 136 us -> 83.9 us (0.62)
  blocking collectives: 46.9 us -> 0 us
  starting transfers between devices: 14.9 us -> 18.7 us
  waiting for transfers between devices: 33 us -> 30 us
  Pallas kernels: 31.3 us -> 28.6 us
  local copies, waits for them, and re-layouts: 5.72 us -> 3.34 us
    all_gather x1 -> x0, blocking collectives: 33 us -> none  [body(): lax.all_gather(jnp.concatenate([group_basis[0], top_basis], axis=1), 'row...]
    all_to_all x4 -> x0, waiting for transfers between devices: 28.9 us -> none  [the longest x1 12.8 us: body(): top_rows = lax.all_to_all(top, 'col', 0, 0, tiled=True)]
    ppermute x1 -> x17, waiting for transfers between devices: 4.07 us -> 30 us  [swap(): return lax.ppermute(value, axis, crossed(sizes[axis], bit))]
    ppermute x1 -> x17, starting transfers between devices: 1.7 us -> 18.7 us  [swap(): return lax.ppermute(value, axis, crossed(sizes[axis], bit))]
    all_to_all x1 -> x0, blocking collectives: 13.9 us -> none  [body(): packed = lax.all_to_all(packed, both, 0, 0, tiled=True)]
    all_to_all x4 -> x0, starting transfers between devices: 13.2 us -> none  [the longest x1 3.65 us: body(): lax.all_to_all(keep + other, 'row', 0, 0, axis_index_groups=parities, til...]
    pallas_call x5 -> x9, Pallas kernels: 31.3 us -> 28.6 us  [the longest x2 19.8 us: leaf_half(): pl.pallas_call(functools.partial(leaf_kernel, half), in_specs=[SMEM] * 2...]
    reshape x2 -> x0, local copies, waits for them, and re-layouts: 1.54 us -> none  [body(): table = jnp.concatenate([tile_mask.reshape(-1), block_map.reshape(-1)])]
  transfers between devices with their start and end apart: 5 -> 17, of which waited for: 5 -> 8; matrix products, arithmetic and copies ran while one was open for 2% -> 1% of each run, Pallas kernels for 6% -> 34%
where the time goes in v3:
time: 83.9 us; the launch traced here: 83.5 us
  waiting for transfers between devices  30 us (36%)
  Pallas kernels  28.6 us (34%)
  starting transfers between devices  18.7 us (22%)
  local copies, waits for them, and re-layouts  3.34 us (4%)
  other arithmetic  2.14 us (3%)
    ppermute x17, waiting for transfers between devices, swap(): return lax.ppermute(value, axis, crossed(sizes[axis], bit))  30 us
    pallas_call x2, Pallas kernels, leaf_half(): pl.pallas_call(functools.partial(leaf_kernel, half), in_specs=[SMEM] * 2...  19.8 us
    ppermute x17, starting transfers between devices, swap(): return lax.ppermute(value, axis, crossed(sizes[axis], bit))  18.7 us
    pallas_call x1, Pallas kernels, finish(): pl.pallas_call(finish_kernel, in_specs=[VMEM] * 5, out_specs=[VMEM] * 3,...  7.16 us
    unnamed x16, local copies, waits for them, and re-layouts  3.34 us
  transfers between devices with their start and end apart: 17, of which 8 were waited for; matrix products, arithmetic and copies ran while one was open for 1% of the time, Pallas kernels for 34%

profile of v3, /device:TPU:0, one launch (start us, length us, event | category | flops | bytes accessed | tf_op | source)
XLA Modules:
  0.0 83.5 jit_solution(5169794332990625431)
XLA Ops:
  0.6 0.8 pad_maximum_fusion.1.after_ref
  1.4 0.0 copy-start
  1.4 0.0 copy-start.1
  1.4 0.0 copy-start.2
  1.4 3.0 %collective-permute-start.1 = (f32[64,256]{1,0:T(8,128)S(1)}, f32[64,256]{1,0:T(8,128)S(1)}, u32[]{:S(2)}, u32[]{:S(2)}) collective-permute-start(f32[64,256]{1,0:T(8,128)S(1)} %pad_maximum_fusion.1.after_ref), channel_id=1, source_target_pairs={{0,4},{4,0},{8,12},{12,8},{16,20},{20,16},{24,28},{28,24},{1,5},{5... | collective-permute-start | bytes 196616 | tf_op jit(solution)/shard_map/ppermute | solution.py:395
  4.4 0.0 copy-start.3
  4.4 1.0 %copy-done.3 = bf16[1,2048,128]{2,1,0:T(8,128)(2,1)S(1)} copy-done((bf16[1,2048,128]{2,1,0:T(8,128)(2,1)S(1)}, bf16[1,2048,128]{2,1,0:T(8,128)(2,1)}, u32[]{:S(2)}) %copy-start.3) | copy-done | bytes 524312
  5.5 0.0 copy-start.4
  5.5 0.9 %copy-done.4 = f32[1,64,512]{2,1,0:T(8,128)S(1)} copy-done((f32[1,64,512]{2,1,0:T(8,128)S(1)}, f32[1,64,512]{2,1,0:T(8,128)}, u32[]{:S(2)}) %copy-start.4) | copy-done | bytes 131096
  6.4 0.0 copy-start.6
  6.4 0.7 copy-done.6
  7.1 0.0 copy-start.7
  7.1 0.7 copy-done.7
  7.8 0.0 copy-start.5
  7.8 10.0 %leaf_group.1 = (f32[128,512]{1,0:T(8,128)S(1)}, f32[256,512]{1,0:T(8,128)S(1)}, f32[256,512]{1,0:T(8,128)S(1)}) custom-call(s32[1,16,16]{2,1,0:T(8,128)S(1)} %copy-done.6, s32[1,2,4]{2,1,0:T(2,128)S(1)} %copy-done.7, bf16[1,2048,2048]{2,1,0:T(8,128)(2,1)} %mass_hbm.3, bf16[1,2048,1024]{2,1,0:T(8,128)(2,1)} %modes_hbm.3, ...), custom_call_target="tpu_custom_call" | custom-call | flops 5637144576 | bytes 13107200 | tf_op jit(solution)/shard_map/leaf_group/pallas_call | solution.py:158
  17.8 0.4 collective-permute-start
  18.2 0.0 collective-permute-done.1
  18.2 0.0 copy-done
  18.2 0.0 copy-done.1
  18.2 0.0 copy-done.2
  18.2 0.0 copy-done.5
  18.2 9.8 %leaf_top.1 = (f32[128,512]{1,0:T(8,128)S(1)}, f32[256,512]{1,0:T(8,128)S(1)}, f32[256,512]{1,0:T(8,128)S(1)}) custom-call(s32[1,16,16]{2,1,0:T(8,128)S(1)} %copy-done.6, s32[1,2,4]{2,1,0:T(2,128)S(1)} %copy-done.7, bf16[1,2048,2048]{2,1,0:T(8,128)(2,1)} %mass_hbm.3, bf16[1,2048,1024]{2,1,0:T(8,128)(2,1)S(1)} %copy-done.2, ...), custom_call_target="tpu_custom_call" | custom-call | flops 5637144576 | bytes 13107200 | tf_op jit(solution)/shard_map/leaf_top/pallas_call | solution.py:158
  28.0 0.1 collective-permute-start.12
  28.1 2.2 %collective-permute-start.2 = (f32[128,256]{1,0:T(8,128)S(1)}, f32[128,256]{1,0:T(8,128)S(1)}, u32[]{:S(2)}, u32[]{:S(2)}) collective-permute-start(f32[128,256]{1,0:T(8,128)S(1)} %pad_maximum_fusion.after_ref.refs_0_), channel_id=1, source_target_pairs={{0,8},{4,12},{8,0},{12,4},{16,24},{20,28},{24,16},{28,20},{1,9},{5... | collective-permute-start | bytes 393224 | tf_op jit(solution)/shard_map/ppermute | solution.py:395
  30.3 2.6 %collective-permute-start.3 = (f32[128,256]{1,0:T(8,128)S(1)}, f32[128,256]{1,0:T(8,128)S(1)}, u32[]{:S(2)}, u32[]{:S(2)}) collective-permute-start(f32[128,256]{1,0:T(8,128)S(1)} %pad_maximum_fusion.after_ref.refs_0_), channel_id=1, source_target_pairs={{0,16},{4,20},{8,24},{12,28},{16,0},{20,4},{24,8},{28,12},{1,17},{... | collective-permute-start | bytes 393224 | tf_op jit(solution)/shard_map/ppermute | solution.py:395
  32.9 0.0 collective-permute-start.4
  32.9 3.7 %collective-permute-done.2.refs_1_ = f32[128,256]{1,0:T(8,128)S(1)} collective-permute-done((f32[128,256]{1,0:T(8,128)S(1)}, f32[128,256]{1,0:T(8,128)S(1)}, u32[]{:S(2)}, u32[]{:S(2)}) %collective-permute-start.2) | collective-permute-done | bytes 131104 | tf_op jit(solution)/shard_map/ppermute | solution.py:395
  36.6 6.6 %collective-permute-done.3.refs_2_ = f32[128,256]{1,0:T(8,128)S(1)} collective-permute-done((f32[128,256]{1,0:T(8,128)S(1)}, f32[128,256]{1,0:T(8,128)S(1)}, u32[]{:S(2)}, u32[]{:S(2)}) %collective-permute-start.3) | collective-permute-done | bytes 131104 | tf_op jit(solution)/shard_map/ppermute | solution.py:395
  43.2 0.0 collective-permute-done.4.refs_3_
  43.2 0.0 collective-permute-done.other_ref
  43.2 1.4 %prepare.1 = (f32[136,128]{1,0:T(8,128)S(1)}, f32[2,128,128]{2,1,0:T(8,128)S(1)}, f32[128,512]{1,0:T(8,128)S(1)}, f32[128,512]{1,0:T(8,128)S(1)}) custom-call(f32[256,512]{1,0:T(8,128)S(1)} %get-tuple-element.28.keep_ref, f32[256,512]{1,0:T(8,128)S(1)} %get-tuple-element.29.send_ref, f32[256,512]{1,0:T(8,128)S(1)} %collective-permute-done.other_ref, ...), custom_call_target="tpu_custom_call" | custom-call | flops 402653184 | bytes 3145728 | tf_op jit(solution)/shard_map/prepare/pallas_call | solution.py:255
  44.6 0.0 collective-permute-done.12.other_ref
  44.6 0.1 fold.6
  44.7 1.6 %collective-permute-start.13 = (f32[128,512]{1,0:T(8,128)S(1)}, f32[128,512]{1,0:T(8,128)S(1)}, u32[]{:S(2)}, u32[]{:S(2)}) collective-permute-start(f32[128,512]{1,0:T(8,128)S(1)} %get-tuple-element.44), channel_id=1, source_target_pairs={{0,2},{1,3},{2,0},{3,1},{4,6},{5,7},{6,4},{7,5},{8,10},{9,11},{10,... | collective-permute-start | bytes 786440 | tf_op jit(solution)/shard_map/ppermute | solution.py:395
  46.3 3.6 %collective-permute-start.10 = (f32[128,512]{1,0:T(8,128)S(1)}, f32[128,512]{1,0:T(8,128)S(1)}, u32[]{:S(2)}, u32[]{:S(2)}) collective-permute-start(f32[128,512]{1,0:T(8,128)S(1)} %get-tuple-element.40), channel_id=1, source_target_pairs={{0,16},{4,20},{8,24},{12,28},{16,0},{20,4},{24,8},{28,12},{1,17},{... | collective-permute-start | bytes 786440 | tf_op jit(solution)/shard_map/ppermute | solution.py:395
  49.9 1.1 %collective-permute-start.5 = (f32[136,128]{1,0:T(8,128)S(1)}, f32[136,128]{1,0:T(8,128)S(1)}, u32[]{:S(2)}, u32[]{:S(2)}) collective-permute-start(f32[136,128]{1,0:T(8,128)S(1)} %get-tuple-element.34.after_ref), channel_id=1, source_target_pairs={{0,4},{4,0},{8,12},{12,8},{16,20},{20,16},{24,28},{28,24},{1,5},{5... | collective-permute-start | bytes 208904 | tf_op jit(solution)/shard_map/ppermute | solution.py:395
  51.1 3.2 %collective-permute-done.5 = f32[136,128]{1,0:T(8,128)S(1)} collective-permute-done((f32[136,128]{1,0:T(8,128)S(1)}, f32[136,128]{1,0:T(8,128)S(1)}, u32[]{:S(2)}, u32[]{:S(2)}) %collective-permute-start.5) | collective-permute-done | bytes 69664 | tf_op jit(solution)/shard_map/ppermute | solution.py:395
  54.3 0.1 collective-permute-start.6
  54.3 6.4 %collective-permute-done.6 = f32[136,128]{1,0:T(8,128)S(1)} collective-permute-done((f32[136,128]{1,0:T(8,128)S(1)}, f32[136,128]{1,0:T(8,128)S(1)}, u32[]{:S(2)}, u32[]{:S(2)}) %collective-permute-start.6) | collective-permute-done | bytes 69664 | tf_op jit(solution)/shard_map/ppermute | solution.py:395
  60.7 0.1 collective-permute-start.7
  60.8 0.0 collective-permute-done.13.other_ref
  60.9 1.2 %collective-permute-start.14 = (f32[64,512]{1,0:T(8,128)S(1)}, f32[64,512]{1,0:T(8,128)S(1)}, u32[]{:S(2)}, u32[]{:S(2)}) collective-permute-start(f32[64,512]{1,0:T(8,128)S(1)} %get-tuple-element.46), channel_id=1, source_target_pairs={{0,4},{4,0},{8,12},{12,8},{16,20},{20,16},{24,28},{28,24},{1,5},{5... | collective-permute-start | bytes 393224 | tf_op jit(solution)/shard_map/ppermute | solution.py:395
  62.1 3.9 %collective-permute-done.7 = f32[136,128]{1,0:T(8,128)S(1)} collective-permute-done((f32[136,128]{1,0:T(8,128)S(1)}, f32[136,128]{1,0:T(8,128)S(1)}, u32[]{:S(2)}, u32[]{:S(2)}) %collective-permute-start.7) | collective-permute-done | bytes 69664 | tf_op jit(solution)/shard_map/ppermute | solution.py:395
  66.0 0.1 collective-permute-start.8
  66.1 0.0 collective-permute-done.10.other_ref
  66.1 0.1 collective-permute-start.11
  66.2 1.1 %collective-permute-done.8 = f32[136,128]{1,0:T(8,128)S(1)} collective-permute-done((f32[136,128]{1,0:T(8,128)S(1)}, f32[136,128]{1,0:T(8,128)S(1)}, u32[]{:S(2)}, u32[]{:S(2)}) %collective-permute-start.8) | collective-permute-done | bytes 69664 | tf_op jit(solution)/shard_map/ppermute | solution.py:395
  67.3 0.6 collective-permute-start.9
  67.9 0.0 collective-permute-done.14.other_ref
  67.9 1.0 %collective-permute-start.15 = (f32[32,512]{1,0:T(8,128)S(1)}, f32[32,512]{1,0:T(8,128)S(1)}, u32[]{:S(2)}, u32[]{:S(2)}) collective-permute-start(f32[32,512]{1,0:T(8,128)S(1)} %get-tuple-element.48), channel_id=1, source_target_pairs={{0,16},{4,20},{8,24},{12,28},{16,0},{20,4},{24,8},{28,12},{1,17},{... | collective-permute-start | bytes 196616 | tf_op jit(solution)/shard_map/ppermute | solution.py:395
  69.0 2.7 %collective-permute-done.9 = f32[136,128]{1,0:T(8,128)S(1)} collective-permute-done((f32[136,128]{1,0:T(8,128)S(1)}, f32[136,128]{1,0:T(8,128)S(1)}, u32[]{:S(2)}, u32[]{:S(2)}) %collective-permute-start.9) | collective-permute-done | bytes 69664 | tf_op jit(solution)/shard_map/ppermute | solution.py:395
  71.7 7.2 %finish.1 = (f32[1,128,2,128]{3,2,1,0:T(2,128)}, f32[1,64,128]{2,1,0:T(8,128)}, f32[64,128]{1,0:T(8,128)}) custom-call(f32[136,128]{1,0:T(8,128)S(1)} %add.23.near_ref, f32[136,128]{1,0:T(8,128)S(1)} %add.25.far_ref, f32[2,128,128]{2,1,0:T(8,128)S(1)} %get-tuple-element.35.terms_ref, f32[1,64,128]{2,1,0:T(8,128)S(1)} %copy-done.1, f32[64,128]{1,0:T(8,128)S(1)} %copy-done), custom_call_target="tpu_custom_call" | custom-call | flops 41943040 | bytes 393216 | tf_op jit(solution)/shard_map/finish/pallas_call | solution.py:369
  78.9 0.0 collective-permute-done.15.other_ref
  78.9 1.0 %collective-permute-start.16 = (f32[16,512]{1,0:T(8,128)S(1)}, f32[16,512]{1,0:T(8,128)S(1)}, u32[]{:S(2)}, u32[]{:S(2)}) collective-permute-start(f32[16,512]{1,0:T(8,128)S(1)} %get-tuple-element.50), channel_id=1, source_target_pairs={{0,8},{4,12},{8,0},{12,4},{16,24},{20,28},{24,16},{28,20},{1,9},{5... | collective-permute-start | bytes 98312 | tf_op jit(solution)/shard_map/ppermute | solution.py:395
  79.9 0.0 collective-permute-done.11
  79.9 0.7 multiply_bitcast_fusion
  80.6 2.3 %collective-permute-done.16 = f32[16,512]{1,0:T(8,128)S(1)} collective-permute-done((f32[16,512]{1,0:T(8,128)S(1)}, f32[16,512]{1,0:T(8,128)S(1)}, u32[]{:S(2)}, u32[]{:S(2)}) %collective-permute-start.16) | collective-permute-done | bytes 32800 | tf_op jit(solution)/shard_map/ppermute | solution.py:395
  82.9 0.6 add_multiply_fusion
  (10 shorter events, 0.2 us)
Async XLA Ops:
  1.4 16.7 %copy-start = (f32[64,128]{1,0:T(8,128)S(1)}, f32[64,128]{1,0:T(8,128)}, u32[]{:S(2)}) copy-start(f32[64,128]{1,0:T(8,128)} %top_basis_ref.1) | copy-start | bytes 98308
  1.4 16.7 %copy-start.1 = (f32[1,64,128]{2,1,0:T(8,128)S(1)}, f32[1,64,128]{2,1,0:T(8,128)}, u32[]{:S(2)}) copy-start(f32[1,64,128]{2,1,0:T(8,128)} %group_basis_ref.1) | copy-start | bytes 98308
  1.4 16.8 %copy-start.2 = (bf16[1,2048,1024]{2,1,0:T(8,128)(2,1)S(1)}, bf16[1,2048,1024]{2,1,0:T(8,128)(2,1)}, u32[]{:S(2)}) copy-start(bf16[1,2048,1024]{2,1,0:T(8,128)(2,1)} %modes_hbm.3) | copy-start | bytes 12582916
  1.4 16.7 %collective-permute-start.1 = (f32[64,256]{1,0:T(8,128)S(1)}, f32[64,256]{1,0:T(8,128)S(1)}, u32[]{:S(2)}, u32[]{:S(2)}) collective-permute-start(f32[64,256]{1,0:T(8,128)S(1)} %pad_maximum_fusion.1.after_ref), channel_id=1, source_target_pairs={{0,4},{4,0},{8,12},{12,8},{16,20},{20,16},{24,28},{28,24},{1,5},{5... | collective-permute-start | bytes 196616 | tf_op jit(solution)/shard_map/ppermute | solution.py:395
  4.4 1.0 %copy-start.3 = (bf16[1,2048,128]{2,1,0:T(8,128)(2,1)S(1)}, bf16[1,2048,128]{2,1,0:T(8,128)(2,1)}, u32[]{:S(2)}) copy-start(bf16[1,2048,128]{2,1,0:T(8,128)(2,1)} %fixed_hbm.3) | copy-start | bytes 1572868
  5.5 0.9 %copy-start.4 = (f32[1,64,512]{2,1,0:T(8,128)S(1)}, f32[1,64,512]{2,1,0:T(8,128)}, u32[]{:S(2)}) copy-start(f32[1,64,512]{2,1,0:T(8,128)} %own_hbm.2) | copy-start | bytes 393220
  6.4 0.7 copy-start.6
  7.1 0.7 copy-start.7
  7.8 10.4 %copy-start.5 = (f32[16,512]{1,0:T(8,128)S(1)}, f32[16,512]{1,0:T(8,128)}, u32[]{:S(2)}) copy-start(f32[16,512]{1,0:T(8,128)} %own_hbm.3) | copy-start | bytes 98308
  17.8 25.4 %collective-permute-start = (f32[256,512]{1,0:T(8,128)S(1)}, f32[256,512]{1,0:T(8,128)S(1)}, u32[]{:S(2)}, u32[]{:S(2)}) collective-permute-start(f32[256,512]{1,0:T(8,128)S(1)} %get-tuple-element.29.send_ref), channel_id=1, source_target_pairs={{0,4},{4,0},{8,12},{12,8},{16,20},{20,16},{24,28},{28,24},{1,5},{5... | collective-permute-start | bytes 1572872 | tf_op jit(solution)/shard_map/ppermute | solution.py:395
  28.0 16.6 %collective-permute-start.12 = (f32[256,512]{1,0:T(8,128)S(1)}, f32[256,512]{1,0:T(8,128)S(1)}, u32[]{:S(2)}, u32[]{:S(2)}) collective-permute-start(f32[256,512]{1,0:T(8,128)S(1)} %get-tuple-element.31.top_send_ref), channel_id=1, source_target_pairs={{0,1},{1,0},{2,3},{3,2},{4,5},{5,4},{6,7},{7,6},{8,9},{9,8},{10,11... | collective-permute-start | bytes 1572872 | tf_op jit(solution)/shard_map/ppermute | solution.py:395
  28.1 8.5 %collective-permute-start.2 = (f32[128,256]{1,0:T(8,128)S(1)}, f32[128,256]{1,0:T(8,128)S(1)}, u32[]{:S(2)}, u32[]{:S(2)}) collective-permute-start(f32[128,256]{1,0:T(8,128)S(1)} %pad_maximum_fusion.after_ref.refs_0_), channel_id=1, source_target_pairs={{0,8},{4,12},{8,0},{12,4},{16,24},{20,28},{24,16},{28,20},{1,9},{5... | collective-permute-start | bytes 393224 | tf_op jit(solution)/shard_map/ppermute | solution.py:395
  30.3 12.9 %collective-permute-start.3 = (f32[128,256]{1,0:T(8,128)S(1)}, f32[128,256]{1,0:T(8,128)S(1)}, u32[]{:S(2)}, u32[]{:S(2)}) collective-permute-start(f32[128,256]{1,0:T(8,128)S(1)} %pad_maximum_fusion.after_ref.refs_0_), channel_id=1, source_target_pairs={{0,16},{4,20},{8,24},{12,28},{16,0},{20,4},{24,8},{28,12},{1,17},{... | collective-permute-start | bytes 393224 | tf_op jit(solution)/shard_map/ppermute | solution.py:395
  32.9 10.3 %collective-permute-start.4 = (f32[128,256]{1,0:T(8,128)S(1)}, f32[128,256]{1,0:T(8,128)S(1)}, u32[]{:S(2)}, u32[]{:S(2)}) collective-permute-start(f32[128,256]{1,0:T(8,128)S(1)} %pad_maximum_fusion.after_ref.refs_0_), channel_id=1, source_target_pairs={{0,24},{4,28},{8,16},{12,20},{16,8},{20,12},{24,0},{28,4},{1,25},{... | collective-permute-start | bytes 393224 | tf_op jit(solution)/shard_map/ppermute | solution.py:395
  44.7 16.1 %collective-permute-start.13 = (f32[128,512]{1,0:T(8,128)S(1)}, f32[128,512]{1,0:T(8,128)S(1)}, u32[]{:S(2)}, u32[]{:S(2)}) collective-permute-start(f32[128,512]{1,0:T(8,128)S(1)} %get-tuple-element.44), channel_id=1, source_target_pairs={{0,2},{1,3},{2,0},{3,1},{4,6},{5,7},{6,4},{7,5},{8,10},{9,11},{10,... | collective-permute-start | bytes 786440 | tf_op jit(solution)/shard_map/ppermute | solution.py:395
  46.3 19.8 %collective-permute-start.10 = (f32[128,512]{1,0:T(8,128)S(1)}, f32[128,512]{1,0:T(8,128)S(1)}, u32[]{:S(2)}, u32[]{:S(2)}) collective-permute-start(f32[128,512]{1,0:T(8,128)S(1)} %get-tuple-element.40), channel_id=1, source_target_pairs={{0,16},{4,20},{8,24},{12,28},{16,0},{20,4},{24,8},{28,12},{1,17},{... | collective-permute-start | bytes 786440 | tf_op jit(solution)/shard_map/ppermute | solution.py:395
  49.9 4.3 %collective-permute-start.5 = (f32[136,128]{1,0:T(8,128)S(1)}, f32[136,128]{1,0:T(8,128)S(1)}, u32[]{:S(2)}, u32[]{:S(2)}) collective-permute-start(f32[136,128]{1,0:T(8,128)S(1)} %get-tuple-element.34.after_ref), channel_id=1, source_target_pairs={{0,4},{4,0},{8,12},{12,8},{16,20},{20,16},{24,28},{28,24},{1,5},{5... | collective-permute-start | bytes 208904 | tf_op jit(solution)/shard_map/ppermute | solution.py:395
  54.3 6.5 %collective-permute-start.6 = (f32[136,128]{1,0:T(8,128)S(1)}, f32[136,128]{1,0:T(8,128)S(1)}, u32[]{:S(2)}, u32[]{:S(2)}) collective-permute-start(f32[136,128]{1,0:T(8,128)S(1)} %add.21), channel_id=1, source_target_pairs={{0,8},{4,12},{8,0},{12,4},{16,24},{20,28},{24,16},{28,20},{1,9},{5... | collective-permute-start | bytes 208904 | tf_op jit(solution)/shard_map/ppermute | solution.py:395
  60.7 5.3 %collective-permute-start.7 = (f32[136,128]{1,0:T(8,128)S(1)}, f32[136,128]{1,0:T(8,128)S(1)}, u32[]{:S(2)}, u32[]{:S(2)}) collective-permute-start(f32[136,128]{1,0:T(8,128)S(1)} %add.22), channel_id=1, source_target_pairs={{0,16},{4,20},{8,24},{12,28},{16,0},{20,4},{24,8},{28,12},{1,17},{... | collective-permute-start | bytes 208904 | tf_op jit(solution)/shard_map/ppermute | solution.py:395
  60.9 7.1 %collective-permute-start.14 = (f32[64,512]{1,0:T(8,128)S(1)}, f32[64,512]{1,0:T(8,128)S(1)}, u32[]{:S(2)}, u32[]{:S(2)}) collective-permute-start(f32[64,512]{1,0:T(8,128)S(1)} %get-tuple-element.46), channel_id=1, source_target_pairs={{0,4},{4,0},{8,12},{12,8},{16,20},{20,16},{24,28},{28,24},{1,5},{5... | collective-permute-start | bytes 393224 | tf_op jit(solution)/shard_map/ppermute | solution.py:395
  66.0 1.3 %collective-permute-start.8 = (f32[136,128]{1,0:T(8,128)S(1)}, f32[136,128]{1,0:T(8,128)S(1)}, u32[]{:S(2)}, u32[]{:S(2)}) collective-permute-start(f32[136,128]{1,0:T(8,128)S(1)} %add.23.near_ref), channel_id=1, source_target_pairs={{0,1},{1,0},{2,3},{3,2},{4,5},{5,4},{6,7},{7,6},{8,9},{9,8},{10,11... | collective-permute-start | bytes 208904 | tf_op jit(solution)/shard_map/ppermute | solution.py:395
  66.1 13.8 %collective-permute-start.11 = (f32[64,512]{1,0:T(8,128)S(1)}, f32[64,512]{1,0:T(8,128)S(1)}, u32[]{:S(2)}, u32[]{:S(2)}) collective-permute-start(f32[64,512]{1,0:T(8,128)S(1)} %get-tuple-element.42), channel_id=1, source_target_pairs={{0,8},{4,12},{8,0},{12,4},{16,24},{20,28},{24,16},{28,20},{1,9},{5... | collective-permute-start | bytes 393224 | tf_op jit(solution)/shard_map/ppermute | solution.py:395
  67.3 4.4 %collective-permute-start.9 = (f32[136,128]{1,0:T(8,128)S(1)}, f32[136,128]{1,0:T(8,128)S(1)}, u32[]{:S(2)}, u32[]{:S(2)}) collective-permute-start(f32[136,128]{1,0:T(8,128)S(1)} %add.24), channel_id=1, source_target_pairs={{0,2},{1,3},{2,0},{3,1},{4,6},{5,7},{6,4},{7,5},{8,10},{9,11},{10,... | collective-permute-start | bytes 208904 | tf_op jit(solution)/shard_map/ppermute | solution.py:395
  67.9 11.0 %collective-permute-start.15 = (f32[32,512]{1,0:T(8,128)S(1)}, f32[32,512]{1,0:T(8,128)S(1)}, u32[]{:S(2)}, u32[]{:S(2)}) collective-permute-start(f32[32,512]{1,0:T(8,128)S(1)} %get-tuple-element.48), channel_id=1, source_target_pairs={{0,16},{4,20},{8,24},{12,28},{16,0},{20,4},{24,8},{28,12},{1,17},{... | collective-permute-start | bytes 196616 | tf_op jit(solution)/shard_map/ppermute | solution.py:395
  78.9 4.0 %collective-permute-start.16 = (f32[16,512]{1,0:T(8,128)S(1)}, f32[16,512]{1,0:T(8,128)S(1)}, u32[]{:S(2)}, u32[]{:S(2)}) collective-permute-start(f32[16,512]{1,0:T(8,128)S(1)} %get-tuple-element.50), channel_id=1, source_target_pairs={{0,8},{4,12},{8,0},{12,4},{16,24},{20,28},{24,16},{28,20},{1,9},{5... | collective-permute-start | bytes 98312 | tf_op jit(solution)/shard_map/ppermute | solution.py:395

commit v4 on v3

--- a/solution.py
+++ b/solution.py
@@ -71,11 +71,21 @@
     return order
 
 
-def leaf_kernel(
-    half, mask_ref, map_ref, mass_hbm, modes_hbm, fixed_hbm, own_hbm, after_ref, moved_ref, *refs
-):
-    chunks = refs[:-8]
-    mass_ref, modes_ref, fixed_ref, own_ref, whole_ref, partial_ref, projected_ref, sems = refs[-8:]
+def share_place(steps):
+    place = 0
+    for axis, bit in steps:
+        place = 2 * place + lax.rem(lax.axis_index(axis) // bit, 2)
+    return place
+
+
+def leaf_kernel(half, mask_ref, map_ref, mass_hbm, modes_hbm, *refs):
+    if half == 0:
+        after_ref, keep_ref, send_ref, loaded_ref = refs[:4]
+    else:
+        fixed_hbm, first_ref, after_ref, keep_ref, send_ref, moved_ref = refs[:6]
+        fixed_ref, loaded_ref = refs[-2:]
+        refs = refs[:-2]
+    mass_ref, modes_ref, whole_ref, partial_ref, sems = refs[-5:]
     row, col = lax.axis_index("row"), lax.axis_index("col")
     row_count, col_count = lax.axis_size("row"), lax.axis_size("col")
     rows, size = modes_ref.shape
@@ -85,20 +95,17 @@
     def mass_copy(i):
         window = pl.ds(pl.multiple_of(i * height, height), height)
         return pltpu.make_async_copy(
-            mass_hbm.at[0, window], mass_ref.at[window], sems.at[3 + i]
+            mass_hbm.at[0, window], mass_ref.at[window], sems.at[2 + i]
         )
 
     half_modes = modes_hbm.at[0, :, pl.ds(half * size, size)]
     modes_copy = pltpu.make_async_copy(half_modes, modes_ref, sems.at[0])
-    fixed_copy = pltpu.make_async_copy(fixed_hbm.at[0], fixed_ref, sems.at[1])
-    own_source = own_hbm.at[0] if half == 0 else own_hbm
-    own_copy = pltpu.make_async_copy(own_source, own_ref, sems.at[2])
     modes_copy.start()
-    mass_copy(0).start()
-    fixed_copy.start()
-    for i in range(1, MASS_PARTS):
+    for i in range(MASS_PARTS):
         mass_copy(i).start()
-    own_copy.start()
+    if half == 1:
+        fixed_copy = pltpu.make_async_copy(fixed_hbm.at[0], fixed_ref, sems.at[1])
+        fixed_copy.start()
     modes_copy.wait()
 
     def part(i, first):
@@ -114,17 +121,13 @@
             lines.append(jnp.concatenate(pieces, axis=1))
         masked = jnp.concatenate(lines, axis=0)
         loaded = jnp.dot(masked, modes_ref[...], preferred_element_type=F32).astype(BF16)
-        if first:
-            fixed_copy.wait()
         window = pl.ds(pl.multiple_of(i * height, height), height)
+        loaded_ref[window, :] = loaded
         partial = rows_first(modes_ref[window, :], loaded)
-        projected = rows_first(fixed_ref[window, :], loaded)
         if first:
             partial_ref[...] = partial
-            projected_ref[...] = projected
         else:
             partial_ref[...] += partial
-            projected_ref[...] += projected
 
     part(0, True)
     lax.fori_loop(1, MASS_PARTS, lambda i, _: part(i, False), None)
@@ -132,52 +135,58 @@
     blocks = size // TILE
     to = [pl.multiple_of(map_ref[0, half, a] * TILE, TILE) for a in range(blocks)]
     for b in range(blocks):
-        source = slice(b * TILE, (b + 1) * TILE)
-        moved_ref[:, pl.ds(to[b], TILE)] = projected_ref[:, source]
         for a in range(blocks):
             whole_ref[pl.ds(to[a], TILE), pl.ds(to[b], TILE)] = partial_ref[
-                a * TILE : (a + 1) * TILE, source
+                a * TILE : (a + 1) * TILE, b * TILE : (b + 1) * TILE
             ]
-    own_copy.wait()
-    share = own_ref.shape[0]
     order = cut_order(half, row_count, col_count)
-    add_own(whole_ref, own_ref[...], row if half == 0 else row * col_count + col)
+    share = size // len(order)
     bit = lax.rem(row if half == 0 else col, 2)
-    for k, chunk in enumerate(chunks):
-        for i, place in enumerate(order):
-            if i < len(order) // 2:
-                step = order[i + len(order) // 2] - place
-                copy_rows(chunk, i * share, whole_ref, place + step * lax.rem(bit + k, 2), share)
-
-
-def leaf_half(half, tile_mask, block_map, leaf_mass, constraint_modes, fixed, own, after):
+    for k, chunk in enumerate((keep_ref, send_ref)):
+        for i in range(len(order) // 2):
+            step = order[i + len(order) // 2] - order[i]
+            copy_rows(chunk, i * share, whole_ref, order[i] + step * lax.rem(bit + k, 2), share)
+    if half == 1:
+        fixed_copy.wait()
+        for k, ref in enumerate((first_ref, loaded_ref)):
+            projected = rows_first(fixed_ref[...], ref[...])
+            for b in range(blocks):
+                at = pl.multiple_of(map_ref[0, k, b] * TILE, TILE)
+                moved_ref[k, :, pl.ds(at, TILE)] = projected[:, b * TILE : (b + 1) * TILE]
+
+
+def leaf_half(half, tile_mask, block_map, leaf_mass, constraint_modes, more, after):
     rows, size = constraint_modes.shape[1], constraint_modes.shape[2] // 2
-    modes = fixed.shape[2]
-    outs = [jax.ShapeDtypeStruct((modes, size), F32)]
-    outs += [jax.ShapeDtypeStruct((size // 2, size), F32)] * 2
+    outs = [jax.ShapeDtypeStruct((size // 2, size), F32)] * 2
+    scratch = [
+        pltpu.VMEM((rows, rows), BF16),
+        pltpu.VMEM((rows, size), BF16),
+        pltpu.VMEM((size, size), F32),
+        pltpu.VMEM((size, size), F32),
+        pltpu.SemaphoreType.DMA((2 + MASS_PARTS,)),
+    ]
+    if half == 0:
+        outs.append(jax.ShapeDtypeStruct((rows, size), BF16))
+        specs = []
+    else:
+        modes = more[0].shape[2]
+        outs.append(jax.ShapeDtypeStruct((2, modes, size), F32))
+        scratch += [pltpu.VMEM((rows, modes), BF16), pltpu.VMEM((rows, size), BF16)]
+        specs = [HBM, VMEM]
     return pl.pallas_call(
         functools.partial(leaf_kernel, half),
-        in_specs=[SMEM] * 2 + [HBM] * 4 + [pl.BlockSpec(memory_space=pl.ANY)],
+        in_specs=[SMEM] * 2 + [HBM] * 2 + specs + [pl.BlockSpec(memory_space=pl.ANY)],
         out_specs=[VMEM] * len(outs),
         out_shape=outs,
-        scratch_shapes=[
-            pltpu.VMEM((rows, rows), BF16),
-            pltpu.VMEM((rows, size), BF16),
-            pltpu.VMEM((rows, modes), BF16),
-            pltpu.VMEM(own.shape[-2:], F32),
-            pltpu.VMEM((size, size), F32),
-            pltpu.VMEM((size, size), F32),
-            pltpu.VMEM((modes, size), F32),
-            pltpu.SemaphoreType.DMA((3 + MASS_PARTS,)),
-        ],
+        scratch_shapes=scratch,
         compiler_params=params(LEAF_MEGABYTES),
         cost_estimate=pl.CostEstimate(
-            flops=2 * rows * size * (rows + size + modes),
-            bytes_accessed=2 * rows * (rows + size + modes) + 8 * size * size,
+            flops=2 * rows * size * (rows + size),
+            bytes_accessed=2 * rows * (rows + size) + 8 * size * size,
             transcendentals=0,
         ),
         name="leaf_group" if half == 0 else "leaf_top",
-    )(tile_mask, block_map, leaf_mass, constraint_modes, fixed, own, after)
+    )(tile_mask, block_map, leaf_mass, constraint_modes, *more, after)
 
 
 def split(value):
@@ -204,15 +213,25 @@
 
 
 def prepare_kernel(
-    count, step, keep_ref, send_ref, other_ref, top_keep_ref, top_send_ref, first_ref, second_ref, *refs
+    count, keep_in, send_ref, other_ref, top_keep_in, top_send_ref, moved_ref, group_own_ref,
+    top_own_ref, *refs,
 ):
     pieces = refs[:count]
-    packed_ref, terms_ref, next_ref, next_send_ref, bases_ref = refs[count:]
-    halve(step, keep_ref, other_ref, next_ref, next_send_ref)
+    (
+        packed_ref, terms_ref, next_ref, next_send_ref, top_keep_ref, top_next_ref, bases_ref, keep_ref
+    ) = refs[count:]
     modes = terms_ref.shape[2]
     size = bases_ref.shape[0]
     row, col = lax.axis_index("row"), lax.axis_index("col")
     row_count, col_count = lax.axis_size("row"), lax.axis_size("col")
+    group_steps = exchanges(0, row_count, col_count)
+    top_steps = exchanges(1, row_count, col_count)
+    keep_ref[...] = keep_in[...]
+    add_own(keep_ref, group_own_ref[0], share_place(group_steps[1:]))
+    halve(group_steps[1], keep_ref, other_ref, next_ref, next_send_ref)
+    top_keep_ref[...] = top_keep_in[...]
+    add_own(top_keep_ref, top_own_ref[...], share_place(top_steps[1:]))
+    top_next_ref[...] = top_send_ref[...]
     line = size // row_count
     for k, piece in enumerate(pieces):
         pair = lax.bitwise_xor(row // 2, k)
@@ -240,8 +259,7 @@
         applied = three_pass(split(matrix), basis)
         gram = three_pass(split(ordered), split(applied), turn=True)
         grams.append(0.5 * (gram + gram.T))
-        moved = (first_ref, second_ref)[half]
-        terms_ref[half] = three_pass(split(moved[...]), basis)
+        terms_ref[half] = three_pass(split(moved_ref[half]), basis)
     down = lax.broadcasted_iota(jnp.int32, (modes, modes), 0)
     across = lax.broadcasted_iota(jnp.int32, (modes, modes), 1)
     packed_ref[:modes, :] = jnp.where(down >= across, grams[0], grams[1])
@@ -249,26 +267,29 @@
     packed_ref[modes:, :] = jnp.broadcast_to(diagonal, (SUBLANES, modes))
 
 
-def prepare(step, keep, send, other, top_keep, top_send, first, second, pieces):
-    modes, size = first.shape
+def prepare(keep, send, other, top_keep, top_send, moved, group_own, top_own, pieces):
+    _, modes, size = moved.shape
     part = jax.ShapeDtypeStruct((keep.shape[0] // 2, size), F32)
+    half = jax.ShapeDtypeStruct(keep.shape, F32)
     return pl.pallas_call(
-        functools.partial(prepare_kernel, len(pieces), step),
-        in_specs=[VMEM] * (7 + len(pieces)),
-        out_specs=[VMEM] * 4,
+        functools.partial(prepare_kernel, len(pieces)),
+        in_specs=[VMEM] * (8 + len(pieces)),
+        out_specs=[VMEM] * 6,
         out_shape=[
             jax.ShapeDtypeStruct((modes + SUBLANES, modes), F32),
             jax.ShapeDtypeStruct((2, modes, modes), F32),
             part,
             part,
+            half,
+            half,
         ],
-        scratch_shapes=[pltpu.VMEM((size, 2 * modes), F32)],
+        scratch_shapes=[pltpu.VMEM((size, 2 * modes), F32), pltpu.VMEM(keep.shape, F32)],
         compiler_params=params(32),
         cost_estimate=pl.CostEstimate(
             flops=12 * size * size * modes, bytes_accessed=12 * size * size, transcendentals=0
         ),
         name="prepare",
-    )(keep, send, other, top_keep, top_send, first, second, *pieces)
+    )(keep, send, other, top_keep, top_send, moved, group_own, top_own, *pieces)
 
 
 def fold_kernel(step, keep_ref, other_ref, after_ref, next_ref, send_ref):
@@ -342,7 +363,13 @@
     return uppers, [jnp.concatenate(d, axis=0) for d in diagonals]
 
 
-def finish_kernel(near_ref, far_ref, terms_ref, group_basis_ref, top_basis_ref, coupling_ref, group_ref, top_ref):
+def finish_kernel(
+    near_ref, far_ref, terms_ref, group_basis_ref, top_basis_ref, keep_ref, other_ref, top_keep_ref,
+    top_other_ref, coupling_ref, group_ref, top_ref, assembled_ref, top_assembled_ref,
+):
+    size = assembled_ref.shape[2]
+    assembled_ref[0] = size * (keep_ref[...] + other_ref[...])
+    top_assembled_ref[...] = size * (top_keep_ref[...] + top_other_ref[...])
     modes = near_ref.shape[1]
     down = lax.broadcasted_iota(jnp.int32, (modes, modes), 0)
     across = lax.broadcasted_iota(jnp.int32, (modes, modes), 1)
@@ -364,23 +391,25 @@
             top_ref[...] = result[modes:]
 
 
-def finish(near, far, terms, group_basis, top_basis):
+def finish(near, far, terms, group_basis, top_basis, group_parts, top_parts):
     modes = near.shape[1]
     return pl.pallas_call(
         finish_kernel,
-        in_specs=[VMEM] * 5,
-        out_specs=[VMEM] * 3,
+        in_specs=[VMEM] * 9,
+        out_specs=[VMEM] * 5,
         out_shape=[
             jax.ShapeDtypeStruct((1, modes, 2, modes), F32),
             jax.ShapeDtypeStruct(group_basis.shape, F32),
             jax.ShapeDtypeStruct(top_basis.shape, F32),
+            jax.ShapeDtypeStruct((1,) + group_parts[0].shape, F32),
+            jax.ShapeDtypeStruct(top_parts[0].shape, F32),
         ],
         compiler_params=params(32),
         cost_estimate=pl.CostEstimate(
             flops=20 * modes**3, bytes_accessed=24 * modes * modes, transcendentals=2 * modes
         ),
         name="finish",
-    )(near, far, terms, group_basis, top_basis)
+    )(near, far, terms, group_basis, top_basis, *group_parts, *top_parts)
 
 
 def body(
@@ -389,47 +418,41 @@
 ):
     row_count, col_count = lax.axis_size("row"), lax.axis_size("col")
     sizes = {"row": row_count, "col": col_count}
-    size = group_mass.shape[2]
 
     def swap(value, axis, bit):
         return lax.ppermute(value, axis, crossed(sizes[axis], bit))
 
-    def half_of(half, own, after):
-        return leaf_half(
-            half, tile_mask, block_map, leaf_mass, constraint_modes, leaf_fixed_modes, own, after
-        )
-
-    basis = jnp.concatenate([group_basis[0], top_basis], axis=1)
-    beside = swap(basis, "row", 1)
-    first, keep, send = half_of(0, group_mass, basis)
-    pair = jnp.concatenate([basis, beside], axis=0)
-    pieces = [pair] + [swap(pair, "row", 2 * k) for k in range(1, row_count // 2)]
-    second, top_keep, top_send = half_of(1, top_mass, pair)
-    group_steps = exchanges(0, row_count, col_count)
-    packed, terms, keep, send = prepare(
-        group_steps[1], keep, send, swap(send, *group_steps[0]), top_keep, top_send, first, second,
-        pieces,
-    )
+    def half_of(half, more, after):
+        return leaf_half(half, tile_mask, block_map, leaf_mass, constraint_modes, more, after)
 
     def summed(value, axis):
         for b in range(bits_of(sizes[axis])):
             value = value + swap(value, axis, 1 << b)
         return value
 
+    def scattered(keep, send, steps, after):
+        other = swap(send, *steps[0])
+        for step, later in zip(steps[:-1], steps[1:]):
+            keep, send = fold(later, keep, other, after)
+            other = swap(send, *later)
+        return keep, other
+
+    group_steps = exchanges(0, row_count, col_count)
+    basis = jnp.concatenate([group_basis[0], top_basis], axis=1)
+    beside = swap(basis, "row", 1)
+    keep, send, loaded = half_of(0, [], basis)
+    pair = jnp.concatenate([basis, beside], axis=0)
+    pieces = [pair] + [swap(pair, "row", 2 * k) for k in range(1, row_count // 2)]
+    other = swap(send, *group_steps[0])
+    top_keep, top_send, moved = half_of(1, [leaf_fixed_modes, loaded], pair)
+    packed, terms, keep, send, top_keep, top_send = prepare(
+        keep, send, other, top_keep, top_send, moved, group_mass, top_mass, pieces
+    )
     near = summed(packed, "row")
     far = summed(near, "col")
-    coupling, group_modes, top_modes = finish(near, far, terms, group_basis, top_basis)
-
-    def scattered(keep, send, steps):
-        for i, step in enumerate(steps):
-            other = swap(send, *step)
-            if i == len(steps) - 1:
-                return size * (keep + other)
-            keep, send = fold(steps[i + 1], keep, other, packed)
-
-    group_assembled = scattered(keep, send, group_steps[1:])[None]
-    assembled = scattered(top_keep, top_send, exchanges(1, row_count, col_count))
-    return coupling, group_modes, top_modes, group_assembled, assembled
+    group_parts = scattered(keep, send, group_steps[1:], packed)
+    top_parts = scattered(top_keep, top_send, exchanges(1, row_count, col_count), packed)
+    return finish(near, far, terms, group_basis, top_basis, group_parts, top_parts)
 
 
 def solution(mesh):

time: 83.9 us -> 73.3 us (0.87)
  waiting for transfers between devices: 30 us -> 18.7 us
  starting transfers between devices: 18.7 us -> 22.3 us
  local copies, waits for them, and re-layouts: 3.34 us -> 1.4 us
  other arithmetic: 2.14 us -> 0.84 us
    ppermute x17, waiting for transfers between devices: 30 us -> 18.7 us  [swap(): return lax.ppermute(value, axis, crossed(sizes[axis], bit))]
    ppermute x17, starting transfers between devices: 18.7 us -> 22.3 us  [swap(): return lax.ppermute(value, axis, crossed(sizes[axis], bit))]
    unnamed x16, local copies, waits for them, and re-layouts: 3.34 us -> 1.4 us
  transfers between devices with their start and end apart: 17 -> 17, of which waited for: 8 -> 6; matrix products, arithmetic and copies ran while one was open for 1% -> 0% of each run, Pallas kernels for 34% -> 28%
where the time goes in v4:
time: 73.3 us; the launch traced here: 73.1 us
  Pallas kernels  29 us (40%)
  starting transfers between devices  22.3 us (30%)
  waiting for transfers between devices  18.7 us (26%)
  local copies, waits for them, and re-layouts  1.4 us (2%)
  between operations  0.85 us (1%)
  other arithmetic  0.84 us (1%)
    ppermute x17, starting transfers between devices, swap(): return lax.ppermute(value, axis, crossed(sizes[axis], bit))  22.3 us
    pallas_call x2, Pallas kernels, leaf_half(): pl.pallas_call(functools.partial(leaf_kernel, half), in_specs=[SMEM] * 2...  20.1 us
    ppermute x17, waiting for transfers between devices, swap(): return lax.ppermute(value, axis, crossed(sizes[axis], bit))  18.7 us
    pallas_call x1, Pallas kernels, finish(): pl.pallas_call(finish_kernel, in_specs=[VMEM] * 9, out_specs=[VMEM] * 5,...  7.17 us
    pallas_call x1, Pallas kernels, prepare(): pl.pallas_call(functools.partial(prepare_kernel, len(pieces)), in_specs=[...  1.5 us
  transfers between devices with their start and end apart: 17, of which 6 were waited for; matrix products, arithmetic and copies ran while one was open for 0% of the time, Pallas kernels for 28%

profile of v4, /device:TPU:0, one launch (start us, length us, event | category | flops | bytes accessed | tf_op | source)
XLA Modules:
  0.0 73.1 jit_solution(5786424539004808870)
XLA Ops:
  0.6 0.8 %pad_maximum_fusion.1.refs_0_ = f32[64,256]{1,0:T(8,128)S(1)} fusion(f32[64,128]{1,0:T(8,128)} %top_basis_ref.1, f32[64,128]{1,0:T(8,128)} %bitcast.1), kind=kLoop, calls=%fused_computation.1 | loop fusion | flops 16384 | bytes 131072 | tf_op jit(solution)/shard_map/concatenate | solution.py:441
  1.4 0.0 copy-start
  1.4 0.0 copy-start.1
  1.4 0.0 copy-start.4
  1.4 3.0 %collective-permute-start.1 = (f32[64,256]{1,0:T(8,128)S(1)}, f32[64,256]{1,0:T(8,128)S(1)}, u32[]{:S(2)}, u32[]{:S(2)}) collective-permute-start(f32[64,256]{1,0:T(8,128)S(1)} %pad_maximum_fusion.1.refs_0_), channel_id=1, source_target_pairs={{0,4},{4,0},{8,12},{12,8},{16,20},{20,16},{24,28},{28,24},{1,5},{5... | collective-permute-start | bytes 196616 | tf_op jit(solution)/shard_map/ppermute | solution.py:423
  4.4 0.0 copy-start.5
  4.4 0.7 copy-done.5
  5.1 0.0 copy-start.6
  5.1 0.7 copy-done.6
  5.8 0.0 copy-start.7
  5.8 9.6 %leaf_group.1 = (f32[256,512]{1,0:T(8,128)S(1)}, f32[256,512]{1,0:T(8,128)S(1)}, bf16[2048,512]{1,0:T(8,128)(2,1)S(1)}) custom-call(s32[1,16,16]{2,1,0:T(8,128)S(1)} %copy-done.5, s32[1,2,4]{2,1,0:T(2,128)S(1)} %copy-done.6, bf16[1,2048,2048]{2,1,0:T(8,128)(2,1)} %mass_hbm.3, bf16[1,2048,1024]{2,1,0:T(8,128)(2,1)} %modes_hbm.3, ...), custom_call_target="tpu_custom_call" | custom-call | flops 5368709120 | bytes 12582912 | tf_op jit(solution)/shard_map/leaf_group/pallas_call | solution.py:176
  15.4 0.1 collective-permute-start
  15.5 0.0 collective-permute-done.1
  15.5 0.0 copy-done
  15.5 0.0 copy-done.1
  15.6 2.1 %collective-permute-start.2 = (f32[128,256]{1,0:T(8,128)S(1)}, f32[128,256]{1,0:T(8,128)S(1)}, u32[]{:S(2)}, u32[]{:S(2)}) collective-permute-start(f32[128,256]{1,0:T(8,128)S(1)} %pad_maximum_fusion.refs_2_.refs_0_), channel_id=1, source_target_pairs={{0,8},{4,12},{8,0},{12,4},{16,24},{20,28},{24,16},{28,20},{1,9},{5... | collective-permute-start | bytes 393224 | tf_op jit(solution)/shard_map/ppermute | solution.py:423
  17.6 2.6 %collective-permute-start.3 = (f32[128,256]{1,0:T(8,128)S(1)}, f32[128,256]{1,0:T(8,128)S(1)}, u32[]{:S(2)}, u32[]{:S(2)}) collective-permute-start(f32[128,256]{1,0:T(8,128)S(1)} %pad_maximum_fusion.refs_2_.refs_0_), channel_id=1, source_target_pairs={{0,16},{4,20},{8,24},{12,28},{16,0},{20,4},{24,8},{28,12},{1,17},{... | collective-permute-start | bytes 393224 | tf_op jit(solution)/shard_map/ppermute | solution.py:423
  20.3 0.0 collective-permute-start.4
  20.3 0.0 copy-done.4
  20.3 0.0 copy-done.7
  20.3 0.0 copy-start.2
  20.3 0.0 copy-start.3
  20.3 10.5 %leaf_top.1 = (f32[256,512]{1,0:T(8,128)S(1)}, f32[256,512]{1,0:T(8,128)S(1)}, f32[2,128,512]{2,1,0:T(8,128)S(1)}) custom-call(s32[1,16,16]{2,1,0:T(8,128)S(1)} %copy-done.5, s32[1,2,4]{2,1,0:T(2,128)S(1)} %copy-done.7, bf16[1,2048,2048]{2,1,0:T(8,128)(2,1)} %mass_hbm.3, bf16[1,2048,1024]{2,1,0:T(8,128)(2,1)} %modes_hbm.3, ...), custom_call_target="tpu_custom_call" | custom-call | flops 5368709120 | bytes 12582912 | tf_op jit(solution)/shard_map/leaf_top/pallas_call | solution.py:176
  30.9 0.0 collective-permute-done.2.refs_1_
  30.9 0.0 collective-permute-done.3.refs_2_
  30.9 0.0 collective-permute-done.4.refs_3_
  30.9 0.0 collective-permute-done.other_ref
  30.9 0.0 copy-done.2
  30.9 0.0 copy-done.3
  30.9 1.5 %prepare.1 = (f32[136,128]{1,0:T(8,128)S(1)}, f32[2,128,128]{2,1,0:T(8,128)S(1)}, f32[128,512]{1,0:T(8,128)S(1)}, f32[128,512]{1,0:T(8,128)S(1)}, f32[256,512]{1,0:T(8,128)S(1)}, /*index=5*/f32[256,512]{1,0:T(8,128)S(1)}) custom-call(f32[256,512]{1,0:T(8,128)S(1)} %get-tuple-element.27.keep_in, f32[256,512]{1,0:T(8,128)S(1)} %get-tuple-element.28.send_ref, ...), custom_call_target="tpu_custom_call" | custom-call | flops 402653184 | bytes 3145728 | tf_op jit(solution)/shard_map/prepare/pallas_call | solution.py:274
  32.4 0.1 collective-permute-start.12
  32.5 1.9 %collective-permute-done.12.other_ref = f32[256,512]{1,0:T(8,128)S(1)} collective-permute-done((f32[256,512]{1,0:T(8,128)S(1)}, f32[256,512]{1,0:T(8,128)S(1)}, u32[]{:S(2)}, u32[]{:S(2)}) %collective-permute-start.12) | collective-permute-done | bytes 524320 | tf_op jit(solution)/shard_map/ppermute | solution.py:423
  34.4 0.1 fold.6
  34.5 1.8 %collective-permute-start.13 = (f32[128,512]{1,0:T(8,128)S(1)}, f32[128,512]{1,0:T(8,128)S(1)}, u32[]{:S(2)}, u32[]{:S(2)}) collective-permute-start(f32[128,512]{1,0:T(8,128)S(1)} %get-tuple-element.42), channel_id=1, source_target_pairs={{0,2},{1,3},{2,0},{3,1},{4,6},{5,7},{6,4},{7,5},{8,10},{9,11},{10,... | collective-permute-start | bytes 786440 | tf_op jit(solution)/shard_map/ppermute | solution.py:423
  36.2 1.9 %collective-permute-start.10 = (f32[128,512]{1,0:T(8,128)S(1)}, f32[128,512]{1,0:T(8,128)S(1)}, u32[]{:S(2)}, u32[]{:S(2)}) collective-permute-start(f32[128,512]{1,0:T(8,128)S(1)} %get-tuple-element.36), channel_id=1, source_target_pairs={{0,16},{4,20},{8,24},{12,28},{16,0},{20,4},{24,8},{28,12},{1,17},{... | collective-permute-start | bytes 786440 | tf_op jit(solution)/shard_map/ppermute | solution.py:423
  38.2 1.5 %collective-permute-start.5 = (f32[136,128]{1,0:T(8,128)S(1)}, f32[136,128]{1,0:T(8,128)S(1)}, u32[]{:S(2)}, u32[]{:S(2)}) collective-permute-start(f32[136,128]{1,0:T(8,128)S(1)} %get-tuple-element.33.after_ref), channel_id=1, source_target_pairs={{0,4},{4,0},{8,12},{12,8},{16,20},{20,16},{24,28},{28,24},{1,5},{5... | collective-permute-start | bytes 208904 | tf_op jit(solution)/shard_map/ppermute | solution.py:423
  39.6 2.8 %collective-permute-done.5 = f32[136,128]{1,0:T(8,128)S(1)} collective-permute-done((f32[136,128]{1,0:T(8,128)S(1)}, f32[136,128]{1,0:T(8,128)S(1)}, u32[]{:S(2)}, u32[]{:S(2)}) %collective-permute-start.5) | collective-permute-done | bytes 69664 | tf_op jit(solution)/shard_map/ppermute | solution.py:423
  42.5 2.3 %collective-permute-start.6 = (f32[136,128]{1,0:T(8,128)S(1)}, f32[136,128]{1,0:T(8,128)S(1)}, u32[]{:S(2)}, u32[]{:S(2)}) collective-permute-start(f32[136,128]{1,0:T(8,128)S(1)} %add.15), channel_id=1, source_target_pairs={{0,8},{4,12},{8,0},{12,4},{16,24},{20,28},{24,16},{28,20},{1,9},{5... | collective-permute-start | bytes 208904 | tf_op jit(solution)/shard_map/ppermute | solution.py:423
  44.8 0.0 collective-permute-done.13.other_ref
  44.8 1.6 %collective-permute-start.14 = (f32[64,512]{1,0:T(8,128)S(1)}, f32[64,512]{1,0:T(8,128)S(1)}, u32[]{:S(2)}, u32[]{:S(2)}) collective-permute-start(f32[64,512]{1,0:T(8,128)S(1)} %get-tuple-element.44), channel_id=1, source_target_pairs={{0,4},{4,0},{8,12},{12,8},{16,20},{20,16},{24,28},{28,24},{1,5},{5... | collective-permute-start | bytes 393224 | tf_op jit(solution)/shard_map/ppermute | solution.py:423
  46.4 4.2 %collective-permute-done.6 = f32[136,128]{1,0:T(8,128)S(1)} collective-permute-done((f32[136,128]{1,0:T(8,128)S(1)}, f32[136,128]{1,0:T(8,128)S(1)}, u32[]{:S(2)}, u32[]{:S(2)}) %collective-permute-start.6) | collective-permute-done | bytes 69664 | tf_op jit(solution)/shard_map/ppermute | solution.py:423
  50.6 0.1 collective-permute-start.7
  50.7 5.2 %collective-permute-done.7 = f32[136,128]{1,0:T(8,128)S(1)} collective-permute-done((f32[136,128]{1,0:T(8,128)S(1)}, f32[136,128]{1,0:T(8,128)S(1)}, u32[]{:S(2)}, u32[]{:S(2)}) %collective-permute-start.7) | collective-permute-done | bytes 69664 | tf_op jit(solution)/shard_map/ppermute | solution.py:423
  55.9 0.1 collective-permute-start.8
  56.0 0.0 collective-permute-done.10.other_ref
  56.0 0.1 collective-permute-start.11
  56.1 0.0 collective-permute-done.14.other_ref
  56.2 2.3 %collective-permute-start.15 = (f32[32,512]{1,0:T(8,128)S(1)}, f32[32,512]{1,0:T(8,128)S(1)}, u32[]{:S(2)}, u32[]{:S(2)}) collective-permute-start(f32[32,512]{1,0:T(8,128)S(1)} %get-tuple-element.46), channel_id=1, source_target_pairs={{0,16},{4,20},{8,24},{12,28},{16,0},{20,4},{24,8},{28,12},{1,17},{... | collective-permute-start | bytes 196616 | tf_op jit(solution)/shard_map/ppermute | solution.py:423
  58.5 0.0 collective-permute-done.8
  58.5 0.6 collective-permute-start.9
  59.1 2.7 %collective-permute-done.15.other_ref = f32[32,512]{1,0:T(8,128)S(1)} collective-permute-done((f32[32,512]{1,0:T(8,128)S(1)}, f32[32,512]{1,0:T(8,128)S(1)}, u32[]{:S(2)}, u32[]{:S(2)}) %collective-permute-start.15) | collective-permute-done | bytes 65568 | tf_op jit(solution)/shard_map/ppermute | solution.py:423
  61.7 2.3 %collective-permute-start.16 = (f32[16,512]{1,0:T(8,128)S(1)}, f32[16,512]{1,0:T(8,128)S(1)}, u32[]{:S(2)}, u32[]{:S(2)}) collective-permute-start(f32[16,512]{1,0:T(8,128)S(1)} %get-tuple-element.48), channel_id=1, source_target_pairs={{0,8},{4,12},{8,0},{12,4},{16,24},{20,28},{24,16},{28,20},{1,9},{5... | collective-permute-start | bytes 98312 | tf_op jit(solution)/shard_map/ppermute | solution.py:423
  64.0 0.0 collective-permute-done.9
  64.0 0.0 collective-permute-done.11.other_ref
  64.1 1.9 %collective-permute-done.16.top_other_ref = f32[16,512]{1,0:T(8,128)S(1)} collective-permute-done((f32[16,512]{1,0:T(8,128)S(1)}, f32[16,512]{1,0:T(8,128)S(1)}, u32[]{:S(2)}, u32[]{:S(2)}) %collective-permute-start.16) | collective-permute-done | bytes 32800 | tf_op jit(solution)/shard_map/ppermute | solution.py:423
  65.9 7.2 %finish.1 = (f32[1,128,2,128]{3,2,1,0:T(2,128)}, f32[1,64,128]{2,1,0:T(8,128)}, f32[64,128]{1,0:T(8,128)}, f32[1,64,512]{2,1,0:T(8,128)}, f32[16,512]{1,0:T(8,128)}) custom-call(f32[136,128]{1,0:T(8,128)S(1)} %add.17.near_ref, f32[136,128]{1,0:T(8,128)S(1)} %add.19.far_ref, f32[2,128,128]{2,1,0:T(8,128)S(1)} %get-tuple-element.34.terms_ref, ...), custom_call_target="tpu_custom_call" | custom-call | flops 41943040 | bytes 393216 | tf_op jit(solution)/shard_map/finish/pallas_call | solution.py:396
  (10 shorter events, 0.2 us)
Async XLA Ops:
  1.4 14.1 %copy-start = (f32[64,128]{1,0:T(8,128)S(1)}, f32[64,128]{1,0:T(8,128)}, u32[]{:S(2)}) copy-start(f32[64,128]{1,0:T(8,128)} %top_basis_ref.1) | copy-start | bytes 98308
  1.4 14.1 %copy-start.1 = (f32[1,64,128]{2,1,0:T(8,128)S(1)}, f32[1,64,128]{2,1,0:T(8,128)}, u32[]{:S(2)}) copy-start(f32[1,64,128]{2,1,0:T(8,128)} %group_basis_ref.1) | copy-start | bytes 98308
  1.4 18.9 %copy-start.4 = (bf16[1,2048,128]{2,1,0:T(8,128)(2,1)S(1)}, bf16[1,2048,128]{2,1,0:T(8,128)(2,1)}, u32[]{:S(2)}) copy-start(bf16[1,2048,128]{2,1,0:T(8,128)(2,1)} %refs_0_.1) | copy-start | bytes 1572868
  1.4 14.1 %collective-permute-start.1 = (f32[64,256]{1,0:T(8,128)S(1)}, f32[64,256]{1,0:T(8,128)S(1)}, u32[]{:S(2)}, u32[]{:S(2)}) collective-permute-start(f32[64,256]{1,0:T(8,128)S(1)} %pad_maximum_fusion.1.refs_0_), channel_id=1, source_target_pairs={{0,4},{4,0},{8,12},{12,8},{16,20},{20,16},{24,28},{28,24},{1,5},{5... | collective-permute-start | bytes 196616 | tf_op jit(solution)/shard_map/ppermute | solution.py:423
  4.4 0.7 copy-start.5
  5.1 0.7 copy-start.6
  5.8 14.5 %copy-start.7 = (s32[1,2,4]{2,1,0:T(2,128)S(1)}, s32[1,2,4]{2,1,0:T(2,128)}, u32[]{:S(2)}) copy-start(s32[1,2,4]{2,1,0:T(2,128)} %map_ref.3) | copy-start | bytes 100
  15.4 15.5 %collective-permute-start = (f32[256,512]{1,0:T(8,128)S(1)}, f32[256,512]{1,0:T(8,128)S(1)}, u32[]{:S(2)}, u32[]{:S(2)}) collective-permute-start(f32[256,512]{1,0:T(8,128)S(1)} %get-tuple-element.28.send_ref), channel_id=1, source_target_pairs={{0,4},{4,0},{8,12},{12,8},{16,20},{20,16},{24,28},{28,24},{1,5},{5... | collective-permute-start | bytes 1572872 | tf_op jit(solution)/shard_map/ppermute | solution.py:423
  15.6 15.3 %collective-permute-start.2 = (f32[128,256]{1,0:T(8,128)S(1)}, f32[128,256]{1,0:T(8,128)S(1)}, u32[]{:S(2)}, u32[]{:S(2)}) collective-permute-start(f32[128,256]{1,0:T(8,128)S(1)} %pad_maximum_fusion.refs_2_.refs_0_), channel_id=1, source_target_pairs={{0,8},{4,12},{8,0},{12,4},{16,24},{20,28},{24,16},{28,20},{1,9},{5... | collective-permute-start | bytes 393224 | tf_op jit(solution)/shard_map/ppermute | solution.py:423
  17.6 13.2 %collective-permute-start.3 = (f32[128,256]{1,0:T(8,128)S(1)}, f32[128,256]{1,0:T(8,128)S(1)}, u32[]{:S(2)}, u32[]{:S(2)}) collective-permute-start(f32[128,256]{1,0:T(8,128)S(1)} %pad_maximum_fusion.refs_2_.refs_0_), channel_id=1, source_target_pairs={{0,16},{4,20},{8,24},{12,28},{16,0},{20,4},{24,8},{28,12},{1,17},{... | collective-permute-start | bytes 393224 | tf_op jit(solution)/shard_map/ppermute | solution.py:423
  20.3 10.6 %collective-permute-start.4 = (f32[128,256]{1,0:T(8,128)S(1)}, f32[128,256]{1,0:T(8,128)S(1)}, u32[]{:S(2)}, u32[]{:S(2)}) collective-permute-start(f32[128,256]{1,0:T(8,128)S(1)} %pad_maximum_fusion.refs_2_.refs_0_), channel_id=1, source_target_pairs={{0,24},{4,28},{8,16},{12,20},{16,8},{20,12},{24,0},{28,4},{1,25},{... | collective-permute-start | bytes 393224 | tf_op jit(solution)/shard_map/ppermute | solution.py:423
  20.3 10.6 %copy-start.2 = (f32[1,64,512]{2,1,0:T(8,128)S(1)}, f32[1,64,512]{2,1,0:T(8,128)}, u32[]{:S(2)}) copy-start(f32[1,64,512]{2,1,0:T(8,128)} %group_own_ref.1) | copy-start | bytes 393220
  20.3 10.6 %copy-start.3 = (f32[16,512]{1,0:T(8,128)S(1)}, f32[16,512]{1,0:T(8,128)}, u32[]{:S(2)}) copy-start(f32[16,512]{1,0:T(8,128)} %top_own_ref.1) | copy-start | bytes 98308
  32.4 2.0 %collective-permute-start.12 = (f32[256,512]{1,0:T(8,128)S(1)}, f32[256,512]{1,0:T(8,128)S(1)}, u32[]{:S(2)}, u32[]{:S(2)}) collective-permute-start(f32[256,512]{1,0:T(8,128)S(1)} %get-tuple-element.40), channel_id=1, source_target_pairs={{0,1},{1,0},{2,3},{3,2},{4,5},{5,4},{6,7},{7,6},{8,9},{9,8},{10,11... | collective-permute-start | bytes 1572872 | tf_op jit(solution)/shard_map/ppermute | solution.py:423
  34.5 10.3 %collective-permute-start.13 = (f32[128,512]{1,0:T(8,128)S(1)}, f32[128,512]{1,0:T(8,128)S(1)}, u32[]{:S(2)}, u32[]{:S(2)}) collective-permute-start(f32[128,512]{1,0:T(8,128)S(1)} %get-tuple-element.42), channel_id=1, source_target_pairs={{0,2},{1,3},{2,0},{3,1},{4,6},{5,7},{6,4},{7,5},{8,10},{9,11},{10,... | collective-permute-start | bytes 786440 | tf_op jit(solution)/shard_map/ppermute | solution.py:423
  36.2 19.7 %collective-permute-start.10 = (f32[128,512]{1,0:T(8,128)S(1)}, f32[128,512]{1,0:T(8,128)S(1)}, u32[]{:S(2)}, u32[]{:S(2)}) collective-permute-start(f32[128,512]{1,0:T(8,128)S(1)} %get-tuple-element.36), channel_id=1, source_target_pairs={{0,16},{4,20},{8,24},{12,28},{16,0},{20,4},{24,8},{28,12},{1,17},{... | collective-permute-start | bytes 786440 | tf_op jit(solution)/shard_map/ppermute | solution.py:423
  38.2 4.3 %collective-permute-start.5 = (f32[136,128]{1,0:T(8,128)S(1)}, f32[136,128]{1,0:T(8,128)S(1)}, u32[]{:S(2)}, u32[]{:S(2)}) collective-permute-start(f32[136,128]{1,0:T(8,128)S(1)} %get-tuple-element.33.after_ref), channel_id=1, source_target_pairs={{0,4},{4,0},{8,12},{12,8},{16,20},{20,16},{24,28},{28,24},{1,5},{5... | collective-permute-start | bytes 208904 | tf_op jit(solution)/shard_map/ppermute | solution.py:423
  42.5 8.1 %collective-permute-start.6 = (f32[136,128]{1,0:T(8,128)S(1)}, f32[136,128]{1,0:T(8,128)S(1)}, u32[]{:S(2)}, u32[]{:S(2)}) collective-permute-start(f32[136,128]{1,0:T(8,128)S(1)} %add.15), channel_id=1, source_target_pairs={{0,8},{4,12},{8,0},{12,4},{16,24},{20,28},{24,16},{28,20},{1,9},{5... | collective-permute-start | bytes 208904 | tf_op jit(solution)/shard_map/ppermute | solution.py:423
  44.8 11.3 %collective-permute-start.14 = (f32[64,512]{1,0:T(8,128)S(1)}, f32[64,512]{1,0:T(8,128)S(1)}, u32[]{:S(2)}, u32[]{:S(2)}) collective-permute-start(f32[64,512]{1,0:T(8,128)S(1)} %get-tuple-element.44), channel_id=1, source_target_pairs={{0,4},{4,0},{8,12},{12,8},{16,20},{20,16},{24,28},{28,24},{1,5},{5... | collective-permute-start | bytes 393224 | tf_op jit(solution)/shard_map/ppermute | solution.py:423
  50.6 5.3 %collective-permute-start.7 = (f32[136,128]{1,0:T(8,128)S(1)}, f32[136,128]{1,0:T(8,128)S(1)}, u32[]{:S(2)}, u32[]{:S(2)}) collective-permute-start(f32[136,128]{1,0:T(8,128)S(1)} %add.16), channel_id=1, source_target_pairs={{0,16},{4,20},{8,24},{12,28},{16,0},{20,4},{24,8},{28,12},{1,17},{... | collective-permute-start | bytes 208904 | tf_op jit(solution)/shard_map/ppermute | solution.py:423
  55.9 2.6 %collective-permute-start.8 = (f32[136,128]{1,0:T(8,128)S(1)}, f32[136,128]{1,0:T(8,128)S(1)}, u32[]{:S(2)}, u32[]{:S(2)}) collective-permute-start(f32[136,128]{1,0:T(8,128)S(1)} %add.17.near_ref), channel_id=1, source_target_pairs={{0,1},{1,0},{2,3},{3,2},{4,5},{5,4},{6,7},{7,6},{8,9},{9,8},{10,11... | collective-permute-start | bytes 208904 | tf_op jit(solution)/shard_map/ppermute | solution.py:423
  56.0 8.0 %collective-permute-start.11 = (f32[64,512]{1,0:T(8,128)S(1)}, f32[64,512]{1,0:T(8,128)S(1)}, u32[]{:S(2)}, u32[]{:S(2)}) collective-permute-start(f32[64,512]{1,0:T(8,128)S(1)} %get-tuple-element.38), channel_id=1, source_target_pairs={{0,8},{4,12},{8,0},{12,4},{16,24},{20,28},{24,16},{28,20},{1,9},{5... | collective-permute-start | bytes 393224 | tf_op jit(solution)/shard_map/ppermute | solution.py:423
  56.2 5.6 %collective-permute-start.15 = (f32[32,512]{1,0:T(8,128)S(1)}, f32[32,512]{1,0:T(8,128)S(1)}, u32[]{:S(2)}, u32[]{:S(2)}) collective-permute-start(f32[32,512]{1,0:T(8,128)S(1)} %get-tuple-element.46), channel_id=1, source_target_pairs={{0,16},{4,20},{8,24},{12,28},{16,0},{20,4},{24,8},{28,12},{1,17},{... | collective-permute-start | bytes 196616 | tf_op jit(solution)/shard_map/ppermute | solution.py:423
  58.5 5.5 %collective-permute-start.9 = (f32[136,128]{1,0:T(8,128)S(1)}, f32[136,128]{1,0:T(8,128)S(1)}, u32[]{:S(2)}, u32[]{:S(2)}) collective-permute-start(f32[136,128]{1,0:T(8,128)S(1)} %add.18), channel_id=1, source_target_pairs={{0,2},{1,3},{2,0},{3,1},{4,6},{5,7},{6,4},{7,5},{8,10},{9,11},{10,... | collective-permute-start | bytes 208904 | tf_op jit(solution)/shard_map/ppermute | solution.py:423
  61.7 4.2 %collective-permute-start.16 = (f32[16,512]{1,0:T(8,128)S(1)}, f32[16,512]{1,0:T(8,128)S(1)}, u32[]{:S(2)}, u32[]{:S(2)}) collective-permute-start(f32[16,512]{1,0:T(8,128)S(1)} %get-tuple-element.48), channel_id=1, source_target_pairs={{0,8},{4,12},{8,0},{12,4},{16,24},{20,28},{24,16},{28,20},{1,9},{5... | collective-permute-start | bytes 98312 | tf_op jit(solution)/shard_map/ppermute | solution.py:423

commit v5 on v4

--- a/solution.py
+++ b/solution.py
@@ -123,14 +123,17 @@
         loaded = jnp.dot(masked, modes_ref[...], preferred_element_type=F32).astype(BF16)
         window = pl.ds(pl.multiple_of(i * height, height), height)
         loaded_ref[window, :] = loaded
-        partial = rows_first(modes_ref[window, :], loaded)
-        if first:
-            partial_ref[...] = partial
-        else:
-            partial_ref[...] += partial
-
+        if not first:
+            add_partial(i - 1)
+
+    def add_partial(i):
+        window = pl.ds(pl.multiple_of(i * height, height), height)
+        partial_ref[...] += rows_first(modes_ref[window, :], loaded_ref[window, :])
+
+    partial_ref[...] = jnp.zeros_like(partial_ref)
     part(0, True)
     lax.fori_loop(1, MASS_PARTS, lambda i, _: part(i, False), None)
+    add_partial(MASS_PARTS - 1)
 
     blocks = size // TILE
     to = [pl.multiple_of(map_ref[0, half, a] * TILE, TILE) for a in range(blocks)]
@@ -292,21 +295,58 @@
     )(keep, send, other, top_keep, top_send, moved, group_own, top_own, *pieces)
 
 
-def fold_kernel(step, keep_ref, other_ref, after_ref, next_ref, send_ref):
-    halve(step, keep_ref, other_ref, next_ref, send_ref)
-
-
-def fold(step, keep, other, after):
+def fold_kernel(step, after_count, keep_ref, other_ref, *refs):
+    halve(step, keep_ref, other_ref, *refs[after_count:])
+
+
+def fold(step, keep, other, *after):
     part = jax.ShapeDtypeStruct((keep.shape[0] // 2, keep.shape[1]), F32)
     return pl.pallas_call(
-        functools.partial(fold_kernel, step),
-        in_specs=[VMEM] * 2 + [pl.BlockSpec(memory_space=pl.ANY)],
+        functools.partial(fold_kernel, step, len(after)),
+        in_specs=[VMEM] * 2 + [pl.BlockSpec(memory_space=pl.ANY)] * len(after),
         out_specs=[VMEM] * 2,
         out_shape=[part, part],
         compiler_params=params(16),
         cost_estimate=pl.CostEstimate(flops=1, bytes_accessed=1, transcendentals=0),
         name="fold",
-    )(keep, other, after)
+    )(keep, other, *after)
+
+
+def add_kernel(left_ref, right_ref, *refs):
+    refs[-1][...] = left_ref[...] + right_ref[...]
+
+
+def add(left, right, *after):
+    return pl.pallas_call(
+        add_kernel,
+        in_specs=[VMEM] * 2 + [pl.BlockSpec(memory_space=pl.ANY)] * len(after),
+        out_specs=VMEM,
+        out_shape=jax.ShapeDtypeStruct(left.shape, F32),
+        compiler_params=params(16),
+        cost_estimate=pl.CostEstimate(flops=1, bytes_accessed=1, transcendentals=0),
+        name="add",
+    )(left, right, *after)
+
+
+def last_kernel(keep_ref, other_ref, top_keep_ref, top_other_ref, after_ref, group_ref, top_ref):
+    size = group_ref.shape[2]
+    group_ref[0] = size * (keep_ref[...] + other_ref[...])
+    top_ref[...] = size * (top_keep_ref[...] + top_other_ref[...])
+
+
+def last(keep, other, top_keep, top_other, after):
+    return pl.pallas_call(
+        last_kernel,
+        in_specs=[VMEM] * 4 + [pl.BlockSpec(memory_space=pl.ANY)],
+        out_specs=[VMEM] * 2,
+        out_shape=[
+            jax.ShapeDtypeStruct((1,) + keep.shape, F32),
+            jax.ShapeDtypeStruct(top_keep.shape, F32),
+        ],
+        compiler_params=params(16),
+        cost_estimate=pl.CostEstimate(flops=1, bytes_accessed=1, transcendentals=0),
+        name="last",
+    )(keep, other, top_keep, top_other, after)
 
 
 def factor(matrices):
@@ -364,12 +404,8 @@
 
 
 def finish_kernel(
-    near_ref, far_ref, terms_ref, group_basis_ref, top_basis_ref, keep_ref, other_ref, top_keep_ref,
-    top_other_ref, coupling_ref, group_ref, top_ref, assembled_ref, top_assembled_ref,
+    near_ref, far_ref, terms_ref, group_basis_ref, top_basis_ref, coupling_ref, group_ref, top_ref,
 ):
-    size = assembled_ref.shape[2]
-    assembled_ref[0] = size * (keep_ref[...] + other_ref[...])
-    top_assembled_ref[...] = size * (top_keep_ref[...] + top_other_ref[...])
     modes = near_ref.shape[1]
     down = lax.broadcasted_iota(jnp.int32, (modes, modes), 0)
     across = lax.broadcasted_iota(jnp.int32, (modes, modes), 1)
@@ -391,25 +427,23 @@
             top_ref[...] = result[modes:]
 
 
-def finish(near, far, terms, group_basis, top_basis, group_parts, top_parts):
+def finish(near, far, terms, group_basis, top_basis):
     modes = near.shape[1]
     return pl.pallas_call(
         finish_kernel,
-        in_specs=[VMEM] * 9,
-        out_specs=[VMEM] * 5,
+        in_specs=[VMEM] * 5,
+        out_specs=[VMEM] * 3,
         out_shape=[
             jax.ShapeDtypeStruct((1, modes, 2, modes), F32),
             jax.ShapeDtypeStruct(group_basis.shape, F32),
             jax.ShapeDtypeStruct(top_basis.shape, F32),
-            jax.ShapeDtypeStruct((1,) + group_parts[0].shape, F32),
-            jax.ShapeDtypeStruct(top_parts[0].shape, F32),
         ],
         compiler_params=params(32),
         cost_estimate=pl.CostEstimate(
             flops=20 * modes**3, bytes_accessed=24 * modes * modes, transcendentals=2 * modes
         ),
         name="finish",
-    )(near, far, terms, group_basis, top_basis, *group_parts, *top_parts)
+    )(near, far, terms, group_basis, top_basis)
 
 
 def body(
@@ -424,18 +458,6 @@
 
     def half_of(half, more, after):
         return leaf_half(half, tile_mask, block_map, leaf_mass, constraint_modes, more, after)
-
-    def summed(value, axis):
-        for b in range(bits_of(sizes[axis])):
-            value = value + swap(value, axis, 1 << b)
-        return value
-
-    def scattered(keep, send, steps, after):
-        other = swap(send, *steps[0])
-        for step, later in zip(steps[:-1], steps[1:]):
-            keep, send = fold(later, keep, other, after)
-            other = swap(send, *later)
-        return keep, other
 
     group_steps = exchanges(0, row_count, col_count)
     basis = jnp.concatenate([group_basis[0], top_basis], axis=1)
@@ -448,11 +470,37 @@
     packed, terms, keep, send, top_keep, top_send = prepare(
         keep, send, other, top_keep, top_send, moved, group_mass, top_mass, pieces
     )
-    near = summed(packed, "row")
-    far = summed(near, "col")
-    group_parts = scattered(keep, send, group_steps[1:], packed)
-    top_parts = scattered(top_keep, top_send, exchanges(1, row_count, col_count), packed)
-    return finish(near, far, terms, group_basis, top_basis, group_parts, top_parts)
+    group_left = group_steps[1:]
+    top_left = exchanges(1, row_count, col_count)
+    sums = [("row", 1 << b) for b in range(bits_of(row_count))]
+    sums += [("col", 1 << b) for b in range(bits_of(col_count))]
+    value = near = packed
+    group_other, top_other = None, swap(top_send, *top_left[0])
+    for i, step in enumerate(sums):
+        other = swap(value, *step)
+        after = []
+        if i == 0:
+            group_other = swap(send, *group_left[0])
+        if len(top_left) > 1 and i != 1:
+            top_keep, top_send = fold(top_left[1], top_keep, top_other, value)
+            top_left = top_left[1:]
+            top_other = swap(top_send, *top_left[0])
+            after.append(top_send)
+        if len(group_left) > 1 and i >= len(sums) - len(group_left) + 1:
+            keep, send = fold(group_left[1], keep, group_other, value)
+            group_left = group_left[1:]
+            group_other = swap(send, *group_left[0])
+            after.append(send)
+        value = add(value, other, *after)
+        if i == bits_of(row_count) - 1:
+            near = value
+    while len(top_left) > 1:
+        top_keep, top_send = fold(top_left[1], top_keep, top_other, value)
+        top_left = top_left[1:]
+        top_other = swap(top_send, *top_left[0])
+    coupling, group_modes, top_modes = finish(near, value, terms, group_basis, top_basis)
+    assembled, top_assembled = last(keep, group_other, top_keep, top_other, top_modes)
+    return coupling, group_modes, top_modes, assembled, top_assembled
 
 
 def solution(mesh):

time: 73.3 us -> 74.6 us (1.018)
  waiting for transfers between devices: 18.7 us -> 15.1 us
  starting transfers between devices: 22.3 us -> 25 us
  Pallas kernels: 29 us -> 30.4 us
  local copies, waits for them, and re-layouts: 1.4 us -> 2.16 us
    ppermute x17, waiting for transfers between devices: 18.7 us -> 15.1 us  [swap(): return lax.ppermute(value, axis, crossed(sizes[axis], bit))]
    ppermute x17, starting transfers between devices: 22.3 us -> 25 us  [swap(): return lax.ppermute(value, axis, crossed(sizes[axis], bit))]
    unnamed x16 -> x18, local copies, waits for them, and re-layouts: 1.4 us -> 2.16 us
    pallas_call x6 -> x12, Pallas kernels: 7.36 us -> 8.08 us  [the longest x1 7.17 us: finish(): pl.pallas_call(finish_kernel, in_specs=[VMEM] * 5, out_specs=[VMEM] * 3,...]
  transfers between devices with their start and end apart: 17 -> 17, of which waited for: 6 -> 6; matrix products, arithmetic and copies ran while one was open for 0% -> 0% of each run, Pallas kernels for 28% -> 38%
where the time goes in v5:
time: 74.6 us; the launch traced here: 74.3 us
  Pallas kernels  30.4 us (41%)
  starting transfers between devices  25 us (34%)
  waiting for transfers between devices  15.1 us (20%)
  local copies, waits for them, and re-layouts  2.16 us (3%)
  between operations  0.85 us (1%)
  other arithmetic  0.79 us (1%)
    ppermute x17, starting transfers between devices, swap(): return lax.ppermute(value, axis, crossed(sizes[axis], bit))  25 us
    pallas_call x2, Pallas kernels, leaf_half(): pl.pallas_call(functools.partial(leaf_kernel, half), in_specs=[SMEM] * 2...  20.8 us
    ppermute x17, waiting for transfers between devices, swap(): return lax.ppermute(value, axis, crossed(sizes[axis], bit))  15.1 us
    pallas_call x1, Pallas kernels, finish(): pl.pallas_call(finish_kernel, in_specs=[VMEM] * 5, out_specs=[VMEM] * 3,...  7.17 us
    unnamed x18, local copies, waits for them, and re-layouts  2.16 us
    pallas_call x1, Pallas kernels, prepare(): pl.pallas_call(functools.partial(prepare_kernel, len(pieces)), in_specs=[...  1.5 us
  transfers between devices with their start and end apart: 17, of which 6 were waited for; matrix products, arithmetic and copies ran while one was open for 0% of the time, Pallas kernels for 38%

profile of v5, /device:TPU:0, one launch (start us, length us, event | category | flops | bytes accessed | tf_op | source)
XLA Modules:
  0.0 74.3 jit_solution(8017625628449603174)
XLA Ops:
  0.6 0.8 %pad_maximum_fusion.1.refs_0_ = f32[64,256]{1,0:T(8,128)S(1)} fusion(f32[64,128]{1,0:T(8,128)} %top_basis_ref.1, f32[64,128]{1,0:T(8,128)} %bitcast.1), kind=kLoop, calls=%fused_computation.1 | loop fusion | flops 16384 | bytes 131072 | tf_op jit(solution)/shard_map/concatenate | solution.py:463
  1.4 0.0 copy-start
  1.4 0.0 copy-start.1
  1.4 0.0 copy-start.5
  1.4 3.0 %collective-permute-start.1 = (f32[64,256]{1,0:T(8,128)S(1)}, f32[64,256]{1,0:T(8,128)S(1)}, u32[]{:S(2)}, u32[]{:S(2)}) collective-permute-start(f32[64,256]{1,0:T(8,128)S(1)} %pad_maximum_fusion.1.refs_0_), channel_id=1, source_target_pairs={{0,4},{4,0},{8,12},{12,8},{16,20},{20,16},{24,28},{28,24},{1,5},{5... | collective-permute-start | bytes 196616 | tf_op jit(solution)/shard_map/ppermute | solution.py:457
  4.4 0.0 copy-start.6
  4.4 0.7 copy-done.6
  5.1 0.0 copy-start.7
  5.1 0.7 copy-done.7
  5.8 0.0 copy-start.8
  5.8 9.9 %leaf_group.1 = (f32[256,512]{1,0:T(8,128)S(1)}, f32[256,512]{1,0:T(8,128)S(1)}, bf16[2048,512]{1,0:T(8,128)(2,1)S(1)}) custom-call(s32[1,16,16]{2,1,0:T(8,128)S(1)} %copy-done.6, s32[1,2,4]{2,1,0:T(2,128)S(1)} %copy-done.7, bf16[1,2048,2048]{2,1,0:T(8,128)(2,1)} %mass_hbm.3, bf16[1,2048,1024]{2,1,0:T(8,128)(2,1)} %modes_hbm.3, ...), custom_call_target="tpu_custom_call" | custom-call | flops 5368709120 | bytes 12582912 | tf_op jit(solution)/shard_map/leaf_group/pallas_call | solution.py:179
  15.8 0.2 collective-permute-start
  15.9 0.0 collective-permute-done.1
  15.9 0.0 copy-done
  15.9 0.0 copy-done.1
  16.0 2.1 %collective-permute-start.2 = (f32[128,256]{1,0:T(8,128)S(1)}, f32[128,256]{1,0:T(8,128)S(1)}, u32[]{:S(2)}, u32[]{:S(2)}) collective-permute-start(f32[128,256]{1,0:T(8,128)S(1)} %pad_maximum_fusion.refs_2_.refs_0_), channel_id=1, source_target_pairs={{0,8},{4,12},{8,0},{12,4},{16,24},{20,28},{24,16},{28,20},{1,9},{5... | collective-permute-start | bytes 393224 | tf_op jit(solution)/shard_map/ppermute | solution.py:457
  18.0 2.6 %collective-permute-start.3 = (f32[128,256]{1,0:T(8,128)S(1)}, f32[128,256]{1,0:T(8,128)S(1)}, u32[]{:S(2)}, u32[]{:S(2)}) collective-permute-start(f32[128,256]{1,0:T(8,128)S(1)} %pad_maximum_fusion.refs_2_.refs_0_), channel_id=1, source_target_pairs={{0,16},{4,20},{8,24},{12,28},{16,0},{20,4},{24,8},{28,12},{1,17},{... | collective-permute-start | bytes 393224 | tf_op jit(solution)/shard_map/ppermute | solution.py:457
  20.6 0.0 collective-permute-start.4
  20.6 0.0 copy-done.5
  20.6 0.0 copy-done.8
  20.6 0.0 copy-start.2
  20.6 0.0 copy-start.3
  20.6 10.9 %leaf_top.1 = (f32[256,512]{1,0:T(8,128)S(1)}, f32[256,512]{1,0:T(8,128)S(1)}, f32[2,128,512]{2,1,0:T(8,128)S(1)}) custom-call(s32[1,16,16]{2,1,0:T(8,128)S(1)} %copy-done.6, s32[1,2,4]{2,1,0:T(2,128)S(1)} %copy-done.8, bf16[1,2048,2048]{2,1,0:T(8,128)(2,1)} %mass_hbm.3, bf16[1,2048,1024]{2,1,0:T(8,128)(2,1)} %modes_hbm.3, ...), custom_call_target="tpu_custom_call" | custom-call | flops 5368709120 | bytes 12582912 | tf_op jit(solution)/shard_map/leaf_top/pallas_call | solution.py:179
  31.5 0.0 collective-permute-done.2.refs_1_
  31.6 0.0 collective-permute-done.3.refs_2_
  31.6 0.0 collective-permute-done.4.refs_3_
  31.6 0.0 collective-permute-done.other_ref
  31.6 0.0 copy-done.2
  31.6 0.0 copy-done.3
  31.6 1.5 %prepare.1 = (f32[136,128]{1,0:T(8,128)S(1)}, f32[2,128,128]{2,1,0:T(8,128)S(1)}, f32[128,512]{1,0:T(8,128)S(1)}, f32[128,512]{1,0:T(8,128)S(1)}, f32[256,512]{1,0:T(8,128)S(1)}, /*index=5*/f32[256,512]{1,0:T(8,128)S(1)}) custom-call(f32[256,512]{1,0:T(8,128)S(1)} %get-tuple-element.32.keep_in, f32[256,512]{1,0:T(8,128)S(1)} %get-tuple-element.33.send_ref, ...), custom_call_target="tpu_custom_call" | custom-call | flops 402653184 | bytes 3145728 | tf_op jit(solution)/shard_map/prepare/pallas_call | solution.py:277
  33.1 0.1 collective-permute-start.6
  33.2 1.9 %collective-permute-done.6.other_ref = f32[256,512]{1,0:T(8,128)S(1)} collective-permute-done((f32[256,512]{1,0:T(8,128)S(1)}, f32[256,512]{1,0:T(8,128)S(1)}, u32[]{:S(2)}, u32[]{:S(2)}) %collective-permute-start.6) | collective-permute-done | bytes 524320 | tf_op jit(solution)/shard_map/ppermute | solution.py:457
  35.1 0.1 fold.5
  35.2 1.8 %collective-permute-start.9 = (f32[128,512]{1,0:T(8,128)S(1)}, f32[128,512]{1,0:T(8,128)S(1)}, u32[]{:S(2)}, u32[]{:S(2)}) collective-permute-start(f32[128,512]{1,0:T(8,128)S(1)} %get-tuple-element.41.refs_0_), channel_id=1, source_target_pairs={{0,2},{1,3},{2,0},{3,1},{4,6},{5,7},{6,4},{7,5},{8,10},{9,11},{10,... | collective-permute-start | bytes 786440 | tf_op jit(solution)/shard_map/ppermute | solution.py:457
  37.0 1.5 %collective-permute-start.5 = (f32[136,128]{1,0:T(8,128)S(1)}, f32[136,128]{1,0:T(8,128)S(1)}, u32[]{:S(2)}, u32[]{:S(2)}) collective-permute-start(f32[136,128]{1,0:T(8,128)S(1)} %get-tuple-element.38.refs_0_.left_ref), channel_id=1, source_target_pairs={{0,4},{4,0},{8,12},{12,8},{16,20},{20,16},{24,28},{28,24},{1,5},{5... | collective-permute-start | bytes 208904 | tf_op jit(solution)/shard_map/ppermute | solution.py:457
  38.5 1.7 %collective-permute-start.14 = (f32[128,512]{1,0:T(8,128)S(1)}, f32[128,512]{1,0:T(8,128)S(1)}, u32[]{:S(2)}, u32[]{:S(2)}) collective-permute-start(f32[128,512]{1,0:T(8,128)S(1)} %get-tuple-element.49), channel_id=1, source_target_pairs={{0,16},{4,20},{8,24},{12,28},{16,0},{20,4},{24,8},{28,12},{1,17},{... | collective-permute-start | bytes 786440 | tf_op jit(solution)/shard_map/ppermute | solution.py:457
  40.1 1.1 %collective-permute-done.5.right_ref = f32[136,128]{1,0:T(8,128)S(1)} collective-permute-done((f32[136,128]{1,0:T(8,128)S(1)}, f32[136,128]{1,0:T(8,128)S(1)}, u32[]{:S(2)}, u32[]{:S(2)}) %collective-permute-start.5) | collective-permute-done | bytes 69664 | tf_op jit(solution)/shard_map/ppermute | solution.py:457
  41.3 1.4 %collective-permute-start.7 = (f32[136,128]{1,0:T(8,128)S(1)}, f32[136,128]{1,0:T(8,128)S(1)}, u32[]{:S(2)}, u32[]{:S(2)}) collective-permute-start(f32[136,128]{1,0:T(8,128)S(1)} %add.5.left_ref), channel_id=1, source_target_pairs={{0,8},{4,12},{8,0},{12,4},{16,24},{20,28},{24,16},{28,20},{1,9},{5... | collective-permute-start | bytes 208904 | tf_op jit(solution)/shard_map/ppermute | solution.py:457
  42.7 4.3 %collective-permute-done.7.right_ref = f32[136,128]{1,0:T(8,128)S(1)} collective-permute-done((f32[136,128]{1,0:T(8,128)S(1)}, f32[136,128]{1,0:T(8,128)S(1)}, u32[]{:S(2)}, u32[]{:S(2)}) %collective-permute-start.7) | collective-permute-done | bytes 69664 | tf_op jit(solution)/shard_map/ppermute | solution.py:457
  47.0 3.3 %collective-permute-start.8 = (f32[136,128]{1,0:T(8,128)S(1)}, f32[136,128]{1,0:T(8,128)S(1)}, u32[]{:S(2)}, u32[]{:S(2)}) collective-permute-start(f32[136,128]{1,0:T(8,128)S(1)} %add.6.refs_0_.left_ref), channel_id=1, source_target_pairs={{0,16},{4,20},{8,24},{12,28},{16,0},{20,4},{24,8},{28,12},{1,17},{... | collective-permute-start | bytes 208904 | tf_op jit(solution)/shard_map/ppermute | solution.py:457
  50.3 0.0 collective-permute-done.9.other_ref
  50.3 0.6 collective-permute-start.11
  50.9 4.8 %collective-permute-done.8.right_ref = f32[136,128]{1,0:T(8,128)S(1)} collective-permute-done((f32[136,128]{1,0:T(8,128)S(1)}, f32[136,128]{1,0:T(8,128)S(1)}, u32[]{:S(2)}, u32[]{:S(2)}) %collective-permute-start.8) | collective-permute-done | bytes 69664 | tf_op jit(solution)/shard_map/ppermute | solution.py:457
  55.8 0.1 collective-permute-start.10
  55.8 0.0 collective-permute-done.11.other_ref
  55.9 1.2 %collective-permute-done.10.right_ref = f32[136,128]{1,0:T(8,128)S(1)} collective-permute-done((f32[136,128]{1,0:T(8,128)S(1)}, f32[136,128]{1,0:T(8,128)S(1)}, u32[]{:S(2)}, u32[]{:S(2)}) %collective-permute-start.10) | collective-permute-done | bytes 69664 | tf_op jit(solution)/shard_map/ppermute | solution.py:457
  57.1 0.0 collective-permute-done.14.other_ref
  57.2 0.1 collective-permute-start.15
  57.2 3.1 %collective-permute-start.13 = (f32[32,512]{1,0:T(8,128)S(1)}, f32[32,512]{1,0:T(8,128)S(1)}, u32[]{:S(2)}, u32[]{:S(2)}) collective-permute-start(f32[32,512]{1,0:T(8,128)S(1)} %get-tuple-element.45.refs_0_), channel_id=1, source_target_pairs={{0,16},{4,20},{8,24},{12,28},{16,0},{20,4},{24,8},{28,12},{1,17},{... | collective-permute-start | bytes 196616 | tf_op jit(solution)/shard_map/ppermute | solution.py:457
  60.4 0.5 collective-permute-start.12
  60.9 1.8 %collective-permute-done.13.other_ref = f32[32,512]{1,0:T(8,128)S(1)} collective-permute-done((f32[32,512]{1,0:T(8,128)S(1)}, f32[32,512]{1,0:T(8,128)S(1)}, u32[]{:S(2)}, u32[]{:S(2)}) %collective-permute-start.13) | collective-permute-done | bytes 65568 | tf_op jit(solution)/shard_map/ppermute | solution.py:457
  62.7 3.0 %collective-permute-start.16 = (f32[16,512]{1,0:T(8,128)S(1)}, f32[16,512]{1,0:T(8,128)S(1)}, u32[]{:S(2)}, u32[]{:S(2)}) collective-permute-start(f32[16,512]{1,0:T(8,128)S(1)} %get-tuple-element.47.refs_0_), channel_id=1, source_target_pairs={{0,8},{4,12},{8,0},{12,4},{16,24},{20,28},{24,16},{28,20},{1,9},{5... | collective-permute-start | bytes 98312 | tf_op jit(solution)/shard_map/ppermute | solution.py:457
  65.7 0.0 collective-permute-done.12.right_ref
  65.7 7.2 %finish.1 = (f32[1,128,2,128]{3,2,1,0:T(2,128)}, f32[1,64,128]{2,1,0:T(8,128)}, f32[64,128]{1,0:T(8,128)}) custom-call(f32[136,128]{1,0:T(8,128)S(1)} %add.7.refs_0_.left_ref.near_ref, f32[136,128]{1,0:T(8,128)S(1)} %add.9.far_ref, f32[2,128,128]{2,1,0:T(8,128)S(1)} %get-tuple-element.51.terms_ref, f32[1,64,128]{2,1,0:T(8,128)S(1)} %copy-done.1, ...), custom_call_target="tpu_custom_call" | custom-call | flops 41943040 | bytes 393216 | tf_op jit(solution)/shard_map/finish/pallas_call | solution.py:432
  72.9 0.0 collective-permute-done.16.top_other_ref
  72.9 0.0 collective-permute-done.15.other_ref
  72.9 0.0 copy-start.4
  72.9 0.8 %copy-done.4 = f32[64,128]{1,0:T(8,128)S(1)} copy-done((f32[64,128]{1,0:T(8,128)S(1)}, f32[64,128]{1,0:T(8,128)}, u32[]{:S(2)}) %copy-start.4) | copy-done | bytes 32792
  73.6 0.7 last.1
  (10 shorter events, 0.2 us)
Async XLA Ops:
  1.4 14.5 %copy-start = (f32[64,128]{1,0:T(8,128)S(1)}, f32[64,128]{1,0:T(8,128)}, u32[]{:S(2)}) copy-start(f32[64,128]{1,0:T(8,128)} %top_basis_ref.1) | copy-start | bytes 98308
  1.4 14.5 %copy-start.1 = (f32[1,64,128]{2,1,0:T(8,128)S(1)}, f32[1,64,128]{2,1,0:T(8,128)}, u32[]{:S(2)}) copy-start(f32[1,64,128]{2,1,0:T(8,128)} %group_basis_ref.1) | copy-start | bytes 98308
  1.4 19.2 %copy-start.5 = (bf16[1,2048,128]{2,1,0:T(8,128)(2,1)S(1)}, bf16[1,2048,128]{2,1,0:T(8,128)(2,1)}, u32[]{:S(2)}) copy-start(bf16[1,2048,128]{2,1,0:T(8,128)(2,1)} %refs_0_.1) | copy-start | bytes 1572868
  1.4 14.5 %collective-permute-start.1 = (f32[64,256]{1,0:T(8,128)S(1)}, f32[64,256]{1,0:T(8,128)S(1)}, u32[]{:S(2)}, u32[]{:S(2)}) collective-permute-start(f32[64,256]{1,0:T(8,128)S(1)} %pad_maximum_fusion.1.refs_0_), channel_id=1, source_target_pairs={{0,4},{4,0},{8,12},{12,8},{16,20},{20,16},{24,28},{28,24},{1,5},{5... | collective-permute-start | bytes 196616 | tf_op jit(solution)/shard_map/ppermute | solution.py:457
  4.4 0.7 copy-start.6
  5.1 0.7 copy-start.7
  5.8 14.8 %copy-start.8 = (s32[1,2,4]{2,1,0:T(2,128)S(1)}, s32[1,2,4]{2,1,0:T(2,128)}, u32[]{:S(2)}) copy-start(s32[1,2,4]{2,1,0:T(2,128)} %map_ref.3) | copy-start | bytes 100
  15.8 15.8 %collective-permute-start = (f32[256,512]{1,0:T(8,128)S(1)}, f32[256,512]{1,0:T(8,128)S(1)}, u32[]{:S(2)}, u32[]{:S(2)}) collective-permute-start(f32[256,512]{1,0:T(8,128)S(1)} %get-tuple-element.33.send_ref), channel_id=1, source_target_pairs={{0,4},{4,0},{8,12},{12,8},{16,20},{20,16},{24,28},{28,24},{1,5},{5... | collective-permute-start | bytes 1572872 | tf_op jit(solution)/shard_map/ppermute | solution.py:457
  16.0 15.6 %collective-permute-start.2 = (f32[128,256]{1,0:T(8,128)S(1)}, f32[128,256]{1,0:T(8,128)S(1)}, u32[]{:S(2)}, u32[]{:S(2)}) collective-permute-start(f32[128,256]{1,0:T(8,128)S(1)} %pad_maximum_fusion.refs_2_.refs_0_), channel_id=1, source_target_pairs={{0,8},{4,12},{8,0},{12,4},{16,24},{20,28},{24,16},{28,20},{1,9},{5... | collective-permute-start | bytes 393224 | tf_op jit(solution)/shard_map/ppermute | solution.py:457
  18.0 13.5 %collective-permute-start.3 = (f32[128,256]{1,0:T(8,128)S(1)}, f32[128,256]{1,0:T(8,128)S(1)}, u32[]{:S(2)}, u32[]{:S(2)}) collective-permute-start(f32[128,256]{1,0:T(8,128)S(1)} %pad_maximum_fusion.refs_2_.refs_0_), channel_id=1, source_target_pairs={{0,16},{4,20},{8,24},{12,28},{16,0},{20,4},{24,8},{28,12},{1,17},{... | collective-permute-start | bytes 393224 | tf_op jit(solution)/shard_map/ppermute | solution.py:457
  20.6 11.0 %collective-permute-start.4 = (f32[128,256]{1,0:T(8,128)S(1)}, f32[128,256]{1,0:T(8,128)S(1)}, u32[]{:S(2)}, u32[]{:S(2)}) collective-permute-start(f32[128,256]{1,0:T(8,128)S(1)} %pad_maximum_fusion.refs_2_.refs_0_), channel_id=1, source_target_pairs={{0,24},{4,28},{8,16},{12,20},{16,8},{20,12},{24,0},{28,4},{1,25},{... | collective-permute-start | bytes 393224 | tf_op jit(solution)/shard_map/ppermute | solution.py:457
  20.6 11.0 %copy-start.2 = (f32[1,64,512]{2,1,0:T(8,128)S(1)}, f32[1,64,512]{2,1,0:T(8,128)}, u32[]{:S(2)}) copy-start(f32[1,64,512]{2,1,0:T(8,128)} %group_own_ref.1) | copy-start | bytes 393220
  20.6 11.0 %copy-start.3 = (f32[16,512]{1,0:T(8,128)S(1)}, f32[16,512]{1,0:T(8,128)}, u32[]{:S(2)}) copy-start(f32[16,512]{1,0:T(8,128)} %top_own_ref.1) | copy-start | bytes 98308
  33.1 2.0 %collective-permute-start.6 = (f32[256,512]{1,0:T(8,128)S(1)}, f32[256,512]{1,0:T(8,128)S(1)}, u32[]{:S(2)}, u32[]{:S(2)}) collective-permute-start(f32[256,512]{1,0:T(8,128)S(1)} %get-tuple-element.40), channel_id=1, source_target_pairs={{0,1},{1,0},{2,3},{3,2},{4,5},{5,4},{6,7},{7,6},{8,9},{9,8},{10,11... | collective-permute-start | bytes 1572872 | tf_op jit(solution)/shard_map/ppermute | solution.py:457
  35.2 15.1 %collective-permute-start.9 = (f32[128,512]{1,0:T(8,128)S(1)}, f32[128,512]{1,0:T(8,128)S(1)}, u32[]{:S(2)}, u32[]{:S(2)}) collective-permute-start(f32[128,512]{1,0:T(8,128)S(1)} %get-tuple-element.41.refs_0_), channel_id=1, source_target_pairs={{0,2},{1,3},{2,0},{3,1},{4,6},{5,7},{6,4},{7,5},{8,10},{9,11},{10,... | collective-permute-start | bytes 786440 | tf_op jit(solution)/shard_map/ppermute | solution.py:457
  37.0 4.3 %collective-permute-start.5 = (f32[136,128]{1,0:T(8,128)S(1)}, f32[136,128]{1,0:T(8,128)S(1)}, u32[]{:S(2)}, u32[]{:S(2)}) collective-permute-start(f32[136,128]{1,0:T(8,128)S(1)} %get-tuple-element.38.refs_0_.left_ref), channel_id=1, source_target_pairs={{0,4},{4,0},{8,12},{12,8},{16,20},{20,16},{24,28},{28,24},{1,5},{5... | collective-permute-start | bytes 208904 | tf_op jit(solution)/shard_map/ppermute | solution.py:457
  38.5 18.6 %collective-permute-start.14 = (f32[128,512]{1,0:T(8,128)S(1)}, f32[128,512]{1,0:T(8,128)S(1)}, u32[]{:S(2)}, u32[]{:S(2)}) collective-permute-start(f32[128,512]{1,0:T(8,128)S(1)} %get-tuple-element.49), channel_id=1, source_target_pairs={{0,16},{4,20},{8,24},{12,28},{16,0},{20,4},{24,8},{28,12},{1,17},{... | collective-permute-start | bytes 786440 | tf_op jit(solution)/shard_map/ppermute | solution.py:457
  41.3 5.7 %collective-permute-start.7 = (f32[136,128]{1,0:T(8,128)S(1)}, f32[136,128]{1,0:T(8,128)S(1)}, u32[]{:S(2)}, u32[]{:S(2)}) collective-permute-start(f32[136,128]{1,0:T(8,128)S(1)} %add.5.left_ref), channel_id=1, source_target_pairs={{0,8},{4,12},{8,0},{12,4},{16,24},{20,28},{24,16},{28,20},{1,9},{5... | collective-permute-start | bytes 208904 | tf_op jit(solution)/shard_map/ppermute | solution.py:457
  47.0 8.7 %collective-permute-start.8 = (f32[136,128]{1,0:T(8,128)S(1)}, f32[136,128]{1,0:T(8,128)S(1)}, u32[]{:S(2)}, u32[]{:S(2)}) collective-permute-start(f32[136,128]{1,0:T(8,128)S(1)} %add.6.refs_0_.left_ref), channel_id=1, source_target_pairs={{0,16},{4,20},{8,24},{12,28},{16,0},{20,4},{24,8},{28,12},{1,17},{... | collective-permute-start | bytes 208904 | tf_op jit(solution)/shard_map/ppermute | solution.py:457
  50.3 5.5 %collective-permute-start.11 = (f32[64,512]{1,0:T(8,128)S(1)}, f32[64,512]{1,0:T(8,128)S(1)}, u32[]{:S(2)}, u32[]{:S(2)}) collective-permute-start(f32[64,512]{1,0:T(8,128)S(1)} %get-tuple-element.43.refs_0_), channel_id=1, source_target_pairs={{0,4},{4,0},{8,12},{12,8},{16,20},{20,16},{24,28},{28,24},{1,5},{5... | collective-permute-start | bytes 393224 | tf_op jit(solution)/shard_map/ppermute | solution.py:457
  55.8 1.3 %collective-permute-start.10 = (f32[136,128]{1,0:T(8,128)S(1)}, f32[136,128]{1,0:T(8,128)S(1)}, u32[]{:S(2)}, u32[]{:S(2)}) collective-permute-start(f32[136,128]{1,0:T(8,128)S(1)} %add.7.refs_0_.left_ref.near_ref), channel_id=1, source_target_pairs={{0,1},{1,0},{2,3},{3,2},{4,5},{5,4},{6,7},{7,6},{8,9},{9,8},{10,11... | collective-permute-start | bytes 208904 | tf_op jit(solution)/shard_map/ppermute | solution.py:457
  57.2 15.7 %collective-permute-start.15 = (f32[64,512]{1,0:T(8,128)S(1)}, f32[64,512]{1,0:T(8,128)S(1)}, u32[]{:S(2)}, u32[]{:S(2)}) collective-permute-start(f32[64,512]{1,0:T(8,128)S(1)} %get-tuple-element.50.refs_1_), channel_id=1, source_target_pairs={{0,8},{4,12},{8,0},{12,4},{16,24},{20,28},{24,16},{28,20},{1,9},{5... | collective-permute-start | bytes 393224 | tf_op jit(solution)/shard_map/ppermute | solution.py:457
  57.2 5.4 %collective-permute-start.13 = (f32[32,512]{1,0:T(8,128)S(1)}, f32[32,512]{1,0:T(8,128)S(1)}, u32[]{:S(2)}, u32[]{:S(2)}) collective-permute-start(f32[32,512]{1,0:T(8,128)S(1)} %get-tuple-element.45.refs_0_), channel_id=1, source_target_pairs={{0,16},{4,20},{8,24},{12,28},{16,0},{20,4},{24,8},{28,12},{1,17},{... | collective-permute-start | bytes 196616 | tf_op jit(solution)/shard_map/ppermute | solution.py:457
  60.4 5.3 %collective-permute-start.12 = (f32[136,128]{1,0:T(8,128)S(1)}, f32[136,128]{1,0:T(8,128)S(1)}, u32[]{:S(2)}, u32[]{:S(2)}) collective-permute-start(f32[136,128]{1,0:T(8,128)S(1)} %add.8.refs_0_.left_ref), channel_id=1, source_target_pairs={{0,2},{1,3},{2,0},{3,1},{4,6},{5,7},{6,4},{7,5},{8,10},{9,11},{10,... | collective-permute-start | bytes 208904 | tf_op jit(solution)/shard_map/ppermute | solution.py:457
  62.7 10.2 %collective-permute-start.16 = (f32[16,512]{1,0:T(8,128)S(1)}, f32[16,512]{1,0:T(8,128)S(1)}, u32[]{:S(2)}, u32[]{:S(2)}) collective-permute-start(f32[16,512]{1,0:T(8,128)S(1)} %get-tuple-element.47.refs_0_), channel_id=1, source_target_pairs={{0,8},{4,12},{8,0},{12,4},{16,24},{20,28},{24,16},{28,20},{1,9},{5... | collective-permute-start | bytes 98312 | tf_op jit(solution)/shard_map/ppermute | solution.py:457
  72.9 0.8 %copy-start.4 = (f32[64,128]{1,0:T(8,128)S(1)}, f32[64,128]{1,0:T(8,128)}, u32[]{:S(2)}) copy-start(f32[64,128]{1,0:T(8,128)} %get-tuple-element.29.after_ref) | copy-start | bytes 98308

commit v6 on v5

--- a/solution.py
+++ b/solution.py
@@ -14,7 +14,7 @@
 VMEM = pl.BlockSpec(memory_space=pltpu.VMEM)
 SMEM = pl.BlockSpec(memory_space=pltpu.SMEM)
 HBM = pl.BlockSpec(memory_space=pltpu.HBM)
-MASS_PARTS = 4
+MASS_PARTS = 2
 LEAF_MEGABYTES = 48
 
 
@@ -123,17 +123,14 @@
         loaded = jnp.dot(masked, modes_ref[...], preferred_element_type=F32).astype(BF16)
         window = pl.ds(pl.multiple_of(i * height, height), height)
         loaded_ref[window, :] = loaded
-        if not first:
-            add_partial(i - 1)
-
-    def add_partial(i):
-        window = pl.ds(pl.multiple_of(i * height, height), height)
-        partial_ref[...] += rows_first(modes_ref[window, :], loaded_ref[window, :])
-
-    partial_ref[...] = jnp.zeros_like(partial_ref)
+        partial = rows_first(modes_ref[window, :], loaded)
+        if first:
+            partial_ref[...] = partial
+        else:
+            partial_ref[...] += partial
+
     part(0, True)
     lax.fori_loop(1, MASS_PARTS, lambda i, _: part(i, False), None)
-    add_partial(MASS_PARTS - 1)
 
     blocks = size // TILE
     to = [pl.multiple_of(map_ref[0, half, a] * TILE, TILE) for a in range(blocks)]
@@ -216,13 +213,13 @@
 
 
 def prepare_kernel(
-    count, keep_in, send_ref, other_ref, top_keep_in, top_send_ref, moved_ref, group_own_ref,
+    count, keep_in, send_ref, top_keep_in, top_send_ref, moved_ref, group_own_ref,
     top_own_ref, *refs,
 ):
-    pieces = refs[:count]
+    pieces = refs[1 : count + 1]
     (
-        packed_ref, terms_ref, next_ref, next_send_ref, top_keep_ref, top_next_ref, bases_ref, keep_ref
-    ) = refs[count:]
+        packed_ref, terms_ref, keep_ref, top_keep_ref, top_next_ref, bases_ref
+    ) = refs[count + 1 :]
     modes = terms_ref.shape[2]
     size = bases_ref.shape[0]
     row, col = lax.axis_index("row"), lax.axis_index("col")
@@ -231,7 +228,6 @@
     top_steps = exchanges(1, row_count, col_count)
     keep_ref[...] = keep_in[...]
     add_own(keep_ref, group_own_ref[0], share_place(group_steps[1:]))
-    halve(group_steps[1], keep_ref, other_ref, next_ref, next_send_ref)
     top_keep_ref[...] = top_keep_in[...]
     add_own(top_keep_ref, top_own_ref[...], share_place(top_steps[1:]))
     top_next_ref[...] = top_send_ref[...]
@@ -270,29 +266,27 @@
     packed_ref[modes:, :] = jnp.broadcast_to(diagonal, (SUBLANES, modes))
 
 
-def prepare(keep, send, other, top_keep, top_send, moved, group_own, top_own, pieces):
+def prepare(keep, send, top_keep, top_send, moved, group_own, top_own, after, pieces):
     _, modes, size = moved.shape
-    part = jax.ShapeDtypeStruct((keep.shape[0] // 2, size), F32)
     half = jax.ShapeDtypeStruct(keep.shape, F32)
     return pl.pallas_call(
         functools.partial(prepare_kernel, len(pieces)),
-        in_specs=[VMEM] * (8 + len(pieces)),
-        out_specs=[VMEM] * 6,
+        in_specs=[VMEM] * 7 + [pl.BlockSpec(memory_space=pl.ANY)] + [VMEM] * len(pieces),
+        out_specs=[VMEM] * 5,
         out_shape=[
             jax.ShapeDtypeStruct((modes + SUBLANES, modes), F32),
             jax.ShapeDtypeStruct((2, modes, modes), F32),
-            part,
-            part,
+            half,
             half,
             half,
         ],
-        scratch_shapes=[pltpu.VMEM((size, 2 * modes), F32), pltpu.VMEM(keep.shape, F32)],
+        scratch_shapes=[pltpu.VMEM((size, 2 * modes), F32)],
         compiler_params=params(32),
         cost_estimate=pl.CostEstimate(
             flops=12 * size * size * modes, bytes_accessed=12 * size * size, transcendentals=0
         ),
         name="prepare",
-    )(keep, send, other, top_keep, top_send, moved, group_own, top_own, *pieces)
+    )(keep, send, top_keep, top_send, moved, group_own, top_own, after, *pieces)
 
 
 def fold_kernel(step, after_count, keep_ref, other_ref, *refs):
@@ -367,21 +361,23 @@
             ]
             strip = state[start:stop, :]
             small = [s[start:stop, :] for s in spread]
-            scaled = []
+            units, levels, scales = [], [], []
             rest = strip
             for q in range(width):
                 scale = lax.rsqrt(small[q][q : q + 1, :])
-                tail = [small[t][q : q + 1, :] * scale for t in range(q + 1, width)]
-                level = rest[q : q + 1, :] * scale
-                rest = rest - small[q] * (scale * level)
-                small[q] = jnp.where(line == q, 1.0, small[q]) * scale
+                inverse = scale * scale
+                level = rest[q : q + 1, :]
+                rest = rest - (small[q] * level) * inverse
+                unit = jnp.where(line == q, 1.0, small[q])
                 for t in range(q + 1, width):
-                    small[t] = jnp.where(line == q, 0.0, small[t]) - small[q] * tail[t - q - 1]
-                scaled.append(level)
-            small = [jnp.where(line <= q, s, 0.0) for q, s in enumerate(small)]
-            solved = small[0] * scaled[0]
+                    product = unit * small[t][q : q + 1, :]
+                    small[t] = jnp.where(line == q, 0.0, small[t]) - product * inverse
+                units.append(jnp.where(line <= q, unit, 0.0))
+                levels.append(level * inverse)
+                scales.append(scale)
+            solved = units[0] * levels[0]
             for q in range(1, width):
-                solved = solved + small[q] * scaled[q]
+                solved = solved + units[q] * levels[q]
             solved = jnp.where(lane >= stop, solved, 0.0)
             update = spread[0] * solved[0:1, :]
             for q in range(1, width):
@@ -397,7 +393,7 @@
             states[m] = jnp.concatenate(parts, axis=0)
             diagonal = jnp.zeros((width, size), F32)
             for q in range(width):
-                diagonal = jnp.where(lane == start + q, small[q], diagonal)
+                diagonal = jnp.where(lane == start + q, units[q] * scales[q], diagonal)
             diagonals[m].append(diagonal)
     uppers = [jnp.where(across >= down, state, 0.0) for state in states]
     return uppers, [jnp.concatenate(d, axis=0) for d in diagonals]
@@ -405,6 +401,7 @@
 
 def finish_kernel(
     near_ref, far_ref, terms_ref, group_basis_ref, top_basis_ref, coupling_ref, group_ref, top_ref,
+    token_ref,
 ):
     modes = near_ref.shape[1]
     down = lax.broadcasted_iota(jnp.int32, (modes, modes), 0)
@@ -425,6 +422,7 @@
             group_ref[0] = result[modes:]
         else:
             top_ref[...] = result[modes:]
+            token_ref[...] = result[:SUBLANES]
 
 
 def finish(near, far, terms, group_basis, top_basis):
@@ -432,11 +430,12 @@
     return pl.pallas_call(
         finish_kernel,
         in_specs=[VMEM] * 5,
-        out_specs=[VMEM] * 3,
+        out_specs=[VMEM] * 4,
         out_shape=[
             jax.ShapeDtypeStruct((1, modes, 2, modes), F32),
             jax.ShapeDtypeStruct(group_basis.shape, F32),
             jax.ShapeDtypeStruct(top_basis.shape, F32),
+            jax.ShapeDtypeStruct((SUBLANES, modes), F32),
         ],
         compiler_params=params(32),
         cost_estimate=pl.CostEstimate(
@@ -467,39 +466,42 @@
     pieces = [pair] + [swap(pair, "row", 2 * k) for k in range(1, row_count // 2)]
     other = swap(send, *group_steps[0])
     top_keep, top_send, moved = half_of(1, [leaf_fixed_modes, loaded], pair)
-    packed, terms, keep, send, top_keep, top_send = prepare(
-        keep, send, other, top_keep, top_send, moved, group_mass, top_mass, pieces
+    packed, terms, keep, top_keep, top_send = prepare(
+        keep, send, top_keep, top_send, moved, group_mass, top_mass, other, pieces
     )
-    group_left = group_steps[1:]
     top_left = exchanges(1, row_count, col_count)
-    sums = [("row", 1 << b) for b in range(bits_of(row_count))]
+    sums = [("row", 1 << b) for b in range(1, bits_of(row_count))] + [("row", 1)]
+    row_steps = len(sums)
     sums += [("col", 1 << b) for b in range(bits_of(col_count))]
     value = near = packed
-    group_other, top_other = None, swap(top_send, *top_left[0])
+    top_other = swap(top_send, *top_left[0])
+    after = []
     for i, step in enumerate(sums):
-        other = swap(value, *step)
+        value = add(value, swap(value, *step), *after)
         after = []
-        if i == 0:
-            group_other = swap(send, *group_left[0])
-        if len(top_left) > 1 and i != 1:
+        if i == row_steps - 1:
+            near = value
+        if len(top_left) > 1:
             top_keep, top_send = fold(top_left[1], top_keep, top_other, value)
             top_left = top_left[1:]
             top_other = swap(top_send, *top_left[0])
             after.append(top_send)
-        if len(group_left) > 1 and i >= len(sums) - len(group_left) + 1:
-            keep, send = fold(group_left[1], keep, group_other, value)
-            group_left = group_left[1:]
-            group_other = swap(send, *group_left[0])
+        behind = i - (row_steps - 2)
+        if behind == 0 or (behind >= 3 and len(group_steps) > 1):
+            keep, send = fold(group_steps[1], keep, other, value)
+            group_steps = group_steps[1:]
+            other = swap(send, *group_steps[0])
             after.append(send)
-        value = add(value, other, *after)
-        if i == bits_of(row_count) - 1:
-            near = value
+    while len(group_steps) > 1:
+        keep, send = fold(group_steps[1], keep, other, value)
+        group_steps = group_steps[1:]
+        other = swap(send, *group_steps[0])
     while len(top_left) > 1:
         top_keep, top_send = fold(top_left[1], top_keep, top_other, value)
         top_left = top_left[1:]
         top_other = swap(top_send, *top_left[0])
-    coupling, group_modes, top_modes = finish(near, value, terms, group_basis, top_basis)
-    assembled, top_assembled = last(keep, group_other, top_keep, top_other, top_modes)
+    coupling, group_modes, top_modes, token = finish(near, value, terms, group_basis, top_basis)
+    assembled, top_assembled = last(keep, other, top_keep, top_other, token)
     return coupling, group_modes, top_modes, assembled, top_assembled
 
 

time: 74.6 us -> 70.7 us (0.948)
  starting transfers between devices: 25 us -> 21.4 us
  local copies, waits for them, and re-layouts: 2.16 us -> 1.4 us
    ppermute x17, starting transfers between devices: 25 us -> 21.4 us  [swap(): return lax.ppermute(value, axis, crossed(sizes[axis], bit))]
    pallas_call x1, Pallas kernels: 7.17 us -> 8.45 us  [finish(): pl.pallas_call(finish_kernel, in_specs=[VMEM] * 5, out_specs=[VMEM] * 4,...]
    pallas_call x2, Pallas kernels: 20.8 us -> 19.8 us  [leaf_half(): pl.pallas_call(functools.partial(leaf_kernel, half), in_specs=[SMEM] * 2...]
    unnamed x18 -> x16, local copies, waits for them, and re-layouts: 2.16 us -> 1.4 us
  transfers between devices with their start and end apart: 17 -> 17, of which waited for: 6 -> 5; matrix products, arithmetic and copies ran while one was open for 0% -> 0% of each run, Pallas kernels for 38% -> 40%
where the time goes in v6:
time: 70.7 us; the launch traced here: 70.4 us
  Pallas kernels  30.7 us (43%)
  starting transfers between devices  21.4 us (30%)
  waiting for transfers between devices  15.3 us (22%)
  local copies, waits for them, and re-layouts  1.4 us (2%)
  between operations  0.86 us (1%)
  other arithmetic  0.79 us (1%)
    ppermute x17, starting transfers between devices, swap(): return lax.ppermute(value, axis, crossed(sizes[axis], bit))  21.4 us
    pallas_call x2, Pallas kernels, leaf_half(): pl.pallas_call(functools.partial(leaf_kernel, half), in_specs=[SMEM] * 2...  19.8 us
    ppermute x17, waiting for transfers between devices, swap(): return lax.ppermute(value, axis, crossed(sizes[axis], bit))  15.3 us
    pallas_call x1, Pallas kernels, finish(): pl.pallas_call(finish_kernel, in_specs=[VMEM] * 5, out_specs=[VMEM] * 4,...  8.45 us
    pallas_call x1, Pallas kernels, prepare(): pl.pallas_call(functools.partial(prepare_kernel, len(pieces)), in_specs=[...  1.43 us
  transfers between devices with their start and end apart: 17, of which 5 were waited for; matrix products, arithmetic and copies ran while one was open for 0% of the time, Pallas kernels for 40%

profile of v6, /device:TPU:0, one launch (start us, length us, event | category | flops | bytes accessed | tf_op | source)
XLA Modules:
  0.0 70.4 jit_solution(2922778141840565921)
XLA Ops:
  0.6 0.8 %pad_maximum_fusion.1.refs_0_ = f32[64,256]{1,0:T(8,128)S(1)} fusion(f32[64,128]{1,0:T(8,128)} %top_basis_ref.1, f32[64,128]{1,0:T(8,128)} %bitcast.1), kind=kLoop, calls=%fused_computation.1 | loop fusion | flops 16384 | bytes 131072 | tf_op jit(solution)/shard_map/concatenate | solution.py:462
  1.4 0.0 copy-start
  1.4 0.0 copy-start.1
  1.4 0.0 copy-start.4
  1.4 3.0 %collective-permute-start = (f32[64,256]{1,0:T(8,128)S(1)}, f32[64,256]{1,0:T(8,128)S(1)}, u32[]{:S(2)}, u32[]{:S(2)}) collective-permute-start(f32[64,256]{1,0:T(8,128)S(1)} %pad_maximum_fusion.1.refs_0_), channel_id=1, source_target_pairs={{0,4},{4,0},{8,12},{12,8},{16,20},{20,16},{24,28},{28,24},{1,5},{5... | collective-permute-start | bytes 196616 | tf_op jit(solution)/shard_map/ppermute | solution.py:456
  4.4 0.0 copy-start.5
  4.4 0.7 copy-done.5
  5.1 0.0 copy-start.6
  5.1 0.7 copy-done.6
  5.8 0.0 copy-start.7
  5.8 9.5 %leaf_group.1 = (f32[256,512]{1,0:T(8,128)S(1)}, f32[256,512]{1,0:T(8,128)S(1)}, bf16[2048,512]{1,0:T(8,128)(2,1)S(1)}) custom-call(s32[1,16,16]{2,1,0:T(8,128)S(1)} %copy-done.5, s32[1,2,4]{2,1,0:T(2,128)S(1)} %copy-done.6, bf16[1,2048,2048]{2,1,0:T(8,128)(2,1)} %mass_hbm.3, bf16[1,2048,1024]{2,1,0:T(8,128)(2,1)} %modes_hbm.3, ...), custom_call_target="tpu_custom_call" | custom-call | flops 5368709120 | bytes 12582912 | tf_op jit(solution)/shard_map/leaf_group/pallas_call | solution.py:176
  15.3 0.1 collective-permute-start.1
  15.5 0.0 collective-permute-done
  15.5 0.0 copy-done
  15.5 0.0 copy-done.1
  15.5 2.1 %collective-permute-start.2 = (f32[128,256]{1,0:T(8,128)S(1)}, f32[128,256]{1,0:T(8,128)S(1)}, u32[]{:S(2)}, u32[]{:S(2)}) collective-permute-start(f32[128,256]{1,0:T(8,128)S(1)} %pad_maximum_fusion.refs_2_.refs_1_), channel_id=1, source_target_pairs={{0,8},{4,12},{8,0},{12,4},{16,24},{20,28},{24,16},{28,20},{1,9},{5... | collective-permute-start | bytes 393224 | tf_op jit(solution)/shard_map/ppermute | solution.py:456
  17.6 2.6 %collective-permute-start.3 = (f32[128,256]{1,0:T(8,128)S(1)}, f32[128,256]{1,0:T(8,128)S(1)}, u32[]{:S(2)}, u32[]{:S(2)}) collective-permute-start(f32[128,256]{1,0:T(8,128)S(1)} %pad_maximum_fusion.refs_2_.refs_1_), channel_id=1, source_target_pairs={{0,16},{4,20},{8,24},{12,28},{16,0},{20,4},{24,8},{28,12},{1,17},{... | collective-permute-start | bytes 393224 | tf_op jit(solution)/shard_map/ppermute | solution.py:456
  20.2 0.0 collective-permute-start.4
  20.2 0.0 copy-done.4
  20.2 0.0 copy-done.7
  20.2 0.0 copy-start.2
  20.2 0.0 copy-start.3
  20.2 10.3 %leaf_top.1 = (f32[256,512]{1,0:T(8,128)S(1)}, f32[256,512]{1,0:T(8,128)S(1)}, f32[2,128,512]{2,1,0:T(8,128)S(1)}) custom-call(s32[1,16,16]{2,1,0:T(8,128)S(1)} %copy-done.5, s32[1,2,4]{2,1,0:T(2,128)S(1)} %copy-done.7, bf16[1,2048,2048]{2,1,0:T(8,128)(2,1)} %mass_hbm.3, bf16[1,2048,1024]{2,1,0:T(8,128)(2,1)} %modes_hbm.3, ...), custom_call_target="tpu_custom_call" | custom-call | flops 5368709120 | bytes 12582912 | tf_op jit(solution)/shard_map/leaf_top/pallas_call | solution.py:176
  30.5 0.0 collective-permute-done.2.refs_2_
  30.5 0.0 collective-permute-done.3.refs_3_
  30.5 0.0 collective-permute-done.4.refs_4_
  30.5 0.0 collective-permute-done.1.refs_0_.other_ref
  30.6 0.0 copy-done.2
  30.6 0.0 copy-done.3
  30.6 1.4 %prepare.1 = (f32[136,128]{1,0:T(8,128)S(1)}, f32[2,128,128]{2,1,0:T(8,128)S(1)}, f32[256,512]{1,0:T(8,128)S(1)}, f32[256,512]{1,0:T(8,128)S(1)}, f32[256,512]{1,0:T(8,128)S(1)}) custom-call(f32[256,512]{1,0:T(8,128)S(1)} %get-tuple-element.34.keep_in, f32[256,512]{1,0:T(8,128)S(1)} %get-tuple-element.35.send_ref, ...), custom_call_target="tpu_custom_call" | custom-call | flops 402653184 | bytes 3145728 | tf_op jit(solution)/shard_map/prepare/pallas_call | solution.py:272
  32.0 0.1 collective-permute-start.7
  32.1 1.4 %collective-permute-start.5 = (f32[136,128]{1,0:T(8,128)S(1)}, f32[136,128]{1,0:T(8,128)S(1)}, u32[]{:S(2)}, u32[]{:S(2)}) collective-permute-start(f32[136,128]{1,0:T(8,128)S(1)} %get-tuple-element.40.left_ref), channel_id=1, source_target_pairs={{0,8},{4,12},{8,0},{12,4},{16,24},{20,28},{24,16},{28,20},{1,9},{5... | collective-permute-start | bytes 208904 | tf_op jit(solution)/shard_map/ppermute | solution.py:456
  33.5 3.2 %collective-permute-done.5.right_ref = f32[136,128]{1,0:T(8,128)S(1)} collective-permute-done((f32[136,128]{1,0:T(8,128)S(1)}, f32[136,128]{1,0:T(8,128)S(1)}, u32[]{:S(2)}, u32[]{:S(2)}) %collective-permute-start.5) | collective-permute-done | bytes 69664 | tf_op jit(solution)/shard_map/ppermute | solution.py:456
  36.7 0.0 collective-permute-done.7.other_ref
  36.7 0.1 fold.6
  36.8 1.9 %collective-permute-start.9 = (f32[128,512]{1,0:T(8,128)S(1)}, f32[128,512]{1,0:T(8,128)S(1)}, u32[]{:S(2)}, u32[]{:S(2)}) collective-permute-start(f32[128,512]{1,0:T(8,128)S(1)} %get-tuple-element.43.refs_0_), channel_id=1, source_target_pairs={{0,2},{1,3},{2,0},{3,1},{4,6},{5,7},{6,4},{7,5},{8,10},{9,11},{10,... | collective-permute-start | bytes 786440 | tf_op jit(solution)/shard_map/ppermute | solution.py:456
  38.6 2.4 %collective-permute-start.6 = (f32[136,128]{1,0:T(8,128)S(1)}, f32[136,128]{1,0:T(8,128)S(1)}, u32[]{:S(2)}, u32[]{:S(2)}) collective-permute-start(f32[136,128]{1,0:T(8,128)S(1)} %add.5.refs_0_.left_ref), channel_id=1, source_target_pairs={{0,16},{4,20},{8,24},{12,28},{16,0},{20,4},{24,8},{28,12},{1,17},{... | collective-permute-start | bytes 208904 | tf_op jit(solution)/shard_map/ppermute | solution.py:456
  41.0 3.7 %collective-permute-done.6.right_ref = f32[136,128]{1,0:T(8,128)S(1)} collective-permute-done((f32[136,128]{1,0:T(8,128)S(1)}, f32[136,128]{1,0:T(8,128)S(1)}, u32[]{:S(2)}, u32[]{:S(2)}) %collective-permute-start.6) | collective-permute-done | bytes 69664 | tf_op jit(solution)/shard_map/ppermute | solution.py:456
  44.7 0.1 fold.8
  44.8 1.7 %collective-permute-start.14 = (f32[128,512]{1,0:T(8,128)S(1)}, f32[128,512]{1,0:T(8,128)S(1)}, u32[]{:S(2)}, u32[]{:S(2)}) collective-permute-start(f32[128,512]{1,0:T(8,128)S(1)} %get-tuple-element.47.refs_1_), channel_id=1, source_target_pairs={{0,16},{4,20},{8,24},{12,28},{16,0},{20,4},{24,8},{28,12},{1,17},{... | collective-permute-start | bytes 786440 | tf_op jit(solution)/shard_map/ppermute | solution.py:456
  46.5 1.5 %collective-permute-start.8 = (f32[136,128]{1,0:T(8,128)S(1)}, f32[136,128]{1,0:T(8,128)S(1)}, u32[]{:S(2)}, u32[]{:S(2)}) collective-permute-start(f32[136,128]{1,0:T(8,128)S(1)} %add.6.refs_0_.left_ref), channel_id=1, source_target_pairs={{0,4},{4,0},{8,12},{12,8},{16,20},{20,16},{24,28},{28,24},{1,5},{5... | collective-permute-start | bytes 208904 | tf_op jit(solution)/shard_map/ppermute | solution.py:456
  47.9 0.0 collective-permute-done.9.other_ref
  48.0 0.6 collective-permute-start.11
  48.6 2.2 %collective-permute-done.8.right_ref = f32[136,128]{1,0:T(8,128)S(1)} collective-permute-done((f32[136,128]{1,0:T(8,128)S(1)}, f32[136,128]{1,0:T(8,128)S(1)}, u32[]{:S(2)}, u32[]{:S(2)}) %collective-permute-start.8) | collective-permute-done | bytes 69664 | tf_op jit(solution)/shard_map/ppermute | solution.py:456
  50.8 0.1 collective-permute-start.10
  50.9 2.1 %collective-permute-done.11.other_ref = f32[64,512]{1,0:T(8,128)S(1)} collective-permute-done((f32[64,512]{1,0:T(8,128)S(1)}, f32[64,512]{1,0:T(8,128)S(1)}, u32[]{:S(2)}, u32[]{:S(2)}) %collective-permute-start.11) | collective-permute-done | bytes 131104 | tf_op jit(solution)/shard_map/ppermute | solution.py:456
  53.0 0.0 collective-permute-done.10.right_ref
  53.1 0.6 collective-permute-start.12
  53.6 1.3 %collective-permute-start.13 = (f32[32,512]{1,0:T(8,128)S(1)}, f32[32,512]{1,0:T(8,128)S(1)}, u32[]{:S(2)}, u32[]{:S(2)}) collective-permute-start(f32[32,512]{1,0:T(8,128)S(1)} %get-tuple-element.49.refs_0_), channel_id=1, source_target_pairs={{0,16},{4,20},{8,24},{12,28},{16,0},{20,4},{24,8},{28,12},{1,17},{... | collective-permute-start | bytes 196616 | tf_op jit(solution)/shard_map/ppermute | solution.py:456
  54.9 4.2 %collective-permute-done.13.other_ref = f32[32,512]{1,0:T(8,128)S(1)} collective-permute-done((f32[32,512]{1,0:T(8,128)S(1)}, f32[32,512]{1,0:T(8,128)S(1)}, u32[]{:S(2)}, u32[]{:S(2)}) %collective-permute-start.13) | collective-permute-done | bytes 65568 | tf_op jit(solution)/shard_map/ppermute | solution.py:456
  59.1 0.0 collective-permute-done.12.right_ref
  59.2 0.0 collective-permute-done.14.other_ref
  59.2 1.9 %collective-permute-start.15 = (f32[64,512]{1,0:T(8,128)S(1)}, f32[64,512]{1,0:T(8,128)S(1)}, u32[]{:S(2)}, u32[]{:S(2)}) collective-permute-start(f32[64,512]{1,0:T(8,128)S(1)} %get-tuple-element.58), channel_id=1, source_target_pairs={{0,8},{4,12},{8,0},{12,4},{16,24},{20,28},{24,16},{28,20},{1,9},{5... | collective-permute-start | bytes 393224 | tf_op jit(solution)/shard_map/ppermute | solution.py:456
  61.1 0.2 collective-permute-start.16
  61.3 8.4 %finish.1 = (f32[1,128,2,128]{3,2,1,0:T(2,128)}, f32[1,64,128]{2,1,0:T(8,128)}, f32[64,128]{1,0:T(8,128)}, f32[8,128]{1,0:T(8,128)S(1)}) custom-call(f32[136,128]{1,0:T(8,128)S(1)} %add.7.refs_0_.left_ref.near_ref, f32[136,128]{1,0:T(8,128)S(1)} %add.9.far_ref.refs_0_, f32[2,128,128]{2,1,0:T(8,128)S(1)} %get-tuple-element.52.terms_ref, ...), custom_call_target="tpu_custom_call" | custom-call | flops 41943040 | bytes 393216 | tf_op jit(solution)/shard_map/finish/pallas_call | solution.py:430
  69.8 0.0 collective-permute-done.16.top_other_ref
  69.8 0.0 collective-permute-done.15.other_ref
  69.8 0.7 last.1
  (10 shorter events, 0.2 us)
Async XLA Ops:
  1.4 14.1 %copy-start = (f32[64,128]{1,0:T(8,128)S(1)}, f32[64,128]{1,0:T(8,128)}, u32[]{:S(2)}) copy-start(f32[64,128]{1,0:T(8,128)} %top_basis_ref.1) | copy-start | bytes 98308
  1.4 14.1 %copy-start.1 = (f32[1,64,128]{2,1,0:T(8,128)S(1)}, f32[1,64,128]{2,1,0:T(8,128)}, u32[]{:S(2)}) copy-start(f32[1,64,128]{2,1,0:T(8,128)} %group_basis_ref.1) | copy-start | bytes 98308
  1.4 18.8 %copy-start.4 = (bf16[1,2048,128]{2,1,0:T(8,128)(2,1)S(1)}, bf16[1,2048,128]{2,1,0:T(8,128)(2,1)}, u32[]{:S(2)}) copy-start(bf16[1,2048,128]{2,1,0:T(8,128)(2,1)} %refs_0_.1) | copy-start | bytes 1572868
  1.4 14.1 %collective-permute-start = (f32[64,256]{1,0:T(8,128)S(1)}, f32[64,256]{1,0:T(8,128)S(1)}, u32[]{:S(2)}, u32[]{:S(2)}) collective-permute-start(f32[64,256]{1,0:T(8,128)S(1)} %pad_maximum_fusion.1.refs_0_), channel_id=1, source_target_pairs={{0,4},{4,0},{8,12},{12,8},{16,20},{20,16},{24,28},{28,24},{1,5},{5... | collective-permute-start | bytes 196616 | tf_op jit(solution)/shard_map/ppermute | solution.py:456
  4.4 0.7 copy-start.5
  5.1 0.7 copy-start.6
  5.8 14.4 %copy-start.7 = (s32[1,2,4]{2,1,0:T(2,128)S(1)}, s32[1,2,4]{2,1,0:T(2,128)}, u32[]{:S(2)}) copy-start(s32[1,2,4]{2,1,0:T(2,128)} %map_ref.3) | copy-start | bytes 100
  15.3 15.2 %collective-permute-start.1 = (f32[256,512]{1,0:T(8,128)S(1)}, f32[256,512]{1,0:T(8,128)S(1)}, u32[]{:S(2)}, u32[]{:S(2)}) collective-permute-start(f32[256,512]{1,0:T(8,128)S(1)} %get-tuple-element.35.send_ref), channel_id=1, source_target_pairs={{0,4},{4,0},{8,12},{12,8},{16,20},{20,16},{24,28},{28,24},{1,5},{5... | collective-permute-start | bytes 1572872 | tf_op jit(solution)/shard_map/ppermute | solution.py:456
  15.5 15.0 %collective-permute-start.2 = (f32[128,256]{1,0:T(8,128)S(1)}, f32[128,256]{1,0:T(8,128)S(1)}, u32[]{:S(2)}, u32[]{:S(2)}) collective-permute-start(f32[128,256]{1,0:T(8,128)S(1)} %pad_maximum_fusion.refs_2_.refs_1_), channel_id=1, source_target_pairs={{0,8},{4,12},{8,0},{12,4},{16,24},{20,28},{24,16},{28,20},{1,9},{5... | collective-permute-start | bytes 393224 | tf_op jit(solution)/shard_map/ppermute | solution.py:456
  17.6 12.9 %collective-permute-start.3 = (f32[128,256]{1,0:T(8,128)S(1)}, f32[128,256]{1,0:T(8,128)S(1)}, u32[]{:S(2)}, u32[]{:S(2)}) collective-permute-start(f32[128,256]{1,0:T(8,128)S(1)} %pad_maximum_fusion.refs_2_.refs_1_), channel_id=1, source_target_pairs={{0,16},{4,20},{8,24},{12,28},{16,0},{20,4},{24,8},{28,12},{1,17},{... | collective-permute-start | bytes 393224 | tf_op jit(solution)/shard_map/ppermute | solution.py:456
  20.2 10.3 %collective-permute-start.4 = (f32[128,256]{1,0:T(8,128)S(1)}, f32[128,256]{1,0:T(8,128)S(1)}, u32[]{:S(2)}, u32[]{:S(2)}) collective-permute-start(f32[128,256]{1,0:T(8,128)S(1)} %pad_maximum_fusion.refs_2_.refs_1_), channel_id=1, source_target_pairs={{0,24},{4,28},{8,16},{12,20},{16,8},{20,12},{24,0},{28,4},{1,25},{... | collective-permute-start | bytes 393224 | tf_op jit(solution)/shard_map/ppermute | solution.py:456
  20.2 10.3 %copy-start.2 = (f32[1,64,512]{2,1,0:T(8,128)S(1)}, f32[1,64,512]{2,1,0:T(8,128)}, u32[]{:S(2)}) copy-start(f32[1,64,512]{2,1,0:T(8,128)} %group_own_ref.1) | copy-start | bytes 393220
  20.2 10.3 %copy-start.3 = (f32[16,512]{1,0:T(8,128)S(1)}, f32[16,512]{1,0:T(8,128)}, u32[]{:S(2)}) copy-start(f32[16,512]{1,0:T(8,128)} %top_own_ref.1) | copy-start | bytes 98308
  32.0 4.7 %collective-permute-start.7 = (f32[256,512]{1,0:T(8,128)S(1)}, f32[256,512]{1,0:T(8,128)S(1)}, u32[]{:S(2)}, u32[]{:S(2)}) collective-permute-start(f32[256,512]{1,0:T(8,128)S(1)} %get-tuple-element.42), channel_id=1, source_target_pairs={{0,1},{1,0},{2,3},{3,2},{4,5},{5,4},{6,7},{7,6},{8,9},{9,8},{10,11... | collective-permute-start | bytes 1572872 | tf_op jit(solution)/shard_map/ppermute | solution.py:456
  32.1 4.6 %collective-permute-start.5 = (f32[136,128]{1,0:T(8,128)S(1)}, f32[136,128]{1,0:T(8,128)S(1)}, u32[]{:S(2)}, u32[]{:S(2)}) collective-permute-start(f32[136,128]{1,0:T(8,128)S(1)} %get-tuple-element.40.left_ref), channel_id=1, source_target_pairs={{0,8},{4,12},{8,0},{12,4},{16,24},{20,28},{24,16},{28,20},{1,9},{5... | collective-permute-start | bytes 208904 | tf_op jit(solution)/shard_map/ppermute | solution.py:456
  36.8 11.2 %collective-permute-start.9 = (f32[128,512]{1,0:T(8,128)S(1)}, f32[128,512]{1,0:T(8,128)S(1)}, u32[]{:S(2)}, u32[]{:S(2)}) collective-permute-start(f32[128,512]{1,0:T(8,128)S(1)} %get-tuple-element.43.refs_0_), channel_id=1, source_target_pairs={{0,2},{1,3},{2,0},{3,1},{4,6},{5,7},{6,4},{7,5},{8,10},{9,11},{10,... | collective-permute-start | bytes 786440 | tf_op jit(solution)/shard_map/ppermute | solution.py:456
  38.6 6.0 %collective-permute-start.6 = (f32[136,128]{1,0:T(8,128)S(1)}, f32[136,128]{1,0:T(8,128)S(1)}, u32[]{:S(2)}, u32[]{:S(2)}) collective-permute-start(f32[136,128]{1,0:T(8,128)S(1)} %add.5.refs_0_.left_ref), channel_id=1, source_target_pairs={{0,16},{4,20},{8,24},{12,28},{16,0},{20,4},{24,8},{28,12},{1,17},{... | collective-permute-start | bytes 208904 | tf_op jit(solution)/shard_map/ppermute | solution.py:456
  44.8 14.4 %collective-permute-start.14 = (f32[128,512]{1,0:T(8,128)S(1)}, f32[128,512]{1,0:T(8,128)S(1)}, u32[]{:S(2)}, u32[]{:S(2)}) collective-permute-start(f32[128,512]{1,0:T(8,128)S(1)} %get-tuple-element.47.refs_1_), channel_id=1, source_target_pairs={{0,16},{4,20},{8,24},{12,28},{16,0},{20,4},{24,8},{28,12},{1,17},{... | collective-permute-start | bytes 786440 | tf_op jit(solution)/shard_map/ppermute | solution.py:456
  46.5 4.3 %collective-permute-start.8 = (f32[136,128]{1,0:T(8,128)S(1)}, f32[136,128]{1,0:T(8,128)S(1)}, u32[]{:S(2)}, u32[]{:S(2)}) collective-permute-start(f32[136,128]{1,0:T(8,128)S(1)} %add.6.refs_0_.left_ref), channel_id=1, source_target_pairs={{0,4},{4,0},{8,12},{12,8},{16,20},{20,16},{24,28},{28,24},{1,5},{5... | collective-permute-start | bytes 208904 | tf_op jit(solution)/shard_map/ppermute | solution.py:456
  48.0 5.0 %collective-permute-start.11 = (f32[64,512]{1,0:T(8,128)S(1)}, f32[64,512]{1,0:T(8,128)S(1)}, u32[]{:S(2)}, u32[]{:S(2)}) collective-permute-start(f32[64,512]{1,0:T(8,128)S(1)} %get-tuple-element.45.refs_0_), channel_id=1, source_target_pairs={{0,4},{4,0},{8,12},{12,8},{16,20},{20,16},{24,28},{28,24},{1,5},{5... | collective-permute-start | bytes 393224 | tf_op jit(solution)/shard_map/ppermute | solution.py:456
  50.8 2.2 %collective-permute-start.10 = (f32[136,128]{1,0:T(8,128)S(1)}, f32[136,128]{1,0:T(8,128)S(1)}, u32[]{:S(2)}, u32[]{:S(2)}) collective-permute-start(f32[136,128]{1,0:T(8,128)S(1)} %add.7.refs_0_.left_ref.near_ref), channel_id=1, source_target_pairs={{0,1},{1,0},{2,3},{3,2},{4,5},{5,4},{6,7},{7,6},{8,9},{9,8},{10,11... | collective-permute-start | bytes 208904 | tf_op jit(solution)/shard_map/ppermute | solution.py:456
  53.1 6.0 %collective-permute-start.12 = (f32[136,128]{1,0:T(8,128)S(1)}, f32[136,128]{1,0:T(8,128)S(1)}, u32[]{:S(2)}, u32[]{:S(2)}) collective-permute-start(f32[136,128]{1,0:T(8,128)S(1)} %add.8.refs_0_.left_ref), channel_id=1, source_target_pairs={{0,2},{1,3},{2,0},{3,1},{4,6},{5,7},{6,4},{7,5},{8,10},{9,11},{10,... | collective-permute-start | bytes 208904 | tf_op jit(solution)/shard_map/ppermute | solution.py:456
  53.6 5.5 %collective-permute-start.13 = (f32[32,512]{1,0:T(8,128)S(1)}, f32[32,512]{1,0:T(8,128)S(1)}, u32[]{:S(2)}, u32[]{:S(2)}) collective-permute-start(f32[32,512]{1,0:T(8,128)S(1)} %get-tuple-element.49.refs_0_), channel_id=1, source_target_pairs={{0,16},{4,20},{8,24},{12,28},{16,0},{20,4},{24,8},{28,12},{1,17},{... | collective-permute-start | bytes 196616 | tf_op jit(solution)/shard_map/ppermute | solution.py:456
  59.2 10.5 %collective-permute-start.15 = (f32[64,512]{1,0:T(8,128)S(1)}, f32[64,512]{1,0:T(8,128)S(1)}, u32[]{:S(2)}, u32[]{:S(2)}) collective-permute-start(f32[64,512]{1,0:T(8,128)S(1)} %get-tuple-element.58), channel_id=1, source_target_pairs={{0,8},{4,12},{8,0},{12,4},{16,24},{20,28},{24,16},{28,20},{1,9},{5... | collective-permute-start | bytes 393224 | tf_op jit(solution)/shard_map/ppermute | solution.py:456
  61.1 8.6 %collective-permute-start.16 = (f32[16,512]{1,0:T(8,128)S(1)}, f32[16,512]{1,0:T(8,128)S(1)}, u32[]{:S(2)}, u32[]{:S(2)}) collective-permute-start(f32[16,512]{1,0:T(8,128)S(1)} %get-tuple-element.51.refs_0_), channel_id=1, source_target_pairs={{0,8},{4,12},{8,0},{12,4},{16,24},{20,28},{24,16},{28,20},{1,9},{5... | collective-permute-start | bytes 98312 | tf_op jit(solution)/shard_map/ppermute | solution.py:456

commit v7 on v6

--- a/solution.py
+++ b/solution.py
@@ -14,8 +14,7 @@
 VMEM = pl.BlockSpec(memory_space=pltpu.VMEM)
 SMEM = pl.BlockSpec(memory_space=pltpu.SMEM)
 HBM = pl.BlockSpec(memory_space=pltpu.HBM)
-MASS_PARTS = 2
-LEAF_MEGABYTES = 48
+MASS_PARTS = 4
 
 
 def params(megabytes):
@@ -78,60 +77,8 @@
     return place
 
 
-def leaf_kernel(half, mask_ref, map_ref, mass_hbm, modes_hbm, *refs):
-    if half == 0:
-        after_ref, keep_ref, send_ref, loaded_ref = refs[:4]
-    else:
-        fixed_hbm, first_ref, after_ref, keep_ref, send_ref, moved_ref = refs[:6]
-        fixed_ref, loaded_ref = refs[-2:]
-        refs = refs[:-2]
-    mass_ref, modes_ref, whole_ref, partial_ref, sems = refs[-5:]
-    row, col = lax.axis_index("row"), lax.axis_index("col")
-    row_count, col_count = lax.axis_size("row"), lax.axis_size("col")
-    rows, size = modes_ref.shape
-    tiles = rows // TILE
-    height = rows // MASS_PARTS
-
-    def mass_copy(i):
-        window = pl.ds(pl.multiple_of(i * height, height), height)
-        return pltpu.make_async_copy(
-            mass_hbm.at[0, window], mass_ref.at[window], sems.at[2 + i]
-        )
-
-    half_modes = modes_hbm.at[0, :, pl.ds(half * size, size)]
-    modes_copy = pltpu.make_async_copy(half_modes, modes_ref, sems.at[0])
-    modes_copy.start()
-    for i in range(MASS_PARTS):
-        mass_copy(i).start()
-    if half == 1:
-        fixed_copy = pltpu.make_async_copy(fixed_hbm.at[0], fixed_ref, sems.at[1])
-        fixed_copy.start()
-    modes_copy.wait()
-
-    def part(i, first):
-        mass_copy(i).wait()
-        lines = []
-        for a in range(height // TILE):
-            pieces = []
-            for b in range(tiles):
-                kept = mask_ref[0, i * (height // TILE) + a, b]
-                window = pl.ds(pl.multiple_of(i * height + a * TILE, TILE), TILE)
-                piece = mass_ref[window, b * TILE : (b + 1) * TILE]
-                pieces.append(jnp.where(kept != 0, piece, jnp.zeros_like(piece)))
-            lines.append(jnp.concatenate(pieces, axis=1))
-        masked = jnp.concatenate(lines, axis=0)
-        loaded = jnp.dot(masked, modes_ref[...], preferred_element_type=F32).astype(BF16)
-        window = pl.ds(pl.multiple_of(i * height, height), height)
-        loaded_ref[window, :] = loaded
-        partial = rows_first(modes_ref[window, :], loaded)
-        if first:
-            partial_ref[...] = partial
-        else:
-            partial_ref[...] += partial
-
-    part(0, True)
-    lax.fori_loop(1, MASS_PARTS, lambda i, _: part(i, False), None)
-
+def cut_matrix(half, map_ref, partial_ref, whole_ref, keep_ref, send_ref):
+    size = partial_ref.shape[0]
     blocks = size // TILE
     to = [pl.multiple_of(map_ref[0, half, a] * TILE, TILE) for a in range(blocks)]
     for b in range(blocks):
@@ -139,54 +86,124 @@
             whole_ref[pl.ds(to[a], TILE), pl.ds(to[b], TILE)] = partial_ref[
                 a * TILE : (a + 1) * TILE, b * TILE : (b + 1) * TILE
             ]
-    order = cut_order(half, row_count, col_count)
+    order = cut_order(half, lax.axis_size("row"), lax.axis_size("col"))
     share = size // len(order)
-    bit = lax.rem(row if half == 0 else col, 2)
+    bit = lax.rem(lax.axis_index(("row", "col")[half]), 2)
     for k, chunk in enumerate((keep_ref, send_ref)):
         for i in range(len(order) // 2):
             step = order[i + len(order) // 2] - order[i]
             copy_rows(chunk, i * share, whole_ref, order[i] + step * lax.rem(bit + k, 2), share)
-    if half == 1:
-        fixed_copy.wait()
-        for k, ref in enumerate((first_ref, loaded_ref)):
-            projected = rows_first(fixed_ref[...], ref[...])
-            for b in range(blocks):
-                at = pl.multiple_of(map_ref[0, k, b] * TILE, TILE)
-                moved_ref[k, :, pl.ds(at, TILE)] = projected[:, b * TILE : (b + 1) * TILE]
-
-
-def leaf_half(half, tile_mask, block_map, leaf_mass, constraint_modes, more, after):
+
+
+def group_kernel(
+    mask_ref, map_ref, mass_hbm, modes_ref, after_ref, keep_ref, send_ref, loaded_ref, mass_ref,
+    whole_ref, partial_ref, sems,
+):
+    rows, size = loaded_ref.shape
+    tiles = rows // TILE
+    height = rows // MASS_PARTS
+    mass_copies = [
+        pltpu.make_async_copy(
+            mass_hbm.at[0, pl.ds(i * height, height)],
+            mass_ref.at[pl.ds(i * height, height)],
+            sems.at[i],
+        )
+        for i in range(MASS_PARTS)
+    ]
+    for copy in mass_copies:
+        copy.start()
+    for start, stop in ((0, 1), (1, MASS_PARTS)):
+        for i in range(start, stop):
+            mass_copies[i].wait()
+        lines = []
+        for a in range(start * height // TILE, stop * height // TILE):
+            pieces = []
+            for b in range(tiles):
+                piece = mass_ref[a * TILE : (a + 1) * TILE, b * TILE : (b + 1) * TILE]
+                pieces.append(jnp.where(mask_ref[0, a, b] != 0, piece, jnp.zeros_like(piece)))
+            lines.append(jnp.concatenate(pieces, axis=1))
+        masked = jnp.concatenate(lines, axis=0)
+        window = slice(start * height, stop * height)
+        mass_ref[window, :] = masked
+        loaded = jnp.dot(masked, modes_ref[0, :, :size], preferred_element_type=F32).astype(BF16)
+        loaded_ref[window, :] = loaded
+        partial = rows_first(modes_ref[0, window, :size], loaded)
+        if start == 0:
+            partial_ref[...] = partial
+        else:
+            partial_ref[...] += partial
+    cut_matrix(0, map_ref, partial_ref, whole_ref, keep_ref, send_ref)
+
+
+def leaf_group(tile_mask, block_map, leaf_mass, constraint_modes, after):
     rows, size = constraint_modes.shape[1], constraint_modes.shape[2] // 2
-    outs = [jax.ShapeDtypeStruct((size // 2, size), F32)] * 2
-    scratch = [
-        pltpu.VMEM((rows, rows), BF16),
-        pltpu.VMEM((rows, size), BF16),
-        pltpu.VMEM((size, size), F32),
-        pltpu.VMEM((size, size), F32),
-        pltpu.SemaphoreType.DMA((2 + MASS_PARTS,)),
-    ]
-    if half == 0:
-        outs.append(jax.ShapeDtypeStruct((rows, size), BF16))
-        specs = []
-    else:
-        modes = more[0].shape[2]
-        outs.append(jax.ShapeDtypeStruct((2, modes, size), F32))
-        scratch += [pltpu.VMEM((rows, modes), BF16), pltpu.VMEM((rows, size), BF16)]
-        specs = [HBM, VMEM]
-    return pl.pallas_call(
-        functools.partial(leaf_kernel, half),
-        in_specs=[SMEM] * 2 + [HBM] * 2 + specs + [pl.BlockSpec(memory_space=pl.ANY)],
-        out_specs=[VMEM] * len(outs),
-        out_shape=outs,
-        scratch_shapes=scratch,
-        compiler_params=params(LEAF_MEGABYTES),
+    part = jax.ShapeDtypeStruct((size // 2, size), F32)
+    half = jax.ShapeDtypeStruct((rows, size), BF16)
+    return pl.pallas_call(
+        group_kernel,
+        in_specs=[SMEM] * 2 + [HBM, VMEM, pl.BlockSpec(memory_space=pl.ANY)],
+        out_specs=[VMEM] * 4,
+        out_shape=[part, part, half, jax.ShapeDtypeStruct((rows, rows), BF16)],
+        scratch_shapes=[
+            pltpu.VMEM((size, size), F32),
+            pltpu.VMEM((size, size), F32),
+            pltpu.SemaphoreType.DMA((MASS_PARTS,)),
+        ],
+        compiler_params=params(32),
         cost_estimate=pl.CostEstimate(
             flops=2 * rows * size * (rows + size),
             bytes_accessed=2 * rows * (rows + size) + 8 * size * size,
             transcendentals=0,
         ),
-        name="leaf_group" if half == 0 else "leaf_top",
-    )(tile_mask, block_map, leaf_mass, constraint_modes, *more, after)
+        name="leaf_group",
+    )(tile_mask, block_map, leaf_mass, constraint_modes, after)
+
+
+def top_kernel(
+    map_ref, mass_ref, modes_ref, fixed_ref, first_ref, after_ref, keep_ref, send_ref, moved_ref,
+    whole_ref, partial_ref, loaded_ref,
+):
+    rows, size = loaded_ref.shape
+    height = rows // 2
+    for i in range(2):
+        window = slice(i * height, (i + 1) * height)
+        loaded = jnp.dot(mass_ref[window, :], modes_ref[0, :, size:], preferred_element_type=F32)
+        loaded = loaded.astype(BF16)
+        loaded_ref[window, :] = loaded
+        partial = rows_first(modes_ref[0, window, size:], loaded)
+        if i == 0:
+            partial_ref[...] = partial
+        else:
+            partial_ref[...] += partial
+    for k, ref in enumerate((first_ref, loaded_ref)):
+        projected = rows_first(fixed_ref[0], ref[...])
+        for b in range(size // TILE):
+            at = pl.multiple_of(map_ref[0, k, b] * TILE, TILE)
+            moved_ref[k, :, pl.ds(at, TILE)] = projected[:, b * TILE : (b + 1) * TILE]
+    cut_matrix(1, map_ref, partial_ref, whole_ref, keep_ref, send_ref)
+
+
+def leaf_top(block_map, mass, modes, fixed, first, after):
+    rows, size = modes.shape[1], modes.shape[2] // 2
+    part = jax.ShapeDtypeStruct((size // 2, size), F32)
+    return pl.pallas_call(
+        top_kernel,
+        in_specs=[SMEM] + [VMEM] * 4 + [pl.BlockSpec(memory_space=pl.ANY)],
+        out_specs=[VMEM] * 3,
+        out_shape=[part, part, jax.ShapeDtypeStruct((2, fixed.shape[2], size), F32)],
+        scratch_shapes=[
+            pltpu.VMEM((size, size), F32),
+            pltpu.VMEM((size, size), F32),
+            pltpu.VMEM((rows, size), BF16),
+        ],
+        compiler_params=params(32),
+        cost_estimate=pl.CostEstimate(
+            flops=2 * rows * size * (rows + size),
+            bytes_accessed=2 * rows * (rows + size) + 8 * size * size,
+            transcendentals=0,
+        ),
+        name="leaf_top",
+    )(block_map, mass, modes, fixed, first, after)
 
 
 def split(value):
@@ -361,23 +378,21 @@
             ]
             strip = state[start:stop, :]
             small = [s[start:stop, :] for s in spread]
-            units, levels, scales = [], [], []
+            scaled = []
             rest = strip
             for q in range(width):
                 scale = lax.rsqrt(small[q][q : q + 1, :])
-                inverse = scale * scale
-                level = rest[q : q + 1, :]
-                rest = rest - (small[q] * level) * inverse
-                unit = jnp.where(line == q, 1.0, small[q])
+                tail = [small[t][q : q + 1, :] * scale for t in range(q + 1, width)]
+                level = rest[q : q + 1, :] * scale
+                rest = rest - small[q] * (scale * level)
+                small[q] = jnp.where(line == q, 1.0, small[q]) * scale
                 for t in range(q + 1, width):
-                    product = unit * small[t][q : q + 1, :]
-                    small[t] = jnp.where(line == q, 0.0, small[t]) - product * inverse
-                units.append(jnp.where(line <= q, unit, 0.0))
-                levels.append(level * inverse)
-                scales.append(scale)
-            solved = units[0] * levels[0]
+                    small[t] = jnp.where(line == q, 0.0, small[t]) - small[q] * tail[t - q - 1]
+                scaled.append(level)
+            small = [jnp.where(line <= q, s, 0.0) for q, s in enumerate(small)]
+            solved = small[0] * scaled[0]
             for q in range(1, width):
-                solved = solved + units[q] * levels[q]
+                solved = solved + small[q] * scaled[q]
             solved = jnp.where(lane >= stop, solved, 0.0)
             update = spread[0] * solved[0:1, :]
             for q in range(1, width):
@@ -393,7 +408,7 @@
             states[m] = jnp.concatenate(parts, axis=0)
             diagonal = jnp.zeros((width, size), F32)
             for q in range(width):
-                diagonal = jnp.where(lane == start + q, units[q] * scales[q], diagonal)
+                diagonal = jnp.where(lane == start + q, small[q], diagonal)
             diagonals[m].append(diagonal)
     uppers = [jnp.where(across >= down, state, 0.0) for state in states]
     return uppers, [jnp.concatenate(d, axis=0) for d in diagonals]
@@ -455,17 +470,18 @@
     def swap(value, axis, bit):
         return lax.ppermute(value, axis, crossed(sizes[axis], bit))
 
-    def half_of(half, more, after):
-        return leaf_half(half, tile_mask, block_map, leaf_mass, constraint_modes, more, after)
-
     group_steps = exchanges(0, row_count, col_count)
     basis = jnp.concatenate([group_basis[0], top_basis], axis=1)
     beside = swap(basis, "row", 1)
-    keep, send, loaded = half_of(0, [], basis)
+    keep, send, loaded, mass = leaf_group(
+        tile_mask, block_map, leaf_mass, constraint_modes, basis
+    )
     pair = jnp.concatenate([basis, beside], axis=0)
     pieces = [pair] + [swap(pair, "row", 2 * k) for k in range(1, row_count // 2)]
     other = swap(send, *group_steps[0])
-    top_keep, top_send, moved = half_of(1, [leaf_fixed_modes, loaded], pair)
+    top_keep, top_send, moved = leaf_top(
+        block_map, mass, constraint_modes, leaf_fixed_modes, loaded, pair
+    )
     packed, terms, keep, top_keep, top_send = prepare(
         keep, send, top_keep, top_send, moved, group_mass, top_mass, other, pieces
     )

time: 70.7 us -> 71.6 us (1.013)
  Pallas kernels: 30.7 us -> 25.6 us
  waiting for transfers between devices: 15.3 us -> 18.2 us
  local copies, waits for them, and re-layouts: 1.4 us -> 3.59 us
  starting transfers between devices: 21.4 us -> 22.3 us
    pallas_call x2, Pallas kernels: 19.8 us -> 16 us  [the longest x1 9.1 us: leaf_group(): pl.pallas_call(group_kernel, in_specs=[SMEM] * 2 + [HBM, VMEM, pl.BlockSp...]
    ppermute x17, waiting for transfers between devices: 15.3 us -> 18.2 us  [swap(): return lax.ppermute(value, axis, crossed(sizes[axis], bit))]
    unnamed x16 -> x18, local copies, waits for them, and re-layouts: 1.4 us -> 3.59 us
    pallas_call x1, Pallas kernels: 8.45 us -> 7.16 us  [finish(): pl.pallas_call(finish_kernel, in_specs=[VMEM] * 5, out_specs=[VMEM] * 4,...]
    ppermute x17, starting transfers between devices: 21.4 us -> 22.3 us  [swap(): return lax.ppermute(value, axis, crossed(sizes[axis], bit))]
  transfers between devices with their start and end apart: 17 -> 17, of which waited for: 5 -> 6; matrix products, arithmetic and copies ran while one was open for 0% -> 0% of each run, Pallas kernels for 40% -> 33%
where the time goes in v7:
time: 71.6 us; the launch traced here: 71.3 us
  Pallas kernels  25.6 us (36%)
  starting transfers between devices  22.3 us (31%)
  waiting for transfers between devices  18.2 us (25%)
  local copies, waits for them, and re-layouts  3.59 us (5%)
  between operations  0.84 us (1%)
  other arithmetic  0.79 us (1%)
    ppermute x17, starting transfers between devices, swap(): return lax.ppermute(value, axis, crossed(sizes[axis], bit))  22.3 us
    ppermute x17, waiting for transfers between devices, swap(): return lax.ppermute(value, axis, crossed(sizes[axis], bit))  18.2 us
    pallas_call x1, Pallas kernels, leaf_group(): pl.pallas_call(group_kernel, in_specs=[SMEM] * 2 + [HBM, VMEM, pl.BlockSp...  9.1 us
    pallas_call x1, Pallas kernels, finish(): pl.pallas_call(finish_kernel, in_specs=[VMEM] * 5, out_specs=[VMEM] * 4,...  7.16 us
    pallas_call x1, Pallas kernels, leaf_top(): pl.pallas_call(top_kernel, in_specs=[SMEM] + [VMEM] * 4 + [pl.BlockSpec(m...  6.93 us
    unnamed x18, local copies, waits for them, and re-layouts  3.59 us
  transfers between devices with their start and end apart: 17, of which 6 were waited for; matrix products, arithmetic and copies ran while one was open for 0% of the time, Pallas kernels for 33%

profile of v7, /device:TPU:0, one launch (start us, length us, event | category | flops | bytes accessed | tf_op | source)
XLA Modules:
  0.0 71.3 jit_solution(16105959402250737713)
XLA Ops:
  0.6 0.8 %pad_maximum_fusion.1.after_ref = f32[64,256]{1,0:T(8,128)S(1)} fusion(f32[64,128]{1,0:T(8,128)} %top_basis_ref.1, f32[64,128]{1,0:T(8,128)} %bitcast.1), kind=kLoop, calls=%fused_computation.1 | loop fusion | flops 16384 | bytes 131072 | tf_op jit(solution)/shard_map/concatenate | solution.py:474
  1.4 0.0 copy-start
  1.4 0.0 copy-start.1
  1.4 3.0 %collective-permute-start = (f32[64,256]{1,0:T(8,128)S(1)}, f32[64,256]{1,0:T(8,128)S(1)}, u32[]{:S(2)}, u32[]{:S(2)}) collective-permute-start(f32[64,256]{1,0:T(8,128)S(1)} %pad_maximum_fusion.1.after_ref), channel_id=1, source_target_pairs={{0,4},{4,0},{8,12},{12,8},{16,20},{20,16},{24,28},{28,24},{1,5},{5... | collective-permute-start | bytes 196616 | tf_op jit(solution)/shard_map/ppermute | solution.py:471
  4.4 0.0 copy-start.4
  4.4 2.2 %copy-done.4 = bf16[1,2048,1024]{2,1,0:T(8,128)(2,1)S(1)} copy-done((bf16[1,2048,1024]{2,1,0:T(8,128)(2,1)S(1)}, bf16[1,2048,1024]{2,1,0:T(8,128)(2,1)}, u32[]{:S(2)}) %copy-start.4) | copy-done | bytes 4194328
  6.6 0.0 copy-start.7
  6.6 0.7 copy-done.7
  7.3 0.0 copy-start.8
  7.3 0.7 copy-done.8
  8.0 0.0 copy-start.5
  8.0 0.0 copy-start.6
  8.0 9.1 %leaf_group.1 = (f32[256,512]{1,0:T(8,128)S(1)}, f32[256,512]{1,0:T(8,128)S(1)}, bf16[2048,512]{1,0:T(8,128)(2,1)S(1)}, bf16[2048,2048]{1,0:T(8,128)(2,1)S(1)}) custom-call(s32[1,16,16]{2,1,0:T(8,128)S(1)} %copy-done.7, s32[1,2,4]{2,1,0:T(2,128)S(1)} %copy-done.8, bf16[1,2048,2048]{2,1,0:T(8,128)(2,1)} %mass_hbm.1, bf16[1,2048,1024]{2,1,0:T(8,128)(2,1)S(1)} %copy-done.4, ...), custom_call_target="tpu_custom_call" | custom-call | flops 5368709120 | bytes 12582912 | tf_op jit(solution)/shard_map/leaf_group/pallas_call | solution.py:142
  17.1 0.1 collective-permute-start.1
  17.2 0.0 collective-permute-done
  17.2 0.0 copy-done
  17.2 0.0 copy-done.1
  17.2 2.1 %collective-permute-start.2 = (f32[128,256]{1,0:T(8,128)S(1)}, f32[128,256]{1,0:T(8,128)S(1)}, u32[]{:S(2)}, u32[]{:S(2)}) collective-permute-start(f32[128,256]{1,0:T(8,128)S(1)} %pad_maximum_fusion.after_ref.refs_1_), channel_id=1, source_target_pairs={{0,8},{4,12},{8,0},{12,4},{16,24},{20,28},{24,16},{28,20},{1,9},{5... | collective-permute-start | bytes 393224 | tf_op jit(solution)/shard_map/ppermute | solution.py:471
  19.4 2.6 %collective-permute-start.3 = (f32[128,256]{1,0:T(8,128)S(1)}, f32[128,256]{1,0:T(8,128)S(1)}, u32[]{:S(2)}, u32[]{:S(2)}) collective-permute-start(f32[128,256]{1,0:T(8,128)S(1)} %pad_maximum_fusion.after_ref.refs_1_), channel_id=1, source_target_pairs={{0,16},{4,20},{8,24},{12,28},{16,0},{20,4},{24,8},{28,12},{1,17},{... | collective-permute-start | bytes 393224 | tf_op jit(solution)/shard_map/ppermute | solution.py:471
  22.0 0.0 collective-permute-start.4
  22.0 0.0 copy-done.5
  22.0 0.0 copy-done.6
  22.0 0.0 copy-start.2
  22.0 0.0 copy-start.3
  22.0 6.9 %leaf_top.1 = (f32[256,512]{1,0:T(8,128)S(1)}, f32[256,512]{1,0:T(8,128)S(1)}, f32[2,128,512]{2,1,0:T(8,128)S(1)}) custom-call(s32[1,2,4]{2,1,0:T(2,128)S(1)} %copy-done.8, bf16[2048,2048]{1,0:T(8,128)(2,1)S(1)} %get-tuple-element.37.mass_ref, bf16[1,2048,1024]{2,1,0:T(8,128)(2,1)S(1)} %copy-done.5, bf16[1,2048,128]{2,1,0:T(8,128)(2,1)S(1)} %copy-done.6, ...), custom_call_target="tpu_custom_call" | custom-call | flops 5368709120 | bytes 12582912 | tf_op jit(solution)/shard_map/leaf_top/pallas_call | solution.py:189
  28.9 0.0 collective-permute-done.2.refs_2_
  29.0 2.8 %collective-permute-done.3.refs_3_ = f32[128,256]{1,0:T(8,128)S(1)} collective-permute-done((f32[128,256]{1,0:T(8,128)S(1)}, f32[128,256]{1,0:T(8,128)S(1)}, u32[]{:S(2)}, u32[]{:S(2)}) %collective-permute-start.3) | collective-permute-done | bytes 131104 | tf_op jit(solution)/shard_map/ppermute | solution.py:471
  31.7 0.0 collective-permute-done.4.refs_4_
  31.8 0.0 collective-permute-done.1.refs_0_.other_ref
  31.8 0.0 copy-done.2
  31.8 0.0 copy-done.3
  31.8 1.4 %prepare.1 = (f32[136,128]{1,0:T(8,128)S(1)}, f32[2,128,128]{2,1,0:T(8,128)S(1)}, f32[256,512]{1,0:T(8,128)S(1)}, f32[256,512]{1,0:T(8,128)S(1)}, f32[256,512]{1,0:T(8,128)S(1)}) custom-call(f32[256,512]{1,0:T(8,128)S(1)} %get-tuple-element.35.keep_in, f32[256,512]{1,0:T(8,128)S(1)} %get-tuple-element.36.send_ref, ...), custom_call_target="tpu_custom_call" | custom-call | flops 402653184 | bytes 3145728 | tf_op jit(solution)/shard_map/prepare/pallas_call | solution.py:289
  33.2 0.1 collective-permute-start.7
  33.3 2.0 %collective-permute-start.5 = (f32[136,128]{1,0:T(8,128)S(1)}, f32[136,128]{1,0:T(8,128)S(1)}, u32[]{:S(2)}, u32[]{:S(2)}) collective-permute-start(f32[136,128]{1,0:T(8,128)S(1)} %get-tuple-element.42.left_ref), channel_id=1, source_target_pairs={{0,8},{4,12},{8,0},{12,4},{16,24},{20,28},{24,16},{28,20},{1,9},{5... | collective-permute-start | bytes 208904 | tf_op jit(solution)/shard_map/ppermute | solution.py:471
  35.3 2.8 %collective-permute-done.5.right_ref = f32[136,128]{1,0:T(8,128)S(1)} collective-permute-done((f32[136,128]{1,0:T(8,128)S(1)}, f32[136,128]{1,0:T(8,128)S(1)}, u32[]{:S(2)}, u32[]{:S(2)}) %collective-permute-start.5) | collective-permute-done | bytes 69664 | tf_op jit(solution)/shard_map/ppermute | solution.py:471
  38.1 0.0 collective-permute-done.7.other_ref
  38.1 0.1 fold.6
  38.2 1.6 %collective-permute-start.9 = (f32[128,512]{1,0:T(8,128)S(1)}, f32[128,512]{1,0:T(8,128)S(1)}, u32[]{:S(2)}, u32[]{:S(2)}) collective-permute-start(f32[128,512]{1,0:T(8,128)S(1)} %get-tuple-element.45.refs_0_), channel_id=1, source_target_pairs={{0,2},{1,3},{2,0},{3,1},{4,6},{5,7},{6,4},{7,5},{8,10},{9,11},{10,... | collective-permute-start | bytes 786440 | tf_op jit(solution)/shard_map/ppermute | solution.py:471
  39.8 2.8 %collective-permute-start.6 = (f32[136,128]{1,0:T(8,128)S(1)}, f32[136,128]{1,0:T(8,128)S(1)}, u32[]{:S(2)}, u32[]{:S(2)}) collective-permute-start(f32[136,128]{1,0:T(8,128)S(1)} %add.5.refs_0_.left_ref), channel_id=1, source_target_pairs={{0,16},{4,20},{8,24},{12,28},{16,0},{20,4},{24,8},{28,12},{1,17},{... | collective-permute-start | bytes 208904 | tf_op jit(solution)/shard_map/ppermute | solution.py:471
  42.5 2.8 %collective-permute-done.6.right_ref = f32[136,128]{1,0:T(8,128)S(1)} collective-permute-done((f32[136,128]{1,0:T(8,128)S(1)}, f32[136,128]{1,0:T(8,128)S(1)}, u32[]{:S(2)}, u32[]{:S(2)}) %collective-permute-start.6) | collective-permute-done | bytes 69664 | tf_op jit(solution)/shard_map/ppermute | solution.py:471
  45.3 0.1 fold.8
  45.4 2.7 %collective-permute-start.14 = (f32[128,512]{1,0:T(8,128)S(1)}, f32[128,512]{1,0:T(8,128)S(1)}, u32[]{:S(2)}, u32[]{:S(2)}) collective-permute-start(f32[128,512]{1,0:T(8,128)S(1)} %get-tuple-element.49.refs_1_), channel_id=1, source_target_pairs={{0,16},{4,20},{8,24},{12,28},{16,0},{20,4},{24,8},{28,12},{1,17},{... | collective-permute-start | bytes 786440 | tf_op jit(solution)/shard_map/ppermute | solution.py:471
  48.1 1.5 %collective-permute-start.8 = (f32[136,128]{1,0:T(8,128)S(1)}, f32[136,128]{1,0:T(8,128)S(1)}, u32[]{:S(2)}, u32[]{:S(2)}) collective-permute-start(f32[136,128]{1,0:T(8,128)S(1)} %add.6.refs_0_.left_ref), channel_id=1, source_target_pairs={{0,4},{4,0},{8,12},{12,8},{16,20},{20,16},{24,28},{28,24},{1,5},{5... | collective-permute-start | bytes 208904 | tf_op jit(solution)/shard_map/ppermute | solution.py:471
  49.6 0.0 collective-permute-done.9.other_ref
  49.6 0.6 collective-permute-start.11
  50.2 2.2 %collective-permute-done.8.right_ref = f32[136,128]{1,0:T(8,128)S(1)} collective-permute-done((f32[136,128]{1,0:T(8,128)S(1)}, f32[136,128]{1,0:T(8,128)S(1)}, u32[]{:S(2)}, u32[]{:S(2)}) %collective-permute-start.8) | collective-permute-done | bytes 69664 | tf_op jit(solution)/shard_map/ppermute | solution.py:471
  52.4 0.1 collective-permute-start.10
  52.5 2.2 %collective-permute-done.11.other_ref = f32[64,512]{1,0:T(8,128)S(1)} collective-permute-done((f32[64,512]{1,0:T(8,128)S(1)}, f32[64,512]{1,0:T(8,128)S(1)}, u32[]{:S(2)}, u32[]{:S(2)}) %collective-permute-start.11) | collective-permute-done | bytes 131104 | tf_op jit(solution)/shard_map/ppermute | solution.py:471
  54.7 0.0 collective-permute-done.10.right_ref
  54.7 0.6 collective-permute-start.12
  55.3 0.5 collective-permute-start.13
  55.8 5.4 %collective-permute-done.13.other_ref = f32[32,512]{1,0:T(8,128)S(1)} collective-permute-done((f32[32,512]{1,0:T(8,128)S(1)}, f32[32,512]{1,0:T(8,128)S(1)}, u32[]{:S(2)}, u32[]{:S(2)}) %collective-permute-start.13) | collective-permute-done | bytes 65568 | tf_op jit(solution)/shard_map/ppermute | solution.py:471
  61.3 0.0 collective-permute-done.12.right_ref
  61.3 0.0 collective-permute-done.14.other_ref
  61.4 0.1 collective-permute-start.15
  61.4 2.0 %collective-permute-start.16 = (f32[16,512]{1,0:T(8,128)S(1)}, f32[16,512]{1,0:T(8,128)S(1)}, u32[]{:S(2)}, u32[]{:S(2)}) collective-permute-start(f32[16,512]{1,0:T(8,128)S(1)} %get-tuple-element.53.refs_0_), channel_id=1, source_target_pairs={{0,8},{4,12},{8,0},{12,4},{16,24},{20,28},{24,16},{28,20},{1,9},{5... | collective-permute-start | bytes 98312 | tf_op jit(solution)/shard_map/ppermute | solution.py:471
  63.4 7.2 %finish.1 = (f32[1,128,2,128]{3,2,1,0:T(2,128)}, f32[1,64,128]{2,1,0:T(8,128)}, f32[64,128]{1,0:T(8,128)}, f32[8,128]{1,0:T(8,128)S(1)}) custom-call(f32[136,128]{1,0:T(8,128)S(1)} %add.7.refs_0_.left_ref.near_ref, f32[136,128]{1,0:T(8,128)S(1)} %add.9.far_ref.refs_0_, f32[2,128,128]{2,1,0:T(8,128)S(1)} %get-tuple-element.54.terms_ref, ...), custom_call_target="tpu_custom_call" | custom-call | flops 41943040 | bytes 393216 | tf_op jit(solution)/shard_map/finish/pallas_call | solution.py:445
  70.6 0.0 collective-permute-done.16.top_other_ref
  70.6 0.0 collective-permute-done.15.other_ref
  70.6 0.7 last.1
  (10 shorter events, 0.2 us)
Async XLA Ops:
  1.4 15.8 %copy-start = (f32[64,128]{1,0:T(8,128)S(1)}, f32[64,128]{1,0:T(8,128)}, u32[]{:S(2)}) copy-start(f32[64,128]{1,0:T(8,128)} %top_basis_ref.1) | copy-start | bytes 98308
  1.4 15.8 %copy-start.1 = (f32[1,64,128]{2,1,0:T(8,128)S(1)}, f32[1,64,128]{2,1,0:T(8,128)}, u32[]{:S(2)}) copy-start(f32[1,64,128]{2,1,0:T(8,128)} %group_basis_ref.1) | copy-start | bytes 98308
  1.4 15.8 %collective-permute-start = (f32[64,256]{1,0:T(8,128)S(1)}, f32[64,256]{1,0:T(8,128)S(1)}, u32[]{:S(2)}, u32[]{:S(2)}) collective-permute-start(f32[64,256]{1,0:T(8,128)S(1)} %pad_maximum_fusion.1.after_ref), channel_id=1, source_target_pairs={{0,4},{4,0},{8,12},{12,8},{16,20},{20,16},{24,28},{28,24},{1,5},{5... | collective-permute-start | bytes 196616 | tf_op jit(solution)/shard_map/ppermute | solution.py:471
  4.4 2.2 %copy-start.4 = (bf16[1,2048,1024]{2,1,0:T(8,128)(2,1)S(1)}, bf16[1,2048,1024]{2,1,0:T(8,128)(2,1)}, u32[]{:S(2)}) copy-start(bf16[1,2048,1024]{2,1,0:T(8,128)(2,1)} %modes_ref.3) | copy-start | bytes 12582916
  6.6 0.7 copy-start.7
  7.3 0.7 copy-start.8
  8.0 14.0 %copy-start.5 = (bf16[1,2048,1024]{2,1,0:T(8,128)(2,1)S(1)}, bf16[1,2048,1024]{2,1,0:T(8,128)(2,1)}, u32[]{:S(2)}) copy-start(bf16[1,2048,1024]{2,1,0:T(8,128)(2,1)} %modes_ref.3) | copy-start | bytes 12582916
  8.0 14.0 %copy-start.6 = (bf16[1,2048,128]{2,1,0:T(8,128)(2,1)S(1)}, bf16[1,2048,128]{2,1,0:T(8,128)(2,1)}, u32[]{:S(2)}) copy-start(bf16[1,2048,128]{2,1,0:T(8,128)(2,1)} %fixed_ref.1) | copy-start | bytes 1572868
  17.1 14.6 %collective-permute-start.1 = (f32[256,512]{1,0:T(8,128)S(1)}, f32[256,512]{1,0:T(8,128)S(1)}, u32[]{:S(2)}, u32[]{:S(2)}) collective-permute-start(f32[256,512]{1,0:T(8,128)S(1)} %get-tuple-element.36.send_ref), channel_id=1, source_target_pairs={{0,4},{4,0},{8,12},{12,8},{16,20},{20,16},{24,28},{28,24},{1,5},{5... | collective-permute-start | bytes 1572872 | tf_op jit(solution)/shard_map/ppermute | solution.py:471
  17.2 11.7 %collective-permute-start.2 = (f32[128,256]{1,0:T(8,128)S(1)}, f32[128,256]{1,0:T(8,128)S(1)}, u32[]{:S(2)}, u32[]{:S(2)}) collective-permute-start(f32[128,256]{1,0:T(8,128)S(1)} %pad_maximum_fusion.after_ref.refs_1_), channel_id=1, source_target_pairs={{0,8},{4,12},{8,0},{12,4},{16,24},{20,28},{24,16},{28,20},{1,9},{5... | collective-permute-start | bytes 393224 | tf_op jit(solution)/shard_map/ppermute | solution.py:471
  19.4 12.4 %collective-permute-start.3 = (f32[128,256]{1,0:T(8,128)S(1)}, f32[128,256]{1,0:T(8,128)S(1)}, u32[]{:S(2)}, u32[]{:S(2)}) collective-permute-start(f32[128,256]{1,0:T(8,128)S(1)} %pad_maximum_fusion.after_ref.refs_1_), channel_id=1, source_target_pairs={{0,16},{4,20},{8,24},{12,28},{16,0},{20,4},{24,8},{28,12},{1,17},{... | collective-permute-start | bytes 393224 | tf_op jit(solution)/shard_map/ppermute | solution.py:471
  22.0 9.8 %collective-permute-start.4 = (f32[128,256]{1,0:T(8,128)S(1)}, f32[128,256]{1,0:T(8,128)S(1)}, u32[]{:S(2)}, u32[]{:S(2)}) collective-permute-start(f32[128,256]{1,0:T(8,128)S(1)} %pad_maximum_fusion.after_ref.refs_1_), channel_id=1, source_target_pairs={{0,24},{4,28},{8,16},{12,20},{16,8},{20,12},{24,0},{28,4},{1,25},{... | collective-permute-start | bytes 393224 | tf_op jit(solution)/shard_map/ppermute | solution.py:471
  22.0 9.8 %copy-start.2 = (f32[1,64,512]{2,1,0:T(8,128)S(1)}, f32[1,64,512]{2,1,0:T(8,128)}, u32[]{:S(2)}) copy-start(f32[1,64,512]{2,1,0:T(8,128)} %group_own_ref.1) | copy-start | bytes 393220
  22.0 9.8 %copy-start.3 = (f32[16,512]{1,0:T(8,128)S(1)}, f32[16,512]{1,0:T(8,128)}, u32[]{:S(2)}) copy-start(f32[16,512]{1,0:T(8,128)} %top_own_ref.1) | copy-start | bytes 98308
  33.2 4.9 %collective-permute-start.7 = (f32[256,512]{1,0:T(8,128)S(1)}, f32[256,512]{1,0:T(8,128)S(1)}, u32[]{:S(2)}, u32[]{:S(2)}) collective-permute-start(f32[256,512]{1,0:T(8,128)S(1)} %get-tuple-element.44), channel_id=1, source_target_pairs={{0,1},{1,0},{2,3},{3,2},{4,5},{5,4},{6,7},{7,6},{8,9},{9,8},{10,11... | collective-permute-start | bytes 1572872 | tf_op jit(solution)/shard_map/ppermute | solution.py:471
  33.3 4.8 %collective-permute-start.5 = (f32[136,128]{1,0:T(8,128)S(1)}, f32[136,128]{1,0:T(8,128)S(1)}, u32[]{:S(2)}, u32[]{:S(2)}) collective-permute-start(f32[136,128]{1,0:T(8,128)S(1)} %get-tuple-element.42.left_ref), channel_id=1, source_target_pairs={{0,8},{4,12},{8,0},{12,4},{16,24},{20,28},{24,16},{28,20},{1,9},{5... | collective-permute-start | bytes 208904 | tf_op jit(solution)/shard_map/ppermute | solution.py:471
  38.2 11.4 %collective-permute-start.9 = (f32[128,512]{1,0:T(8,128)S(1)}, f32[128,512]{1,0:T(8,128)S(1)}, u32[]{:S(2)}, u32[]{:S(2)}) collective-permute-start(f32[128,512]{1,0:T(8,128)S(1)} %get-tuple-element.45.refs_0_), channel_id=1, source_target_pairs={{0,2},{1,3},{2,0},{3,1},{4,6},{5,7},{6,4},{7,5},{8,10},{9,11},{10,... | collective-permute-start | bytes 786440 | tf_op jit(solution)/shard_map/ppermute | solution.py:471
  39.8 5.6 %collective-permute-start.6 = (f32[136,128]{1,0:T(8,128)S(1)}, f32[136,128]{1,0:T(8,128)S(1)}, u32[]{:S(2)}, u32[]{:S(2)}) collective-permute-start(f32[136,128]{1,0:T(8,128)S(1)} %add.5.refs_0_.left_ref), channel_id=1, source_target_pairs={{0,16},{4,20},{8,24},{12,28},{16,0},{20,4},{24,8},{28,12},{1,17},{... | collective-permute-start | bytes 208904 | tf_op jit(solution)/shard_map/ppermute | solution.py:471
  45.4 15.9 %collective-permute-start.14 = (f32[128,512]{1,0:T(8,128)S(1)}, f32[128,512]{1,0:T(8,128)S(1)}, u32[]{:S(2)}, u32[]{:S(2)}) collective-permute-start(f32[128,512]{1,0:T(8,128)S(1)} %get-tuple-element.49.refs_1_), channel_id=1, source_target_pairs={{0,16},{4,20},{8,24},{12,28},{16,0},{20,4},{24,8},{28,12},{1,17},{... | collective-permute-start | bytes 786440 | tf_op jit(solution)/shard_map/ppermute | solution.py:471
  48.1 4.3 %collective-permute-start.8 = (f32[136,128]{1,0:T(8,128)S(1)}, f32[136,128]{1,0:T(8,128)S(1)}, u32[]{:S(2)}, u32[]{:S(2)}) collective-permute-start(f32[136,128]{1,0:T(8,128)S(1)} %add.6.refs_0_.left_ref), channel_id=1, source_target_pairs={{0,4},{4,0},{8,12},{12,8},{16,20},{20,16},{24,28},{28,24},{1,5},{5... | collective-permute-start | bytes 208904 | tf_op jit(solution)/shard_map/ppermute | solution.py:471
  49.6 5.0 %collective-permute-start.11 = (f32[64,512]{1,0:T(8,128)S(1)}, f32[64,512]{1,0:T(8,128)S(1)}, u32[]{:S(2)}, u32[]{:S(2)}) collective-permute-start(f32[64,512]{1,0:T(8,128)S(1)} %get-tuple-element.47.refs_0_), channel_id=1, source_target_pairs={{0,4},{4,0},{8,12},{12,8},{16,20},{20,16},{24,28},{28,24},{1,5},{5... | collective-permute-start | bytes 393224 | tf_op jit(solution)/shard_map/ppermute | solution.py:471
  52.4 2.3 %collective-permute-start.10 = (f32[136,128]{1,0:T(8,128)S(1)}, f32[136,128]{1,0:T(8,128)S(1)}, u32[]{:S(2)}, u32[]{:S(2)}) collective-permute-start(f32[136,128]{1,0:T(8,128)S(1)} %add.7.refs_0_.left_ref.near_ref), channel_id=1, source_target_pairs={{0,1},{1,0},{2,3},{3,2},{4,5},{5,4},{6,7},{7,6},{8,9},{9,8},{10,11... | collective-permute-start | bytes 208904 | tf_op jit(solution)/shard_map/ppermute | solution.py:471
  54.7 6.6 %collective-permute-start.12 = (f32[136,128]{1,0:T(8,128)S(1)}, f32[136,128]{1,0:T(8,128)S(1)}, u32[]{:S(2)}, u32[]{:S(2)}) collective-permute-start(f32[136,128]{1,0:T(8,128)S(1)} %add.8.refs_0_.left_ref), channel_id=1, source_target_pairs={{0,2},{1,3},{2,0},{3,1},{4,6},{5,7},{6,4},{7,5},{8,10},{9,11},{10,... | collective-permute-start | bytes 208904 | tf_op jit(solution)/shard_map/ppermute | solution.py:471
  55.3 6.0 %collective-permute-start.13 = (f32[32,512]{1,0:T(8,128)S(1)}, f32[32,512]{1,0:T(8,128)S(1)}, u32[]{:S(2)}, u32[]{:S(2)}) collective-permute-start(f32[32,512]{1,0:T(8,128)S(1)} %get-tuple-element.51.refs_0_), channel_id=1, source_target_pairs={{0,16},{4,20},{8,24},{12,28},{16,0},{20,4},{24,8},{28,12},{1,17},{... | collective-permute-start | bytes 196616 | tf_op jit(solution)/shard_map/ppermute | solution.py:471
  61.4 9.3 %collective-permute-start.15 = (f32[64,512]{1,0:T(8,128)S(1)}, f32[64,512]{1,0:T(8,128)S(1)}, u32[]{:S(2)}, u32[]{:S(2)}) collective-permute-start(f32[64,512]{1,0:T(8,128)S(1)} %get-tuple-element.60), channel_id=1, source_target_pairs={{0,8},{4,12},{8,0},{12,4},{16,24},{20,28},{24,16},{28,20},{1,9},{5... | collective-permute-start | bytes 393224 | tf_op jit(solution)/shard_map/ppermute | solution.py:471
  61.4 9.2 %collective-permute-start.16 = (f32[16,512]{1,0:T(8,128)S(1)}, f32[16,512]{1,0:T(8,128)S(1)}, u32[]{:S(2)}, u32[]{:S(2)}) collective-permute-start(f32[16,512]{1,0:T(8,128)S(1)} %get-tuple-element.53.refs_0_), channel_id=1, source_target_pairs={{0,8},{4,12},{8,0},{12,4},{16,24},{20,28},{24,16},{28,20},{1,9},{5... | collective-permute-start | bytes 98312 | tf_op jit(solution)/shard_map/ppermute | solution.py:471

commit v8 on v7

--- a/solution.py
+++ b/solution.py
@@ -233,10 +233,10 @@
     count, keep_in, send_ref, top_keep_in, top_send_ref, moved_ref, group_own_ref,
     top_own_ref, *refs,
 ):
-    pieces = refs[1 : count + 1]
+    pieces = refs[:count]
     (
-        packed_ref, terms_ref, keep_ref, top_keep_ref, top_next_ref, bases_ref
-    ) = refs[count + 1 :]
+        packed_ref, terms_ref, keep_ref, next_ref, top_keep_ref, top_next_ref, bases_ref
+    ) = refs[count:]
     modes = terms_ref.shape[2]
     size = bases_ref.shape[0]
     row, col = lax.axis_index("row"), lax.axis_index("col")
@@ -247,13 +247,13 @@
     add_own(keep_ref, group_own_ref[0], share_place(group_steps[1:]))
     top_keep_ref[...] = top_keep_in[...]
     add_own(top_keep_ref, top_own_ref[...], share_place(top_steps[1:]))
+    next_ref[...] = send_ref[...]
     top_next_ref[...] = top_send_ref[...]
     line = size // row_count
-    for k, piece in enumerate(pieces):
-        pair = lax.bitwise_xor(row // 2, k)
-        for i in range(2):
-            at = (2 * pair + lax.rem(row + i, 2)) * line
-            bases_ref[pl.ds(pl.multiple_of(at, line), line), :] = piece[i * line : (i + 1) * line, :]
+    for i, piece in enumerate(pieces):
+        for k in range(row_count // 2):
+            at = (2 * lax.bitwise_xor(row // 2, k) + lax.rem(row + i, 2)) * line
+            bases_ref[pl.ds(pl.multiple_of(at, line), line), :] = piece[k * line : (k + 1) * line, :]
     grams = []
     for half in range(2):
         lanes = slice(half * modes, (half + 1) * modes)
@@ -283,16 +283,17 @@
     packed_ref[modes:, :] = jnp.broadcast_to(diagonal, (SUBLANES, modes))
 
 
-def prepare(keep, send, top_keep, top_send, moved, group_own, top_own, after, pieces):
+def prepare(keep, send, top_keep, top_send, moved, group_own, top_own, pieces):
     _, modes, size = moved.shape
     half = jax.ShapeDtypeStruct(keep.shape, F32)
     return pl.pallas_call(
         functools.partial(prepare_kernel, len(pieces)),
-        in_specs=[VMEM] * 7 + [pl.BlockSpec(memory_space=pl.ANY)] + [VMEM] * len(pieces),
-        out_specs=[VMEM] * 5,
+        in_specs=[VMEM] * (7 + len(pieces)),
+        out_specs=[VMEM] * 6,
         out_shape=[
             jax.ShapeDtypeStruct((modes + SUBLANES, modes), F32),
             jax.ShapeDtypeStruct((2, modes, modes), F32),
+            half,
             half,
             half,
             half,
@@ -303,7 +304,7 @@
             flops=12 * size * size * modes, bytes_accessed=12 * size * size, transcendentals=0
         ),
         name="prepare",
-    )(keep, send, top_keep, top_send, moved, group_own, top_own, after, *pieces)
+    )(keep, send, top_keep, top_send, moved, group_own, top_own, *pieces)
 
 
 def fold_kernel(step, after_count, keep_ref, other_ref, *refs):
@@ -472,24 +473,24 @@
 
     group_steps = exchanges(0, row_count, col_count)
     basis = jnp.concatenate([group_basis[0], top_basis], axis=1)
-    beside = swap(basis, "row", 1)
+    lines = [basis] + [swap(basis, "row", 2 * k) for k in range(1, row_count // 2)]
     keep, send, loaded, mass = leaf_group(
         tile_mask, block_map, leaf_mass, constraint_modes, basis
     )
-    pair = jnp.concatenate([basis, beside], axis=0)
-    pieces = [pair] + [swap(pair, "row", 2 * k) for k in range(1, row_count // 2)]
-    other = swap(send, *group_steps[0])
+    near_lines = jnp.concatenate(lines, axis=0)
+    pieces = [near_lines, swap(near_lines, "row", 1)]
     top_keep, top_send, moved = leaf_top(
-        block_map, mass, constraint_modes, leaf_fixed_modes, loaded, pair
+        block_map, mass, constraint_modes, leaf_fixed_modes, loaded, near_lines
     )
-    packed, terms, keep, top_keep, top_send = prepare(
-        keep, send, top_keep, top_send, moved, group_mass, top_mass, other, pieces
+    packed, terms, keep, send, top_keep, top_send = prepare(
+        keep, send, top_keep, top_send, moved, group_mass, top_mass, pieces
     )
     top_left = exchanges(1, row_count, col_count)
     sums = [("row", 1 << b) for b in range(1, bits_of(row_count))] + [("row", 1)]
     row_steps = len(sums)
     sums += [("col", 1 << b) for b in range(bits_of(col_count))]
     value = near = packed
+    other = swap(send, *group_steps[0])
     top_other = swap(top_send, *top_left[0])
     after = []
     for i, step in enumerate(sums):

time: 71.6 us -> 72.4 us (1.011)
  no operation moved by 1% of the time
where the time goes in v8:
time: 72.4 us; the launch traced here: 72.1 us
  Pallas kernels  25.6 us (35%)
  starting transfers between devices  22.5 us (31%)
  waiting for transfers between devices  18.7 us (26%)
  local copies, waits for them, and re-layouts  3.58 us (5%)
  between operations  0.85 us (1%)
  other arithmetic  0.8 us (1%)
    ppermute x17, starting transfers between devices, swap(): return lax.ppermute(value, axis, crossed(sizes[axis], bit))  22.5 us
    ppermute x17, waiting for transfers between devices, swap(): return lax.ppermute(value, axis, crossed(sizes[axis], bit))  18.7 us
    pallas_call x1, Pallas kernels, leaf_group(): pl.pallas_call(group_kernel, in_specs=[SMEM] * 2 + [HBM, VMEM, pl.BlockSp...  9.1 us
    pallas_call x1, Pallas kernels, finish(): pl.pallas_call(finish_kernel, in_specs=[VMEM] * 5, out_specs=[VMEM] * 4,...  7.16 us
    pallas_call x1, Pallas kernels, leaf_top(): pl.pallas_call(top_kernel, in_specs=[SMEM] + [VMEM] * 4 + [pl.BlockSpec(m...  6.94 us
    unnamed x18, local copies, waits for them, and re-layouts  3.58 us
  transfers between devices with their start and end apart: 17, of which 6 were waited for; matrix products, arithmetic and copies ran while one was open for 0% of the time, Pallas kernels for 33%

profile of v8, /device:TPU:0, one launch (start us, length us, event | category | flops | bytes accessed | tf_op | source)
XLA Modules:
  0.0 72.1 jit_solution(12462455156158926314)
XLA Ops:
  0.6 0.8 %pad_maximum_fusion.1.after_ref = f32[64,256]{1,0:T(8,128)S(1)} fusion(f32[64,128]{1,0:T(8,128)} %top_basis_ref.1, f32[64,128]{1,0:T(8,128)} %bitcast.1), kind=kLoop, calls=%fused_computation.1 | loop fusion | flops 16384 | bytes 131072 | tf_op jit(solution)/shard_map/concatenate | solution.py:475
  1.4 0.0 copy-start
  1.4 0.0 copy-start.1
  1.4 5.1 %collective-permute-start.2 = (f32[64,256]{1,0:T(8,128)S(1)}, f32[64,256]{1,0:T(8,128)S(1)}, u32[]{:S(2)}, u32[]{:S(2)}) collective-permute-start(f32[64,256]{1,0:T(8,128)S(1)} %pad_maximum_fusion.1.after_ref), channel_id=1, source_target_pairs={{0,24},{4,28},{8,16},{12,20},{16,8},{20,12},{24,0},{28,4},{1,25},{... | collective-permute-start | bytes 196616 | tf_op jit(solution)/shard_map/ppermute | solution.py:472
  6.5 0.0 collective-permute-start.1
  6.5 0.6 collective-permute-start
  7.2 0.0 copy-start.4
  7.2 2.2 %copy-done.4 = bf16[1,2048,1024]{2,1,0:T(8,128)(2,1)S(1)} copy-done((bf16[1,2048,1024]{2,1,0:T(8,128)(2,1)S(1)}, bf16[1,2048,1024]{2,1,0:T(8,128)(2,1)}, u32[]{:S(2)}) %copy-start.4) | copy-done | bytes 4194328
  9.4 0.0 copy-start.7
  9.4 0.7 copy-done.7
  10.1 0.0 copy-start.8
  10.1 0.7 copy-done.8
  10.7 0.0 copy-start.5
  10.7 0.0 copy-start.6
  10.8 9.1 %leaf_group.1 = (f32[256,512]{1,0:T(8,128)S(1)}, f32[256,512]{1,0:T(8,128)S(1)}, bf16[2048,512]{1,0:T(8,128)(2,1)S(1)}, bf16[2048,2048]{1,0:T(8,128)(2,1)S(1)}) custom-call(s32[1,16,16]{2,1,0:T(8,128)S(1)} %copy-done.7, s32[1,2,4]{2,1,0:T(2,128)S(1)} %copy-done.8, bf16[1,2048,2048]{2,1,0:T(8,128)(2,1)} %mass_hbm.1, bf16[1,2048,1024]{2,1,0:T(8,128)(2,1)S(1)} %copy-done.4, ...), custom_call_target="tpu_custom_call" | custom-call | flops 5368709120 | bytes 12582912 | tf_op jit(solution)/shard_map/leaf_group/pallas_call | solution.py:142
  19.9 0.0 collective-permute-done.2
  19.9 0.0 collective-permute-done.1
  19.9 0.0 collective-permute-done
  19.9 0.0 copy-done
  19.9 0.0 copy-done.1
  19.9 1.7 %collective-permute-start.3 = (f32[256,256]{1,0:T(8,128)S(1)}, f32[256,256]{1,0:T(8,128)S(1)}, u32[]{:S(2)}, u32[]{:S(2)}) collective-permute-start(f32[256,256]{1,0:T(8,128)S(1)} %pad_maximum_fusion.after_ref.refs_0_), channel_id=1, source_target_pairs={{0,4},{4,0},{8,12},{12,8},{16,20},{20,16},{24,28},{28,24},{1,5},{5... | collective-permute-start | bytes 786440 | tf_op jit(solution)/shard_map/ppermute | solution.py:472
  21.6 0.0 copy-done.5
  21.7 0.0 copy-done.6
  21.7 0.0 copy-start.2
  21.7 0.0 copy-start.3
  21.7 6.9 %leaf_top.1 = (f32[256,512]{1,0:T(8,128)S(1)}, f32[256,512]{1,0:T(8,128)S(1)}, f32[2,128,512]{2,1,0:T(8,128)S(1)}) custom-call(s32[1,2,4]{2,1,0:T(2,128)S(1)} %copy-done.8, bf16[2048,2048]{1,0:T(8,128)(2,1)S(1)} %get-tuple-element.38.mass_ref, bf16[1,2048,1024]{2,1,0:T(8,128)(2,1)S(1)} %copy-done.5, bf16[1,2048,128]{2,1,0:T(8,128)(2,1)S(1)} %copy-done.6, ...), custom_call_target="tpu_custom_call" | custom-call | flops 5368709120 | bytes 12582912 | tf_op jit(solution)/shard_map/leaf_top/pallas_call | solution.py:189
  28.6 0.0 collective-permute-done.3.refs_1_
  28.6 0.0 copy-done.2
  28.6 0.0 copy-done.3
  28.6 1.4 %prepare.1 = (f32[136,128]{1,0:T(8,128)S(1)}, f32[2,128,128]{2,1,0:T(8,128)S(1)}, f32[256,512]{1,0:T(8,128)S(1)}, f32[256,512]{1,0:T(8,128)S(1)}, f32[256,512]{1,0:T(8,128)S(1)}, /*index=5*/f32[256,512]{1,0:T(8,128)S(1)}) custom-call(f32[256,512]{1,0:T(8,128)S(1)} %get-tuple-element.36.keep_in, f32[256,512]{1,0:T(8,128)S(1)} %get-tuple-element.37.send_ref, ...), custom_call_target="tpu_custom_call" | custom-call | flops 402653184 | bytes 3145728 | tf_op jit(solution)/shard_map/prepare/pallas_call | solution.py:289
  30.1 0.1 collective-permute-start.6
  30.1 0.5 collective-permute-start.9
  30.6 1.4 %collective-permute-start.4 = (f32[136,128]{1,0:T(8,128)S(1)}, f32[136,128]{1,0:T(8,128)S(1)}, u32[]{:S(2)}, u32[]{:S(2)}) collective-permute-start(f32[136,128]{1,0:T(8,128)S(1)} %get-tuple-element.43.left_ref), channel_id=1, source_target_pairs={{0,8},{4,12},{8,0},{12,4},{16,24},{20,28},{24,16},{28,20},{1,9},{5... | collective-permute-start | bytes 208904 | tf_op jit(solution)/shard_map/ppermute | solution.py:472
  32.0 2.9 %collective-permute-done.4.right_ref = f32[136,128]{1,0:T(8,128)S(1)} collective-permute-done((f32[136,128]{1,0:T(8,128)S(1)}, f32[136,128]{1,0:T(8,128)S(1)}, u32[]{:S(2)}, u32[]{:S(2)}) %collective-permute-start.4) | collective-permute-done | bytes 69664 | tf_op jit(solution)/shard_map/ppermute | solution.py:472
  34.9 0.0 collective-permute-done.6.other_ref
  34.9 0.1 fold.6
  35.0 1.7 %collective-permute-start.8 = (f32[128,512]{1,0:T(8,128)S(1)}, f32[128,512]{1,0:T(8,128)S(1)}, u32[]{:S(2)}, u32[]{:S(2)}) collective-permute-start(f32[128,512]{1,0:T(8,128)S(1)} %get-tuple-element.46.refs_0_), channel_id=1, source_target_pairs={{0,2},{1,3},{2,0},{3,1},{4,6},{5,7},{6,4},{7,5},{8,10},{9,11},{10,... | collective-permute-start | bytes 786440 | tf_op jit(solution)/shard_map/ppermute | solution.py:472
  36.7 2.4 %collective-permute-start.5 = (f32[136,128]{1,0:T(8,128)S(1)}, f32[136,128]{1,0:T(8,128)S(1)}, u32[]{:S(2)}, u32[]{:S(2)}) collective-permute-start(f32[136,128]{1,0:T(8,128)S(1)} %add.5.refs_0_.left_ref), channel_id=1, source_target_pairs={{0,16},{4,20},{8,24},{12,28},{16,0},{20,4},{24,8},{28,12},{1,17},{... | collective-permute-start | bytes 208904 | tf_op jit(solution)/shard_map/ppermute | solution.py:472
  39.1 2.8 %collective-permute-done.5.right_ref = f32[136,128]{1,0:T(8,128)S(1)} collective-permute-done((f32[136,128]{1,0:T(8,128)S(1)}, f32[136,128]{1,0:T(8,128)S(1)}, u32[]{:S(2)}, u32[]{:S(2)}) %collective-permute-start.5) | collective-permute-done | bytes 69664 | tf_op jit(solution)/shard_map/ppermute | solution.py:472
  42.0 2.5 %collective-permute-done.9.other_ref = f32[256,512]{1,0:T(8,128)S(1)} collective-permute-done((f32[256,512]{1,0:T(8,128)S(1)}, f32[256,512]{1,0:T(8,128)S(1)}, u32[]{:S(2)}, u32[]{:S(2)}) %collective-permute-start.9) | collective-permute-done | bytes 524320 | tf_op jit(solution)/shard_map/ppermute | solution.py:472
  44.5 0.1 fold.8
  44.6 2.4 %collective-permute-start.14 = (f32[128,512]{1,0:T(8,128)S(1)}, f32[128,512]{1,0:T(8,128)S(1)}, u32[]{:S(2)}, u32[]{:S(2)}) collective-permute-start(f32[128,512]{1,0:T(8,128)S(1)} %get-tuple-element.51.refs_1_), channel_id=1, source_target_pairs={{0,16},{4,20},{8,24},{12,28},{16,0},{20,4},{24,8},{28,12},{1,17},{... | collective-permute-start | bytes 786440 | tf_op jit(solution)/shard_map/ppermute | solution.py:472
  47.0 0.5 collective-permute-start.7
  47.5 0.0 collective-permute-done.8.other_ref
  47.5 1.6 %collective-permute-start.11 = (f32[64,512]{1,0:T(8,128)S(1)}, f32[64,512]{1,0:T(8,128)S(1)}, u32[]{:S(2)}, u32[]{:S(2)}) collective-permute-start(f32[64,512]{1,0:T(8,128)S(1)} %get-tuple-element.48.refs_0_), channel_id=1, source_target_pairs={{0,4},{4,0},{8,12},{12,8},{16,20},{20,16},{24,28},{28,24},{1,5},{5... | collective-permute-start | bytes 393224 | tf_op jit(solution)/shard_map/ppermute | solution.py:472
  49.1 2.7 %collective-permute-done.7.right_ref = f32[136,128]{1,0:T(8,128)S(1)} collective-permute-done((f32[136,128]{1,0:T(8,128)S(1)}, f32[136,128]{1,0:T(8,128)S(1)}, u32[]{:S(2)}, u32[]{:S(2)}) %collective-permute-start.7) | collective-permute-done | bytes 69664 | tf_op jit(solution)/shard_map/ppermute | solution.py:472
  51.8 0.1 collective-permute-start.10
  51.9 1.3 %collective-permute-done.11.other_ref = f32[64,512]{1,0:T(8,128)S(1)} collective-permute-done((f32[64,512]{1,0:T(8,128)S(1)}, f32[64,512]{1,0:T(8,128)S(1)}, u32[]{:S(2)}, u32[]{:S(2)}) %collective-permute-start.11) | collective-permute-done | bytes 131104 | tf_op jit(solution)/shard_map/ppermute | solution.py:472
  53.3 0.0 collective-permute-done.10.right_ref
  53.3 1.6 %collective-permute-start.12 = (f32[136,128]{1,0:T(8,128)S(1)}, f32[136,128]{1,0:T(8,128)S(1)}, u32[]{:S(2)}, u32[]{:S(2)}) collective-permute-start(f32[136,128]{1,0:T(8,128)S(1)} %add.8.refs_0_.left_ref), channel_id=1, source_target_pairs={{0,2},{1,3},{2,0},{3,1},{4,6},{5,7},{6,4},{7,5},{8,10},{9,11},{10,... | collective-permute-start | bytes 208904 | tf_op jit(solution)/shard_map/ppermute | solution.py:472
  54.9 0.8 %collective-permute-start.13 = (f32[32,512]{1,0:T(8,128)S(1)}, f32[32,512]{1,0:T(8,128)S(1)}, u32[]{:S(2)}, u32[]{:S(2)}) collective-permute-start(f32[32,512]{1,0:T(8,128)S(1)} %get-tuple-element.53.refs_0_), channel_id=1, source_target_pairs={{0,16},{4,20},{8,24},{12,28},{16,0},{20,4},{24,8},{28,12},{1,17},{... | collective-permute-start | bytes 196616 | tf_op jit(solution)/shard_map/ppermute | solution.py:472
  55.7 6.3 %collective-permute-done.13.other_ref = f32[32,512]{1,0:T(8,128)S(1)} collective-permute-done((f32[32,512]{1,0:T(8,128)S(1)}, f32[32,512]{1,0:T(8,128)S(1)}, u32[]{:S(2)}, u32[]{:S(2)}) %collective-permute-start.13) | collective-permute-done | bytes 65568 | tf_op jit(solution)/shard_map/ppermute | solution.py:472
  62.0 0.0 collective-permute-done.12.right_ref
  62.1 0.0 collective-permute-done.14.other_ref
  62.1 0.3 collective-permute-start.15
  62.4 1.8 %collective-permute-start.16 = (f32[16,512]{1,0:T(8,128)S(1)}, f32[16,512]{1,0:T(8,128)S(1)}, u32[]{:S(2)}, u32[]{:S(2)}) collective-permute-start(f32[16,512]{1,0:T(8,128)S(1)} %get-tuple-element.55.refs_0_), channel_id=1, source_target_pairs={{0,8},{4,12},{8,0},{12,4},{16,24},{20,28},{24,16},{28,20},{1,9},{5... | collective-permute-start | bytes 98312 | tf_op jit(solution)/shard_map/ppermute | solution.py:472
  64.2 7.2 %finish.1 = (f32[1,128,2,128]{3,2,1,0:T(2,128)}, f32[1,64,128]{2,1,0:T(8,128)}, f32[64,128]{1,0:T(8,128)}, f32[8,128]{1,0:T(8,128)S(1)}) custom-call(f32[136,128]{1,0:T(8,128)S(1)} %add.7.refs_0_.left_ref.near_ref, f32[136,128]{1,0:T(8,128)S(1)} %add.9.far_ref.refs_0_, f32[2,128,128]{2,1,0:T(8,128)S(1)} %get-tuple-element.56.terms_ref, ...), custom_call_target="tpu_custom_call" | custom-call | flops 41943040 | bytes 393216 | tf_op jit(solution)/shard_map/finish/pallas_call | solution.py:446
  71.4 0.0 collective-permute-done.16.top_other_ref
  71.4 0.0 collective-permute-done.15.other_ref
  71.4 0.7 last.1
  (10 shorter events, 0.2 us)
Async XLA Ops:
  1.4 18.5 %copy-start = (f32[64,128]{1,0:T(8,128)S(1)}, f32[64,128]{1,0:T(8,128)}, u32[]{:S(2)}) copy-start(f32[64,128]{1,0:T(8,128)} %top_basis_ref.1) | copy-start | bytes 98308
  1.4 18.5 %copy-start.1 = (f32[1,64,128]{2,1,0:T(8,128)S(1)}, f32[1,64,128]{2,1,0:T(8,128)}, u32[]{:S(2)}) copy-start(f32[1,64,128]{2,1,0:T(8,128)} %group_basis_ref.1) | copy-start | bytes 98308
  1.4 18.4 %collective-permute-start.2 = (f32[64,256]{1,0:T(8,128)S(1)}, f32[64,256]{1,0:T(8,128)S(1)}, u32[]{:S(2)}, u32[]{:S(2)}) collective-permute-start(f32[64,256]{1,0:T(8,128)S(1)} %pad_maximum_fusion.1.after_ref), channel_id=1, source_target_pairs={{0,24},{4,28},{8,16},{12,20},{16,8},{20,12},{24,0},{28,4},{1,25},{... | collective-permute-start | bytes 196616 | tf_op jit(solution)/shard_map/ppermute | solution.py:472
  6.5 13.3 %collective-permute-start.1 = (f32[64,256]{1,0:T(8,128)S(1)}, f32[64,256]{1,0:T(8,128)S(1)}, u32[]{:S(2)}, u32[]{:S(2)}) collective-permute-start(f32[64,256]{1,0:T(8,128)S(1)} %pad_maximum_fusion.1.after_ref), channel_id=1, source_target_pairs={{0,16},{4,20},{8,24},{12,28},{16,0},{20,4},{24,8},{28,12},{1,17},{... | collective-permute-start | bytes 196616 | tf_op jit(solution)/shard_map/ppermute | solution.py:472
  6.5 13.3 %collective-permute-start = (f32[64,256]{1,0:T(8,128)S(1)}, f32[64,256]{1,0:T(8,128)S(1)}, u32[]{:S(2)}, u32[]{:S(2)}) collective-permute-start(f32[64,256]{1,0:T(8,128)S(1)} %pad_maximum_fusion.1.after_ref), channel_id=1, source_target_pairs={{0,8},{4,12},{8,0},{12,4},{16,24},{20,28},{24,16},{28,20},{1,9},{5... | collective-permute-start | bytes 196616 | tf_op jit(solution)/shard_map/ppermute | solution.py:472
  7.2 2.2 %copy-start.4 = (bf16[1,2048,1024]{2,1,0:T(8,128)(2,1)S(1)}, bf16[1,2048,1024]{2,1,0:T(8,128)(2,1)}, u32[]{:S(2)}) copy-start(bf16[1,2048,1024]{2,1,0:T(8,128)(2,1)} %modes_ref.3) | copy-start | bytes 12582916
  9.4 0.7 copy-start.7
  10.1 0.7 copy-start.8
  10.7 10.9 %copy-start.5 = (bf16[1,2048,1024]{2,1,0:T(8,128)(2,1)S(1)}, bf16[1,2048,1024]{2,1,0:T(8,128)(2,1)}, u32[]{:S(2)}) copy-start(bf16[1,2048,1024]{2,1,0:T(8,128)(2,1)} %modes_ref.3) | copy-start | bytes 12582916
  10.7 10.9 %copy-start.6 = (bf16[1,2048,128]{2,1,0:T(8,128)(2,1)S(1)}, bf16[1,2048,128]{2,1,0:T(8,128)(2,1)}, u32[]{:S(2)}) copy-start(bf16[1,2048,128]{2,1,0:T(8,128)(2,1)} %fixed_ref.1) | copy-start | bytes 1572868
  19.9 8.7 %collective-permute-start.3 = (f32[256,256]{1,0:T(8,128)S(1)}, f32[256,256]{1,0:T(8,128)S(1)}, u32[]{:S(2)}, u32[]{:S(2)}) collective-permute-start(f32[256,256]{1,0:T(8,128)S(1)} %pad_maximum_fusion.after_ref.refs_0_), channel_id=1, source_target_pairs={{0,4},{4,0},{8,12},{12,8},{16,20},{20,16},{24,28},{28,24},{1,5},{5... | collective-permute-start | bytes 786440 | tf_op jit(solution)/shard_map/ppermute | solution.py:472
  21.7 7.0 %copy-start.2 = (f32[1,64,512]{2,1,0:T(8,128)S(1)}, f32[1,64,512]{2,1,0:T(8,128)}, u32[]{:S(2)}) copy-start(f32[1,64,512]{2,1,0:T(8,128)} %group_own_ref.1) | copy-start | bytes 393220
  21.7 7.0 %copy-start.3 = (f32[16,512]{1,0:T(8,128)S(1)}, f32[16,512]{1,0:T(8,128)}, u32[]{:S(2)}) copy-start(f32[16,512]{1,0:T(8,128)} %top_own_ref.1) | copy-start | bytes 98308
  30.1 4.9 %collective-permute-start.6 = (f32[256,512]{1,0:T(8,128)S(1)}, f32[256,512]{1,0:T(8,128)S(1)}, u32[]{:S(2)}, u32[]{:S(2)}) collective-permute-start(f32[256,512]{1,0:T(8,128)S(1)} %get-tuple-element.45), channel_id=1, source_target_pairs={{0,1},{1,0},{2,3},{3,2},{4,5},{5,4},{6,7},{7,6},{8,9},{9,8},{10,11... | collective-permute-start | bytes 1572872 | tf_op jit(solution)/shard_map/ppermute | solution.py:472
  30.1 14.3 %collective-permute-start.9 = (f32[256,512]{1,0:T(8,128)S(1)}, f32[256,512]{1,0:T(8,128)S(1)}, u32[]{:S(2)}, u32[]{:S(2)}) collective-permute-start(f32[256,512]{1,0:T(8,128)S(1)} %get-tuple-element.50), channel_id=1, source_target_pairs={{0,4},{4,0},{8,12},{12,8},{16,20},{20,16},{24,28},{28,24},{1,5},{5... | collective-permute-start | bytes 1572872 | tf_op jit(solution)/shard_map/ppermute | solution.py:472
  30.6 4.3 %collective-permute-start.4 = (f32[136,128]{1,0:T(8,128)S(1)}, f32[136,128]{1,0:T(8,128)S(1)}, u32[]{:S(2)}, u32[]{:S(2)}) collective-permute-start(f32[136,128]{1,0:T(8,128)S(1)} %get-tuple-element.43.left_ref), channel_id=1, source_target_pairs={{0,8},{4,12},{8,0},{12,4},{16,24},{20,28},{24,16},{28,20},{1,9},{5... | collective-permute-start | bytes 208904 | tf_op jit(solution)/shard_map/ppermute | solution.py:472
  35.0 12.5 %collective-permute-start.8 = (f32[128,512]{1,0:T(8,128)S(1)}, f32[128,512]{1,0:T(8,128)S(1)}, u32[]{:S(2)}, u32[]{:S(2)}) collective-permute-start(f32[128,512]{1,0:T(8,128)S(1)} %get-tuple-element.46.refs_0_), channel_id=1, source_target_pairs={{0,2},{1,3},{2,0},{3,1},{4,6},{5,7},{6,4},{7,5},{8,10},{9,11},{10,... | collective-permute-start | bytes 786440 | tf_op jit(solution)/shard_map/ppermute | solution.py:472
  36.7 5.2 %collective-permute-start.5 = (f32[136,128]{1,0:T(8,128)S(1)}, f32[136,128]{1,0:T(8,128)S(1)}, u32[]{:S(2)}, u32[]{:S(2)}) collective-permute-start(f32[136,128]{1,0:T(8,128)S(1)} %add.5.refs_0_.left_ref), channel_id=1, source_target_pairs={{0,16},{4,20},{8,24},{12,28},{16,0},{20,4},{24,8},{28,12},{1,17},{... | collective-permute-start | bytes 208904 | tf_op jit(solution)/shard_map/ppermute | solution.py:472
  44.6 17.5 %collective-permute-start.14 = (f32[128,512]{1,0:T(8,128)S(1)}, f32[128,512]{1,0:T(8,128)S(1)}, u32[]{:S(2)}, u32[]{:S(2)}) collective-permute-start(f32[128,512]{1,0:T(8,128)S(1)} %get-tuple-element.51.refs_1_), channel_id=1, source_target_pairs={{0,16},{4,20},{8,24},{12,28},{16,0},{20,4},{24,8},{28,12},{1,17},{... | collective-permute-start | bytes 786440 | tf_op jit(solution)/shard_map/ppermute | solution.py:472
  47.0 4.9 %collective-permute-start.7 = (f32[136,128]{1,0:T(8,128)S(1)}, f32[136,128]{1,0:T(8,128)S(1)}, u32[]{:S(2)}, u32[]{:S(2)}) collective-permute-start(f32[136,128]{1,0:T(8,128)S(1)} %add.6.refs_0_.left_ref), channel_id=1, source_target_pairs={{0,4},{4,0},{8,12},{12,8},{16,20},{20,16},{24,28},{28,24},{1,5},{5... | collective-permute-start | bytes 208904 | tf_op jit(solution)/shard_map/ppermute | solution.py:472
  47.5 5.7 %collective-permute-start.11 = (f32[64,512]{1,0:T(8,128)S(1)}, f32[64,512]{1,0:T(8,128)S(1)}, u32[]{:S(2)}, u32[]{:S(2)}) collective-permute-start(f32[64,512]{1,0:T(8,128)S(1)} %get-tuple-element.48.refs_0_), channel_id=1, source_target_pairs={{0,4},{4,0},{8,12},{12,8},{16,20},{20,16},{24,28},{28,24},{1,5},{5... | collective-permute-start | bytes 393224 | tf_op jit(solution)/shard_map/ppermute | solution.py:472
  51.8 1.4 %collective-permute-start.10 = (f32[136,128]{1,0:T(8,128)S(1)}, f32[136,128]{1,0:T(8,128)S(1)}, u32[]{:S(2)}, u32[]{:S(2)}) collective-permute-start(f32[136,128]{1,0:T(8,128)S(1)} %add.7.refs_0_.left_ref.near_ref), channel_id=1, source_target_pairs={{0,1},{1,0},{2,3},{3,2},{4,5},{5,4},{6,7},{7,6},{8,9},{9,8},{10,11... | collective-permute-start | bytes 208904 | tf_op jit(solution)/shard_map/ppermute | solution.py:472
  53.3 8.7 %collective-permute-start.12 = (f32[136,128]{1,0:T(8,128)S(1)}, f32[136,128]{1,0:T(8,128)S(1)}, u32[]{:S(2)}, u32[]{:S(2)}) collective-permute-start(f32[136,128]{1,0:T(8,128)S(1)} %add.8.refs_0_.left_ref), channel_id=1, source_target_pairs={{0,2},{1,3},{2,0},{3,1},{4,6},{5,7},{6,4},{7,5},{8,10},{9,11},{10,... | collective-permute-start | bytes 208904 | tf_op jit(solution)/shard_map/ppermute | solution.py:472
  54.9 7.1 %collective-permute-start.13 = (f32[32,512]{1,0:T(8,128)S(1)}, f32[32,512]{1,0:T(8,128)S(1)}, u32[]{:S(2)}, u32[]{:S(2)}) collective-permute-start(f32[32,512]{1,0:T(8,128)S(1)} %get-tuple-element.53.refs_0_), channel_id=1, source_target_pairs={{0,16},{4,20},{8,24},{12,28},{16,0},{20,4},{24,8},{28,12},{1,17},{... | collective-permute-start | bytes 196616 | tf_op jit(solution)/shard_map/ppermute | solution.py:472
  62.1 9.3 %collective-permute-start.15 = (f32[64,512]{1,0:T(8,128)S(1)}, f32[64,512]{1,0:T(8,128)S(1)}, u32[]{:S(2)}, u32[]{:S(2)}) collective-permute-start(f32[64,512]{1,0:T(8,128)S(1)} %get-tuple-element.62), channel_id=1, source_target_pairs={{0,8},{4,12},{8,0},{12,4},{16,24},{20,28},{24,16},{28,20},{1,9},{5... | collective-permute-start | bytes 393224 | tf_op jit(solution)/shard_map/ppermute | solution.py:472
  62.4 9.0 %collective-permute-start.16 = (f32[16,512]{1,0:T(8,128)S(1)}, f32[16,512]{1,0:T(8,128)S(1)}, u32[]{:S(2)}, u32[]{:S(2)}) collective-permute-start(f32[16,512]{1,0:T(8,128)S(1)} %get-tuple-element.55.refs_0_), channel_id=1, source_target_pairs={{0,8},{4,12},{8,0},{12,4},{16,24},{20,28},{24,16},{28,20},{1,9},{5... | collective-permute-start | bytes 98312 | tf_op jit(solution)/shard_map/ppermute | solution.py:472

commit v9 on v6

--- a/solution.py
+++ b/solution.py
@@ -361,23 +361,21 @@
             ]
             strip = state[start:stop, :]
             small = [s[start:stop, :] for s in spread]
-            units, levels, scales = [], [], []
+            scaled = []
             rest = strip
             for q in range(width):
                 scale = lax.rsqrt(small[q][q : q + 1, :])
-                inverse = scale * scale
-                level = rest[q : q + 1, :]
-                rest = rest - (small[q] * level) * inverse
-                unit = jnp.where(line == q, 1.0, small[q])
+                tail = [small[t][q : q + 1, :] * scale for t in range(q + 1, width)]
+                level = rest[q : q + 1, :] * scale
+                rest = rest - small[q] * (scale * level)
+                small[q] = jnp.where(line == q, 1.0, small[q]) * scale
                 for t in range(q + 1, width):
-                    product = unit * small[t][q : q + 1, :]
-                    small[t] = jnp.where(line == q, 0.0, small[t]) - product * inverse
-                units.append(jnp.where(line <= q, unit, 0.0))
-                levels.append(level * inverse)
-                scales.append(scale)
-            solved = units[0] * levels[0]
+                    small[t] = jnp.where(line == q, 0.0, small[t]) - small[q] * tail[t - q - 1]
+                scaled.append(level)
+            small = [jnp.where(line <= q, s, 0.0) for q, s in enumerate(small)]
+            solved = small[0] * scaled[0]
             for q in range(1, width):
-                solved = solved + units[q] * levels[q]
+                solved = solved + small[q] * scaled[q]
             solved = jnp.where(lane >= stop, solved, 0.0)
             update = spread[0] * solved[0:1, :]
             for q in range(1, width):
@@ -393,7 +391,7 @@
             states[m] = jnp.concatenate(parts, axis=0)
             diagonal = jnp.zeros((width, size), F32)
             for q in range(width):
-                diagonal = jnp.where(lane == start + q, units[q] * scales[q], diagonal)
+                diagonal = jnp.where(lane == start + q, small[q], diagonal)
             diagonals[m].append(diagonal)
     uppers = [jnp.where(across >= down, state, 0.0) for state in states]
     return uppers, [jnp.concatenate(d, axis=0) for d in diagonals]
@@ -481,26 +479,25 @@
         after = []
         if i == row_steps - 1:
             near = value
-        if len(top_left) > 1:
+        if len(top_left) > 2:
             top_keep, top_send = fold(top_left[1], top_keep, top_other, value)
             top_left = top_left[1:]
             top_other = swap(top_send, *top_left[0])
             after.append(top_send)
-        behind = i - (row_steps - 2)
-        if behind == 0 or (behind >= 3 and len(group_steps) > 1):
+        if i == row_steps - 2:
             keep, send = fold(group_steps[1], keep, other, value)
             group_steps = group_steps[1:]
             other = swap(send, *group_steps[0])
             after.append(send)
+    coupling, group_modes, top_modes, token = finish(near, value, terms, group_basis, top_basis)
     while len(group_steps) > 1:
-        keep, send = fold(group_steps[1], keep, other, value)
+        keep, send = fold(group_steps[1], keep, other, token)
         group_steps = group_steps[1:]
         other = swap(send, *group_steps[0])
     while len(top_left) > 1:
-        top_keep, top_send = fold(top_left[1], top_keep, top_other, value)
+        top_keep, top_send = fold(top_left[1], top_keep, top_other, token)
         top_left = top_left[1:]
         top_other = swap(top_send, *top_left[0])
-    coupling, group_modes, top_modes, token = finish(near, value, terms, group_basis, top_basis)
     assembled, top_assembled = last(keep, other, top_keep, top_other, token)
     return coupling, group_modes, top_modes, assembled, top_assembled
 

time: 70.7 us -> 77.3 us (1.093)
  waiting for transfers between devices: 15.3 us -> 24.1 us
  Pallas kernels: 30.7 us -> 29.4 us
  starting transfers between devices: 21.4 us -> 20.4 us
    ppermute x17, waiting for transfers between devices: 15.3 us -> 24.1 us  [swap(): return lax.ppermute(value, axis, crossed(sizes[axis], bit))]
    pallas_call x1, Pallas kernels: 8.45 us -> 7.17 us  [finish(): pl.pallas_call(finish_kernel, in_specs=[VMEM] * 5, out_specs=[VMEM] * 4,...]
    ppermute x17, starting transfers between devices: 21.4 us -> 20.4 us  [swap(): return lax.ppermute(value, axis, crossed(sizes[axis], bit))]
  transfers between devices with their start and end apart: 17 -> 17, of which waited for: 5 -> 7; matrix products, arithmetic and copies ran while one was open for 0% -> 0% of each run, Pallas kernels for 40% -> 35%
where the time goes in v9:
time: 77.3 us; the launch traced here: 77 us
  Pallas kernels  29.4 us (38%)
  waiting for transfers between devices  24.1 us (31%)
  starting transfers between devices  20.4 us (26%)
  local copies, waits for them, and re-layouts  1.4 us (2%)
  between operations  0.84 us (1%)
  other arithmetic  0.79 us (1%)
    ppermute x17, waiting for transfers between devices, swap(): return lax.ppermute(value, axis, crossed(sizes[axis], bit))  24.1 us
    ppermute x17, starting transfers between devices, swap(): return lax.ppermute(value, axis, crossed(sizes[axis], bit))  20.4 us
    pallas_call x2, Pallas kernels, leaf_half(): pl.pallas_call(functools.partial(leaf_kernel, half), in_specs=[SMEM] * 2...  19.8 us
    pallas_call x1, Pallas kernels, finish(): pl.pallas_call(finish_kernel, in_specs=[VMEM] * 5, out_specs=[VMEM] * 4,...  7.17 us
  transfers between devices with their start and end apart: 17, of which 7 were waited for; matrix products, arithmetic and copies ran while one was open for 0% of the time, Pallas kernels for 35%

profile of v9, /device:TPU:0, one launch (start us, length us, event | category | flops | bytes accessed | tf_op | source)
XLA Modules:
  0.0 77.0 jit_solution(11127562644505901404)
XLA Ops:
  0.6 0.8 %pad_maximum_fusion.1.refs_0_ = f32[64,256]{1,0:T(8,128)S(1)} fusion(f32[64,128]{1,0:T(8,128)} %top_basis_ref.1, f32[64,128]{1,0:T(8,128)} %bitcast.1), kind=kLoop, calls=%fused_computation.1 | loop fusion | flops 16384 | bytes 131072 | tf_op jit(solution)/shard_map/concatenate | solution.py:460
  1.4 0.0 copy-start
  1.4 0.0 copy-start.1
  1.4 0.0 copy-start.4
  1.4 3.0 %collective-permute-start = (f32[64,256]{1,0:T(8,128)S(1)}, f32[64,256]{1,0:T(8,128)S(1)}, u32[]{:S(2)}, u32[]{:S(2)}) collective-permute-start(f32[64,256]{1,0:T(8,128)S(1)} %pad_maximum_fusion.1.refs_0_), channel_id=1, source_target_pairs={{0,4},{4,0},{8,12},{12,8},{16,20},{20,16},{24,28},{28,24},{1,5},{5... | collective-permute-start | bytes 196616 | tf_op jit(solution)/shard_map/ppermute | solution.py:454
  4.4 0.0 copy-start.5
  4.4 0.7 copy-done.5
  5.1 0.0 copy-start.6
  5.1 0.7 copy-done.6
  5.8 0.0 copy-start.7
  5.8 9.5 %leaf_group.1 = (f32[256,512]{1,0:T(8,128)S(1)}, f32[256,512]{1,0:T(8,128)S(1)}, bf16[2048,512]{1,0:T(8,128)(2,1)S(1)}) custom-call(s32[1,16,16]{2,1,0:T(8,128)S(1)} %copy-done.5, s32[1,2,4]{2,1,0:T(2,128)S(1)} %copy-done.6, bf16[1,2048,2048]{2,1,0:T(8,128)(2,1)} %mass_hbm.3, bf16[1,2048,1024]{2,1,0:T(8,128)(2,1)} %modes_hbm.3, ...), custom_call_target="tpu_custom_call" | custom-call | flops 5368709120 | bytes 12582912 | tf_op jit(solution)/shard_map/leaf_group/pallas_call | solution.py:176
  15.3 0.2 collective-permute-start.1
  15.5 0.0 collective-permute-done
  15.5 0.0 copy-done
  15.5 0.0 copy-done.1
  15.5 2.1 %collective-permute-start.2 = (f32[128,256]{1,0:T(8,128)S(1)}, f32[128,256]{1,0:T(8,128)S(1)}, u32[]{:S(2)}, u32[]{:S(2)}) collective-permute-start(f32[128,256]{1,0:T(8,128)S(1)} %pad_maximum_fusion.refs_2_.refs_1_), channel_id=1, source_target_pairs={{0,8},{4,12},{8,0},{12,4},{16,24},{20,28},{24,16},{28,20},{1,9},{5... | collective-permute-start | bytes 393224 | tf_op jit(solution)/shard_map/ppermute | solution.py:454
  17.6 2.6 %collective-permute-start.3 = (f32[128,256]{1,0:T(8,128)S(1)}, f32[128,256]{1,0:T(8,128)S(1)}, u32[]{:S(2)}, u32[]{:S(2)}) collective-permute-start(f32[128,256]{1,0:T(8,128)S(1)} %pad_maximum_fusion.refs_2_.refs_1_), channel_id=1, source_target_pairs={{0,16},{4,20},{8,24},{12,28},{16,0},{20,4},{24,8},{28,12},{1,17},{... | collective-permute-start | bytes 393224 | tf_op jit(solution)/shard_map/ppermute | solution.py:454
  20.2 0.0 collective-permute-start.4
  20.2 0.0 copy-done.4
  20.2 0.0 copy-done.7
  20.2 0.0 copy-start.2
  20.2 0.0 copy-start.3
  20.2 10.3 %leaf_top.1 = (f32[256,512]{1,0:T(8,128)S(1)}, f32[256,512]{1,0:T(8,128)S(1)}, f32[2,128,512]{2,1,0:T(8,128)S(1)}) custom-call(s32[1,16,16]{2,1,0:T(8,128)S(1)} %copy-done.5, s32[1,2,4]{2,1,0:T(2,128)S(1)} %copy-done.7, bf16[1,2048,2048]{2,1,0:T(8,128)(2,1)} %mass_hbm.3, bf16[1,2048,1024]{2,1,0:T(8,128)(2,1)} %modes_hbm.3, ...), custom_call_target="tpu_custom_call" | custom-call | flops 5368709120 | bytes 12582912 | tf_op jit(solution)/shard_map/leaf_top/pallas_call | solution.py:176
  30.5 0.0 collective-permute-done.2.refs_2_
  30.5 0.0 collective-permute-done.3.refs_3_
  30.6 0.0 collective-permute-done.4.refs_4_
  30.6 0.0 collective-permute-done.1.refs_0_.other_ref
  30.6 0.0 copy-done.2
  30.6 0.0 copy-done.3
  30.6 1.4 %prepare.1 = (f32[136,128]{1,0:T(8,128)S(1)}, f32[2,128,128]{2,1,0:T(8,128)S(1)}, f32[256,512]{1,0:T(8,128)S(1)}, f32[256,512]{1,0:T(8,128)S(1)}, f32[256,512]{1,0:T(8,128)S(1)}) custom-call(f32[256,512]{1,0:T(8,128)S(1)} %get-tuple-element.34.keep_in, f32[256,512]{1,0:T(8,128)S(1)} %get-tuple-element.35.send_ref, ...), custom_call_target="tpu_custom_call" | custom-call | flops 402653184 | bytes 3145728 | tf_op jit(solution)/shard_map/prepare/pallas_call | solution.py:272
  32.0 0.1 collective-permute-start.7
  32.1 1.4 %collective-permute-start.5 = (f32[136,128]{1,0:T(8,128)S(1)}, f32[136,128]{1,0:T(8,128)S(1)}, u32[]{:S(2)}, u32[]{:S(2)}) collective-permute-start(f32[136,128]{1,0:T(8,128)S(1)} %get-tuple-element.40.left_ref), channel_id=1, source_target_pairs={{0,8},{4,12},{8,0},{12,4},{16,24},{20,28},{24,16},{28,20},{1,9},{5... | collective-permute-start | bytes 208904 | tf_op jit(solution)/shard_map/ppermute | solution.py:454
  33.5 3.2 %collective-permute-done.5.right_ref = f32[136,128]{1,0:T(8,128)S(1)} collective-permute-done((f32[136,128]{1,0:T(8,128)S(1)}, f32[136,128]{1,0:T(8,128)S(1)}, u32[]{:S(2)}, u32[]{:S(2)}) %collective-permute-start.5) | collective-permute-done | bytes 69664 | tf_op jit(solution)/shard_map/ppermute | solution.py:454
  36.7 0.0 collective-permute-done.7.other_ref
  36.7 0.1 fold.6
  36.8 1.8 %collective-permute-start.9 = (f32[128,512]{1,0:T(8,128)S(1)}, f32[128,512]{1,0:T(8,128)S(1)}, u32[]{:S(2)}, u32[]{:S(2)}) collective-permute-start(f32[128,512]{1,0:T(8,128)S(1)} %get-tuple-element.43.refs_0_), channel_id=1, source_target_pairs={{0,2},{1,3},{2,0},{3,1},{4,6},{5,7},{6,4},{7,5},{8,10},{9,11},{10,... | collective-permute-start | bytes 786440 | tf_op jit(solution)/shard_map/ppermute | solution.py:454
  38.6 2.4 %collective-permute-start.6 = (f32[136,128]{1,0:T(8,128)S(1)}, f32[136,128]{1,0:T(8,128)S(1)}, u32[]{:S(2)}, u32[]{:S(2)}) collective-permute-start(f32[136,128]{1,0:T(8,128)S(1)} %add.5.refs_0_.left_ref), channel_id=1, source_target_pairs={{0,16},{4,20},{8,24},{12,28},{16,0},{20,4},{24,8},{28,12},{1,17},{... | collective-permute-start | bytes 208904 | tf_op jit(solution)/shard_map/ppermute | solution.py:454
  41.0 3.7 %collective-permute-done.6.right_ref = f32[136,128]{1,0:T(8,128)S(1)} collective-permute-done((f32[136,128]{1,0:T(8,128)S(1)}, f32[136,128]{1,0:T(8,128)S(1)}, u32[]{:S(2)}, u32[]{:S(2)}) %collective-permute-start.6) | collective-permute-done | bytes 69664 | tf_op jit(solution)/shard_map/ppermute | solution.py:454
  44.7 0.1 fold.8
  44.8 1.7 %collective-permute-start.13 = (f32[128,512]{1,0:T(8,128)S(1)}, f32[128,512]{1,0:T(8,128)S(1)}, u32[]{:S(2)}, u32[]{:S(2)}) collective-permute-start(f32[128,512]{1,0:T(8,128)S(1)} %get-tuple-element.47.refs_1_), channel_id=1, source_target_pairs={{0,16},{4,20},{8,24},{12,28},{16,0},{20,4},{24,8},{28,12},{1,17},{... | collective-permute-start | bytes 786440 | tf_op jit(solution)/shard_map/ppermute | solution.py:454
  46.5 1.4 %collective-permute-start.8 = (f32[136,128]{1,0:T(8,128)S(1)}, f32[136,128]{1,0:T(8,128)S(1)}, u32[]{:S(2)}, u32[]{:S(2)}) collective-permute-start(f32[136,128]{1,0:T(8,128)S(1)} %add.6.refs_0_.left_ref), channel_id=1, source_target_pairs={{0,4},{4,0},{8,12},{12,8},{16,20},{20,16},{24,28},{28,24},{1,5},{5... | collective-permute-start | bytes 208904 | tf_op jit(solution)/shard_map/ppermute | solution.py:454
  47.9 0.0 collective-permute-done.9.other_ref
  48.0 0.7 collective-permute-start.11
  48.6 2.2 %collective-permute-done.8.right_ref = f32[136,128]{1,0:T(8,128)S(1)} collective-permute-done((f32[136,128]{1,0:T(8,128)S(1)}, f32[136,128]{1,0:T(8,128)S(1)}, u32[]{:S(2)}, u32[]{:S(2)}) %collective-permute-start.8) | collective-permute-done | bytes 69664 | tf_op jit(solution)/shard_map/ppermute | solution.py:454
  50.8 0.1 collective-permute-start.10
  50.9 2.1 %collective-permute-done.11.other_ref = f32[64,512]{1,0:T(8,128)S(1)} collective-permute-done((f32[64,512]{1,0:T(8,128)S(1)}, f32[64,512]{1,0:T(8,128)S(1)}, u32[]{:S(2)}, u32[]{:S(2)}) %collective-permute-start.11) | collective-permute-done | bytes 131104 | tf_op jit(solution)/shard_map/ppermute | solution.py:454
  53.0 0.0 collective-permute-done.10.right_ref
  53.0 0.6 collective-permute-start.12
  53.7 3.8 %collective-permute-done.12.right_ref = f32[136,128]{1,0:T(8,128)S(1)} collective-permute-done((f32[136,128]{1,0:T(8,128)S(1)}, f32[136,128]{1,0:T(8,128)S(1)}, u32[]{:S(2)}, u32[]{:S(2)}) %collective-permute-start.12) | collective-permute-done | bytes 69664 | tf_op jit(solution)/shard_map/ppermute | solution.py:454
  57.4 7.2 %finish.1 = (f32[1,128,2,128]{3,2,1,0:T(2,128)}, f32[1,64,128]{2,1,0:T(8,128)}, f32[64,128]{1,0:T(8,128)}, f32[8,128]{1,0:T(8,128)S(1)}) custom-call(f32[136,128]{1,0:T(8,128)S(1)} %add.7.refs_0_.left_ref.near_ref, f32[136,128]{1,0:T(8,128)S(1)} %add.9.far_ref, f32[2,128,128]{2,1,0:T(8,128)S(1)} %get-tuple-element.50.terms_ref, f32[1,64,128]{2,1,0:T(8,128)S(1)} %copy-done.1, ...), custom_call_target="tpu_custom_call" | custom-call | flops 41943040 | bytes 393216 | tf_op jit(solution)/shard_map/finish/pallas_call | solution.py:428
  64.6 0.0 collective-permute-done.13.other_ref
  64.7 2.2 %collective-permute-start.14 = (f32[64,512]{1,0:T(8,128)S(1)}, f32[64,512]{1,0:T(8,128)S(1)}, u32[]{:S(2)}, u32[]{:S(2)}) collective-permute-start(f32[64,512]{1,0:T(8,128)S(1)} %get-tuple-element.57), channel_id=1, source_target_pairs={{0,8},{4,12},{8,0},{12,4},{16,24},{20,28},{24,16},{28,20},{1,9},{5... | collective-permute-start | bytes 393224 | tf_op jit(solution)/shard_map/ppermute | solution.py:454
  66.9 0.1 collective-permute-start.15
  67.0 5.3 %collective-permute-done.15.other_ref = f32[32,512]{1,0:T(8,128)S(1)} collective-permute-done((f32[32,512]{1,0:T(8,128)S(1)}, f32[32,512]{1,0:T(8,128)S(1)}, u32[]{:S(2)}, u32[]{:S(2)}) %collective-permute-start.15) | collective-permute-done | bytes 65568 | tf_op jit(solution)/shard_map/ppermute | solution.py:454
  72.3 0.1 collective-permute-start.16
  72.4 3.9 %collective-permute-done.16.top_other_ref = f32[16,512]{1,0:T(8,128)S(1)} collective-permute-done((f32[16,512]{1,0:T(8,128)S(1)}, f32[16,512]{1,0:T(8,128)S(1)}, u32[]{:S(2)}, u32[]{:S(2)}) %collective-permute-start.16) | collective-permute-done | bytes 32800 | tf_op jit(solution)/shard_map/ppermute | solution.py:454
  76.3 0.0 collective-permute-done.14.other_ref
  76.3 0.7 last.1
  (10 shorter events, 0.2 us)
Async XLA Ops:
  1.4 14.1 %copy-start = (f32[64,128]{1,0:T(8,128)S(1)}, f32[64,128]{1,0:T(8,128)}, u32[]{:S(2)}) copy-start(f32[64,128]{1,0:T(8,128)} %top_basis_ref.1) | copy-start | bytes 98308
  1.4 14.1 %copy-start.1 = (f32[1,64,128]{2,1,0:T(8,128)S(1)}, f32[1,64,128]{2,1,0:T(8,128)}, u32[]{:S(2)}) copy-start(f32[1,64,128]{2,1,0:T(8,128)} %group_basis_ref.1) | copy-start | bytes 98308
  1.4 18.8 %copy-start.4 = (bf16[1,2048,128]{2,1,0:T(8,128)(2,1)S(1)}, bf16[1,2048,128]{2,1,0:T(8,128)(2,1)}, u32[]{:S(2)}) copy-start(bf16[1,2048,128]{2,1,0:T(8,128)(2,1)} %refs_0_.1) | copy-start | bytes 1572868
  1.4 14.1 %collective-permute-start = (f32[64,256]{1,0:T(8,128)S(1)}, f32[64,256]{1,0:T(8,128)S(1)}, u32[]{:S(2)}, u32[]{:S(2)}) collective-permute-start(f32[64,256]{1,0:T(8,128)S(1)} %pad_maximum_fusion.1.refs_0_), channel_id=1, source_target_pairs={{0,4},{4,0},{8,12},{12,8},{16,20},{20,16},{24,28},{28,24},{1,5},{5... | collective-permute-start | bytes 196616 | tf_op jit(solution)/shard_map/ppermute | solution.py:454
  4.4 0.7 copy-start.5
  5.1 0.7 copy-start.6
  5.8 14.4 %copy-start.7 = (s32[1,2,4]{2,1,0:T(2,128)S(1)}, s32[1,2,4]{2,1,0:T(2,128)}, u32[]{:S(2)}) copy-start(s32[1,2,4]{2,1,0:T(2,128)} %map_ref.3) | copy-start | bytes 100
  15.3 15.2 %collective-permute-start.1 = (f32[256,512]{1,0:T(8,128)S(1)}, f32[256,512]{1,0:T(8,128)S(1)}, u32[]{:S(2)}, u32[]{:S(2)}) collective-permute-start(f32[256,512]{1,0:T(8,128)S(1)} %get-tuple-element.35.send_ref), channel_id=1, source_target_pairs={{0,4},{4,0},{8,12},{12,8},{16,20},{20,16},{24,28},{28,24},{1,5},{5... | collective-permute-start | bytes 1572872 | tf_op jit(solution)/shard_map/ppermute | solution.py:454
  15.5 15.0 %collective-permute-start.2 = (f32[128,256]{1,0:T(8,128)S(1)}, f32[128,256]{1,0:T(8,128)S(1)}, u32[]{:S(2)}, u32[]{:S(2)}) collective-permute-start(f32[128,256]{1,0:T(8,128)S(1)} %pad_maximum_fusion.refs_2_.refs_1_), channel_id=1, source_target_pairs={{0,8},{4,12},{8,0},{12,4},{16,24},{20,28},{24,16},{28,20},{1,9},{5... | collective-permute-start | bytes 393224 | tf_op jit(solution)/shard_map/ppermute | solution.py:454
  17.6 13.0 %collective-permute-start.3 = (f32[128,256]{1,0:T(8,128)S(1)}, f32[128,256]{1,0:T(8,128)S(1)}, u32[]{:S(2)}, u32[]{:S(2)}) collective-permute-start(f32[128,256]{1,0:T(8,128)S(1)} %pad_maximum_fusion.refs_2_.refs_1_), channel_id=1, source_target_pairs={{0,16},{4,20},{8,24},{12,28},{16,0},{20,4},{24,8},{28,12},{1,17},{... | collective-permute-start | bytes 393224 | tf_op jit(solution)/shard_map/ppermute | solution.py:454
  20.2 10.4 %collective-permute-start.4 = (f32[128,256]{1,0:T(8,128)S(1)}, f32[128,256]{1,0:T(8,128)S(1)}, u32[]{:S(2)}, u32[]{:S(2)}) collective-permute-start(f32[128,256]{1,0:T(8,128)S(1)} %pad_maximum_fusion.refs_2_.refs_1_), channel_id=1, source_target_pairs={{0,24},{4,28},{8,16},{12,20},{16,8},{20,12},{24,0},{28,4},{1,25},{... | collective-permute-start | bytes 393224 | tf_op jit(solution)/shard_map/ppermute | solution.py:454
  20.2 10.4 %copy-start.2 = (f32[1,64,512]{2,1,0:T(8,128)S(1)}, f32[1,64,512]{2,1,0:T(8,128)}, u32[]{:S(2)}) copy-start(f32[1,64,512]{2,1,0:T(8,128)} %group_own_ref.1) | copy-start | bytes 393220
  20.2 10.4 %copy-start.3 = (f32[16,512]{1,0:T(8,128)S(1)}, f32[16,512]{1,0:T(8,128)}, u32[]{:S(2)}) copy-start(f32[16,512]{1,0:T(8,128)} %top_own_ref.1) | copy-start | bytes 98308
  32.0 4.7 %collective-permute-start.7 = (f32[256,512]{1,0:T(8,128)S(1)}, f32[256,512]{1,0:T(8,128)S(1)}, u32[]{:S(2)}, u32[]{:S(2)}) collective-permute-start(f32[256,512]{1,0:T(8,128)S(1)} %get-tuple-element.42), channel_id=1, source_target_pairs={{0,1},{1,0},{2,3},{3,2},{4,5},{5,4},{6,7},{7,6},{8,9},{9,8},{10,11... | collective-permute-start | bytes 1572872 | tf_op jit(solution)/shard_map/ppermute | solution.py:454
  32.1 4.6 %collective-permute-start.5 = (f32[136,128]{1,0:T(8,128)S(1)}, f32[136,128]{1,0:T(8,128)S(1)}, u32[]{:S(2)}, u32[]{:S(2)}) collective-permute-start(f32[136,128]{1,0:T(8,128)S(1)} %get-tuple-element.40.left_ref), channel_id=1, source_target_pairs={{0,8},{4,12},{8,0},{12,4},{16,24},{20,28},{24,16},{28,20},{1,9},{5... | collective-permute-start | bytes 208904 | tf_op jit(solution)/shard_map/ppermute | solution.py:454
  36.8 11.1 %collective-permute-start.9 = (f32[128,512]{1,0:T(8,128)S(1)}, f32[128,512]{1,0:T(8,128)S(1)}, u32[]{:S(2)}, u32[]{:S(2)}) collective-permute-start(f32[128,512]{1,0:T(8,128)S(1)} %get-tuple-element.43.refs_0_), channel_id=1, source_target_pairs={{0,2},{1,3},{2,0},{3,1},{4,6},{5,7},{6,4},{7,5},{8,10},{9,11},{10,... | collective-permute-start | bytes 786440 | tf_op jit(solution)/shard_map/ppermute | solution.py:454
  38.6 6.1 %collective-permute-start.6 = (f32[136,128]{1,0:T(8,128)S(1)}, f32[136,128]{1,0:T(8,128)S(1)}, u32[]{:S(2)}, u32[]{:S(2)}) collective-permute-start(f32[136,128]{1,0:T(8,128)S(1)} %add.5.refs_0_.left_ref), channel_id=1, source_target_pairs={{0,16},{4,20},{8,24},{12,28},{16,0},{20,4},{24,8},{28,12},{1,17},{... | collective-permute-start | bytes 208904 | tf_op jit(solution)/shard_map/ppermute | solution.py:454
  44.8 19.8 %collective-permute-start.13 = (f32[128,512]{1,0:T(8,128)S(1)}, f32[128,512]{1,0:T(8,128)S(1)}, u32[]{:S(2)}, u32[]{:S(2)}) collective-permute-start(f32[128,512]{1,0:T(8,128)S(1)} %get-tuple-element.47.refs_1_), channel_id=1, source_target_pairs={{0,16},{4,20},{8,24},{12,28},{16,0},{20,4},{24,8},{28,12},{1,17},{... | collective-permute-start | bytes 786440 | tf_op jit(solution)/shard_map/ppermute | solution.py:454
  46.5 4.3 %collective-permute-start.8 = (f32[136,128]{1,0:T(8,128)S(1)}, f32[136,128]{1,0:T(8,128)S(1)}, u32[]{:S(2)}, u32[]{:S(2)}) collective-permute-start(f32[136,128]{1,0:T(8,128)S(1)} %add.6.refs_0_.left_ref), channel_id=1, source_target_pairs={{0,4},{4,0},{8,12},{12,8},{16,20},{20,16},{24,28},{28,24},{1,5},{5... | collective-permute-start | bytes 208904 | tf_op jit(solution)/shard_map/ppermute | solution.py:454
  48.0 5.0 %collective-permute-start.11 = (f32[64,512]{1,0:T(8,128)S(1)}, f32[64,512]{1,0:T(8,128)S(1)}, u32[]{:S(2)}, u32[]{:S(2)}) collective-permute-start(f32[64,512]{1,0:T(8,128)S(1)} %get-tuple-element.45.refs_0_), channel_id=1, source_target_pairs={{0,4},{4,0},{8,12},{12,8},{16,20},{20,16},{24,28},{28,24},{1,5},{5... | collective-permute-start | bytes 393224 | tf_op jit(solution)/shard_map/ppermute | solution.py:454
  50.8 2.2 %collective-permute-start.10 = (f32[136,128]{1,0:T(8,128)S(1)}, f32[136,128]{1,0:T(8,128)S(1)}, u32[]{:S(2)}, u32[]{:S(2)}) collective-permute-start(f32[136,128]{1,0:T(8,128)S(1)} %add.7.refs_0_.left_ref.near_ref), channel_id=1, source_target_pairs={{0,1},{1,0},{2,3},{3,2},{4,5},{5,4},{6,7},{7,6},{8,9},{9,8},{10,11... | collective-permute-start | bytes 208904 | tf_op jit(solution)/shard_map/ppermute | solution.py:454
  53.0 4.4 %collective-permute-start.12 = (f32[136,128]{1,0:T(8,128)S(1)}, f32[136,128]{1,0:T(8,128)S(1)}, u32[]{:S(2)}, u32[]{:S(2)}) collective-permute-start(f32[136,128]{1,0:T(8,128)S(1)} %add.8.left_ref), channel_id=1, source_target_pairs={{0,2},{1,3},{2,0},{3,1},{4,6},{5,7},{6,4},{7,5},{8,10},{9,11},{10,... | collective-permute-start | bytes 208904 | tf_op jit(solution)/shard_map/ppermute | solution.py:454
  64.7 11.6 %collective-permute-start.14 = (f32[64,512]{1,0:T(8,128)S(1)}, f32[64,512]{1,0:T(8,128)S(1)}, u32[]{:S(2)}, u32[]{:S(2)}) collective-permute-start(f32[64,512]{1,0:T(8,128)S(1)} %get-tuple-element.57), channel_id=1, source_target_pairs={{0,8},{4,12},{8,0},{12,4},{16,24},{20,28},{24,16},{28,20},{1,9},{5... | collective-permute-start | bytes 393224 | tf_op jit(solution)/shard_map/ppermute | solution.py:454
  66.9 5.4 %collective-permute-start.15 = (f32[32,512]{1,0:T(8,128)S(1)}, f32[32,512]{1,0:T(8,128)S(1)}, u32[]{:S(2)}, u32[]{:S(2)}) collective-permute-start(f32[32,512]{1,0:T(8,128)S(1)} %get-tuple-element.49.refs_0_), channel_id=1, source_target_pairs={{0,16},{4,20},{8,24},{12,28},{16,0},{20,4},{24,8},{28,12},{1,17},{... | collective-permute-start | bytes 196616 | tf_op jit(solution)/shard_map/ppermute | solution.py:454
  72.3 4.0 %collective-permute-start.16 = (f32[16,512]{1,0:T(8,128)S(1)}, f32[16,512]{1,0:T(8,128)S(1)}, u32[]{:S(2)}, u32[]{:S(2)}) collective-permute-start(f32[16,512]{1,0:T(8,128)S(1)} %get-tuple-element.60), channel_id=1, source_target_pairs={{0,8},{4,12},{8,0},{12,4},{16,24},{20,28},{24,16},{28,20},{1,9},{5... | collective-permute-start | bytes 98312 | tf_op jit(solution)/shard_map/ppermute | solution.py:454

commit v10 on v9

--- a/solution.py
+++ b/solution.py
@@ -479,25 +479,26 @@
         after = []
         if i == row_steps - 1:
             near = value
-        if len(top_left) > 2:
+        if len(top_left) > 1:
             top_keep, top_send = fold(top_left[1], top_keep, top_other, value)
             top_left = top_left[1:]
             top_other = swap(top_send, *top_left[0])
             after.append(top_send)
-        if i == row_steps - 2:
+        behind = i - (row_steps - 2)
+        if behind == 0 or (behind >= 3 and len(group_steps) > 1):
             keep, send = fold(group_steps[1], keep, other, value)
             group_steps = group_steps[1:]
             other = swap(send, *group_steps[0])
             after.append(send)
-    coupling, group_modes, top_modes, token = finish(near, value, terms, group_basis, top_basis)
     while len(group_steps) > 1:
-        keep, send = fold(group_steps[1], keep, other, token)
+        keep, send = fold(group_steps[1], keep, other, value)
         group_steps = group_steps[1:]
         other = swap(send, *group_steps[0])
     while len(top_left) > 1:
-        top_keep, top_send = fold(top_left[1], top_keep, top_other, token)
+        top_keep, top_send = fold(top_left[1], top_keep, top_other, value)
         top_left = top_left[1:]
         top_other = swap(top_send, *top_left[0])
+    coupling, group_modes, top_modes, token = finish(near, value, terms, group_basis, top_basis)
     assembled, top_assembled = last(keep, other, top_keep, top_other, token)
     return coupling, group_modes, top_modes, assembled, top_assembled
 

time: 77.3 us -> 69.4 us (0.90)
  waiting for transfers between devices: 24.1 us -> 15.4 us
  starting transfers between devices: 20.4 us -> 21.3 us
    ppermute x17, waiting for transfers between devices: 24.1 us -> 15.4 us  [swap(): return lax.ppermute(value, axis, crossed(sizes[axis], bit))]
    ppermute x17, starting transfers between devices: 20.4 us -> 21.3 us  [swap(): return lax.ppermute(value, axis, crossed(sizes[axis], bit))]
  transfers between devices with their start and end apart: 17 -> 17, of which waited for: 7 -> 5; matrix products, arithmetic and copies ran while one was open for 0% -> 0% of each run, Pallas kernels for 35% -> 39%
where the time goes in v10:
time: 69.4 us; the launch traced here: 69.1 us
  Pallas kernels  29.4 us (42%)
  starting transfers between devices  21.3 us (31%)
  waiting for transfers between devices  15.4 us (22%)
  local copies, waits for them, and re-layouts  1.4 us (2%)
  between operations  0.86 us (1%)
  other arithmetic  0.79 us (1%)
    ppermute x17, starting transfers between devices, swap(): return lax.ppermute(value, axis, crossed(sizes[axis], bit))  21.3 us
    pallas_call x2, Pallas kernels, leaf_half(): pl.pallas_call(functools.partial(leaf_kernel, half), in_specs=[SMEM] * 2...  19.8 us
    ppermute x17, waiting for transfers between devices, swap(): return lax.ppermute(value, axis, crossed(sizes[axis], bit))  15.4 us
    pallas_call x1, Pallas kernels, finish(): pl.pallas_call(finish_kernel, in_specs=[VMEM] * 5, out_specs=[VMEM] * 4,...  7.16 us
    pallas_call x1, Pallas kernels, prepare(): pl.pallas_call(functools.partial(prepare_kernel, len(pieces)), in_specs=[...  1.43 us
    unnamed x16, local copies, waits for them, and re-layouts  1.4 us
  transfers between devices with their start and end apart: 17, of which 5 were waited for; matrix products, arithmetic and copies ran while one was open for 0% of the time, Pallas kernels for 39%

profile of v10, /device:TPU:0, one launch (start us, length us, event | category | flops | bytes accessed | tf_op | source)
XLA Modules:
  0.0 69.1 jit_solution(14184968778560996168)
XLA Ops:
  0.6 0.8 %pad_maximum_fusion.1.refs_0_ = f32[64,256]{1,0:T(8,128)S(1)} fusion(f32[64,128]{1,0:T(8,128)} %top_basis_ref.1, f32[64,128]{1,0:T(8,128)} %bitcast.1), kind=kLoop, calls=%fused_computation.1 | loop fusion | flops 16384 | bytes 131072 | tf_op jit(solution)/shard_map/concatenate | solution.py:460
  1.4 0.0 copy-start
  1.4 0.0 copy-start.1
  1.4 0.0 copy-start.4
  1.4 3.0 %collective-permute-start = (f32[64,256]{1,0:T(8,128)S(1)}, f32[64,256]{1,0:T(8,128)S(1)}, u32[]{:S(2)}, u32[]{:S(2)}) collective-permute-start(f32[64,256]{1,0:T(8,128)S(1)} %pad_maximum_fusion.1.refs_0_), channel_id=1, source_target_pairs={{0,4},{4,0},{8,12},{12,8},{16,20},{20,16},{24,28},{28,24},{1,5},{5... | collective-permute-start | bytes 196616 | tf_op jit(solution)/shard_map/ppermute | solution.py:454
  4.4 0.0 copy-start.5
  4.4 0.7 %copy-done.5 = s32[1,16,16]{2,1,0:T(8,128)S(1)} copy-done((s32[1,16,16]{2,1,0:T(8,128)S(1)}, s32[1,16,16]{2,1,0:T(8,128)}, u32[]{:S(2)}) %copy-start.5) | copy-done | bytes 1048
  5.1 0.0 copy-start.6
  5.1 0.7 copy-done.6
  5.8 0.0 copy-start.7
  5.8 9.5 %leaf_group.1 = (f32[256,512]{1,0:T(8,128)S(1)}, f32[256,512]{1,0:T(8,128)S(1)}, bf16[2048,512]{1,0:T(8,128)(2,1)S(1)}) custom-call(s32[1,16,16]{2,1,0:T(8,128)S(1)} %copy-done.5, s32[1,2,4]{2,1,0:T(2,128)S(1)} %copy-done.6, bf16[1,2048,2048]{2,1,0:T(8,128)(2,1)} %mass_hbm.3, bf16[1,2048,1024]{2,1,0:T(8,128)(2,1)} %modes_hbm.3, ...), custom_call_target="tpu_custom_call" | custom-call | flops 5368709120 | bytes 12582912 | tf_op jit(solution)/shard_map/leaf_group/pallas_call | solution.py:176
  15.3 0.2 collective-permute-start.1
  15.5 0.0 collective-permute-done
  15.5 0.0 copy-done
  15.5 0.0 copy-done.1
  15.5 2.1 %collective-permute-start.2 = (f32[128,256]{1,0:T(8,128)S(1)}, f32[128,256]{1,0:T(8,128)S(1)}, u32[]{:S(2)}, u32[]{:S(2)}) collective-permute-start(f32[128,256]{1,0:T(8,128)S(1)} %pad_maximum_fusion.refs_2_.refs_1_), channel_id=1, source_target_pairs={{0,8},{4,12},{8,0},{12,4},{16,24},{20,28},{24,16},{28,20},{1,9},{5... | collective-permute-start | bytes 393224 | tf_op jit(solution)/shard_map/ppermute | solution.py:454
  17.6 2.6 %collective-permute-start.3 = (f32[128,256]{1,0:T(8,128)S(1)}, f32[128,256]{1,0:T(8,128)S(1)}, u32[]{:S(2)}, u32[]{:S(2)}) collective-permute-start(f32[128,256]{1,0:T(8,128)S(1)} %pad_maximum_fusion.refs_2_.refs_1_), channel_id=1, source_target_pairs={{0,16},{4,20},{8,24},{12,28},{16,0},{20,4},{24,8},{28,12},{1,17},{... | collective-permute-start | bytes 393224 | tf_op jit(solution)/shard_map/ppermute | solution.py:454
  20.2 0.0 collective-permute-start.4
  20.2 0.0 copy-done.4
  20.2 0.0 copy-done.7
  20.2 0.0 copy-start.2
  20.2 0.0 copy-start.3
  20.2 10.3 %leaf_top.1 = (f32[256,512]{1,0:T(8,128)S(1)}, f32[256,512]{1,0:T(8,128)S(1)}, f32[2,128,512]{2,1,0:T(8,128)S(1)}) custom-call(s32[1,16,16]{2,1,0:T(8,128)S(1)} %copy-done.5, s32[1,2,4]{2,1,0:T(2,128)S(1)} %copy-done.7, bf16[1,2048,2048]{2,1,0:T(8,128)(2,1)} %mass_hbm.3, bf16[1,2048,1024]{2,1,0:T(8,128)(2,1)} %modes_hbm.3, ...), custom_call_target="tpu_custom_call" | custom-call | flops 5368709120 | bytes 12582912 | tf_op jit(solution)/shard_map/leaf_top/pallas_call | solution.py:176
  30.5 0.0 collective-permute-done.2.refs_2_
  30.5 0.0 collective-permute-done.3.refs_3_
  30.6 0.0 collective-permute-done.4.refs_4_
  30.6 0.0 collective-permute-done.1.refs_0_.other_ref
  30.6 0.0 copy-done.2
  30.6 0.0 copy-done.3
  30.6 1.4 %prepare.1 = (f32[136,128]{1,0:T(8,128)S(1)}, f32[2,128,128]{2,1,0:T(8,128)S(1)}, f32[256,512]{1,0:T(8,128)S(1)}, f32[256,512]{1,0:T(8,128)S(1)}, f32[256,512]{1,0:T(8,128)S(1)}) custom-call(f32[256,512]{1,0:T(8,128)S(1)} %get-tuple-element.34.keep_in, f32[256,512]{1,0:T(8,128)S(1)} %get-tuple-element.35.send_ref, ...), custom_call_target="tpu_custom_call" | custom-call | flops 402653184 | bytes 3145728 | tf_op jit(solution)/shard_map/prepare/pallas_call | solution.py:272
  32.0 0.1 collective-permute-start.7
  32.1 1.4 %collective-permute-start.5 = (f32[136,128]{1,0:T(8,128)S(1)}, f32[136,128]{1,0:T(8,128)S(1)}, u32[]{:S(2)}, u32[]{:S(2)}) collective-permute-start(f32[136,128]{1,0:T(8,128)S(1)} %get-tuple-element.40.left_ref), channel_id=1, source_target_pairs={{0,8},{4,12},{8,0},{12,4},{16,24},{20,28},{24,16},{28,20},{1,9},{5... | collective-permute-start | bytes 208904 | tf_op jit(solution)/shard_map/ppermute | solution.py:454
  33.5 3.2 %collective-permute-done.5.right_ref = f32[136,128]{1,0:T(8,128)S(1)} collective-permute-done((f32[136,128]{1,0:T(8,128)S(1)}, f32[136,128]{1,0:T(8,128)S(1)}, u32[]{:S(2)}, u32[]{:S(2)}) %collective-permute-start.5) | collective-permute-done | bytes 69664 | tf_op jit(solution)/shard_map/ppermute | solution.py:454
  36.7 0.0 collective-permute-done.7.other_ref
  36.7 0.1 fold.6
  36.8 1.8 %collective-permute-start.9 = (f32[128,512]{1,0:T(8,128)S(1)}, f32[128,512]{1,0:T(8,128)S(1)}, u32[]{:S(2)}, u32[]{:S(2)}) collective-permute-start(f32[128,512]{1,0:T(8,128)S(1)} %get-tuple-element.43.refs_0_), channel_id=1, source_target_pairs={{0,2},{1,3},{2,0},{3,1},{4,6},{5,7},{6,4},{7,5},{8,10},{9,11},{10,... | collective-permute-start | bytes 786440 | tf_op jit(solution)/shard_map/ppermute | solution.py:454
  38.6 2.4 %collective-permute-start.6 = (f32[136,128]{1,0:T(8,128)S(1)}, f32[136,128]{1,0:T(8,128)S(1)}, u32[]{:S(2)}, u32[]{:S(2)}) collective-permute-start(f32[136,128]{1,0:T(8,128)S(1)} %add.5.refs_0_.left_ref), channel_id=1, source_target_pairs={{0,16},{4,20},{8,24},{12,28},{16,0},{20,4},{24,8},{28,12},{1,17},{... | collective-permute-start | bytes 208904 | tf_op jit(solution)/shard_map/ppermute | solution.py:454
  41.0 3.7 %collective-permute-done.6.right_ref = f32[136,128]{1,0:T(8,128)S(1)} collective-permute-done((f32[136,128]{1,0:T(8,128)S(1)}, f32[136,128]{1,0:T(8,128)S(1)}, u32[]{:S(2)}, u32[]{:S(2)}) %collective-permute-start.6) | collective-permute-done | bytes 69664 | tf_op jit(solution)/shard_map/ppermute | solution.py:454
  44.7 0.1 fold.8
  44.8 1.7 %collective-permute-start.14 = (f32[128,512]{1,0:T(8,128)S(1)}, f32[128,512]{1,0:T(8,128)S(1)}, u32[]{:S(2)}, u32[]{:S(2)}) collective-permute-start(f32[128,512]{1,0:T(8,128)S(1)} %get-tuple-element.47.refs_1_), channel_id=1, source_target_pairs={{0,16},{4,20},{8,24},{12,28},{16,0},{20,4},{24,8},{28,12},{1,17},{... | collective-permute-start | bytes 786440 | tf_op jit(solution)/shard_map/ppermute | solution.py:454
  46.5 1.5 %collective-permute-start.8 = (f32[136,128]{1,0:T(8,128)S(1)}, f32[136,128]{1,0:T(8,128)S(1)}, u32[]{:S(2)}, u32[]{:S(2)}) collective-permute-start(f32[136,128]{1,0:T(8,128)S(1)} %add.6.refs_0_.left_ref), channel_id=1, source_target_pairs={{0,4},{4,0},{8,12},{12,8},{16,20},{20,16},{24,28},{28,24},{1,5},{5... | collective-permute-start | bytes 208904 | tf_op jit(solution)/shard_map/ppermute | solution.py:454
  48.0 0.0 collective-permute-done.9.other_ref
  48.0 0.6 collective-permute-start.11
  48.6 2.2 %collective-permute-done.8.right_ref = f32[136,128]{1,0:T(8,128)S(1)} collective-permute-done((f32[136,128]{1,0:T(8,128)S(1)}, f32[136,128]{1,0:T(8,128)S(1)}, u32[]{:S(2)}, u32[]{:S(2)}) %collective-permute-start.8) | collective-permute-done | bytes 69664 | tf_op jit(solution)/shard_map/ppermute | solution.py:454
  50.8 0.1 collective-permute-start.10
  50.9 2.2 %collective-permute-done.11.other_ref = f32[64,512]{1,0:T(8,128)S(1)} collective-permute-done((f32[64,512]{1,0:T(8,128)S(1)}, f32[64,512]{1,0:T(8,128)S(1)}, u32[]{:S(2)}, u32[]{:S(2)}) %collective-permute-start.11) | collective-permute-done | bytes 131104 | tf_op jit(solution)/shard_map/ppermute | solution.py:454
  53.1 0.0 collective-permute-done.10.right_ref
  53.1 0.5 collective-permute-start.12
  53.6 1.3 %collective-permute-start.13 = (f32[32,512]{1,0:T(8,128)S(1)}, f32[32,512]{1,0:T(8,128)S(1)}, u32[]{:S(2)}, u32[]{:S(2)}) collective-permute-start(f32[32,512]{1,0:T(8,128)S(1)} %get-tuple-element.49.refs_0_), channel_id=1, source_target_pairs={{0,16},{4,20},{8,24},{12,28},{16,0},{20,4},{24,8},{28,12},{1,17},{... | collective-permute-start | bytes 196616 | tf_op jit(solution)/shard_map/ppermute | solution.py:454
  54.9 4.2 %collective-permute-done.13.other_ref = f32[32,512]{1,0:T(8,128)S(1)} collective-permute-done((f32[32,512]{1,0:T(8,128)S(1)}, f32[32,512]{1,0:T(8,128)S(1)}, u32[]{:S(2)}, u32[]{:S(2)}) %collective-permute-start.13) | collective-permute-done | bytes 65568 | tf_op jit(solution)/shard_map/ppermute | solution.py:454
  59.1 0.0 collective-permute-done.12.right_ref
  59.1 0.0 collective-permute-done.14.other_ref
  59.2 2.0 %collective-permute-start.15 = (f32[64,512]{1,0:T(8,128)S(1)}, f32[64,512]{1,0:T(8,128)S(1)}, u32[]{:S(2)}, u32[]{:S(2)}) collective-permute-start(f32[64,512]{1,0:T(8,128)S(1)} %get-tuple-element.58), channel_id=1, source_target_pairs={{0,8},{4,12},{8,0},{12,4},{16,24},{20,28},{24,16},{28,20},{1,9},{5... | collective-permute-start | bytes 393224 | tf_op jit(solution)/shard_map/ppermute | solution.py:454
  61.2 0.1 collective-permute-start.16
  61.3 7.2 %finish.1 = (f32[1,128,2,128]{3,2,1,0:T(2,128)}, f32[1,64,128]{2,1,0:T(8,128)}, f32[64,128]{1,0:T(8,128)}, f32[8,128]{1,0:T(8,128)S(1)}) custom-call(f32[136,128]{1,0:T(8,128)S(1)} %add.7.refs_0_.left_ref.near_ref, f32[136,128]{1,0:T(8,128)S(1)} %add.9.far_ref.refs_0_, f32[2,128,128]{2,1,0:T(8,128)S(1)} %get-tuple-element.52.terms_ref, ...), custom_call_target="tpu_custom_call" | custom-call | flops 41943040 | bytes 393216 | tf_op jit(solution)/shard_map/finish/pallas_call | solution.py:428
  68.5 0.0 collective-permute-done.16.top_other_ref
  68.5 0.0 collective-permute-done.15.other_ref
  68.5 0.7 last.1
  (10 shorter events, 0.2 us)
Async XLA Ops:
  1.4 14.1 %copy-start = (f32[64,128]{1,0:T(8,128)S(1)}, f32[64,128]{1,0:T(8,128)}, u32[]{:S(2)}) copy-start(f32[64,128]{1,0:T(8,128)} %top_basis_ref.1) | copy-start | bytes 98308
  1.4 14.1 %copy-start.1 = (f32[1,64,128]{2,1,0:T(8,128)S(1)}, f32[1,64,128]{2,1,0:T(8,128)}, u32[]{:S(2)}) copy-start(f32[1,64,128]{2,1,0:T(8,128)} %group_basis_ref.1) | copy-start | bytes 98308
  1.4 18.8 %copy-start.4 = (bf16[1,2048,128]{2,1,0:T(8,128)(2,1)S(1)}, bf16[1,2048,128]{2,1,0:T(8,128)(2,1)}, u32[]{:S(2)}) copy-start(bf16[1,2048,128]{2,1,0:T(8,128)(2,1)} %refs_0_.1) | copy-start | bytes 1572868
  1.4 14.1 %collective-permute-start = (f32[64,256]{1,0:T(8,128)S(1)}, f32[64,256]{1,0:T(8,128)S(1)}, u32[]{:S(2)}, u32[]{:S(2)}) collective-permute-start(f32[64,256]{1,0:T(8,128)S(1)} %pad_maximum_fusion.1.refs_0_), channel_id=1, source_target_pairs={{0,4},{4,0},{8,12},{12,8},{16,20},{20,16},{24,28},{28,24},{1,5},{5... | collective-permute-start | bytes 196616 | tf_op jit(solution)/shard_map/ppermute | solution.py:454
  4.4 0.7 %copy-start.5 = (s32[1,16,16]{2,1,0:T(8,128)S(1)}, s32[1,16,16]{2,1,0:T(8,128)}, u32[]{:S(2)}) copy-start(s32[1,16,16]{2,1,0:T(8,128)} %mask_ref.3) | copy-start | bytes 3076
  5.1 0.7 copy-start.6
  5.8 14.4 %copy-start.7 = (s32[1,2,4]{2,1,0:T(2,128)S(1)}, s32[1,2,4]{2,1,0:T(2,128)}, u32[]{:S(2)}) copy-start(s32[1,2,4]{2,1,0:T(2,128)} %map_ref.3) | copy-start | bytes 100
  15.3 15.2 %collective-permute-start.1 = (f32[256,512]{1,0:T(8,128)S(1)}, f32[256,512]{1,0:T(8,128)S(1)}, u32[]{:S(2)}, u32[]{:S(2)}) collective-permute-start(f32[256,512]{1,0:T(8,128)S(1)} %get-tuple-element.35.send_ref), channel_id=1, source_target_pairs={{0,4},{4,0},{8,12},{12,8},{16,20},{20,16},{24,28},{28,24},{1,5},{5... | collective-permute-start | bytes 1572872 | tf_op jit(solution)/shard_map/ppermute | solution.py:454
  15.5 15.0 %collective-permute-start.2 = (f32[128,256]{1,0:T(8,128)S(1)}, f32[128,256]{1,0:T(8,128)S(1)}, u32[]{:S(2)}, u32[]{:S(2)}) collective-permute-start(f32[128,256]{1,0:T(8,128)S(1)} %pad_maximum_fusion.refs_2_.refs_1_), channel_id=1, source_target_pairs={{0,8},{4,12},{8,0},{12,4},{16,24},{20,28},{24,16},{28,20},{1,9},{5... | collective-permute-start | bytes 393224 | tf_op jit(solution)/shard_map/ppermute | solution.py:454
  17.6 13.0 %collective-permute-start.3 = (f32[128,256]{1,0:T(8,128)S(1)}, f32[128,256]{1,0:T(8,128)S(1)}, u32[]{:S(2)}, u32[]{:S(2)}) collective-permute-start(f32[128,256]{1,0:T(8,128)S(1)} %pad_maximum_fusion.refs_2_.refs_1_), channel_id=1, source_target_pairs={{0,16},{4,20},{8,24},{12,28},{16,0},{20,4},{24,8},{28,12},{1,17},{... | collective-permute-start | bytes 393224 | tf_op jit(solution)/shard_map/ppermute | solution.py:454
  20.2 10.4 %collective-permute-start.4 = (f32[128,256]{1,0:T(8,128)S(1)}, f32[128,256]{1,0:T(8,128)S(1)}, u32[]{:S(2)}, u32[]{:S(2)}) collective-permute-start(f32[128,256]{1,0:T(8,128)S(1)} %pad_maximum_fusion.refs_2_.refs_1_), channel_id=1, source_target_pairs={{0,24},{4,28},{8,16},{12,20},{16,8},{20,12},{24,0},{28,4},{1,25},{... | collective-permute-start | bytes 393224 | tf_op jit(solution)/shard_map/ppermute | solution.py:454
  20.2 10.4 %copy-start.2 = (f32[1,64,512]{2,1,0:T(8,128)S(1)}, f32[1,64,512]{2,1,0:T(8,128)}, u32[]{:S(2)}) copy-start(f32[1,64,512]{2,1,0:T(8,128)} %group_own_ref.1) | copy-start | bytes 393220
  20.2 10.4 %copy-start.3 = (f32[16,512]{1,0:T(8,128)S(1)}, f32[16,512]{1,0:T(8,128)}, u32[]{:S(2)}) copy-start(f32[16,512]{1,0:T(8,128)} %top_own_ref.1) | copy-start | bytes 98308
  32.0 4.7 %collective-permute-start.7 = (f32[256,512]{1,0:T(8,128)S(1)}, f32[256,512]{1,0:T(8,128)S(1)}, u32[]{:S(2)}, u32[]{:S(2)}) collective-permute-start(f32[256,512]{1,0:T(8,128)S(1)} %get-tuple-element.42), channel_id=1, source_target_pairs={{0,1},{1,0},{2,3},{3,2},{4,5},{5,4},{6,7},{7,6},{8,9},{9,8},{10,11... | collective-permute-start | bytes 1572872 | tf_op jit(solution)/shard_map/ppermute | solution.py:454
  32.1 4.6 %collective-permute-start.5 = (f32[136,128]{1,0:T(8,128)S(1)}, f32[136,128]{1,0:T(8,128)S(1)}, u32[]{:S(2)}, u32[]{:S(2)}) collective-permute-start(f32[136,128]{1,0:T(8,128)S(1)} %get-tuple-element.40.left_ref), channel_id=1, source_target_pairs={{0,8},{4,12},{8,0},{12,4},{16,24},{20,28},{24,16},{28,20},{1,9},{5... | collective-permute-start | bytes 208904 | tf_op jit(solution)/shard_map/ppermute | solution.py:454
  36.8 11.2 %collective-permute-start.9 = (f32[128,512]{1,0:T(8,128)S(1)}, f32[128,512]{1,0:T(8,128)S(1)}, u32[]{:S(2)}, u32[]{:S(2)}) collective-permute-start(f32[128,512]{1,0:T(8,128)S(1)} %get-tuple-element.43.refs_0_), channel_id=1, source_target_pairs={{0,2},{1,3},{2,0},{3,1},{4,6},{5,7},{6,4},{7,5},{8,10},{9,11},{10,... | collective-permute-start | bytes 786440 | tf_op jit(solution)/shard_map/ppermute | solution.py:454
  38.6 6.0 %collective-permute-start.6 = (f32[136,128]{1,0:T(8,128)S(1)}, f32[136,128]{1,0:T(8,128)S(1)}, u32[]{:S(2)}, u32[]{:S(2)}) collective-permute-start(f32[136,128]{1,0:T(8,128)S(1)} %add.5.refs_0_.left_ref), channel_id=1, source_target_pairs={{0,16},{4,20},{8,24},{12,28},{16,0},{20,4},{24,8},{28,12},{1,17},{... | collective-permute-start | bytes 208904 | tf_op jit(solution)/shard_map/ppermute | solution.py:454
  44.8 14.4 %collective-permute-start.14 = (f32[128,512]{1,0:T(8,128)S(1)}, f32[128,512]{1,0:T(8,128)S(1)}, u32[]{:S(2)}, u32[]{:S(2)}) collective-permute-start(f32[128,512]{1,0:T(8,128)S(1)} %get-tuple-element.47.refs_1_), channel_id=1, source_target_pairs={{0,16},{4,20},{8,24},{12,28},{16,0},{20,4},{24,8},{28,12},{1,17},{... | collective-permute-start | bytes 786440 | tf_op jit(solution)/shard_map/ppermute | solution.py:454
  46.5 4.3 %collective-permute-start.8 = (f32[136,128]{1,0:T(8,128)S(1)}, f32[136,128]{1,0:T(8,128)S(1)}, u32[]{:S(2)}, u32[]{:S(2)}) collective-permute-start(f32[136,128]{1,0:T(8,128)S(1)} %add.6.refs_0_.left_ref), channel_id=1, source_target_pairs={{0,4},{4,0},{8,12},{12,8},{16,20},{20,16},{24,28},{28,24},{1,5},{5... | collective-permute-start | bytes 208904 | tf_op jit(solution)/shard_map/ppermute | solution.py:454
  48.0 5.0 %collective-permute-start.11 = (f32[64,512]{1,0:T(8,128)S(1)}, f32[64,512]{1,0:T(8,128)S(1)}, u32[]{:S(2)}, u32[]{:S(2)}) collective-permute-start(f32[64,512]{1,0:T(8,128)S(1)} %get-tuple-element.45.refs_0_), channel_id=1, source_target_pairs={{0,4},{4,0},{8,12},{12,8},{16,20},{20,16},{24,28},{28,24},{1,5},{5... | collective-permute-start | bytes 393224 | tf_op jit(solution)/shard_map/ppermute | solution.py:454
  50.8 2.3 %collective-permute-start.10 = (f32[136,128]{1,0:T(8,128)S(1)}, f32[136,128]{1,0:T(8,128)S(1)}, u32[]{:S(2)}, u32[]{:S(2)}) collective-permute-start(f32[136,128]{1,0:T(8,128)S(1)} %add.7.refs_0_.left_ref.near_ref), channel_id=1, source_target_pairs={{0,1},{1,0},{2,3},{3,2},{4,5},{5,4},{6,7},{7,6},{8,9},{9,8},{10,11... | collective-permute-start | bytes 208904 | tf_op jit(solution)/shard_map/ppermute | solution.py:454
  53.1 6.0 %collective-permute-start.12 = (f32[136,128]{1,0:T(8,128)S(1)}, f32[136,128]{1,0:T(8,128)S(1)}, u32[]{:S(2)}, u32[]{:S(2)}) collective-permute-start(f32[136,128]{1,0:T(8,128)S(1)} %add.8.refs_0_.left_ref), channel_id=1, source_target_pairs={{0,2},{1,3},{2,0},{3,1},{4,6},{5,7},{6,4},{7,5},{8,10},{9,11},{10,... | collective-permute-start | bytes 208904 | tf_op jit(solution)/shard_map/ppermute | solution.py:454
  53.6 5.4 %collective-permute-start.13 = (f32[32,512]{1,0:T(8,128)S(1)}, f32[32,512]{1,0:T(8,128)S(1)}, u32[]{:S(2)}, u32[]{:S(2)}) collective-permute-start(f32[32,512]{1,0:T(8,128)S(1)} %get-tuple-element.49.refs_0_), channel_id=1, source_target_pairs={{0,16},{4,20},{8,24},{12,28},{16,0},{20,4},{24,8},{28,12},{1,17},{... | collective-permute-start | bytes 196616 | tf_op jit(solution)/shard_map/ppermute | solution.py:454
  59.2 9.3 %collective-permute-start.15 = (f32[64,512]{1,0:T(8,128)S(1)}, f32[64,512]{1,0:T(8,128)S(1)}, u32[]{:S(2)}, u32[]{:S(2)}) collective-permute-start(f32[64,512]{1,0:T(8,128)S(1)} %get-tuple-element.58), channel_id=1, source_target_pairs={{0,8},{4,12},{8,0},{12,4},{16,24},{20,28},{24,16},{28,20},{1,9},{5... | collective-permute-start | bytes 393224 | tf_op jit(solution)/shard_map/ppermute | solution.py:454
  61.2 7.3 %collective-permute-start.16 = (f32[16,512]{1,0:T(8,128)S(1)}, f32[16,512]{1,0:T(8,128)S(1)}, u32[]{:S(2)}, u32[]{:S(2)}) collective-permute-start(f32[16,512]{1,0:T(8,128)S(1)} %get-tuple-element.51.refs_0_), channel_id=1, source_target_pairs={{0,8},{4,12},{8,0},{12,4},{16,24},{20,28},{24,16},{28,20},{1,9},{5... | collective-permute-start | bytes 98312 | tf_op jit(solution)/shard_map/ppermute | solution.py:454
